TPU v7x, 512 devices: a whole 4x8x8 slice. The times are simulated.
512 devices in a mesh: rep: 2 (over core), tab: 32 (over z, y_hi), tp: 8 (over y_lo, x).
Axes of the slice: x: 4, y: 8 (y_hi: 4, y_lo: 2; y = y_hi * 2 + y_lo), z: 8, core: 2. Of those that a mesh axis runs over, the one named last changes fastest.
Arguments:
- emb_rows: bfloat16 [512, 800, 512], P(('rep', 'tp'), 'tab'), may hold values from -6 to 6
- width_steps: int32 [800], P('tab'), may hold values from 1 to 8
- proj_weight: bfloat16 [800, 512, 192], P('tab', None, ('rep', 'tp')), may hold values from -0.25 to 0.25
- fm_weight: bfloat16 [400, 800], P('tp'), may hold values from -0.21875 to 0.21875
- lcb_weight: bfloat16 [400, 800], P('tp'), may hold values from -0.21875 to 0.21875
- mix_weight: bfloat16 [800, 192], P('tp'), may hold values from -1.796875 to 1.796875
- fm_cot: bfloat16 [512, 400, 192], P(('rep', 'tp', 'tab')), may hold values from -6 to 6
- lcb_cot: bfloat16 [512, 400, 192], P(('rep', 'tp', 'tab')), may hold values from -6 to 6
Outputs:
- fm_out: bfloat16 [512, 400, 192], P(('rep', 'tp', 'tab'))
- lcb_out: bfloat16 [512, 400, 192], P(('rep', 'tp', 'tab'))
- grad_fm: float32 [400, 800], P('tp')
- grad_lcb: float32 [400, 800], P('tp')
All inputs are finite; a program needn't handle non-finite values.
Results may differ from a plain program's by a relative error of at most 0.0069.
Values may be sent and summed in bfloat16 or wider, within the bound.
No kernel may reach another device: no remote copies, remote signals or barrier semaphores. Data moves between devices by JAX's collectives and lax.ppermute only.
A program may use at most 64 MiB of HBM per device.

v0:
```python
import jax
import jax.numpy as jnp
from jax import lax
from jax.sharding import PartitionSpec as P

epsilon = 1e-06


def rms_norm(values):
    inv_rms = lax.rsqrt(jnp.mean(values * values, axis=-1, keepdims=True) + epsilon)
    return (values * inv_rms, inv_rms)


def rms_back(values, grad_in):
    normed, inv_rms = rms_norm(values)
    return inv_rms * (grad_in - normed * jnp.mean(grad_in * normed, axis=-1, keepdims=True))


def per_device(
    emb_rows, width_steps, proj_weight, fm_weight, lcb_weight, mix_weight, fm_cot, lcb_cot
):
    table_count = emb_rows.shape[1]
    widest = emb_rows.shape[2]
    columns = lax.broadcasted_iota(jnp.int32, (table_count, widest), 1)
    keep_mask = (columns < widest // 8 * width_steps[:, None]).astype(jnp.bfloat16)
    masked = lax.all_gather(proj_weight, ("rep", "tp"), axis=2, tiled=True) * keep_mask[:, :, None]
    projected = jnp.einsum(
        "nfw,fwc->nfc", emb_rows, masked, preferred_element_type=jnp.float32
    ).astype(jnp.bfloat16)
    features = lax.all_to_all(projected, "tab", split_axis=0, concat_axis=1, tiled=True)
    fm_full = lax.all_gather(fm_weight, "tp", axis=0, tiled=True)
    lcb_full = lax.all_gather(lcb_weight, "tp", axis=0, tiled=True)
    mix_full = lax.all_gather(mix_weight, "tp", axis=0, tiled=True)
    model_width = features.shape[2]
    feat_total = features.shape[1]
    fm_count = fm_full.shape[0]
    feat_wide = features.astype(jnp.float32)
    products = (
        jnp.einsum("sfd,sgd->sfg", features, features, preferred_element_type=jnp.float32)
        / model_width
    ).astype(jnp.bfloat16)
    mixed_rows = jnp.einsum(
        "sfg,gk->sfk", products, mix_full, preferred_element_type=jnp.float32
    ).astype(jnp.bfloat16)
    fm_pre = (
        jnp.einsum("nf,sfk->snk", fm_full, mixed_rows, preferred_element_type=jnp.float32)
        + feat_wide[:, :fm_count]
    )
    lcb_pre = (
        jnp.einsum("nf,sfd->snd", lcb_full, features, preferred_element_type=jnp.float32)
        + feat_wide[:, fm_count:]
    )
    fm_out = rms_norm(fm_pre)[0].astype(jnp.bfloat16)
    lcb_out = rms_norm(lcb_pre)[0].astype(jnp.bfloat16)
    fm_back = rms_back(fm_pre, fm_cot.astype(jnp.float32)).astype(jnp.bfloat16)
    lcb_back = rms_back(lcb_pre, lcb_cot.astype(jnp.float32)).astype(jnp.bfloat16)
    row_count = fm_count // lax.axis_size("tp")
    fm_term = jnp.einsum("snk,sfk->nf", fm_back, mixed_rows, preferred_element_type=jnp.float32)
    lcb_term = jnp.einsum("snd,sfd->nf", lcb_back, features, preferred_element_type=jnp.float32)
    grad_whole = lax.psum(jnp.concatenate([fm_term, lcb_term], axis=1), ("rep", "tab", "tp"))
    grad_mine = lax.dynamic_slice_in_dim(grad_whole, lax.axis_index("tp") * row_count, row_count, 0)
    return (fm_out, lcb_out, grad_mine[:, :feat_total], grad_mine[:, feat_total:])


def solution(mesh):
    in_specs = (
        P(("rep", "tp"), "tab", None),
        P("tab"),
        P("tab", None, ("rep", "tp")),
        P("tp", None),
        P("tp", None),
        P("tp", None),
        P(("rep", "tp", "tab"), None, None),
        P(("rep", "tp", "tab"), None, None),
    )
    out_specs = (
        P(("rep", "tp", "tab"), None, None),
        P(("rep", "tp", "tab"), None, None),
        P("tp", None),
        P("tp", None),
    )
    return jax.shard_map(
        per_device, mesh=mesh, in_specs=in_specs, out_specs=out_specs, check_vma=False
    )
```

profile of v0, /device:TPU:1, one launch (start us, length us, event | category | flops | bytes accessed | tf_op | source)
XLA Modules:
  0.0 485.0 jit_solution(9569098839905885530)
XLA Ops:
  7.2 0.0 copy-start
  7.2 0.0 all-gather.5.cloned.1.call-start
  7.2 0.7 all-gather.5.cloned.1.call-update
  7.9 0.7 broadcast_multiply_fusion.3
  8.6 0.1 fusion.29
  8.7 55.1 %all-gather.5.cloned.1.call-done = bf16[25,512,192]{1,0,2:T(8,128)(2,1)} async-done(((bf16[25,512,12]{1,0,2:T(8,128)(2,1)}), bf16[25,512,192]{1,0,2:T(8,128)(2,1)}) %all-gather.5.cloned.1.call-update) | async-done | bytes 4915216 | tf_op jit(solution)/shard_map/all_gather | solution.py:26
  63.7 3.2 broadcast_multiply_fusion
  66.9 0.0 copy-done
  67.0 0.0 copy-start.6
  67.0 5.3 %fusion.8 = bf16[32,25,192]{2,0,1:T(8,128)(2,1)S(1)} fusion(bf16[32,25,512]{2,0,1:T(8,128)(2,1)S(1)} %copy-done, bf16[25,512,192]{1,0,2:T(8,128)(2,1)S(1)} %broadcast_multiply_fusion), kind=kOutput, calls=%fused_computation.9 | convolution fusion | flops 157440000 | bytes 6041600 | tf_op jit(solution)/shard_map/nfw,fwc->nfc/dot_general | solution.py:27
  72.3 0.0 copy-start.4
  72.3 1.0 copy.20
  73.3 0.0 copy-start.5
  73.3 12.4 %all-to-all-start = ((bf16[32,25,192]{2,1,0:T(8,128)(2,1)}), bf16[32,25,192]{2,1,0:T(8,128)(2,1)S(1)}, u32[]{:S(2)}, u32[]{:S(2)}) async-start(bf16[32,25,192]{2,1,0:T(8,128)(2,1)} %copy.20), calls=%async_computation | async-start | bytes 1048576 | tf_op jit(solution)/shard_map/all_to_all | solution.py:30
  85.7 0.0 all-reduce.2.cloned.1.call-start
  85.8 0.0 copy-done.6
  85.8 32.2 %all-gather = bf16[8,100,192]{1,2,0:T(8,128)(2,1)S(1)} all-gather(bf16[1,100,192]{1,2,0:T(8,128)(2,1)S(1)} %bitcast.37), channel_id=1, replica_groups=mesh['rep'=2,'tab'=32,'tp'=8] {'tp'}, dimensions={0}, use_global_device_ids=true | all-gather | bytes 345600 | tf_op jit(solution)/shard_map/all_gather | solution.py:33
  117.9 0.3 copy.21
  118.2 1.0 reshape.124
  119.2 0.0 copy-done.4
  119.2 23.4 %all-gather.1 = bf16[8,50,800]{2,1,0:T(8,128)(2,1)S(1)} all-gather(bf16[1,50,800]{2,1,0:T(8,128)(2,1)S(1)} %bitcast.35), channel_id=1, replica_groups=mesh['rep'=2,'tab'=32,'tp'=8] {'tp'}, dimensions={0}, use_global_device_ids=true | all-gather | bytes 720000 | tf_op jit(solution)/shard_map/all_gather | solution.py:31
  142.7 1.2 reshape.126
  143.9 0.0 copy-done.5
  143.9 23.1 %all-gather.2 = bf16[8,50,800]{2,1,0:T(8,128)(2,1)S(1)} all-gather(bf16[1,50,800]{2,1,0:T(8,128)(2,1)S(1)} %bitcast.36), channel_id=1, replica_groups=mesh['rep'=2,'tab'=32,'tp'=8] {'tp'}, dimensions={0}, use_global_device_ids=true | all-gather | bytes 720000 | tf_op jit(solution)/shard_map/all_gather | solution.py:32
  167.0 0.3 reshape.128
  167.3 0.0 all-to-all-done
  167.4 0.2 reshape.122
  167.6 0.8 fusion.32
  168.4 0.0 copy-start.1
  168.4 0.9 copy.24
  169.3 0.2 reshape.119
  169.5 2.1 fusion.7
  171.6 0.0 copy-done.1
  171.7 1.4 multiply_reduce_fusion.1
  173.1 0.0 copy-start.2
  173.1 1.2 copy.25
  174.3 0.0 copy-start.3
  174.3 0.5 multiply_reduce_fusion
  174.8 0.0 copy-done.2
  174.8 1.8 fusion.13
  176.7 0.4 fusion.23
  177.1 0.0 copy-done.3
  177.1 0.5 fusion.20
  177.6 2.0 pad_maximum_fusion
  179.6 0.0 all-reduce.2.cloned.1.call-update
  179.6 296.7 %all-reduce.2.cloned.1.call-done = f32[400,1600]{1,0:T(8,128)} async-done(((f32[400,1600]{1,0:T(8,128)}), f32[400,1600]{1,0:T(8,128)}) %all-reduce.2.cloned.1.call-update) | async-done | bytes 2560016 | tf_op jit(solution)/shard_map/psum | solution.py:60
  476.3 1.9 fusion.31
  (4 shorter events, 0.0 us)
Async XLA Ops:
  7.2 59.8 %copy-start = (bf16[32,25,512]{2,0,1:T(8,128)(2,1)S(1)}, bf16[32,25,512]{2,0,1:T(8,128)(2,1)}, u32[]{:S(2)}) copy-start(bf16[32,25,512]{2,0,1:T(8,128)(2,1)} %param.8) | copy-start | bytes 2457604
  7.2 56.6 %all-gather.5.cloned.1.call-start = ((), (), s32[]{:S(2)}) async-start(), calls=%async_computation.1 | async-start | bytes 6684672 | tf_op jit(solution)/shard_map/all_gather | solution.py:26
  67.0 18.8 %copy-start.6 = (bf16[100,192]{0,1:T(8,128)(2,1)S(1)}, bf16[100,192]{0,1:T(8,128)(2,1)}, u32[]{:S(2)}) copy-start(bf16[100,192]{0,1:T(8,128)(2,1)} %param.13) | copy-start | bytes 115204
  72.3 47.0 %copy-start.4 = (bf16[50,800]{1,0:T(8,128)(2,1)S(1)}, bf16[50,800]{1,0:T(8,128)(2,1)}, u32[]{:S(2)}) copy-start(bf16[50,800]{1,0:T(8,128)(2,1)} %param.11) | copy-start | bytes 240004
  73.3 70.5 %copy-start.5 = (bf16[50,800]{1,0:T(8,128)(2,1)S(1)}, bf16[50,800]{1,0:T(8,128)(2,1)}, u32[]{:S(2)}) copy-start(bf16[50,800]{1,0:T(8,128)(2,1)} %param.12) | copy-start | bytes 240004
  73.3 94.0 %all-to-all-start = ((bf16[32,25,192]{2,1,0:T(8,128)(2,1)}), bf16[32,25,192]{2,1,0:T(8,128)(2,1)S(1)}, u32[]{:S(2)}, u32[]{:S(2)}) async-start(bf16[32,25,192]{2,1,0:T(8,128)(2,1)} %copy.20), calls=%async_computation | async-start | bytes 1048576 | tf_op jit(solution)/shard_map/all_to_all | solution.py:30
  85.7 390.6 %all-reduce.2.cloned.1.call-start = ((), (), s32[]{:S(2)}) async-start(), calls=%async_computation.2 | async-start | bytes 5324800 | tf_op jit(solution)/shard_map/psum | solution.py:60
  168.4 3.3 copy-start.1
  173.1 1.8 copy-start.2
  174.3 2.8 copy-start.3
Sparse Core Ops, SparseCore 0:
  10.2 53.5 all-gather.4
  179.7 296.5 all-reduce.1
where the time goes:
time: 485 us
  waiting for transfers between devices  352 us (73%)
  blocking collectives  78.7 us (16%)
  between operations  14.2 us (3%)
  starting transfers between devices  12.5 us (3%)
  matrix products  10.2 us (2%)
  local copies, waits for them, and re-layouts  9.15 us (2%)
  other arithmetic  7.75 us (2%)
    psum x1, waiting for transfers between devices, per_device(): lax.psum(jnp.concatenate([fm_term, lcb_term], axis=1), ('rep', 'tab', 'tp'))  297 us
    all_gather x1, waiting for transfers between devices, per_device(): lax.all_gather(proj_weight, ('rep', 'tp'), axis=2, tiled=True)  55.1 us
    all_gather x1, blocking collectives, per_device(): mix_full = lax.all_gather(mix_weight, 'tp', axis=0, tiled=True)  32.2 us
    all_gather x1, blocking collectives, per_device(): fm_full = lax.all_gather(fm_weight, 'tp', axis=0, tiled=True)  23.4 us
    all_gather x1, blocking collectives, per_device(): lcb_full = lax.all_gather(lcb_weight, 'tp', axis=0, tiled=True)  23.1 us
    all_to_all x1, starting transfers between devices, per_device(): lax.all_to_all(projected, 'tab', split_axis=0, concat_axis=1, tiled=True)  12.4 us
  transfers between devices with their start and end apart: 3, of which 2 were waited for; matrix products, arithmetic and copies ran while one was open for 1% of the time, Pallas kernels for 0%

commit v1 on v0

v1 whole, which is shorter than its diff:
```python
import functools

import jax
import jax.numpy as jnp
from jax import lax
from jax.experimental import pallas as pl
from jax.experimental.pallas import tpu as pltpu
from jax.sharding import Mesh
from jax.sharding import PartitionSpec as P

F32 = jnp.float32
BF16 = jnp.bfloat16
EPS = 1e-06
VMEM_LIMIT = 48 * 1024 * 1024
SWAP = [(0, 1), (1, 0)]
TAB = ("z", "yh")
TP = ("yl", "x")

VM = pl.BlockSpec(memory_space=pltpu.VMEM)
SM = pl.BlockSpec(memory_space=pltpu.SMEM)


def call(kernel, outs, ins, scratch=(), smem=0, flops=0, size=0):
    return pl.pallas_call(
        kernel,
        out_shape=outs,
        in_specs=[SM] * smem + [VM] * (len(ins) - smem),
        out_specs=jax.tree.map(lambda _: VM, outs),
        scratch_shapes=list(scratch),
        compiler_params=pltpu.CompilerParams(vmem_limit_bytes=VMEM_LIMIT),
        cost_estimate=pl.CostEstimate(flops=flops, bytes_accessed=size, transcendentals=0),
    )(*ins)


def nt_dot(a, b):
    return lax.dot_general(a, b, (((1,), (1,)), ((), ())), preferred_element_type=F32)


def nn_dot(a, b):
    return lax.dot_general(a, b, (((1,), (0,)), ((), ())), preferred_element_type=F32)


def pack_kernel(fm_ref, lcb_ref, mix_ref, out_ref):
    out_ref[...] = jnp.zeros_like(out_ref)
    rows, cols = fm_ref.shape
    for k, ref in enumerate((fm_ref, lcb_ref)):
        for j in range(7):
            wide = min(128, cols - 128 * j)
            out_ref[k * 7 + j, :rows, :wide] = ref[:, 128 * j : 128 * j + wide]
    for j in range(4):
        out_ref[14 + j, :48, : mix_ref.shape[1]] = mix_ref[48 * j : 48 * j + 48, :]


def unpack_kernel(all_ref, fm_ref, lcb_ref, mix_ref, wide_ref, mixw_ref):
    for k, ref in enumerate((fm_ref, lcb_ref)):
        for i in range(8):
            for j in range(7):
                wide_ref[50 * i : 50 * i + 50, 128 * j : 128 * j + 128] = all_ref[i, 7 * k + j][:50].astype(F32)
        ref[...] = wide_ref[:, :800].astype(BF16)
    for i in range(8):
        for j in range(4):
            mixw_ref[48 * j : 48 * j + 48, 100 * i : 100 * i + 100] = all_ref[i, 14 + j][:48, :100].astype(F32)
    mix_ref[...] = mixw_ref[...].astype(BF16)


def project_kernel(idx_ref, emb_ref, emb_y_ref, *rest):
    w_refs, out_ref, acc_ref = rest[:-2], rest[-2], rest[-1]
    mine = idx_ref[0]
    tables, samples = emb_ref.shape[0], emb_ref.shape[1]
    for t in range(tables):
        weight = jnp.concatenate([ref[t] for ref in w_refs], axis=0)
        acc_ref[mine, pl.ds(t, samples, stride=32), :] = nt_dot(emb_ref[t], weight)
        acc_ref[1 - mine, pl.ds(t, samples, stride=32), :] = nt_dot(emb_y_ref[t], weight)
    for k in range(2):
        out_ref[k * samples : k * samples + samples] = acc_ref[k].reshape(samples, 32, 128).astype(BF16)


def rows_kernel(idx_ref, recv_ref, fm_ref, lcb_ref, mix_ref, fcot_ref, lcot_ref,
                fo_ref, lo_ref, keep_ref, send_ref, scr_ref, gt_ref, ft_ref, bf_ref, bl_ref):
    x, rep = idx_ref[1], idx_ref[2]
    for yl in range(2):
        for tab in range(32):
            scr_ref[yl, 25 * tab : 25 * tab + 25, :] = recv_ref[yl * 32 + tab][:25].astype(F32)
        gt_ref[yl] = scr_ref[yl].T
    for r in range(2):
        for yl in range(2):
            for place in range(4):
                far = lax.rem(place - x + 4, 4)
                start = pl.multiple_of((r + rep - 2 * r * rep) * 64 + far * 16, 16)
                row = r * 96 + yl * 48 + place * 12
                ft_ref[row : row + 12, :] = gt_ref[yl, pl.ds(start, 16), :][:12]
    feat = ft_ref[...]
    feat_b = feat.astype(BF16)
    inner = nt_dot(mix_ref[...], feat_b).astype(BF16)
    mixed_b = (nn_dot(inner, feat_b) * (1.0 / 192)).astype(BF16)

    def branch(rows, weight_ref, skip, cot_ref, out_ref, back_ref):
        pre = nt_dot(rows, weight_ref[...]) + skip
        inv = lax.rsqrt(jnp.sum(pre * pre, axis=0, keepdims=True) * (1.0 / 192) + EPS)
        normed = pre * inv
        out_ref[...] = normed.astype(BF16)
        cot = cot_ref[...].astype(F32)
        mean = jnp.sum(cot * normed, axis=0, keepdims=True) * (1.0 / 192)
        back = (inv * (cot - normed * mean)).T
        back_ref[...] = jnp.zeros_like(back_ref)
        for i in range(8):
            back_ref[56 * i : 56 * i + 50, :] = back[50 * i : 50 * i + 50]
        return back_ref[...].astype(BF16)

    back_l = branch(feat_b, lcb_ref, ft_ref[:, 400:800], lcot_ref, lo_ref, bl_ref)
    back_f = branch(mixed_b, fm_ref, ft_ref[:, :400], fcot_ref, fo_ref, bf_ref)
    first = jnp.full((1, 1), rep, jnp.int32) == 0
    keep = nn_dot(jnp.where(first, back_f, back_l), jnp.where(first, mixed_b, feat_b))
    send = nn_dot(jnp.where(first, back_l, back_f), jnp.where(first, feat_b, mixed_b))
    for i in range(8):
        keep_ref[i] = keep[56 * i : 56 * i + 56].astype(BF16)
        send_ref[i] = send[56 * i : 56 * i + 56].astype(BF16)


def per_device(emb_rows, width_steps, proj_weight, fm_weight, lcb_weight, mix_weight, fm_cot, lcb_cot):
    tables, widest = emb_rows.shape[1], emb_rows.shape[2]
    yl, x, rep = lax.axis_index("yl"), lax.axis_index("x"), lax.axis_index("rep")
    idx = jnp.stack([yl, x, rep]).astype(jnp.int32)

    emb = jnp.transpose(emb_rows, (1, 0, 2))
    emb_y = lax.ppermute(emb, "yl", SWAP)

    packed = call(
        pack_kernel,
        jax.ShapeDtypeStruct((18, 56, 128), BF16),
        [fm_weight, lcb_weight, mix_weight.T],
    )
    small = lax.all_gather(packed, TP)

    columns = lax.broadcasted_iota(jnp.int32, (tables, 1, widest), 2)
    keep_mask = columns < widest // 8 * width_steps[:, None, None]
    own = jnp.where(keep_mask, jnp.transpose(proj_weight, (0, 2, 1)), 0).astype(BF16)
    own = jnp.pad(own, ((0, 0), (0, 4), (0, 0)))
    up, down = [(i, (i + 1) % 4) for i in range(4)], [(i, (i + 3) % 4) for i in range(4)]
    half = (tables + 1) // 2
    before = lax.ppermute(own, "x", up)
    after = lax.ppermute(own, "x", down)
    far_a = lax.ppermute(before[:half], "x", up)
    far_b = lax.ppermute(after[half:], "x", down)
    far = jnp.concatenate([far_a, far_b], axis=0)
    mine = [own, after, far, before]
    other = [lax.ppermute(w, "rep", SWAP) for w in mine]

    chunks = call(
        project_kernel,
        jax.ShapeDtypeStruct((64, 32, 128), BF16),
        [idx, emb, emb_y] + mine + other,
        [pltpu.VMEM((2, 1024, 128), F32)],
        smem=1,
        flops=2 * 25 * 64 * 128 * 512,
        size=5 << 20,
    )
    recv = lax.all_to_all(chunks, ("yl",) + TAB, 0, 0, tiled=True)

    fm_full, lcb_full, mix_full = call(
        unpack_kernel,
        (
            jax.ShapeDtypeStruct((400, 800), BF16),
            jax.ShapeDtypeStruct((400, 800), BF16),
            jax.ShapeDtypeStruct((192, 800), BF16),
        ),
        [small],
        [pltpu.VMEM((400, 896), F32), pltpu.VMEM((192, 800), F32)],
        size=4 << 20,
    )
    branch_out = jax.ShapeDtypeStruct((192, 400), BF16)
    partial = jax.ShapeDtypeStruct((8, 56, 800), BF16)
    fm_out, lcb_out, keep, send = call(
        rows_kernel,
        (branch_out, branch_out, partial, partial),
        [idx, recv, fm_full, lcb_full, mix_full, fm_cot[0].T, lcb_cot[0].T],
        [
            pltpu.VMEM((2, 800, 128), F32),
            pltpu.VMEM((2, 128, 800), F32),
            pltpu.VMEM((192, 800), F32),
            pltpu.VMEM((448, 192), F32),
            pltpu.VMEM((448, 192), F32),
        ],
        smem=1,
        flops=700_000_000,
        size=5 << 20,
    )

    got = lax.ppermute(send, "rep", SWAP)
    pair = (keep.astype(F32) + got.astype(F32)).astype(BF16)
    shares = lax.all_to_all(pair, TP, 0, 0, tiled=True)
    share = jnp.sum(shares.astype(F32), axis=0).astype(BF16)
    share = jnp.pad(share, ((0, 8), (0, 224)))
    tiles = jnp.transpose(share.reshape(4, 16, 8, 128), (2, 0, 1, 3)).reshape(32, 16, 128)
    parts = lax.all_to_all(tiles, TAB, 0, 0, tiled=True)
    whole = jnp.sum(parts.astype(F32), axis=0).astype(BF16)
    spread = lax.all_to_all(jnp.broadcast_to(whole[None], (32, 16, 128)), TAB, 0, 0, tiled=True)
    swapped = lax.ppermute(spread, "rep", SWAP)

    def rows_of(blocks):
        wide = jnp.transpose(blocks.reshape(8, 4, 16, 128), (1, 2, 0, 3)).reshape(64, 1024)
        return wide[:50, :800].astype(F32)

    grad_a, grad_b = rows_of(spread), rows_of(swapped)
    first = rep == 0
    grad_fm = jnp.where(first, grad_a, grad_b)
    grad_lcb = jnp.where(first, grad_b, grad_a)
    return fm_out.T[None], lcb_out.T[None], grad_fm, grad_lcb


def solution(mesh):
    fine = Mesh(mesh.devices.reshape(2, 8, 4, 2, 4), ("rep", "z", "yh", "yl", "x"))
    samples = ("rep", "yl", "x") + TAB
    in_specs = (
        P(("rep", "yl", "x"), TAB, None),
        P(TAB),
        P(TAB, None, ("rep", "yl", "x")),
        P(TP, None),
        P(TP, None),
        P(TP, None),
        P(samples, None, None),
        P(samples, None, None),
    )
    out_specs = (P(samples, None, None), P(samples, None, None), P(TP, None), P(TP, None))
    return jax.shard_map(per_device, mesh=fine, in_specs=in_specs, out_specs=out_specs, check_vma=False)
```

time: 485 us -> 176 us (0.36)
  waiting for transfers between devices: 352 us -> 35.6 us
  starting transfers between devices: 12.5 us -> 63.1 us
  blocking collectives: 78.7 us -> 45.2 us
  matrix products: 10.2 us -> 0 us
  Pallas kernels: 0 us -> 8.99 us
    psum x1 -> x0, waiting for transfers between devices: 297 us -> none  [per_device(): lax.psum(jnp.concatenate([fm_term, lcb_term], axis=1), ('rep', 'tab', 'tp'))]
    all_gather x3 -> x0, blocking collectives: 78.7 us -> none  [the longest x1 32.2 us: per_device(): mix_full = lax.all_gather(mix_weight, 'tp', axis=0, tiled=True)]
    all_gather x1, waiting for transfers between devices: 55.1 us -> 0.02 us  [per_device(): small = lax.all_gather(packed, TP)]
    all_to_all x0 -> x3, blocking collectives: none -> 45.2 us  [the longest x1 15.4 us: per_device(): shares = lax.all_to_all(pair, TP, 0, 0, tiled=True)]
    ppermute x0 -> x11, starting transfers between devices: none -> 44.5 us  [the longest x4 12 us: per_device(): other = [lax.ppermute(w, 'rep', SWAP) for w in mine]]
    ppermute x0 -> x11, waiting for transfers between devices: none -> 21.5 us  [the longest x1 15.3 us: per_device(): emb_y = lax.ppermute(emb, 'yl', SWAP)]
    all_to_all x1, waiting for transfers between devices: 0.01 us -> 14.1 us  [per_device(): recv = lax.all_to_all(chunks, ('yl',) + TAB, 0, 0, tiled=True)]
    dot_general x6 -> x0, matrix products: 10.2 us -> none  [the longest x1 5.3 us: per_device(): jnp.einsum('nfw,fwc->nfc', emb_rows, masked, preferred_element_type=jnp.f...]
  transfers between devices with their start and end apart: 3 -> 13, of which waited for: 2 -> 5; matrix products, arithmetic and copies ran while one was open for 1% -> 1% of each run, Pallas kernels for 0% -> 3%
where the time goes in v1:
time: 176 us; the launch traced here: 175 us
  starting transfers between devices  63.1 us (36%)
  blocking collectives  45.2 us (26%)
  waiting for transfers between devices  35.6 us (20%)
  between operations  14.3 us (8%)
  Pallas kernels  8.99 us (5%)
  local copies, waits for them, and re-layouts  4.62 us (3%)
  other arithmetic  3.19 us (2%)
    all_to_all x1, starting transfers between devices, per_device(): recv = lax.all_to_all(chunks, ('yl',) + TAB, 0, 0, tiled=True)  18.6 us
    all_to_all x1, blocking collectives, per_device(): shares = lax.all_to_all(pair, TP, 0, 0, tiled=True)  15.4 us
    all_to_all x1, blocking collectives, per_device(): parts = lax.all_to_all(tiles, TAB, 0, 0, tiled=True)  15.4 us
    ppermute x1, waiting for transfers between devices, per_device(): emb_y = lax.ppermute(emb, 'yl', SWAP)  15.3 us
    all_to_all x1, blocking collectives, per_device(): lax.all_to_all(jnp.broadcast_to(whole[None], (32, 16, 128)), TAB, 0, 0, t...  14.4 us
    all_to_all x1, waiting for transfers between devices, per_device(): recv = lax.all_to_all(chunks, ('yl',) + TAB, 0, 0, tiled=True)  14.1 us
    ppermute x4, starting transfers between devices, per_device(): other = [lax.ppermute(w, 'rep', SWAP) for w in mine]  12 us
    pallas_call x4, Pallas kernels, call(): pl.pallas_call(kernel, out_shape=outs, in_specs=[SM] * smem + [VM] * (len...  8.99 us
  transfers between devices with their start and end apart: 13, of which 5 were waited for; matrix products, arithmetic and copies ran while one was open for 1% of the time, Pallas kernels for 3%

profile of v1, /device:TPU:1, one launch (start us, length us, event | category | flops | bytes accessed | tf_op | source)
XLA Modules:
  0.0 175.1 jit_solution(14118251518054409096)
XLA Ops:
  7.2 0.0 copy-start.1
  7.2 0.0 all-gather.3.cloned.1.call-start
  7.2 0.0 copy-start.4
  7.2 0.9 copy-done.4
  8.2 0.0 copy-start.5
  8.2 0.9 copy-done.5
  9.1 0.0 copy-start.6
  9.1 0.8 copy-done.6
  9.9 0.8 shard_map.112
  10.7 0.0 all-gather.3.cloned.1.call-update
  10.7 0.7 broadcast_multiply_fusion
  11.3 0.1 iota_compare_fusion
  11.4 1.2 fusion
  12.7 3.9 %collective-permute-start.2 = (bf16[25,16,512]{2,1,0:T(8,128)(2,1)S(1)}, bf16[25,16,512]{2,1,0:T(8,128)(2,1)S(1)}, u32[]{:S(2)}, u32[]{:S(2)}) collective-permute-start(bf16[25,16,512]{2,1,0:T(8,128)(2,1)S(1)} %pad.8.rest_0_), channel_id=1, source_target_pairs={{0,1},{1,2},{2,3},{3,0},{4,5},{5,6},{6,7},{7,4},{8,9},{9,10},{10,1... | collective-permute-start | bytes 1228808 | tf_op jit(solution)/shard_map/ppermute | solution.py:141
  16.6 3.2 %collective-permute-start.1 = (bf16[25,16,512]{2,1,0:T(8,128)(2,1)S(1)}, bf16[25,16,512]{2,1,0:T(8,128)(2,1)S(1)}, u32[]{:S(2)}, u32[]{:S(2)}) collective-permute-start(bf16[25,16,512]{2,1,0:T(8,128)(2,1)S(1)} %pad.8.rest_0_), channel_id=1, source_target_pairs={{0,3},{1,0},{2,1},{3,2},{4,7},{5,4},{6,5},{7,6},{8,11},{9,8},{10,9... | collective-permute-start | bytes 1228808 | tf_op jit(solution)/shard_map/ppermute | solution.py:142
  19.8 3.4 %collective-permute-done.2.rest_3_ = bf16[25,16,512]{2,1,0:T(8,128)(2,1)S(1)} collective-permute-done((bf16[25,16,512]{2,1,0:T(8,128)(2,1)S(1)}, bf16[25,16,512]{2,1,0:T(8,128)(2,1)S(1)}, u32[]{:S(2)}, u32[]{:S(2)}) %collective-permute-start.2) | collective-permute-done | bytes 409632 | tf_op jit(solution)/shard_map/ppermute | solution.py:141
  23.3 4.6 %collective-permute-start.3 = (bf16[13,16,512]{2,1,0:T(8,128)(2,1)S(1)}, bf16[13,16,512]{2,1,0:T(8,128)(2,1)S(1)}, u32[]{:S(2)}, u32[]{:S(2)}) collective-permute-start(bf16[13,16,512]{2,1,0:T(8,128)(2,1)S(1)} %slice.16), channel_id=1, source_target_pairs={{0,1},{1,2},{2,3},{3,0},{4,5},{5,6},{6,7},{7,4},{8,9},{9,10},{10,1... | collective-permute-start | bytes 638984 | tf_op jit(solution)/shard_map/ppermute | solution.py:143
  27.9 0.0 copy-done.1
  27.9 4.2 %collective-permute-start = (bf16[25,32,512]{2,1,0:T(8,128)(2,1)S(1)}, bf16[25,32,512]{2,1,0:T(8,128)(2,1)S(1)}, u32[]{:S(2)}, u32[]{:S(2)}) collective-permute-start(bf16[25,32,512]{2,1,0:T(8,128)(2,1)S(1)} %bitcast.44), channel_id=1, source_target_pairs={{0,4},{4,0},{1,5},{5,1},{2,6},{6,2},{3,7},{7,3},{8,12},{12,8},{9,1... | collective-permute-start | bytes 2457608 | tf_op jit(solution)/shard_map/ppermute | solution.py:126
  32.1 0.0 collective-permute-done.1.rest_1_
  32.2 4.6 %collective-permute-start.4 = (bf16[12,16,512]{2,1,0:T(8,128)(2,1)S(1)}, bf16[12,16,512]{2,1,0:T(8,128)(2,1)S(1)}, u32[]{:S(2)}, u32[]{:S(2)}) collective-permute-start(bf16[12,16,512]{2,1,0:T(8,128)(2,1)S(1)} %slice.17), channel_id=1, source_target_pairs={{0,3},{1,0},{2,1},{3,2},{4,7},{5,4},{6,5},{7,6},{8,11},{9,8},{10,9... | collective-permute-start | bytes 589832 | tf_op jit(solution)/shard_map/ppermute | solution.py:144
  36.7 4.9 %collective-permute-start.5 = (bf16[25,16,512]{2,1,0:T(8,128)(2,1)S(1)}, bf16[25,16,512]{2,1,0:T(8,128)(2,1)}, u32[]{:S(2)}, u32[]{:S(2)}) collective-permute-start(bf16[25,16,512]{2,1,0:T(8,128)(2,1)S(1)} %pad.8.rest_0_), channel_id=1, source_target_pairs={{0,256},{256,0},{1,257},{257,1},{2,258},{258,2},{3,259},{259,3},{4... | collective-permute-start | bytes 1228808 | tf_op jit(solution)/shard_map/ppermute | solution.py:147
  41.6 1.9 %collective-permute-start.6 = (bf16[25,16,512]{2,1,0:T(8,128)(2,1)S(1)}, bf16[25,16,512]{2,1,0:T(8,128)(2,1)}, u32[]{:S(2)}, u32[]{:S(2)}) collective-permute-start(bf16[25,16,512]{2,1,0:T(8,128)(2,1)S(1)} %collective-permute-done.1.rest_1_), channel_id=1, source_target_pairs={{0,256},{256,0},{1,257},{257,1},{2,258},{258,2},{3,259},{259,3},{4... | collective-permute-start | bytes 1228808 | tf_op jit(solution)/shard_map/ppermute | solution.py:147
  43.5 0.0 collective-permute-done.3
  43.5 2.4 %collective-permute-start.8 = (bf16[25,16,512]{2,1,0:T(8,128)(2,1)S(1)}, bf16[25,16,512]{2,1,0:T(8,128)(2,1)}, u32[]{:S(2)}, u32[]{:S(2)}) collective-permute-start(bf16[25,16,512]{2,1,0:T(8,128)(2,1)S(1)} %collective-permute-done.2.rest_3_), channel_id=1, source_target_pairs={{0,256},{256,0},{1,257},{257,1},{2,258},{258,2},{3,259},{259,3},{4... | collective-permute-start | bytes 1228808 | tf_op jit(solution)/shard_map/ppermute | solution.py:147
  46.0 0.0 collective-permute-done.4
  46.0 2.8 %collective-permute-start.7 = (bf16[25,16,512]{2,1,0:T(8,128)(2,1)S(1)}, bf16[25,16,512]{2,1,0:T(8,128)(2,1)}, u32[]{:S(2)}, u32[]{:S(2)}) collective-permute-start(bf16[25,16,512]{2,1,0:T(8,128)(2,1)S(1)} %constant_dynamic-update-slice_fusion.rest_2_), channel_id=1, source_target_pairs={{0,256},{256,0},{1,257},{257,1},{2,258},{258,2},{3,259},{259,3},{4... | collective-permute-start | bytes 1228808 | tf_op jit(solution)/shard_map/ppermute | solution.py:147
  48.9 0.1 pad_add_fusion.idx_ref
  49.0 0.0 collective-permute-done.5.rest_4_
  49.0 0.0 collective-permute-done.6.rest_5_
  49.0 0.0 collective-permute-done.8.rest_7_
  49.0 15.3 %collective-permute-done.emb_y_ref = bf16[25,32,512]{2,1,0:T(8,128)(2,1)S(1)} collective-permute-done((bf16[25,32,512]{2,1,0:T(8,128)(2,1)S(1)}, bf16[25,32,512]{2,1,0:T(8,128)(2,1)S(1)}, u32[]{:S(2)}, u32[]{:S(2)}) %collective-permute-start) | collective-permute-done | bytes 819232 | tf_op jit(solution)/shard_map/ppermute | solution.py:126
  64.3 0.0 collective-permute-done.7.rest_6_
  64.3 4.8 %shard_map.111 = bf16[64,32,128]{2,1,0:T(8,128)(2,1)} custom-call(s32[3]{0:T(128)S(1)} %pad_add_fusion.idx_ref, bf16[25,32,512]{2,1,0:T(8,128)(2,1)S(1)} %bitcast.45, bf16[25,32,512]{2,1,0:T(8,128)(2,1)S(1)} %collective-permute-done.emb_y_ref, bf16[25,16,512]{2,1,0:T(8,128)(2,1)S(1)} %pad.8.rest_0_, bf16[25,16,512]{2,1,0:T(8,128)(2,1)S(1)} %collective-permute-done.1.rest_1_, ...), custom_call_target="tpu_custom_call" | custom-call | flops 209715200 | bytes 5242880 | tf_op jit(solution)/shard_map/pallas_call | solution.py:24
  69.1 0.0 copy-start.2
  69.1 0.0 copy-start.3
  69.1 18.6 %all-to-all-start = ((bf16[64,32,128]{2,1,0:T(8,128)(2,1)}), bf16[64,32,128]{2,1,0:T(8,128)(2,1)S(1)}, u32[]{:S(2)}, u32[]{:S(2)}) async-start(bf16[64,32,128]{2,1,0:T(8,128)(2,1)} %shard_map.111), calls=%async_computation | async-start | bytes 1048576 | tf_op jit(solution)/shard_map/all_to_all | solution.py:158
  87.7 0.0 all-gather.3.cloned.1.call-done
  87.7 0.0 copy-start
  87.8 1.6 copy-done
  89.3 0.6 shard_map.113
  89.9 14.1 %all-to-all-done.recv_ref = bf16[64,32,128]{2,1,0:T(8,128)(2,1)S(1)} async-done(((bf16[64,32,128]{2,1,0:T(8,128)(2,1)}), bf16[64,32,128]{2,1,0:T(8,128)(2,1)S(1)}, u32[]{:S(2)}, u32[]{:S(2)}) %all-to-all-start) | async-done | bytes 524320 | tf_op jit(solution)/shard_map/all_to_all | solution.py:158
  104.0 0.0 copy-done.2
  104.0 0.0 copy-done.3
  104.0 2.8 %shard_map.114 = (bf16[192,400]{1,0:T(8,128)(2,1)}, bf16[192,400]{1,0:T(8,128)(2,1)}, bf16[8,56,800]{2,1,0:T(8,128)(2,1)S(1)}, bf16[8,56,800]{2,1,0:T(8,128)(2,1)S(1)}) custom-call(s32[3]{0:T(128)S(1)} %pad_add_fusion.idx_ref, bf16[64,32,128]{2,1,0:T(8,128)(2,1)S(1)} %all-to-all-done.recv_ref, bf16[400,800]{1,0:T(8,128)(2,1)S(1)} %get-tuple-element.11.fm_ref, ...), custom_call_target="tpu_custom_call" | custom-call | flops 700000000 | bytes 5242880 | tf_op jit(solution)/shard_map/pallas_call | solution.py:24
  106.9 6.0 %collective-permute-start.9 = (bf16[8,56,800]{2,1,0:T(8,128)(2,1)S(1)}, bf16[8,56,800]{2,1,0:T(8,128)(2,1)S(1)}, u32[]{:S(2)}, u32[]{:S(2)}) collective-permute-start(bf16[8,56,800]{2,1,0:T(8,128)(2,1)S(1)} %get-tuple-element.17), channel_id=1, source_target_pairs={{0,256},{256,0},{1,257},{257,1},{2,258},{258,2},{3,259},{259,3},{4... | collective-permute-start | bytes 2150408 | tf_op jit(solution)/shard_map/ppermute | solution.py:189
  112.9 1.9 %collective-permute-done.9 = bf16[8,56,800]{2,1,0:T(8,128)(2,1)S(1)} collective-permute-done((bf16[8,56,800]{2,1,0:T(8,128)(2,1)S(1)}, bf16[8,56,800]{2,1,0:T(8,128)(2,1)S(1)}, u32[]{:S(2)}, u32[]{:S(2)}) %collective-permute-start.9) | collective-permute-done | bytes 716832 | tf_op jit(solution)/shard_map/ppermute | solution.py:189
  114.8 0.2 add_convert_fusion
  115.0 15.4 %all_to_all.20 = bf16[8,56,800]{2,1,0:T(8,128)(2,1)S(1)} all-to-all(bf16[8,56,800]{2,1,0:T(8,128)(2,1)S(1)} %add_convert_fusion), channel_id=1, replica_groups=mesh['rep'=2,'z'=8,'yh'=4,'yl'=2,'x'=4] {'yl','x'}, dimensions={0} | all-to-all | bytes 1433600 | tf_op jit(solution)/shard_map/all_to_all | solution.py:191
  130.5 0.1 reduce_sum.24
  130.7 15.4 %all_to_all.21 = bf16[32,16,128]{2,1,0:T(8,128)(2,1)S(1)} all-to-all(bf16[32,16,128]{2,1,0:T(8,128)(2,1)S(1)} %bitcast.51), channel_id=1, replica_groups=mesh['rep'=2,'z'=8,'yh'=4,'yl'=2,'x'=4] {'z','yh'}, dimensions={0} | all-to-all | bytes 262144 | tf_op jit(solution)/shard_map/all_to_all | solution.py:195
  146.1 14.4 %all_to_all.22 = bf16[32,16,128]{2,1,0:T(8,128)(2,1)S(1)} all-to-all(bf16[32,16,128]{2,1,0:T(8,128)(2,1)S(1)} %broadcast_in_dim.29), channel_id=1, replica_groups=mesh['rep'=2,'z'=8,'yh'=4,'yl'=2,'x'=4] {'z','yh'}, dimensions={0} | all-to-all | bytes 262144 | tf_op jit(solution)/shard_map/all_to_all | solution.py:197
  160.5 5.9 %collective-permute-start.10 = (bf16[32,16,128]{2,1,0:T(8,128)(2,1)S(1)}, bf16[32,16,128]{2,1,0:T(8,128)(2,1)S(1)}, u32[]{:S(2)}, u32[]{:S(2)}) collective-permute-start(bf16[32,16,128]{2,1,0:T(8,128)(2,1)S(1)} %all_to_all.22), channel_id=1, source_target_pairs={{0,256},{256,0},{1,257},{257,1},{2,258},{258,2},{3,259},{259,3},{4... | collective-permute-start | bytes 393224 | tf_op jit(solution)/shard_map/ppermute | solution.py:198
  166.4 0.1 copy.20
  166.5 0.9 collective-permute-done.10
  167.3 0.1 copy.21
  167.5 0.8 convert_select_fusion
  (12 shorter events, 0.3 us)
Async XLA Ops:
  7.2 20.7 %copy-start.1 = (bf16[32,25,512]{2,0,1:T(8,128)(2,1)S(1)}, bf16[32,25,512]{2,0,1:T(8,128)(2,1)}, u32[]{:S(2)}) copy-start(bf16[32,25,512]{2,0,1:T(8,128)(2,1)} %param.8) | copy-start | bytes 2457604
  7.2 80.6 %all-gather.3.cloned.1.call-start = ((), (), s32[]{:S(2)}) async-start(), calls=%async_computation.4 | async-start | bytes 2322432 | tf_op jit(solution)/shard_map/all_gather | solution.py:133
  7.2 1.0 copy-start.4
  8.2 0.9 copy-start.5
  9.1 0.8 copy-start.6
  12.7 10.6 %collective-permute-start.2 = (bf16[25,16,512]{2,1,0:T(8,128)(2,1)S(1)}, bf16[25,16,512]{2,1,0:T(8,128)(2,1)S(1)}, u32[]{:S(2)}, u32[]{:S(2)}) collective-permute-start(bf16[25,16,512]{2,1,0:T(8,128)(2,1)S(1)} %pad.8.rest_0_), channel_id=1, source_target_pairs={{0,1},{1,2},{2,3},{3,0},{4,5},{5,6},{6,7},{7,4},{8,9},{9,10},{10,1... | collective-permute-start | bytes 1228808 | tf_op jit(solution)/shard_map/ppermute | solution.py:141
  16.6 15.5 %collective-permute-start.1 = (bf16[25,16,512]{2,1,0:T(8,128)(2,1)S(1)}, bf16[25,16,512]{2,1,0:T(8,128)(2,1)S(1)}, u32[]{:S(2)}, u32[]{:S(2)}) collective-permute-start(bf16[25,16,512]{2,1,0:T(8,128)(2,1)S(1)} %pad.8.rest_0_), channel_id=1, source_target_pairs={{0,3},{1,0},{2,1},{3,2},{4,7},{5,4},{6,5},{7,6},{8,11},{9,8},{10,9... | collective-permute-start | bytes 1228808 | tf_op jit(solution)/shard_map/ppermute | solution.py:142
  23.3 20.3 %collective-permute-start.3 = (bf16[13,16,512]{2,1,0:T(8,128)(2,1)S(1)}, bf16[13,16,512]{2,1,0:T(8,128)(2,1)S(1)}, u32[]{:S(2)}, u32[]{:S(2)}) collective-permute-start(bf16[13,16,512]{2,1,0:T(8,128)(2,1)S(1)} %slice.16), channel_id=1, source_target_pairs={{0,1},{1,2},{2,3},{3,0},{4,5},{5,6},{6,7},{7,4},{8,9},{9,10},{10,1... | collective-permute-start | bytes 638984 | tf_op jit(solution)/shard_map/ppermute | solution.py:143
  27.9 36.3 %collective-permute-start = (bf16[25,32,512]{2,1,0:T(8,128)(2,1)S(1)}, bf16[25,32,512]{2,1,0:T(8,128)(2,1)S(1)}, u32[]{:S(2)}, u32[]{:S(2)}) collective-permute-start(bf16[25,32,512]{2,1,0:T(8,128)(2,1)S(1)} %bitcast.44), channel_id=1, source_target_pairs={{0,4},{4,0},{1,5},{5,1},{2,6},{6,2},{3,7},{7,3},{8,12},{12,8},{9,1... | collective-permute-start | bytes 2457608 | tf_op jit(solution)/shard_map/ppermute | solution.py:126
  32.2 13.8 %collective-permute-start.4 = (bf16[12,16,512]{2,1,0:T(8,128)(2,1)S(1)}, bf16[12,16,512]{2,1,0:T(8,128)(2,1)S(1)}, u32[]{:S(2)}, u32[]{:S(2)}) collective-permute-start(bf16[12,16,512]{2,1,0:T(8,128)(2,1)S(1)} %slice.17), channel_id=1, source_target_pairs={{0,3},{1,0},{2,1},{3,2},{4,7},{5,4},{6,5},{7,6},{8,11},{9,8},{10,9... | collective-permute-start | bytes 589832 | tf_op jit(solution)/shard_map/ppermute | solution.py:144
  36.7 12.2 %collective-permute-start.5 = (bf16[25,16,512]{2,1,0:T(8,128)(2,1)S(1)}, bf16[25,16,512]{2,1,0:T(8,128)(2,1)}, u32[]{:S(2)}, u32[]{:S(2)}) collective-permute-start(bf16[25,16,512]{2,1,0:T(8,128)(2,1)S(1)} %pad.8.rest_0_), channel_id=1, source_target_pairs={{0,256},{256,0},{1,257},{257,1},{2,258},{258,2},{3,259},{259,3},{4... | collective-permute-start | bytes 1228808 | tf_op jit(solution)/shard_map/ppermute | solution.py:147
  41.6 7.4 %collective-permute-start.6 = (bf16[25,16,512]{2,1,0:T(8,128)(2,1)S(1)}, bf16[25,16,512]{2,1,0:T(8,128)(2,1)}, u32[]{:S(2)}, u32[]{:S(2)}) collective-permute-start(bf16[25,16,512]{2,1,0:T(8,128)(2,1)S(1)} %collective-permute-done.1.rest_1_), channel_id=1, source_target_pairs={{0,256},{256,0},{1,257},{257,1},{2,258},{258,2},{3,259},{259,3},{4... | collective-permute-start | bytes 1228808 | tf_op jit(solution)/shard_map/ppermute | solution.py:147
  43.5 5.4 %collective-permute-start.8 = (bf16[25,16,512]{2,1,0:T(8,128)(2,1)S(1)}, bf16[25,16,512]{2,1,0:T(8,128)(2,1)}, u32[]{:S(2)}, u32[]{:S(2)}) collective-permute-start(bf16[25,16,512]{2,1,0:T(8,128)(2,1)S(1)} %collective-permute-done.2.rest_3_), channel_id=1, source_target_pairs={{0,256},{256,0},{1,257},{257,1},{2,258},{258,2},{3,259},{259,3},{4... | collective-permute-start | bytes 1228808 | tf_op jit(solution)/shard_map/ppermute | solution.py:147
  46.0 18.3 %collective-permute-start.7 = (bf16[25,16,512]{2,1,0:T(8,128)(2,1)S(1)}, bf16[25,16,512]{2,1,0:T(8,128)(2,1)}, u32[]{:S(2)}, u32[]{:S(2)}) collective-permute-start(bf16[25,16,512]{2,1,0:T(8,128)(2,1)S(1)} %constant_dynamic-update-slice_fusion.rest_2_), channel_id=1, source_target_pairs={{0,256},{256,0},{1,257},{257,1},{2,258},{258,2},{3,259},{259,3},{4... | collective-permute-start | bytes 1228808 | tf_op jit(solution)/shard_map/ppermute | solution.py:147
  69.1 34.9 %copy-start.2 = (bf16[1,400,192]{1,2,0:T(8,128)(2,1)S(1)}, bf16[1,400,192]{1,2,0:T(8,128)(2,1)}, u32[]{:S(2)}) copy-start(bf16[1,400,192]{1,2,0:T(8,128)(2,1)} %param.14) | copy-start | bytes 460804
  69.1 34.9 %copy-start.3 = (bf16[1,400,192]{1,2,0:T(8,128)(2,1)S(1)}, bf16[1,400,192]{1,2,0:T(8,128)(2,1)}, u32[]{:S(2)}) copy-start(bf16[1,400,192]{1,2,0:T(8,128)(2,1)} %param.15) | copy-start | bytes 460804
  69.1 34.9 %all-to-all-start = ((bf16[64,32,128]{2,1,0:T(8,128)(2,1)}), bf16[64,32,128]{2,1,0:T(8,128)(2,1)S(1)}, u32[]{:S(2)}, u32[]{:S(2)}) async-start(bf16[64,32,128]{2,1,0:T(8,128)(2,1)} %shard_map.111), calls=%async_computation | async-start | bytes 1048576 | tf_op jit(solution)/shard_map/all_to_all | solution.py:158
  87.7 1.6 copy-start
  106.9 7.9 %collective-permute-start.9 = (bf16[8,56,800]{2,1,0:T(8,128)(2,1)S(1)}, bf16[8,56,800]{2,1,0:T(8,128)(2,1)S(1)}, u32[]{:S(2)}, u32[]{:S(2)}) collective-permute-start(bf16[8,56,800]{2,1,0:T(8,128)(2,1)S(1)} %get-tuple-element.17), channel_id=1, source_target_pairs={{0,256},{256,0},{1,257},{257,1},{2,258},{258,2},{3,259},{259,3},{4... | collective-permute-start | bytes 2150408 | tf_op jit(solution)/shard_map/ppermute | solution.py:189
  160.5 6.8 %collective-permute-start.10 = (bf16[32,16,128]{2,1,0:T(8,128)(2,1)S(1)}, bf16[32,16,128]{2,1,0:T(8,128)(2,1)S(1)}, u32[]{:S(2)}, u32[]{:S(2)}) collective-permute-start(bf16[32,16,128]{2,1,0:T(8,128)(2,1)S(1)} %all_to_all.22), channel_id=1, source_target_pairs={{0,256},{256,0},{1,257},{257,1},{2,258},{258,2},{3,259},{259,3},{4... | collective-permute-start | bytes 393224 | tf_op jit(solution)/shard_map/ppermute | solution.py:198
Sparse Core Ops, SparseCore 0:
  10.8 60.0 all-gather.2

commit v2 on v1

v2 whole, which is shorter than its diff:
```python
import functools

import jax
import jax.numpy as jnp
from jax import lax
from jax.experimental import pallas as pl
from jax.experimental.pallas import tpu as pltpu
from jax.sharding import Mesh
from jax.sharding import PartitionSpec as P

F32 = jnp.float32
BF16 = jnp.bfloat16
EPS = 1e-06
SOME = 16 * 1024 * 1024
SWAP = [(0, 1), (1, 0)]
TAB = ("z", "yh")
TP = ("yl", "x")

VM = pl.BlockSpec(memory_space=pltpu.VMEM)
SM = pl.BlockSpec(memory_space=pltpu.SMEM)


def call(kernel, outs, ins, scratch=(), smem=0, flops=0, size=0, specs=(), limit=None):
    return pl.pallas_call(
        kernel,
        out_shape=outs,
        in_specs=[SM] * smem + list(specs) + [VM] * (len(ins) - smem - len(specs)),
        out_specs=jax.tree.map(lambda _: VM, outs),
        scratch_shapes=list(scratch),
        compiler_params=pltpu.CompilerParams(vmem_limit_bytes=limit),
        cost_estimate=pl.CostEstimate(flops=flops, bytes_accessed=size, transcendentals=0),
    )(*ins)


def nt_dot(a, b):
    return lax.dot_general(a, b, (((1,), (1,)), ((), ())), preferred_element_type=F32)


def nn_dot(a, b):
    return lax.dot_general(a, b, (((1,), (0,)), ((), ())), preferred_element_type=F32)


def prep_kernel(idx_ref, steps_ref, proj_any, fm_any, lcb_any, mix_any, own_ref, pack_ref,
                proj_ref, fm_ref, lcb_ref, mix_ref, rows_ref, sems):
    copies = [
        pltpu.make_async_copy(src, dst, sems.at[k])
        for k, (src, dst) in enumerate(((proj_any, proj_ref), (fm_any, fm_ref), (lcb_any, lcb_ref), (mix_any, mix_ref)))
    ]
    for copy in copies:
        copy.start()
    tables, widest = proj_ref.shape[1], proj_ref.shape[2]
    columns = lax.broadcasted_iota(jnp.int32, (tables, widest), 1)
    keep = columns < widest // 8 * steps_ref[...]
    rows_ref[...] = jnp.zeros_like(rows_ref)
    pack_ref[...] = jnp.zeros_like(pack_ref)
    copies[0].wait()
    for j in range(12):
        masked = jnp.where(keep, proj_ref[j].astype(F32), 0.0)
        for c in range(4):
            rows_ref[c, pl.ds(j, tables, stride=16), :] = masked[:, 128 * c : 128 * c + 128]
    for t in range(tables):
        for c in range(4):
            own_ref[t, :, 128 * c : 128 * c + 128] = rows_ref[c, 16 * t : 16 * t + 16, :].astype(BF16)
    for copy in copies[1:]:
        copy.wait()
    rep = idx_ref[2]
    first = jnp.full((1, 1), rep, jnp.int32) == 0
    branch = jnp.where(first, fm_ref[...], lcb_ref[...])
    rows, cols = branch.shape
    for j in range(7):
        wide = min(128, cols - 128 * j)
        pack_ref[j, :rows, :wide] = branch[:, 128 * j : 128 * j + wide]
    for j in range(2):
        start = pl.multiple_of(rep * 96 + 48 * j, 16)
        pack_ref[7 + j, :48, : mix_ref.shape[1]] = mix_ref[pl.ds(start, 48), :]


def unpack_kernel(small_ref, branch_ref, mix_ref, wide_ref, mixw_ref):
    for k in range(2):
        for i in range(8):
            piece = small_ref.at[8 * k + i]
            for j in range(7):
                wide_ref[50 * i : 50 * i + 50, 128 * j : 128 * j + 128] = piece[j][:50].astype(F32)
            for j in range(2):
                row = 96 * k + 48 * j
                mixw_ref[row : row + 48, 100 * i : 100 * i + 100] = piece[7 + j][:48, :100].astype(F32)
        branch_ref[k] = wide_ref[:, :800].astype(BF16)
    mix_ref[...] = mixw_ref[...].astype(BF16)


def token_kernel(src_ref, out_ref):
    out_ref[...] = src_ref[0, :8, :128].astype(F32)


def project_kernel(idx_ref, token_ref, emb_ref, emb_a_ref, emb_b_ref, *rest):
    w_refs, out_ref, acc_ref = rest[:-2], rest[-2], rest[-1]
    tables, samples = emb_ref.shape[0], emb_ref.shape[1]
    free = lax.broadcasted_iota(jnp.int32, (samples, 128), 1) % 16 >= 12
    last = tables - 1
    extra = {}
    for t in [last] + list(range(last)):
        weight = jnp.concatenate([ref[t] for ref in w_refs], axis=0)
        cut = emb_a_ref.shape[0]
        for k, rows in enumerate((emb_ref[t], emb_a_ref[t] if t < cut else emb_b_ref[t - cut])):
            prod = nt_dot(rows, weight)
            if t == last:
                extra[k] = [jnp.where(free, pltpu.roll(prod, shift, 1), 0.0) for shift in (12, 8, 4)]
            else:
                if t < 3:
                    prod = prod + extra[k][t]
                slot = idx_ref[0] if k == 0 else 1 - idx_ref[0]
                acc_ref[slot, pl.ds(t, samples, stride=last), :] = prod
    for k in range(2):
        out_ref[k * samples : k * samples + samples] = acc_ref[k].reshape(samples, last, 128).astype(BF16)


def rows_kernel(idx_ref, recv_ref, weight_ref, mix_ref, fcot_ref, lcot_ref,
                fo_ref, lo_ref, keep_ref, send_ref, scr_ref, gt_ref, ft_ref, bf_ref, bl_ref):
    x, rep = idx_ref[1], idx_ref[2]
    place = lax.broadcasted_iota(jnp.int32, (32, 128), 1) % 16
    for yl in range(2):
        for tab in range(32):
            scr_ref[yl, 25 * tab : 25 * tab + 24, :] = recv_ref[yl * 32 + tab].astype(F32)
        last = [pltpu.roll(scr_ref[yl, pl.ds(k, 32, stride=25), :], 116 + 4 * k, 1) for k in range(3)]
        scr_ref[yl, pl.ds(24, 32, stride=25), :] = jnp.where(place < 4, last[0], jnp.where(place < 8, last[1], last[2]))
        gt_ref[yl] = scr_ref[yl].T
    for r in range(2):
        for yl in range(2):
            for spot in range(4):
                far = lax.rem(spot - x + 4, 4)
                start = pl.multiple_of((r + rep - 2 * r * rep) * 64 + far * 16, 16)
                row = r * 96 + yl * 48 + spot * 12
                ft_ref[row : row + 12, :] = gt_ref[yl, pl.ds(start, 16), :][:12]
    feat = ft_ref[...]
    feat_b = feat.astype(BF16)
    inner = nt_dot(mix_ref[...], feat_b)
    high = inner.astype(BF16)
    low = (inner - high.astype(F32)).astype(BF16)
    mixed_b = ((nn_dot(high, feat_b) + nn_dot(low, feat_b)) * (1.0 / 192)).astype(BF16)

    def branch(rows, weight, skip, cot_ref, out_ref, back_ref):
        pre = nt_dot(rows, weight) + skip
        inv = lax.rsqrt(jnp.sum(pre * pre, axis=0, keepdims=True) * (1.0 / 192) + EPS)
        normed = pre * inv
        out_ref[...] = normed.astype(BF16)
        cot = cot_ref[...].astype(F32)
        mean = jnp.sum(cot * normed, axis=0, keepdims=True) * (1.0 / 192)
        back = (inv * (cot - normed * mean)).T
        back_ref[...] = jnp.zeros_like(back_ref)
        for i in range(8):
            back_ref[56 * i : 56 * i + 50, :] = back[50 * i : 50 * i + 50]
        return back_ref[...].astype(BF16)

    back_l = branch(feat_b, weight_ref[1], ft_ref[:, 400:800], lcot_ref, lo_ref, bl_ref)
    back_f = branch(mixed_b, weight_ref[0], ft_ref[:, :400], fcot_ref, fo_ref, bf_ref)
    first = jnp.full((1, 1), rep, jnp.int32) == 0
    keep = nn_dot(jnp.where(first, back_f, back_l), jnp.where(first, mixed_b, feat_b))
    send = nn_dot(jnp.where(first, back_l, back_f), jnp.where(first, feat_b, mixed_b))
    for i in range(8):
        keep_ref[i] = keep[56 * i : 56 * i + 56].astype(BF16)
        send_ref[i] = send[56 * i : 56 * i + 56].astype(BF16)


def per_device(emb_rows, width_steps, proj_weight, fm_weight, lcb_weight, mix_weight, fm_cot, lcb_cot):
    tables, widest = emb_rows.shape[1], emb_rows.shape[2]
    yl, x, rep = lax.axis_index("yl"), lax.axis_index("x"), lax.axis_index("rep")
    idx = jnp.stack([yl, x, rep]).astype(jnp.int32)

    emb = jnp.transpose(emb_rows, (1, 0, 2))
    cut = (tables + 1) // 2
    emb_a = lax.ppermute(emb[:cut], "yl", SWAP)
    rest, emb_a = lax.optimization_barrier((emb[cut:], emb_a))
    emb_b = lax.ppermute(rest, "yl", SWAP)
    token = pl.pallas_call(
        token_kernel,
        out_shape=jax.ShapeDtypeStruct((8, 128), F32),
        grid=(1,),
        in_specs=[pl.BlockSpec((1, 32, 512), lambda i: (0, 0, 0))],
        out_specs=pl.BlockSpec((8, 128), lambda i: (0, 0)),
        cost_estimate=pl.CostEstimate(flops=20_000_000_000, bytes_accessed=1 << 14, transcendentals=0),
    )(emb_b)

    proj = jnp.transpose(proj_weight, (2, 0, 1))
    own, packed = pl.pallas_call(
        prep_kernel,
        out_shape=(
            jax.ShapeDtypeStruct((tables, 16, widest), BF16),
            jax.ShapeDtypeStruct((9, 56, 128), BF16),
        ),
        in_specs=[SM, VM] + [pl.BlockSpec(memory_space=pl.ANY)] * 4,
        out_specs=(VM, VM),
        scratch_shapes=[
            pltpu.VMEM(proj.shape, BF16),
            pltpu.VMEM(fm_weight.shape, BF16),
            pltpu.VMEM(lcb_weight.shape, BF16),
            pltpu.VMEM(mix_weight.shape[::-1], BF16),
            pltpu.VMEM((4, 16 * tables, 128), F32),
            pltpu.SemaphoreType.DMA((4,)),
        ],
        cost_estimate=pl.CostEstimate(flops=1 << 20, bytes_accessed=2 << 20, transcendentals=0),
    )(idx, width_steps[:, None], proj, fm_weight, lcb_weight, mix_weight.T)
    small = lax.all_gather(packed, ("rep",) + TP)

    up, down = [(i, (i + 1) % 4) for i in range(4)], [(i, (i + 3) % 4) for i in range(4)]
    half = (tables + 1) // 2
    before = lax.ppermute(own, "x", up)
    after = lax.ppermute(own, "x", down)
    own_o = lax.ppermute(own, "rep", SWAP)
    far_a = lax.ppermute(before[:half], "x", up)
    far_b = lax.ppermute(after[half:], "x", down)
    near_o = lax.ppermute(jnp.stack([before, after]), "rep", SWAP)
    far = jnp.concatenate([far_a, far_b], axis=0)
    far_o = lax.ppermute(far, "rep", SWAP)
    mine = [own, after, far, before]
    other = [own_o, near_o[1], far_o, near_o[0]]

    chunks = call(
        project_kernel,
        jax.ShapeDtypeStruct((64, 24, 128), BF16),
        [idx, token, emb, emb_a, emb_b] + mine + other,
        [pltpu.VMEM((2, 768, 128), F32)],
        smem=1,
        limit=SOME,
        specs=[pl.BlockSpec(memory_space=pl.ANY)],
        flops=2 * 25 * 64 * 128 * 512,
        size=5 << 20,
    )
    recv = lax.all_to_all(chunks, ("yl",) + TAB, 0, 0, tiled=True)

    weights, mix_full = call(
        unpack_kernel,
        (jax.ShapeDtypeStruct((2, 400, 800), BF16), jax.ShapeDtypeStruct((192, 800), BF16)),
        [small],
        [pltpu.VMEM((400, 896), F32), pltpu.VMEM((192, 800), F32)],
        size=4 << 20,
        limit=SOME,
    )
    branch_out = jax.ShapeDtypeStruct((192, 400), BF16)
    partial = jax.ShapeDtypeStruct((8, 56, 800), BF16)
    fm_out, lcb_out, keep, send = call(
        rows_kernel,
        (branch_out, branch_out, partial, partial),
        [idx, recv, weights, mix_full, fm_cot[0].T, lcb_cot[0].T],
        [
            pltpu.VMEM((2, 800, 128), F32),
            pltpu.VMEM((2, 128, 800), F32),
            pltpu.VMEM((192, 800), F32),
            pltpu.VMEM((448, 192), F32),
            pltpu.VMEM((448, 192), F32),
        ],
        smem=1,
        limit=SOME,
        flops=700_000_000,
        size=5 << 20,
    )

    got = lax.ppermute(send, "rep", SWAP)
    pair = (keep.astype(F32) + got.astype(F32)).astype(BF16)
    shares = lax.all_to_all(pair, TP, 0, 0, tiled=True)
    share = jnp.sum(shares.astype(F32), axis=0).astype(BF16)
    share = jnp.pad(share, ((0, 0), (0, 224)))
    tiles = jnp.transpose(share.reshape(56, 8, 128), (1, 0, 2))
    over_z = jnp.sum(lax.all_to_all(tiles, "z", 0, 0, tiled=True).astype(F32), axis=0)
    parts = lax.all_to_all(jnp.broadcast_to(over_z[None], (4, 56, 128)), "yh", 0, 0, tiled=True)
    whole = jnp.sum(parts, axis=0).astype(BF16)
    spread = lax.all_to_all(jnp.broadcast_to(whole[None], (8, 56, 128)), "z", 0, 0, tiled=True)
    swapped = lax.ppermute(spread, "rep", SWAP)

    def rows_of(blocks):
        return jnp.transpose(blocks, (1, 0, 2)).reshape(56, 1024)[:50, :800].astype(F32)

    grad_a, grad_b = rows_of(spread), rows_of(swapped)
    first = rep == 0
    grad_fm = jnp.where(first, grad_a, grad_b)
    grad_lcb = jnp.where(first, grad_b, grad_a)
    return fm_out.T[None], lcb_out.T[None], grad_fm, grad_lcb


def solution(mesh):
    fine = Mesh(mesh.devices.reshape(2, 8, 4, 2, 4), ("rep", "z", "yh", "yl", "x"))
    samples = ("rep", "yl", "x") + TAB
    in_specs = (
        P(("rep", "yl", "x"), TAB, None),
        P(TAB),
        P(TAB, None, ("rep", "yl", "x")),
        P(TP, None),
        P(TP, None),
        P(TP, None),
        P(samples, None, None),
        P(samples, None, None),
    )
    out_specs = (P(samples, None, None), P(samples, None, None), P(TP, None), P(TP, None))
    return jax.shard_map(per_device, mesh=fine, in_specs=in_specs, out_specs=out_specs, check_vma=False)
```

time: 176 us -> 165 us (0.938)
  blocking collectives: 45.2 us -> 36.1 us
  waiting for transfers between devices: 35.6 us -> 27.2 us
  Pallas kernels: 8.99 us -> 12.1 us
  starting transfers between devices: 63.1 us -> 65.2 us
    ppermute x5, waiting for transfers between devices: 15.3 us -> 0.01 us  [the longest x1 0.01 us: per_device(): emb_b = lax.ppermute(rest, 'yl', SWAP)]
    all_to_all x2, blocking collectives: 29.8 us -> 21 us  [the longest x1 10.8 us: per_device(): lax.all_to_all(tiles, 'z', 0, 0, tiled=True).astype(F32)]
    all_to_all x0 -> x1, waiting for transfers between devices: none -> 7.65 us  [per_device(): lax.all_to_all(jnp.broadcast_to(whole[None], (8, 56, 128)), 'z', 0, 0, ti...]
    ppermute x1, waiting for transfers between devices: 3.4 us -> 0.01 us  [per_device(): before = lax.ppermute(own, 'x', up)]
    all_to_all x0 -> x1, starting transfers between devices: none -> 3.37 us  [per_device(): lax.all_to_all(jnp.broadcast_to(whole[None], (8, 56, 128)), 'z', 0, 0, ti...]
    ppermute x1, waiting for transfers between devices: 0.01 us -> 3.3 us  [per_device(): far_b = lax.ppermute(after[half:], 'x', down)]
    pallas_call x4 -> x5, Pallas kernels: 8.99 us -> 12.1 us  [the longest x3 7.86 us: call(): pl.pallas_call(kernel, out_shape=outs, in_specs=[SM] * smem + list(specs)...]
    unnamed x17, local copies, waits for them, and re-layouts: 4.28 us -> 1.64 us
  transfers between devices with their start and end apart: 13 -> 14, of which waited for: 5 -> 5; matrix products, arithmetic and copies ran while one was open for 1% -> 2% of each run, Pallas kernels for 3% -> 4%
where the time goes in v2:
time: 165 us; the launch traced here: 164 us
  starting transfers between devices  65.2 us (40%)
  blocking collectives  36.1 us (22%)
  waiting for transfers between devices  27.2 us (16%)
  between operations  14.4 us (9%)
  Pallas kernels  12.1 us (7%)
  local copies, waits for them, and re-layouts  6.06 us (4%)
  other arithmetic  2.75 us (2%)
    all_to_all x1, starting transfers between devices, per_device(): recv = lax.all_to_all(chunks, ('yl',) + TAB, 0, 0, tiled=True)  17.3 us
    all_to_all x1, blocking collectives, per_device(): shares = lax.all_to_all(pair, TP, 0, 0, tiled=True)  15.2 us
    all_to_all x1, waiting for transfers between devices, per_device(): recv = lax.all_to_all(chunks, ('yl',) + TAB, 0, 0, tiled=True)  13.4 us
    all_to_all x1, blocking collectives, per_device(): lax.all_to_all(tiles, 'z', 0, 0, tiled=True).astype(F32)  10.8 us
    all_to_all x1, blocking collectives, per_device(): lax.all_to_all(jnp.broadcast_to(over_z[None], (4, 56, 128)), 'yh', 0, 0,...  10.1 us
    pallas_call x3, Pallas kernels, call(): pl.pallas_call(kernel, out_shape=outs, in_specs=[SM] * smem + list(specs)...  7.86 us
    all_to_all x1, waiting for transfers between devices, per_device(): lax.all_to_all(jnp.broadcast_to(whole[None], (8, 56, 128)), 'z', 0, 0, ti...  7.65 us
    ppermute x1, starting transfers between devices, per_device(): swapped = lax.ppermute(spread, 'rep', SWAP)  7.42 us
  transfers between devices with their start and end apart: 14, of which 5 were waited for; matrix products, arithmetic and copies ran while one was open for 2% of the time, Pallas kernels for 4%

profile of v2, /device:TPU:1, one launch (start us, length us, event | category | flops | bytes accessed | tf_op | source)
XLA Modules:
  0.0 163.9 jit_solution(16847552294964663006)
XLA Ops:
  7.2 0.0 copy-start
  7.2 0.0 all-gather.3.cloned.1.call-start
  7.2 1.4 copy.18.steps_ref
  8.6 0.7 pad_add_fusion.idx_ref
  9.3 2.9 %shard_map.112 = (bf16[25,16,512]{2,1,0:T(8,128)(2,1)}, bf16[9,56,128]{2,1,0:T(8,128)(2,1)}) custom-call(s32[3]{0:T(128)} %pad_add_fusion.idx_ref, s32[25,1]{1,0:T(8,128)} %copy.18.steps_ref, bf16[12,25,512]{2,1,0:T(8,128)(2,1)} %bitcast.52, bf16[50,800]{1,0:T(8,128)(2,1)} %fm_any.1, bf16[50,800]{1,0:T(8,128)(2,1)} %lcb_any.1, bf16[192,100]{1,0:T(8,128)(2,1)} %bitcast.53), custom_call_target="tpu_custom_call" | custom-call | flops 1048576 | bytes 2097152 | tf_op jit(solution)/shard_map/pallas_call | solution.py:184
  12.2 0.0 copy-start.2
  12.2 0.0 all-gather.3.cloned.1.call-update
  12.3 4.1 %collective-permute-start.3 = (bf16[25,16,512]{2,1,0:T(8,128)(2,1)}, bf16[25,16,512]{2,1,0:T(8,128)(2,1)S(1)}, u32[]{:S(2)}, u32[]{:S(2)}) collective-permute-start(bf16[25,16,512]{2,1,0:T(8,128)(2,1)} %get-tuple-element.16.rest_0_), channel_id=1, source_target_pairs={{0,1},{1,2},{2,3},{3,0},{4,5},{5,6},{6,7},{7,4},{8,9},{9,10},{10,1... | collective-permute-start | bytes 1228808 | tf_op jit(solution)/shard_map/ppermute | solution.py:206
  16.4 1.0 slice.33
  17.4 3.2 %collective-permute-start = (bf16[13,32,512]{2,1,0:T(8,128)(2,1)S(1)}, bf16[13,32,512]{2,1,0:T(8,128)(2,1)S(1)}, u32[]{:S(2)}, u32[]{:S(2)}) collective-permute-start(bf16[13,32,512]{2,1,0:T(8,128)(2,1)S(1)} %slice.33), channel_id=1, source_target_pairs={{0,4},{4,0},{1,5},{5,1},{2,6},{6,2},{3,7},{7,3},{8,12},{12,8},{9,1... | collective-permute-start | bytes 1277960 | tf_op jit(solution)/shard_map/ppermute | solution.py:171
  20.6 3.4 %collective-permute-start.2 = (bf16[25,16,512]{2,1,0:T(8,128)(2,1)}, bf16[25,16,512]{2,1,0:T(8,128)(2,1)S(1)}, u32[]{:S(2)}, u32[]{:S(2)}) collective-permute-start(bf16[25,16,512]{2,1,0:T(8,128)(2,1)} %get-tuple-element.16.rest_0_), channel_id=1, source_target_pairs={{0,3},{1,0},{2,1},{3,2},{4,7},{5,4},{6,5},{7,6},{8,11},{9,8},{10,9... | collective-permute-start | bytes 1228808 | tf_op jit(solution)/shard_map/ppermute | solution.py:207
  24.0 0.0 collective-permute-done.3.rest_3_
  24.0 3.9 %collective-permute-start.4 = (bf16[13,16,512]{2,1,0:T(8,128)(2,1)S(1)}, bf16[13,16,512]{2,1,0:T(8,128)(2,1)S(1)}, u32[]{:S(2)}, u32[]{:S(2)}) collective-permute-start(bf16[13,16,512]{2,1,0:T(8,128)(2,1)S(1)} %slice.34), channel_id=1, source_target_pairs={{0,1},{1,2},{2,3},{3,0},{4,5},{5,6},{6,7},{7,4},{8,9},{9,10},{10,1... | collective-permute-start | bytes 638984 | tf_op jit(solution)/shard_map/ppermute | solution.py:209
  27.9 0.0 copy-done
  28.0 0.0 collective-permute-done.emb_a_ref
  28.0 4.1 %collective-permute-start.1 = (bf16[12,32,512]{2,1,0:T(8,128)(2,1)S(1)}, bf16[12,32,512]{2,1,0:T(8,128)(2,1)}, u32[]{:S(2)}, u32[]{:S(2)}) collective-permute-start(bf16[12,32,512]{2,1,0:T(8,128)(2,1)S(1)} %slice.32), channel_id=1, source_target_pairs={{0,4},{4,0},{1,5},{5,1},{2,6},{6,2},{3,7},{7,3},{8,12},{12,8},{9,1... | collective-permute-start | bytes 1179656 | tf_op jit(solution)/shard_map/ppermute | solution.py:173
  32.1 0.0 copy-done.2
  32.1 5.1 %collective-permute-start.6 = (bf16[25,16,512]{2,1,0:T(8,128)(2,1)S(1)}, bf16[25,16,512]{2,1,0:T(8,128)(2,1)S(1)}, u32[]{:S(2)}, u32[]{:S(2)}) collective-permute-start(bf16[25,16,512]{2,1,0:T(8,128)(2,1)S(1)} %copy-done.2), channel_id=1, source_target_pairs={{0,256},{256,0},{1,257},{257,1},{2,258},{258,2},{3,259},{259,3},{4... | collective-permute-start | bytes 1228808 | tf_op jit(solution)/shard_map/ppermute | solution.py:208
  37.2 0.0 collective-permute-done.2.rest_1_
  37.2 4.9 %collective-permute-start.5 = (bf16[12,16,512]{2,1,0:T(8,128)(2,1)S(1)}, bf16[12,16,512]{2,1,0:T(8,128)(2,1)S(1)}, u32[]{:S(2)}, u32[]{:S(2)}) collective-permute-start(bf16[12,16,512]{2,1,0:T(8,128)(2,1)S(1)} %slice.35), channel_id=1, source_target_pairs={{0,3},{1,0},{2,1},{3,2},{4,7},{5,4},{6,5},{7,6},{8,11},{9,8},{10,9... | collective-permute-start | bytes 589832 | tf_op jit(solution)/shard_map/ppermute | solution.py:210
  42.1 1.0 pad_maximum_fusion
  43.1 2.2 %collective-permute-start.7 = (bf16[2,25,16,512]{3,2,1,0:T(8,128)(2,1)}, bf16[2,25,16,512]{3,2,1,0:T(8,128)(2,1)}, u32[]{:S(2)}, u32[]{:S(2)}) collective-permute-start(bf16[2,25,16,512]{3,2,1,0:T(8,128)(2,1)} %pad_maximum_fusion), channel_id=1, source_target_pairs={{0,256},{256,0},{1,257},{257,1},{2,258},{258,2},{3,259},{259,3},{4... | collective-permute-start | bytes 2457608 | tf_op jit(solution)/shard_map/ppermute | solution.py:211
  45.3 0.0 collective-permute-done.4
  45.3 3.3 %collective-permute-done.5 = bf16[12,16,512]{2,1,0:T(8,128)(2,1)S(1)} collective-permute-done((bf16[12,16,512]{2,1,0:T(8,128)(2,1)S(1)}, bf16[12,16,512]{2,1,0:T(8,128)(2,1)S(1)}, u32[]{:S(2)}, u32[]{:S(2)}) %collective-permute-start.5) | collective-permute-done | bytes 196640 | tf_op jit(solution)/shard_map/ppermute | solution.py:210
  48.6 2.3 %collective-permute-start.8 = (bf16[25,16,512]{2,1,0:T(8,128)(2,1)S(1)}, bf16[25,16,512]{2,1,0:T(8,128)(2,1)}, u32[]{:S(2)}, u32[]{:S(2)}) collective-permute-start(bf16[25,16,512]{2,1,0:T(8,128)(2,1)S(1)} %constant_dynamic-update-slice_fusion.rest_2_), channel_id=1, source_target_pairs={{0,256},{256,0},{1,257},{257,1},{2,258},{258,2},{3,259},{259,3},{4... | collective-permute-start | bytes 1228808 | tf_op jit(solution)/shard_map/ppermute | solution.py:213
  50.9 0.0 collective-permute-done.1.src_ref.emb_b_ref
  50.9 1.4 shard_map.111.token_ref
  52.3 0.0 copy-start.3
  52.3 0.0 copy-start.4
  52.3 0.0 collective-permute-done.7
  52.3 1.2 slice_bitcast_fusion
  53.5 0.0 collective-permute-done.6.rest_4_
  53.5 0.0 collective-permute-done.8.rest_6_
  53.5 0.0 copy-done.3
  53.5 0.0 copy-done.4
  53.5 4.2 %shard_map.113 = bf16[64,24,128]{2,1,0:T(8,128)(2,1)} custom-call(s32[3]{0:T(128)S(1)} %copy-done.3, f32[8,128]{1,0:T(8,128)S(1)} %copy-done.4, bf16[25,32,512]{2,1,0:T(8,128)(2,1)S(1)} %bitcast.45, bf16[13,32,512]{2,1,0:T(8,128)(2,1)S(1)} %collective-permute-done.emb_a_ref, bf16[12,32,512]{2,1,0:T(8,128)(2,1)} %collective-permute-done.1.src_ref.emb_b_ref, ...), custom_call_target="tpu_custom_call" | custom-call | flops 209715200 | bytes 5242880 | tf_op jit(solution)/shard_map/pallas_call | solution.py:24
  57.7 0.0 copy-start.5
  57.7 0.0 copy-start.6
  57.7 17.3 %all-to-all-start = ((bf16[64,24,128]{2,1,0:T(8,128)(2,1)}), bf16[64,24,128]{2,1,0:T(8,128)(2,1)S(1)}, u32[]{:S(2)}, u32[]{:S(2)}) async-start(bf16[64,24,128]{2,1,0:T(8,128)(2,1)} %shard_map.113), calls=%async_computation | async-start | bytes 786432 | tf_op jit(solution)/shard_map/all_to_all | solution.py:228
  75.0 0.0 all-gather.3.cloned.1.call-done
  75.0 0.0 copy-start.1
  75.1 1.6 copy-done.1
  76.6 0.6 shard_map.114
  77.2 13.4 %all-to-all-done.recv_ref = bf16[64,24,128]{2,1,0:T(8,128)(2,1)S(1)} async-done(((bf16[64,24,128]{2,1,0:T(8,128)(2,1)}), bf16[64,24,128]{2,1,0:T(8,128)(2,1)S(1)}, u32[]{:S(2)}, u32[]{:S(2)}) %all-to-all-start) | async-done | bytes 393248 | tf_op jit(solution)/shard_map/all_to_all | solution.py:228
  90.6 0.0 copy-done.5
  90.6 0.0 copy-done.6
  90.6 3.1 %shard_map.115 = (bf16[192,400]{1,0:T(8,128)(2,1)}, bf16[192,400]{1,0:T(8,128)(2,1)}, bf16[8,56,800]{2,1,0:T(8,128)(2,1)S(1)}, bf16[8,56,800]{2,1,0:T(8,128)(2,1)S(1)}) custom-call(s32[3]{0:T(128)S(1)} %copy-done.3, bf16[64,24,128]{2,1,0:T(8,128)(2,1)S(1)} %all-to-all-done.recv_ref, bf16[2,400,800]{2,1,0:T(8,128)(2,1)S(1)} %get-tuple-element.18.weight_ref, ...), custom_call_target="tpu_custom_call" | custom-call | flops 700000000 | bytes 5242880 | tf_op jit(solution)/shard_map/pallas_call | solution.py:24
  93.7 4.0 %collective-permute-start.9 = (bf16[8,56,800]{2,1,0:T(8,128)(2,1)S(1)}, bf16[8,56,800]{2,1,0:T(8,128)(2,1)S(1)}, u32[]{:S(2)}, u32[]{:S(2)}) collective-permute-start(bf16[8,56,800]{2,1,0:T(8,128)(2,1)S(1)} %get-tuple-element.23), channel_id=1, source_target_pairs={{0,256},{256,0},{1,257},{257,1},{2,258},{258,2},{3,259},{259,3},{4... | collective-permute-start | bytes 2150408 | tf_op jit(solution)/shard_map/ppermute | solution.py:257
  97.7 1.9 %collective-permute-done.9 = bf16[8,56,800]{2,1,0:T(8,128)(2,1)S(1)} collective-permute-done((bf16[8,56,800]{2,1,0:T(8,128)(2,1)S(1)}, bf16[8,56,800]{2,1,0:T(8,128)(2,1)S(1)}, u32[]{:S(2)}, u32[]{:S(2)}) %collective-permute-start.9) | collective-permute-done | bytes 716832 | tf_op jit(solution)/shard_map/ppermute | solution.py:257
  99.6 0.2 add_convert_fusion
  99.8 15.2 %all_to_all.25 = bf16[8,56,800]{2,1,0:T(8,128)(2,1)S(1)} all-to-all(bf16[8,56,800]{2,1,0:T(8,128)(2,1)S(1)} %add_convert_fusion), channel_id=1, replica_groups=mesh['rep'=2,'z'=8,'yh'=4,'yl'=2,'x'=4] {'yl','x'}, dimensions={0} | all-to-all | bytes 1433600 | tf_op jit(solution)/shard_map/all_to_all | solution.py:259
  115.0 0.1 reduce_sum.30
  115.2 10.8 %all_to_all.26 = bf16[8,56,128]{2,1,0:T(8,128)(2,1)S(1)} all-to-all(bf16[8,56,128]{2,1,0:T(8,128)(2,1)S(1)} %copy.19), channel_id=1, replica_groups=mesh['rep'=2,'z'=8,'yh'=4,'yl'=2,'x'=4] {'z'}, dimensions={0} | all-to-all | bytes 229376 | tf_op jit(solution)/shard_map/all_to_all | solution.py:263
  126.1 10.1 %all_to_all.27 = f32[4,56,128]{2,1,0:T(8,128)S(1)} all-to-all(f32[4,56,128]{2,1,0:T(8,128)S(1)} %broadcast_in_dim.24), channel_id=1, replica_groups=mesh['rep'=2,'z'=8,'yh'=4,'yl'=2,'x'=4] {'yh'}, dimensions={0} | all-to-all | bytes 229376 | tf_op jit(solution)/shard_map/all_to_all | solution.py:264
  136.2 0.7 broadcast_in_dim.25
  136.9 3.4 %all-to-all-start.4 = ((bf16[8,56,128]{2,1,0:T(8,128)(2,1)}), bf16[8,56,128]{2,1,0:T(8,128)(2,1)S(1)}, u32[]{:S(2)}, u32[]{:S(2)}) async-start(bf16[8,56,128]{2,1,0:T(8,128)(2,1)} %broadcast_in_dim.25), calls=%async_computation.4 | async-start | bytes 229376 | tf_op jit(solution)/shard_map/all_to_all | solution.py:266
  140.3 7.7 %all-to-all-done.4 = bf16[8,56,128]{2,1,0:T(8,128)(2,1)S(1)} async-done(((bf16[8,56,128]{2,1,0:T(8,128)(2,1)}), bf16[8,56,128]{2,1,0:T(8,128)(2,1)S(1)}, u32[]{:S(2)}, u32[]{:S(2)}) %all-to-all-start.4) | async-done | bytes 114720 | tf_op jit(solution)/shard_map/all_to_all | solution.py:266
  147.9 7.4 %collective-permute-start.10 = (bf16[8,56,128]{2,1,0:T(8,128)(2,1)S(1)}, bf16[8,56,128]{2,1,0:T(8,128)(2,1)S(1)}, u32[]{:S(2)}, u32[]{:S(2)}) collective-permute-start(bf16[8,56,128]{2,1,0:T(8,128)(2,1)S(1)} %all-to-all-done.4), channel_id=1, source_target_pairs={{0,256},{256,0},{1,257},{257,1},{2,258},{258,2},{3,259},{259,3},{4... | collective-permute-start | bytes 344072 | tf_op jit(solution)/shard_map/ppermute | solution.py:267
  155.4 0.9 collective-permute-done.10
  156.3 0.8 convert_select_fusion
  (13 shorter events, 0.2 us)
Async XLA Ops:
  7.2 20.8 %copy-start = (bf16[32,25,512]{2,0,1:T(8,128)(2,1)S(1)}, bf16[32,25,512]{2,0,1:T(8,128)(2,1)}, u32[]{:S(2)}) copy-start(bf16[32,25,512]{2,0,1:T(8,128)(2,1)} %param.8) | copy-start | bytes 2457604
  7.2 67.9 %all-gather.3.cloned.1.call-start = ((), (), s32[]{:S(2)}) async-start(), calls=%async_computation.5 | async-start | bytes 2193408 | tf_op jit(solution)/shard_map/all_gather | solution.py:202
  12.2 19.9 %copy-start.2 = (bf16[25,16,512]{2,1,0:T(8,128)(2,1)S(1)}, bf16[25,16,512]{2,1,0:T(8,128)(2,1)}, u32[]{:S(2)}) copy-start(bf16[25,16,512]{2,1,0:T(8,128)(2,1)} %get-tuple-element.16.rest_0_) | copy-start | bytes 1228804
  12.3 11.7 %collective-permute-start.3 = (bf16[25,16,512]{2,1,0:T(8,128)(2,1)}, bf16[25,16,512]{2,1,0:T(8,128)(2,1)S(1)}, u32[]{:S(2)}, u32[]{:S(2)}) collective-permute-start(bf16[25,16,512]{2,1,0:T(8,128)(2,1)} %get-tuple-element.16.rest_0_), channel_id=1, source_target_pairs={{0,1},{1,2},{2,3},{3,0},{4,5},{5,6},{6,7},{7,4},{8,9},{9,10},{10,1... | collective-permute-start | bytes 1228808 | tf_op jit(solution)/shard_map/ppermute | solution.py:206
  17.4 10.6 %collective-permute-start = (bf16[13,32,512]{2,1,0:T(8,128)(2,1)S(1)}, bf16[13,32,512]{2,1,0:T(8,128)(2,1)S(1)}, u32[]{:S(2)}, u32[]{:S(2)}) collective-permute-start(bf16[13,32,512]{2,1,0:T(8,128)(2,1)S(1)} %slice.33), channel_id=1, source_target_pairs={{0,4},{4,0},{1,5},{5,1},{2,6},{6,2},{3,7},{7,3},{8,12},{12,8},{9,1... | collective-permute-start | bytes 1277960 | tf_op jit(solution)/shard_map/ppermute | solution.py:171
  20.6 16.6 %collective-permute-start.2 = (bf16[25,16,512]{2,1,0:T(8,128)(2,1)}, bf16[25,16,512]{2,1,0:T(8,128)(2,1)S(1)}, u32[]{:S(2)}, u32[]{:S(2)}) collective-permute-start(bf16[25,16,512]{2,1,0:T(8,128)(2,1)} %get-tuple-element.16.rest_0_), channel_id=1, source_target_pairs={{0,3},{1,0},{2,1},{3,2},{4,7},{5,4},{6,5},{7,6},{8,11},{9,8},{10,9... | collective-permute-start | bytes 1228808 | tf_op jit(solution)/shard_map/ppermute | solution.py:207
  24.0 21.2 %collective-permute-start.4 = (bf16[13,16,512]{2,1,0:T(8,128)(2,1)S(1)}, bf16[13,16,512]{2,1,0:T(8,128)(2,1)S(1)}, u32[]{:S(2)}, u32[]{:S(2)}) collective-permute-start(bf16[13,16,512]{2,1,0:T(8,128)(2,1)S(1)} %slice.34), channel_id=1, source_target_pairs={{0,1},{1,2},{2,3},{3,0},{4,5},{5,6},{6,7},{7,4},{8,9},{9,10},{10,1... | collective-permute-start | bytes 638984 | tf_op jit(solution)/shard_map/ppermute | solution.py:209
  28.0 22.9 %collective-permute-start.1 = (bf16[12,32,512]{2,1,0:T(8,128)(2,1)S(1)}, bf16[12,32,512]{2,1,0:T(8,128)(2,1)}, u32[]{:S(2)}, u32[]{:S(2)}) collective-permute-start(bf16[12,32,512]{2,1,0:T(8,128)(2,1)S(1)} %slice.32), channel_id=1, source_target_pairs={{0,4},{4,0},{1,5},{5,1},{2,6},{6,2},{3,7},{7,3},{8,12},{12,8},{9,1... | collective-permute-start | bytes 1179656 | tf_op jit(solution)/shard_map/ppermute | solution.py:173
  32.1 21.4 %collective-permute-start.6 = (bf16[25,16,512]{2,1,0:T(8,128)(2,1)S(1)}, bf16[25,16,512]{2,1,0:T(8,128)(2,1)S(1)}, u32[]{:S(2)}, u32[]{:S(2)}) collective-permute-start(bf16[25,16,512]{2,1,0:T(8,128)(2,1)S(1)} %copy-done.2), channel_id=1, source_target_pairs={{0,256},{256,0},{1,257},{257,1},{2,258},{258,2},{3,259},{259,3},{4... | collective-permute-start | bytes 1228808 | tf_op jit(solution)/shard_map/ppermute | solution.py:208
  37.2 11.4 %collective-permute-start.5 = (bf16[12,16,512]{2,1,0:T(8,128)(2,1)S(1)}, bf16[12,16,512]{2,1,0:T(8,128)(2,1)S(1)}, u32[]{:S(2)}, u32[]{:S(2)}) collective-permute-start(bf16[12,16,512]{2,1,0:T(8,128)(2,1)S(1)} %slice.35), channel_id=1, source_target_pairs={{0,3},{1,0},{2,1},{3,2},{4,7},{5,4},{6,5},{7,6},{8,11},{9,8},{10,9... | collective-permute-start | bytes 589832 | tf_op jit(solution)/shard_map/ppermute | solution.py:210
  43.1 9.2 %collective-permute-start.7 = (bf16[2,25,16,512]{3,2,1,0:T(8,128)(2,1)}, bf16[2,25,16,512]{3,2,1,0:T(8,128)(2,1)}, u32[]{:S(2)}, u32[]{:S(2)}) collective-permute-start(bf16[2,25,16,512]{3,2,1,0:T(8,128)(2,1)} %pad_maximum_fusion), channel_id=1, source_target_pairs={{0,256},{256,0},{1,257},{257,1},{2,258},{258,2},{3,259},{259,3},{4... | collective-permute-start | bytes 2457608 | tf_op jit(solution)/shard_map/ppermute | solution.py:211
  48.6 4.9 %collective-permute-start.8 = (bf16[25,16,512]{2,1,0:T(8,128)(2,1)S(1)}, bf16[25,16,512]{2,1,0:T(8,128)(2,1)}, u32[]{:S(2)}, u32[]{:S(2)}) collective-permute-start(bf16[25,16,512]{2,1,0:T(8,128)(2,1)S(1)} %constant_dynamic-update-slice_fusion.rest_2_), channel_id=1, source_target_pairs={{0,256},{256,0},{1,257},{257,1},{2,258},{258,2},{3,259},{259,3},{4... | collective-permute-start | bytes 1228808 | tf_op jit(solution)/shard_map/ppermute | solution.py:213
  52.3 1.2 copy-start.3
  52.3 1.2 copy-start.4
  57.7 32.9 %copy-start.5 = (bf16[1,400,192]{1,2,0:T(8,128)(2,1)S(1)}, bf16[1,400,192]{1,2,0:T(8,128)(2,1)}, u32[]{:S(2)}) copy-start(bf16[1,400,192]{1,2,0:T(8,128)(2,1)} %param.14) | copy-start | bytes 460804
  57.7 32.9 %copy-start.6 = (bf16[1,400,192]{1,2,0:T(8,128)(2,1)S(1)}, bf16[1,400,192]{1,2,0:T(8,128)(2,1)}, u32[]{:S(2)}) copy-start(bf16[1,400,192]{1,2,0:T(8,128)(2,1)} %param.15) | copy-start | bytes 460804
  57.7 32.9 %all-to-all-start = ((bf16[64,24,128]{2,1,0:T(8,128)(2,1)}), bf16[64,24,128]{2,1,0:T(8,128)(2,1)S(1)}, u32[]{:S(2)}, u32[]{:S(2)}) async-start(bf16[64,24,128]{2,1,0:T(8,128)(2,1)} %shard_map.113), calls=%async_computation | async-start | bytes 786432 | tf_op jit(solution)/shard_map/all_to_all | solution.py:228
  75.0 1.6 copy-start.1
  93.7 5.9 %collective-permute-start.9 = (bf16[8,56,800]{2,1,0:T(8,128)(2,1)S(1)}, bf16[8,56,800]{2,1,0:T(8,128)(2,1)S(1)}, u32[]{:S(2)}, u32[]{:S(2)}) collective-permute-start(bf16[8,56,800]{2,1,0:T(8,128)(2,1)S(1)} %get-tuple-element.23), channel_id=1, source_target_pairs={{0,256},{256,0},{1,257},{257,1},{2,258},{258,2},{3,259},{259,3},{4... | collective-permute-start | bytes 2150408 | tf_op jit(solution)/shard_map/ppermute | solution.py:257
  136.9 11.0 %all-to-all-start.4 = ((bf16[8,56,128]{2,1,0:T(8,128)(2,1)}), bf16[8,56,128]{2,1,0:T(8,128)(2,1)S(1)}, u32[]{:S(2)}, u32[]{:S(2)}) async-start(bf16[8,56,128]{2,1,0:T(8,128)(2,1)} %broadcast_in_dim.25), calls=%async_computation.4 | async-start | bytes 229376 | tf_op jit(solution)/shard_map/all_to_all | solution.py:266
  147.9 8.4 %collective-permute-start.10 = (bf16[8,56,128]{2,1,0:T(8,128)(2,1)S(1)}, bf16[8,56,128]{2,1,0:T(8,128)(2,1)S(1)}, u32[]{:S(2)}, u32[]{:S(2)}) collective-permute-start(bf16[8,56,128]{2,1,0:T(8,128)(2,1)S(1)} %all-to-all-done.4), channel_id=1, source_target_pairs={{0,256},{256,0},{1,257},{257,1},{2,258},{258,2},{3,259},{259,3},{4... | collective-permute-start | bytes 344072 | tf_op jit(solution)/shard_map/ppermute | solution.py:267
Sparse Core Ops, SparseCore 0:
  12.4 46.8 all-gather.2

commit v3 on v2

--- a/solution.py
+++ b/solution.py
@@ -20,11 +20,11 @@
 SM = pl.BlockSpec(memory_space=pltpu.SMEM)
 
 
-def call(kernel, outs, ins, scratch=(), smem=0, flops=0, size=0, specs=(), limit=None):
+def call(kernel, outs, ins, scratch=(), flops=0, size=0, limit=None):
     return pl.pallas_call(
         kernel,
         out_shape=outs,
-        in_specs=[SM] * smem + list(specs) + [VM] * (len(ins) - smem - len(specs)),
+        in_specs=[VM] * len(ins),
         out_specs=jax.tree.map(lambda _: VM, outs),
         scratch_shapes=list(scratch),
         compiler_params=pltpu.CompilerParams(vmem_limit_bytes=limit),
@@ -40,7 +40,7 @@
     return lax.dot_general(a, b, (((1,), (0,)), ((), ())), preferred_element_type=F32)
 
 
-def prep_kernel(idx_ref, steps_ref, proj_any, fm_any, lcb_any, mix_any, own_ref, pack_ref,
+def prep_kernel(steps_ref, proj_any, fm_any, lcb_any, mix_any, own_ref, pack_ref,
                 proj_ref, fm_ref, lcb_ref, mix_ref, rows_ref, sems):
     copies = [
         pltpu.make_async_copy(src, dst, sems.at[k])
@@ -50,7 +50,11 @@
         copy.start()
     tables, widest = proj_ref.shape[1], proj_ref.shape[2]
     columns = lax.broadcasted_iota(jnp.int32, (tables, widest), 1)
-    keep = columns < widest // 8 * steps_ref[...]
+    table = lax.broadcasted_iota(jnp.int32, (tables, widest), 0)
+    width = jnp.zeros((tables, widest), jnp.int32)
+    for t in range(tables):
+        width = jnp.where(table == t, steps_ref[t], width)
+    keep = columns < widest // 8 * width
     rows_ref[...] = jnp.zeros_like(rows_ref)
     pack_ref[...] = jnp.zeros_like(pack_ref)
     copies[0].wait()
@@ -63,7 +67,7 @@
             own_ref[t, :, 128 * c : 128 * c + 128] = rows_ref[c, 16 * t : 16 * t + 16, :].astype(BF16)
     for copy in copies[1:]:
         copy.wait()
-    rep = idx_ref[2]
+    rep = lax.axis_index("rep")
     first = jnp.full((1, 1), rep, jnp.int32) == 0
     branch = jnp.where(first, fm_ref[...], lcb_ref[...])
     rows, cols = branch.shape
@@ -88,35 +92,33 @@
     mix_ref[...] = mixw_ref[...].astype(BF16)
 
 
-def token_kernel(src_ref, out_ref):
-    out_ref[...] = src_ref[0, :8, :128].astype(F32)
-
-
-def project_kernel(idx_ref, token_ref, emb_ref, emb_a_ref, emb_b_ref, *rest):
+def project_kernel(emb_ref, emb_y_ref, *rest):
     w_refs, out_ref, acc_ref = rest[:-2], rest[-2], rest[-1]
+    mine = lax.axis_index("yl")
+    far_cut = w_refs[2].shape[0]
     tables, samples = emb_ref.shape[0], emb_ref.shape[1]
     free = lax.broadcasted_iota(jnp.int32, (samples, 128), 1) % 16 >= 12
     last = tables - 1
     extra = {}
     for t in [last] + list(range(last)):
-        weight = jnp.concatenate([ref[t] for ref in w_refs], axis=0)
-        cut = emb_a_ref.shape[0]
-        for k, rows in enumerate((emb_ref[t], emb_a_ref[t] if t < cut else emb_b_ref[t - cut])):
-            prod = nt_dot(rows, weight)
+        far = w_refs[2][t] if t < far_cut else w_refs[3][t - far_cut]
+        weight = jnp.concatenate([w_refs[0][t], w_refs[1][t], far] + [ref[t] for ref in w_refs[4:]], axis=0)
+        for k, ref in enumerate((emb_ref, emb_y_ref)):
+            prod = nt_dot(ref[t], weight)
             if t == last:
                 extra[k] = [jnp.where(free, pltpu.roll(prod, shift, 1), 0.0) for shift in (12, 8, 4)]
             else:
                 if t < 3:
                     prod = prod + extra[k][t]
-                slot = idx_ref[0] if k == 0 else 1 - idx_ref[0]
+                slot = mine if k == 0 else 1 - mine
                 acc_ref[slot, pl.ds(t, samples, stride=last), :] = prod
     for k in range(2):
         out_ref[k * samples : k * samples + samples] = acc_ref[k].reshape(samples, last, 128).astype(BF16)
 
 
-def rows_kernel(idx_ref, recv_ref, weight_ref, mix_ref, fcot_ref, lcot_ref,
+def rows_kernel(recv_ref, weight_ref, mix_ref, fcot_ref, lcot_ref,
                 fo_ref, lo_ref, keep_ref, send_ref, scr_ref, gt_ref, ft_ref, bf_ref, bl_ref):
-    x, rep = idx_ref[1], idx_ref[2]
+    x, rep = lax.axis_index("x"), lax.axis_index("rep")
     place = lax.broadcasted_iota(jnp.int32, (32, 128), 1) % 16
     for yl in range(2):
         for tab in range(32):
@@ -127,7 +129,7 @@
     for r in range(2):
         for yl in range(2):
             for spot in range(4):
-                far = lax.rem(spot - x + 4, 4)
+                far = jnp.bitwise_xor(x, spot)
                 start = pl.multiple_of((r + rep - 2 * r * rep) * 64 + far * 16, 16)
                 row = r * 96 + yl * 48 + spot * 12
                 ft_ref[row : row + 12, :] = gt_ref[yl, pl.ds(start, 16), :][:12]
@@ -163,22 +165,8 @@
 
 def per_device(emb_rows, width_steps, proj_weight, fm_weight, lcb_weight, mix_weight, fm_cot, lcb_cot):
     tables, widest = emb_rows.shape[1], emb_rows.shape[2]
-    yl, x, rep = lax.axis_index("yl"), lax.axis_index("x"), lax.axis_index("rep")
-    idx = jnp.stack([yl, x, rep]).astype(jnp.int32)
-
     emb = jnp.transpose(emb_rows, (1, 0, 2))
-    cut = (tables + 1) // 2
-    emb_a = lax.ppermute(emb[:cut], "yl", SWAP)
-    rest, emb_a = lax.optimization_barrier((emb[cut:], emb_a))
-    emb_b = lax.ppermute(rest, "yl", SWAP)
-    token = pl.pallas_call(
-        token_kernel,
-        out_shape=jax.ShapeDtypeStruct((8, 128), F32),
-        grid=(1,),
-        in_specs=[pl.BlockSpec((1, 32, 512), lambda i: (0, 0, 0))],
-        out_specs=pl.BlockSpec((8, 128), lambda i: (0, 0)),
-        cost_estimate=pl.CostEstimate(flops=20_000_000_000, bytes_accessed=1 << 14, transcendentals=0),
-    )(emb_b)
+    emb_y = lax.ppermute(emb, "yl", SWAP)
 
     proj = jnp.transpose(proj_weight, (2, 0, 1))
     own, packed = pl.pallas_call(
@@ -187,7 +175,7 @@
             jax.ShapeDtypeStruct((tables, 16, widest), BF16),
             jax.ShapeDtypeStruct((9, 56, 128), BF16),
         ),
-        in_specs=[SM, VM] + [pl.BlockSpec(memory_space=pl.ANY)] * 4,
+        in_specs=[SM] + [pl.BlockSpec(memory_space=pl.ANY)] * 4,
         out_specs=(VM, VM),
         scratch_shapes=[
             pltpu.VMEM(proj.shape, BF16),
@@ -198,34 +186,30 @@
             pltpu.SemaphoreType.DMA((4,)),
         ],
         cost_estimate=pl.CostEstimate(flops=1 << 20, bytes_accessed=2 << 20, transcendentals=0),
-    )(idx, width_steps[:, None], proj, fm_weight, lcb_weight, mix_weight.T)
+    )(width_steps, proj, fm_weight, lcb_weight, mix_weight.T)
     small = lax.all_gather(packed, ("rep",) + TP)
 
-    up, down = [(i, (i + 1) % 4) for i in range(4)], [(i, (i + 3) % 4) for i in range(4)]
+    side, back = [(i, i ^ 1) for i in range(4)], [(i, i ^ 3) for i in range(4)]
     half = (tables + 1) // 2
-    before = lax.ppermute(own, "x", up)
-    after = lax.ppermute(own, "x", down)
-    own_o = lax.ppermute(own, "rep", SWAP)
-    far_a = lax.ppermute(before[:half], "x", up)
-    far_b = lax.ppermute(after[half:], "x", down)
-    near_o = lax.ppermute(jnp.stack([before, after]), "rep", SWAP)
+    near = lax.ppermute(own, "x", side)
+    next_ = lax.ppermute(own, "x", back)
+    far_a = lax.ppermute(near[:half], "x", back)
+    far_b = lax.ppermute(next_[half:], "x", side)
     far = jnp.concatenate([far_a, far_b], axis=0)
-    far_o = lax.ppermute(far, "rep", SWAP)
-    mine = [own, after, far, before]
-    other = [own_o, near_o[1], far_o, near_o[0]]
+    mine = [own, near, far_a, far_b, next_]
+    other = [lax.ppermute(w, "rep", SWAP) for w in (own, near, far, next_)]
 
     chunks = call(
         project_kernel,
         jax.ShapeDtypeStruct((64, 24, 128), BF16),
-        [idx, token, emb, emb_a, emb_b] + mine + other,
+        [emb, emb_y] + mine + other,
         [pltpu.VMEM((2, 768, 128), F32)],
-        smem=1,
         limit=SOME,
-        specs=[pl.BlockSpec(memory_space=pl.ANY)],
         flops=2 * 25 * 64 * 128 * 512,
         size=5 << 20,
     )
     recv = lax.all_to_all(chunks, ("yl",) + TAB, 0, 0, tiled=True)
+    recv, small = lax.optimization_barrier((recv, small))
 
     weights, mix_full = call(
         unpack_kernel,
@@ -240,7 +224,7 @@
     fm_out, lcb_out, keep, send = call(
         rows_kernel,
         (branch_out, branch_out, partial, partial),
-        [idx, recv, weights, mix_full, fm_cot[0].T, lcb_cot[0].T],
+        [recv, weights, mix_full, fm_cot[0].T, lcb_cot[0].T],
         [
             pltpu.VMEM((2, 800, 128), F32),
             pltpu.VMEM((2, 128, 800), F32),
@@ -248,7 +232,6 @@
             pltpu.VMEM((448, 192), F32),
             pltpu.VMEM((448, 192), F32),
         ],
-        smem=1,
         limit=SOME,
         flops=700_000_000,
         size=5 << 20,
@@ -258,19 +241,19 @@
     pair = (keep.astype(F32) + got.astype(F32)).astype(BF16)
     shares = lax.all_to_all(pair, TP, 0, 0, tiled=True)
     share = jnp.sum(shares.astype(F32), axis=0).astype(BF16)
-    share = jnp.pad(share, ((0, 0), (0, 224)))
-    tiles = jnp.transpose(share.reshape(56, 8, 128), (1, 0, 2))
-    over_z = jnp.sum(lax.all_to_all(tiles, "z", 0, 0, tiled=True).astype(F32), axis=0)
-    parts = lax.all_to_all(jnp.broadcast_to(over_z[None], (4, 56, 128)), "yh", 0, 0, tiled=True)
-    whole = jnp.sum(parts, axis=0).astype(BF16)
-    spread = lax.all_to_all(jnp.broadcast_to(whole[None], (8, 56, 128)), "z", 0, 0, tiled=True)
+    share = jnp.pad(share, ((0, 8), (0, 224)))
+    tiles = jnp.transpose(share.reshape(4, 16, 8, 128), (2, 0, 1, 3)).reshape(32, 16, 128)
+    parts = lax.all_to_all(tiles, TAB, 0, 0, tiled=True)
+    whole = jnp.sum(parts.astype(F32), axis=0).astype(BF16)
+    spread = lax.all_to_all(jnp.broadcast_to(whole[None], (32, 16, 128)), TAB, 0, 0, tiled=True)
     swapped = lax.ppermute(spread, "rep", SWAP)
 
     def rows_of(blocks):
-        return jnp.transpose(blocks, (1, 0, 2)).reshape(56, 1024)[:50, :800].astype(F32)
+        wide = jnp.transpose(blocks.reshape(8, 4, 16, 128), (1, 2, 0, 3)).reshape(64, 1024)
+        return wide[:50, :800].astype(F32)
 
     grad_a, grad_b = rows_of(spread), rows_of(swapped)
-    first = rep == 0
+    first = lax.axis_index("rep") == 0
     grad_fm = jnp.where(first, grad_a, grad_b)
     grad_lcb = jnp.where(first, grad_b, grad_a)
     return fm_out.T[None], lcb_out.T[None], grad_fm, grad_lcb

time: 165 us -> 153 us (0.927)
  blocking collectives: 36.1 us -> 76.1 us
  waiting for transfers between devices: 27.2 us -> 4.48 us
  starting transfers between devices: 65.2 us -> 46.2 us
  local copies, waits for them, and re-layouts: 6.06 us -> 1.93 us
  Pallas kernels: 12.1 us -> 8.42 us
    all_to_all x2 -> x3, blocking collectives: 21 us -> 60.7 us  [the longest x1 31.2 us: per_device(): recv = lax.all_to_all(chunks, ('yl',) + TAB, 0, 0, tiled=True)]
    all_to_all x2 -> x0, waiting for transfers between devices: 21 us -> none  [the longest x1 13.4 us: per_device(): recv = lax.all_to_all(chunks, ('yl',) + TAB, 0, 0, tiled=True)]
    all_to_all x2 -> x0, starting transfers between devices: 20.7 us -> none  [the longest x1 17.3 us: per_device(): recv = lax.all_to_all(chunks, ('yl',) + TAB, 0, 0, tiled=True)]
    pallas_call x4 -> x3, Pallas kernels: 9.21 us -> 5.43 us  [call(): pl.pallas_call(kernel, out_shape=outs, in_specs=[VM] * len(ins), out_spec...]
    ppermute x1, starting transfers between devices: 4.01 us -> 6.61 us  [per_device(): got = lax.ppermute(send, 'rep', SWAP)]
    broadcast_in_dim x3 -> x1, local copies, waits for them, and re-layouts: 2.08 us -> 0.02 us  [per_device(): jnp.broadcast_to(whole[None], (32, 16, 128))]
    ppermute x1, starting transfers between devices: 7.42 us -> 5.67 us  [per_device(): swapped = lax.ppermute(spread, 'rep', SWAP)]
  transfers between devices with their start and end apart: 14 -> 12, of which waited for: 5 -> 3; matrix products, arithmetic and copies ran while one was open for 2% -> 0% of each run, Pallas kernels for 4% -> 2%
where the time goes in v3:
time: 153 us
  blocking collectives  76.1 us (50%)
  starting transfers between devices  46.2 us (30%)
  between operations  14.4 us (9%)
  Pallas kernels  8.42 us (6%)
  waiting for transfers between devices  4.48 us (3%)
  local copies, waits for them, and re-layouts  1.93 us (1%)
    all_to_all x1, blocking collectives, per_device(): recv = lax.all_to_all(chunks, ('yl',) + TAB, 0, 0, tiled=True)  31.2 us
    all_to_all x1, blocking collectives, per_device(): shares = lax.all_to_all(pair, TP, 0, 0, tiled=True)  15.4 us
    all_to_all x1, blocking collectives, per_device(): parts = lax.all_to_all(tiles, TAB, 0, 0, tiled=True)  15.1 us
    all_to_all x1, blocking collectives, per_device(): lax.all_to_all(jnp.broadcast_to(whole[None], (32, 16, 128)), TAB, 0, 0, t...  14.4 us
    ppermute x4, starting transfers between devices, per_device(): other = [lax.ppermute(w, 'rep', SWAP) for w in (own, near, far, next_)]  14.2 us
    ppermute x1, starting transfers between devices, per_device(): far_a = lax.ppermute(near[:half], 'x', back)  6.74 us
    ppermute x1, starting transfers between devices, per_device(): got = lax.ppermute(send, 'rep', SWAP)  6.61 us
    ppermute x1, starting transfers between devices, per_device(): swapped = lax.ppermute(spread, 'rep', SWAP)  5.67 us
  transfers between devices with their start and end apart: 12, of which 3 were waited for; matrix products, arithmetic and copies ran while one was open for 0% of the time, Pallas kernels for 2%

profile of v3, /device:TPU:1, one launch (start us, length us, event | category | flops | bytes accessed | tf_op | source)
XLA Modules:
  0.0 152.7 jit_solution(14203854386753114602)
XLA Ops:
  7.2 0.0 copy-start.1
  7.2 0.0 all-gather.3.cloned.1.call-start
  7.2 3.0 %shard_map.111 = (bf16[25,16,512]{2,1,0:T(8,128)(2,1)}, bf16[9,56,128]{2,1,0:T(8,128)(2,1)}) custom-call(s32[25]{0:T(128)} %steps_ref.1, bf16[12,25,512]{2,1,0:T(8,128)(2,1)} %bitcast.49, bf16[50,800]{1,0:T(8,128)(2,1)} %fm_any.1, bf16[50,800]{1,0:T(8,128)(2,1)} %lcb_any.1, bf16[192,100]{1,0:T(8,128)(2,1)} %bitcast.51), custom_call_target="tpu_custom_call" | custom-call | flops 1048576 | bytes 2097152 | tf_op jit(solution)/shard_map/pallas_call | solution.py:172
  10.2 0.0 copy-start.2
  10.2 0.0 all-gather.3.cloned.1.call-update
  10.3 4.1 %collective-permute-start.1 = (bf16[25,16,512]{2,1,0:T(8,128)(2,1)}, bf16[25,16,512]{2,1,0:T(8,128)(2,1)S(1)}, u32[]{:S(2)}, u32[]{:S(2)}) collective-permute-start(bf16[25,16,512]{2,1,0:T(8,128)(2,1)} %get-tuple-element.14.rest_0_), channel_id=1, source_target_pairs={{0,1},{1,0},{2,3},{3,2},{4,5},{5,4},{6,7},{7,6},{8,9},{9,8},{10,11... | collective-permute-start | bytes 1228808 | tf_op jit(solution)/shard_map/ppermute | solution.py:194
  14.3 3.7 %collective-permute-start.3 = (bf16[25,16,512]{2,1,0:T(8,128)(2,1)}, bf16[25,16,512]{2,1,0:T(8,128)(2,1)S(1)}, u32[]{:S(2)}, u32[]{:S(2)}) collective-permute-start(bf16[25,16,512]{2,1,0:T(8,128)(2,1)} %get-tuple-element.14.rest_0_), channel_id=1, source_target_pairs={{0,3},{1,2},{2,1},{3,0},{4,7},{5,6},{6,5},{7,4},{8,11},{9,10},{10,... | collective-permute-start | bytes 1228808 | tf_op jit(solution)/shard_map/ppermute | solution.py:195
  18.1 3.2 %collective-permute-start = (bf16[25,32,512]{2,1,0:T(8,128)(2,1)}, bf16[25,32,512]{2,1,0:T(8,128)(2,1)S(1)}, u32[]{:S(2)}, u32[]{:S(2)}) collective-permute-start(bf16[25,32,512]{2,1,0:T(8,128)(2,1)} %bitcast.40), channel_id=1, source_target_pairs={{0,4},{4,0},{1,5},{5,1},{2,6},{6,2},{3,7},{7,3},{8,12},{12,8},{9,1... | collective-permute-start | bytes 2457608 | tf_op jit(solution)/shard_map/ppermute | solution.py:169
  21.3 0.0 collective-permute-done.1.rest_1_
  21.3 6.7 %collective-permute-start.2 = (bf16[13,16,512]{2,1,0:T(8,128)(2,1)S(1)}, bf16[13,16,512]{2,1,0:T(8,128)(2,1)S(1)}, u32[]{:S(2)}, u32[]{:S(2)}) collective-permute-start(bf16[13,16,512]{2,1,0:T(8,128)(2,1)S(1)} %slice.16), channel_id=1, source_target_pairs={{0,3},{1,2},{2,1},{3,0},{4,7},{5,6},{6,5},{7,4},{8,11},{9,10},{10,... | collective-permute-start | bytes 638984 | tf_op jit(solution)/shard_map/ppermute | solution.py:196
  28.1 0.0 collective-permute-done.3.rest_4_
  28.1 1.9 %collective-permute-start.4 = (bf16[12,16,512]{2,1,0:T(8,128)(2,1)S(1)}, bf16[12,16,512]{2,1,0:T(8,128)(2,1)S(1)}, u32[]{:S(2)}, u32[]{:S(2)}) collective-permute-start(bf16[12,16,512]{2,1,0:T(8,128)(2,1)S(1)} %slice.17), channel_id=1, source_target_pairs={{0,1},{1,0},{2,3},{3,2},{4,5},{5,4},{6,7},{7,6},{8,9},{9,8},{10,11... | collective-permute-start | bytes 589832 | tf_op jit(solution)/shard_map/ppermute | solution.py:197
  30.0 6.4 %collective-permute-start.5 = (bf16[25,16,512]{2,1,0:T(8,128)(2,1)}, bf16[25,16,512]{2,1,0:T(8,128)(2,1)S(1)}, u32[]{:S(2)}, u32[]{:S(2)}) collective-permute-start(bf16[25,16,512]{2,1,0:T(8,128)(2,1)} %get-tuple-element.14.rest_0_), channel_id=1, source_target_pairs={{0,256},{256,0},{1,257},{257,1},{2,258},{258,2},{3,259},{259,3},{4... | collective-permute-start | bytes 1228808 | tf_op jit(solution)/shard_map/ppermute | solution.py:200
  36.4 1.9 %collective-permute-start.6 = (bf16[25,16,512]{2,1,0:T(8,128)(2,1)S(1)}, bf16[25,16,512]{2,1,0:T(8,128)(2,1)S(1)}, u32[]{:S(2)}, u32[]{:S(2)}) collective-permute-start(bf16[25,16,512]{2,1,0:T(8,128)(2,1)S(1)} %collective-permute-done.1.rest_1_), channel_id=1, source_target_pairs={{0,256},{256,0},{1,257},{257,1},{2,258},{258,2},{3,259},{259,3},{4... | collective-permute-start | bytes 1228808 | tf_op jit(solution)/shard_map/ppermute | solution.py:200
  38.3 0.0 collective-permute-done.4.rest_3_
  38.3 4.0 %collective-permute-start.8 = (bf16[25,16,512]{2,1,0:T(8,128)(2,1)S(1)}, bf16[25,16,512]{2,1,0:T(8,128)(2,1)S(1)}, u32[]{:S(2)}, u32[]{:S(2)}) collective-permute-start(bf16[25,16,512]{2,1,0:T(8,128)(2,1)S(1)} %collective-permute-done.3.rest_4_), channel_id=1, source_target_pairs={{0,256},{256,0},{1,257},{257,1},{2,258},{258,2},{3,259},{259,3},{4... | collective-permute-start | bytes 1228808 | tf_op jit(solution)/shard_map/ppermute | solution.py:200
  42.4 0.0 collective-permute-done.2.rest_2_
  42.4 1.9 %collective-permute-start.7 = (bf16[25,16,512]{2,1,0:T(8,128)(2,1)S(1)}, bf16[25,16,512]{2,1,0:T(8,128)(2,1)S(1)}, u32[]{:S(2)}, u32[]{:S(2)}) collective-permute-start(bf16[25,16,512]{2,1,0:T(8,128)(2,1)S(1)} %pad_maximum_fusion), channel_id=1, source_target_pairs={{0,256},{256,0},{1,257},{257,1},{2,258},{258,2},{3,259},{259,3},{4... | collective-permute-start | bytes 1228808 | tf_op jit(solution)/shard_map/ppermute | solution.py:200
  44.4 0.0 collective-permute-done.5.rest_5_
  44.4 0.0 collective-permute-done.6.rest_6_
  44.4 0.0 collective-permute-done.8.rest_8_
  44.4 0.0 collective-permute-done.emb_y_ref
  44.4 1.7 %collective-permute-done.7.rest_7_ = bf16[25,16,512]{2,1,0:T(8,128)(2,1)S(1)} collective-permute-done((bf16[25,16,512]{2,1,0:T(8,128)(2,1)S(1)}, bf16[25,16,512]{2,1,0:T(8,128)(2,1)S(1)}, u32[]{:S(2)}, u32[]{:S(2)}) %collective-permute-start.7) | collective-permute-done | bytes 409632 | tf_op jit(solution)/shard_map/ppermute | solution.py:200
  46.1 0.0 copy-done.1
  46.1 0.0 copy-done.2
  46.1 2.3 %shard_map.112 = bf16[64,24,128]{2,1,0:T(8,128)(2,1)S(1)} custom-call(bf16[25,32,512]{2,1,0:T(8,128)(2,1)S(1)} %bitcast.41, bf16[25,32,512]{2,1,0:T(8,128)(2,1)S(1)} %collective-permute-done.emb_y_ref, bf16[25,16,512]{2,1,0:T(8,128)(2,1)S(1)} %copy-done.2, bf16[25,16,512]{2,1,0:T(8,128)(2,1)S(1)} %collective-permute-done.1.rest_1_, ...), custom_call_target="tpu_custom_call" | custom-call | flops 209715200 | bytes 5242880 | tf_op jit(solution)/shard_map/pallas_call | solution.py:24
  48.4 0.0 copy-start.3
  48.4 0.0 copy-start.4
  48.4 31.2 %all_to_all.20.recv_ref = bf16[64,24,128]{2,1,0:T(8,128)(2,1)S(1)} all-to-all(bf16[64,24,128]{2,1,0:T(8,128)(2,1)S(1)} %shard_map.112), channel_id=1, replica_groups=mesh['rep'=2,'z'=8,'yh'=4,'yl'=2,'x'=4] {'yl','z','yh'}, dimensions={0} | all-to-all | bytes 786432 | tf_op jit(solution)/shard_map/all_to_all | solution.py:211
  79.6 0.0 all-gather.3.cloned.1.call-done
  79.6 0.0 copy-start
  79.6 1.6 %copy-done = bf16[144,56,128]{2,1,0:T(8,128)(2,1)S(1)} copy-done((bf16[144,56,128]{2,1,0:T(8,128)(2,1)S(1)}, bf16[144,56,128]{2,1,0:T(8,128)(2,1)}, u32[]{:S(2)}) %copy-start) | copy-done | bytes 2064408
  81.2 0.6 shard_map.113
  81.8 0.0 copy-done.3
  81.8 0.0 copy-done.4
  81.8 2.5 %shard_map.114 = (bf16[192,400]{1,0:T(8,128)(2,1)}, bf16[192,400]{1,0:T(8,128)(2,1)}, bf16[8,56,800]{2,1,0:T(8,128)(2,1)S(1)}, bf16[8,56,800]{2,1,0:T(8,128)(2,1)S(1)}) custom-call(bf16[64,24,128]{2,1,0:T(8,128)(2,1)S(1)} %all_to_all.20.recv_ref, bf16[2,400,800]{2,1,0:T(8,128)(2,1)S(1)} %get-tuple-element.18.weight_ref, ...), custom_call_target="tpu_custom_call" | custom-call | flops 700000000 | bytes 5242880 | tf_op jit(solution)/shard_map/pallas_call | solution.py:24
  84.3 6.6 %collective-permute-start.9 = (bf16[8,56,800]{2,1,0:T(8,128)(2,1)S(1)}, bf16[8,56,800]{2,1,0:T(8,128)(2,1)S(1)}, u32[]{:S(2)}, u32[]{:S(2)}) collective-permute-start(bf16[8,56,800]{2,1,0:T(8,128)(2,1)S(1)} %get-tuple-element.23), channel_id=1, source_target_pairs={{0,256},{256,0},{1,257},{257,1},{2,258},{258,2},{3,259},{259,3},{4... | collective-permute-start | bytes 2150408 | tf_op jit(solution)/shard_map/ppermute | solution.py:240
  91.0 1.9 %collective-permute-done.9 = bf16[8,56,800]{2,1,0:T(8,128)(2,1)S(1)} collective-permute-done((bf16[8,56,800]{2,1,0:T(8,128)(2,1)S(1)}, bf16[8,56,800]{2,1,0:T(8,128)(2,1)S(1)}, u32[]{:S(2)}, u32[]{:S(2)}) %collective-permute-start.9) | collective-permute-done | bytes 716832 | tf_op jit(solution)/shard_map/ppermute | solution.py:240
  92.9 0.2 add_convert_fusion
  93.1 15.4 %all_to_all.21 = bf16[8,56,800]{2,1,0:T(8,128)(2,1)S(1)} all-to-all(bf16[8,56,800]{2,1,0:T(8,128)(2,1)S(1)} %add_convert_fusion), channel_id=1, replica_groups=mesh['rep'=2,'z'=8,'yh'=4,'yl'=2,'x'=4] {'yl','x'}, dimensions={0} | all-to-all | bytes 1433600 | tf_op jit(solution)/shard_map/all_to_all | solution.py:242
  108.5 0.1 reduce_sum.24
  108.8 15.1 %all_to_all.22 = bf16[32,16,128]{2,1,0:T(8,128)(2,1)S(1)} all-to-all(bf16[32,16,128]{2,1,0:T(8,128)(2,1)S(1)} %bitcast.46), channel_id=1, replica_groups=mesh['rep'=2,'z'=8,'yh'=4,'yl'=2,'x'=4] {'z','yh'}, dimensions={0} | all-to-all | bytes 262144 | tf_op jit(solution)/shard_map/all_to_all | solution.py:246
  123.9 14.4 %all_to_all.23 = bf16[32,16,128]{2,1,0:T(8,128)(2,1)S(1)} all-to-all(bf16[32,16,128]{2,1,0:T(8,128)(2,1)S(1)} %broadcast_in_dim.14), channel_id=1, replica_groups=mesh['rep'=2,'z'=8,'yh'=4,'yl'=2,'x'=4] {'z','yh'}, dimensions={0} | all-to-all | bytes 262144 | tf_op jit(solution)/shard_map/all_to_all | solution.py:248
  138.3 5.7 %collective-permute-start.10 = (bf16[32,16,128]{2,1,0:T(8,128)(2,1)S(1)}, bf16[32,16,128]{2,1,0:T(8,128)(2,1)S(1)}, u32[]{:S(2)}, u32[]{:S(2)}) collective-permute-start(bf16[32,16,128]{2,1,0:T(8,128)(2,1)S(1)} %all_to_all.23), channel_id=1, source_target_pairs={{0,256},{256,0},{1,257},{257,1},{2,258},{258,2},{3,259},{259,3},{4... | collective-permute-start | bytes 393224 | tf_op jit(solution)/shard_map/ppermute | solution.py:249
  144.0 0.1 copy.16
  144.1 0.9 collective-permute-done.10
  145.0 0.1 copy.17
  145.1 0.8 convert_select_fusion
  (10 shorter events, 0.2 us)
Async XLA Ops:
  7.2 38.9 %copy-start.1 = (bf16[32,25,512]{2,0,1:T(8,128)(2,1)S(1)}, bf16[32,25,512]{2,0,1:T(8,128)(2,1)}, u32[]{:S(2)}) copy-start(bf16[32,25,512]{2,0,1:T(8,128)(2,1)} %param.8) | copy-start | bytes 2457604
  7.2 72.4 %all-gather.3.cloned.1.call-start = ((), (), s32[]{:S(2)}) async-start(), calls=%async_computation.4 | async-start | bytes 2193408 | tf_op jit(solution)/shard_map/all_gather | solution.py:190
  10.2 35.9 %copy-start.2 = (bf16[25,16,512]{2,1,0:T(8,128)(2,1)S(1)}, bf16[25,16,512]{2,1,0:T(8,128)(2,1)}, u32[]{:S(2)}) copy-start(bf16[25,16,512]{2,1,0:T(8,128)(2,1)} %get-tuple-element.14.rest_0_) | copy-start | bytes 1228804
  10.3 11.0 %collective-permute-start.1 = (bf16[25,16,512]{2,1,0:T(8,128)(2,1)}, bf16[25,16,512]{2,1,0:T(8,128)(2,1)S(1)}, u32[]{:S(2)}, u32[]{:S(2)}) collective-permute-start(bf16[25,16,512]{2,1,0:T(8,128)(2,1)} %get-tuple-element.14.rest_0_), channel_id=1, source_target_pairs={{0,1},{1,0},{2,3},{3,2},{4,5},{5,4},{6,7},{7,6},{8,9},{9,8},{10,11... | collective-permute-start | bytes 1228808 | tf_op jit(solution)/shard_map/ppermute | solution.py:194
  14.3 13.7 %collective-permute-start.3 = (bf16[25,16,512]{2,1,0:T(8,128)(2,1)}, bf16[25,16,512]{2,1,0:T(8,128)(2,1)S(1)}, u32[]{:S(2)}, u32[]{:S(2)}) collective-permute-start(bf16[25,16,512]{2,1,0:T(8,128)(2,1)} %get-tuple-element.14.rest_0_), channel_id=1, source_target_pairs={{0,3},{1,2},{2,1},{3,0},{4,7},{5,6},{6,5},{7,4},{8,11},{9,10},{10,... | collective-permute-start | bytes 1228808 | tf_op jit(solution)/shard_map/ppermute | solution.py:195
  18.1 26.3 %collective-permute-start = (bf16[25,32,512]{2,1,0:T(8,128)(2,1)}, bf16[25,32,512]{2,1,0:T(8,128)(2,1)S(1)}, u32[]{:S(2)}, u32[]{:S(2)}) collective-permute-start(bf16[25,32,512]{2,1,0:T(8,128)(2,1)} %bitcast.40), channel_id=1, source_target_pairs={{0,4},{4,0},{1,5},{5,1},{2,6},{6,2},{3,7},{7,3},{8,12},{12,8},{9,1... | collective-permute-start | bytes 2457608 | tf_op jit(solution)/shard_map/ppermute | solution.py:169
  21.3 21.1 %collective-permute-start.2 = (bf16[13,16,512]{2,1,0:T(8,128)(2,1)S(1)}, bf16[13,16,512]{2,1,0:T(8,128)(2,1)S(1)}, u32[]{:S(2)}, u32[]{:S(2)}) collective-permute-start(bf16[13,16,512]{2,1,0:T(8,128)(2,1)S(1)} %slice.16), channel_id=1, source_target_pairs={{0,3},{1,2},{2,1},{3,0},{4,7},{5,6},{6,5},{7,4},{8,11},{9,10},{10,... | collective-permute-start | bytes 638984 | tf_op jit(solution)/shard_map/ppermute | solution.py:196
  28.1 10.2 %collective-permute-start.4 = (bf16[12,16,512]{2,1,0:T(8,128)(2,1)S(1)}, bf16[12,16,512]{2,1,0:T(8,128)(2,1)S(1)}, u32[]{:S(2)}, u32[]{:S(2)}) collective-permute-start(bf16[12,16,512]{2,1,0:T(8,128)(2,1)S(1)} %slice.17), channel_id=1, source_target_pairs={{0,1},{1,0},{2,3},{3,2},{4,5},{5,4},{6,7},{7,6},{8,9},{9,8},{10,11... | collective-permute-start | bytes 589832 | tf_op jit(solution)/shard_map/ppermute | solution.py:197
  30.0 14.3 %collective-permute-start.5 = (bf16[25,16,512]{2,1,0:T(8,128)(2,1)}, bf16[25,16,512]{2,1,0:T(8,128)(2,1)S(1)}, u32[]{:S(2)}, u32[]{:S(2)}) collective-permute-start(bf16[25,16,512]{2,1,0:T(8,128)(2,1)} %get-tuple-element.14.rest_0_), channel_id=1, source_target_pairs={{0,256},{256,0},{1,257},{257,1},{2,258},{258,2},{3,259},{259,3},{4... | collective-permute-start | bytes 1228808 | tf_op jit(solution)/shard_map/ppermute | solution.py:200
  36.4 8.0 %collective-permute-start.6 = (bf16[25,16,512]{2,1,0:T(8,128)(2,1)S(1)}, bf16[25,16,512]{2,1,0:T(8,128)(2,1)S(1)}, u32[]{:S(2)}, u32[]{:S(2)}) collective-permute-start(bf16[25,16,512]{2,1,0:T(8,128)(2,1)S(1)} %collective-permute-done.1.rest_1_), channel_id=1, source_target_pairs={{0,256},{256,0},{1,257},{257,1},{2,258},{258,2},{3,259},{259,3},{4... | collective-permute-start | bytes 1228808 | tf_op jit(solution)/shard_map/ppermute | solution.py:200
  38.3 6.1 %collective-permute-start.8 = (bf16[25,16,512]{2,1,0:T(8,128)(2,1)S(1)}, bf16[25,16,512]{2,1,0:T(8,128)(2,1)S(1)}, u32[]{:S(2)}, u32[]{:S(2)}) collective-permute-start(bf16[25,16,512]{2,1,0:T(8,128)(2,1)S(1)} %collective-permute-done.3.rest_4_), channel_id=1, source_target_pairs={{0,256},{256,0},{1,257},{257,1},{2,258},{258,2},{3,259},{259,3},{4... | collective-permute-start | bytes 1228808 | tf_op jit(solution)/shard_map/ppermute | solution.py:200
  42.4 3.6 %collective-permute-start.7 = (bf16[25,16,512]{2,1,0:T(8,128)(2,1)S(1)}, bf16[25,16,512]{2,1,0:T(8,128)(2,1)S(1)}, u32[]{:S(2)}, u32[]{:S(2)}) collective-permute-start(bf16[25,16,512]{2,1,0:T(8,128)(2,1)S(1)} %pad_maximum_fusion), channel_id=1, source_target_pairs={{0,256},{256,0},{1,257},{257,1},{2,258},{258,2},{3,259},{259,3},{4... | collective-permute-start | bytes 1228808 | tf_op jit(solution)/shard_map/ppermute | solution.py:200
  48.4 33.4 %copy-start.3 = (bf16[1,400,192]{1,2,0:T(8,128)(2,1)S(1)}, bf16[1,400,192]{1,2,0:T(8,128)(2,1)}, u32[]{:S(2)}) copy-start(bf16[1,400,192]{1,2,0:T(8,128)(2,1)} %param.14) | copy-start | bytes 460804
  48.4 33.4 %copy-start.4 = (bf16[1,400,192]{1,2,0:T(8,128)(2,1)S(1)}, bf16[1,400,192]{1,2,0:T(8,128)(2,1)}, u32[]{:S(2)}) copy-start(bf16[1,400,192]{1,2,0:T(8,128)(2,1)} %param.15) | copy-start | bytes 460804
  79.6 1.6 %copy-start = (bf16[144,56,128]{2,1,0:T(8,128)(2,1)S(1)}, bf16[144,56,128]{2,1,0:T(8,128)(2,1)}, u32[]{:S(2)}) copy-start(bf16[144,56,128]{2,1,0:T(8,128)(2,1)} %all-gather.3.cloned.1.call-done) | copy-start | bytes 6193156
  84.3 8.5 %collective-permute-start.9 = (bf16[8,56,800]{2,1,0:T(8,128)(2,1)S(1)}, bf16[8,56,800]{2,1,0:T(8,128)(2,1)S(1)}, u32[]{:S(2)}, u32[]{:S(2)}) collective-permute-start(bf16[8,56,800]{2,1,0:T(8,128)(2,1)S(1)} %get-tuple-element.23), channel_id=1, source_target_pairs={{0,256},{256,0},{1,257},{257,1},{2,258},{258,2},{3,259},{259,3},{4... | collective-permute-start | bytes 2150408 | tf_op jit(solution)/shard_map/ppermute | solution.py:240
  138.3 6.6 %collective-permute-start.10 = (bf16[32,16,128]{2,1,0:T(8,128)(2,1)S(1)}, bf16[32,16,128]{2,1,0:T(8,128)(2,1)S(1)}, u32[]{:S(2)}, u32[]{:S(2)}) collective-permute-start(bf16[32,16,128]{2,1,0:T(8,128)(2,1)S(1)} %all_to_all.23), channel_id=1, source_target_pairs={{0,256},{256,0},{1,257},{257,1},{2,258},{258,2},{3,259},{259,3},{4... | collective-permute-start | bytes 393224 | tf_op jit(solution)/shard_map/ppermute | solution.py:249
Sparse Core Ops, SparseCore 0:
  10.7 46.2 all-gather.2

commit v4 on v3

--- a/solution.py
+++ b/solution.py
@@ -15,6 +15,10 @@
 SWAP = [(0, 1), (1, 0)]
 TAB = ("z", "yh")
 TP = ("yl", "x")
+GROUPS = [
+    [(((rep * 4 + (yh - yl) % 4) * 2 + yl) * 4) + x for rep in range(2) for yl in range(2) for x in range(4)]
+    for yh in range(4)
+]
 
 VM = pl.BlockSpec(memory_space=pltpu.VMEM)
 SM = pl.BlockSpec(memory_space=pltpu.SMEM)
@@ -92,6 +96,10 @@
     mix_ref[...] = mixw_ref[...].astype(BF16)
 
 
+def hold_kernel(src_ref, out_ref):
+    del src_ref, out_ref
+
+
 def project_kernel(emb_ref, emb_y_ref, *rest):
     w_refs, out_ref, acc_ref = rest[:-2], rest[-2], rest[-1]
     mine = lax.axis_index("yl")
@@ -167,6 +175,15 @@
     tables, widest = emb_rows.shape[1], emb_rows.shape[2]
     emb = jnp.transpose(emb_rows, (1, 0, 2))
     emb_y = lax.ppermute(emb, "yl", SWAP)
+    emb_y = pl.pallas_call(
+        hold_kernel,
+        out_shape=jax.ShapeDtypeStruct(emb.shape, BF16),
+        in_specs=[pl.BlockSpec(memory_space=pl.ANY)],
+        out_specs=pl.BlockSpec(memory_space=pl.ANY),
+        input_output_aliases={0: 0},
+        compiler_params=pltpu.CompilerParams(vmem_limit_bytes=1 << 20),
+        cost_estimate=pl.CostEstimate(flops=20_000_000_000, bytes_accessed=0, transcendentals=0),
+    )(emb_y)
 
     proj = jnp.transpose(proj_weight, (2, 0, 1))
     own, packed = pl.pallas_call(
@@ -187,7 +204,7 @@
         ],
         cost_estimate=pl.CostEstimate(flops=1 << 20, bytes_accessed=2 << 20, transcendentals=0),
     )(width_steps, proj, fm_weight, lcb_weight, mix_weight.T)
-    small = lax.all_gather(packed, ("rep",) + TP)
+    small = lax.all_gather(packed, ("rep", "yh", "yl", "x"), axis_index_groups=GROUPS)
 
     side, back = [(i, i ^ 1) for i in range(4)], [(i, i ^ 3) for i in range(4)]
     half = (tables + 1) // 2
@@ -195,7 +212,7 @@
     next_ = lax.ppermute(own, "x", back)
     far_a = lax.ppermute(near[:half], "x", back)
     far_b = lax.ppermute(next_[half:], "x", side)
-    far = jnp.concatenate([far_a, far_b], axis=0)
+    far, emb_y = lax.optimization_barrier((jnp.concatenate([far_a, far_b], axis=0), emb_y))
     mine = [own, near, far_a, far_b, next_]
     other = [lax.ppermute(w, "rep", SWAP) for w in (own, near, far, next_)]
 
@@ -209,7 +226,6 @@
         size=5 << 20,
     )
     recv = lax.all_to_all(chunks, ("yl",) + TAB, 0, 0, tiled=True)
-    recv, small = lax.optimization_barrier((recv, small))
 
     weights, mix_full = call(
         unpack_kernel,

time: 153 us -> 183 us (1.20)
  waiting for transfers between devices: 4.48 us -> 40.1 us
  blocking collectives: 76.1 us -> 55.7 us
  starting transfers between devices: 46.2 us -> 60 us
    all_gather x1, waiting for transfers between devices: 0.01 us -> 32.9 us  [per_device(): lax.all_gather(packed, ('rep', 'yh', 'yl', 'x'), axis_index_groups=GROUPS)]
    all_to_all x1 -> x0, blocking collectives: 31.2 us -> none  [per_device(): recv = lax.all_to_all(chunks, ('yl',) + TAB, 0, 0, tiled=True)]
    all_to_all x0 -> x1, starting transfers between devices: none -> 18.6 us  [per_device(): recv = lax.all_to_all(chunks, ('yl',) + TAB, 0, 0, tiled=True)]
    all_to_all x1, blocking collectives: 15.1 us -> 24.3 us  [per_device(): parts = lax.all_to_all(tiles, TAB, 0, 0, tiled=True)]
    ppermute x1, starting transfers between devices: 6.61 us -> 1.92 us  [per_device(): got = lax.ppermute(send, 'rep', SWAP)]
    ppermute x1, waiting for transfers between devices: 0.01 us -> 2.34 us  [per_device(): near = lax.ppermute(own, 'x', side)]
  transfers between devices with their start and end apart: 12 -> 13, of which waited for: 3 -> 5; matrix products, arithmetic and copies ran while one was open for 0% -> 0% of each run, Pallas kernels for 2% -> 4%
where the time goes in v4:
time: 183 us; the launch traced here: 182 us
  starting transfers between devices  60 us (33%)
  blocking collectives  55.7 us (30%)
  waiting for transfers between devices  40.1 us (22%)
  between operations  14.3 us (8%)
  Pallas kernels  9.05 us (5%)
  local copies, waits for them, and re-layouts  1.92 us (1%)
    all_gather x1, waiting for transfers between devices, per_device(): lax.all_gather(packed, ('rep', 'yh', 'yl', 'x'), axis_index_groups=GROUPS)  32.9 us
    all_to_all x1, blocking collectives, per_device(): parts = lax.all_to_all(tiles, TAB, 0, 0, tiled=True)  24.3 us
    all_to_all x1, starting transfers between devices, per_device(): recv = lax.all_to_all(chunks, ('yl',) + TAB, 0, 0, tiled=True)  18.6 us
    all_to_all x1, blocking collectives, per_device(): shares = lax.all_to_all(pair, TP, 0, 0, tiled=True)  16.9 us
    all_to_all x1, blocking collectives, per_device(): lax.all_to_all(jnp.broadcast_to(whole[None], (32, 16, 128)), TAB, 0, 0, t...  14.4 us
    ppermute x4, starting transfers between devices, per_device(): other = [lax.ppermute(w, 'rep', SWAP) for w in (own, near, far, next_)]  13.1 us
    ppermute x1, starting transfers between devices, per_device(): far_a = lax.ppermute(near[:half], 'x', back)  7.31 us
    ppermute x1, starting transfers between devices, per_device(): swapped = lax.ppermute(spread, 'rep', SWAP)  6.32 us
  transfers between devices with their start and end apart: 13, of which 5 were waited for; matrix products, arithmetic and copies ran while one was open for 0% of the time, Pallas kernels for 4%

profile of v4, /device:TPU:1, one launch (start us, length us, event | category | flops | bytes accessed | tf_op | source)
XLA Modules:
  0.0 182.3 jit_solution(7593410303035949577)
XLA Ops:
  7.2 0.0 all-gather.3.cloned.1.call-start
  7.2 4.0 %collective-permute-start.4 = (bf16[25,32,512]{2,1,0:T(8,128)(2,1)}, bf16[25,32,512]{2,1,0:T(8,128)(2,1)S(1)}, u32[]{:S(2)}, u32[]{:S(2)}) collective-permute-start(bf16[25,32,512]{2,1,0:T(8,128)(2,1)} %bitcast.40), channel_id=1, source_target_pairs={{0,4},{4,0},{1,5},{5,1},{2,6},{6,2},{3,7},{7,3},{8,12},{12,8},{9,1... | collective-permute-start | bytes 2457608 | tf_op jit(solution)/shard_map/ppermute | solution.py:177
  11.3 2.9 %shard_map.111 = (bf16[25,16,512]{2,1,0:T(8,128)(2,1)}, bf16[9,56,128]{2,1,0:T(8,128)(2,1)}) custom-call(s32[25]{0:T(128)} %steps_ref.1, bf16[12,25,512]{2,1,0:T(8,128)(2,1)} %bitcast.49, bf16[50,800]{1,0:T(8,128)(2,1)} %fm_any.1, bf16[50,800]{1,0:T(8,128)(2,1)} %lcb_any.1, bf16[192,100]{1,0:T(8,128)(2,1)} %bitcast.51), custom_call_target="tpu_custom_call" | custom-call | flops 1048576 | bytes 2097152 | tf_op jit(solution)/shard_map/pallas_call | solution.py:189
  14.1 0.0 all-gather.3.cloned.1.call-update
  14.1 3.1 %collective-permute-start = (bf16[25,16,512]{2,1,0:T(8,128)(2,1)}, bf16[25,16,512]{2,1,0:T(8,128)(2,1)S(1)}, u32[]{:S(2)}, u32[]{:S(2)}) collective-permute-start(bf16[25,16,512]{2,1,0:T(8,128)(2,1)} %get-tuple-element.14.rest_0_), channel_id=1, source_target_pairs={{0,1},{1,0},{2,3},{3,2},{4,5},{5,4},{6,7},{7,6},{8,9},{9,8},{10,11... | collective-permute-start | bytes 1228808 | tf_op jit(solution)/shard_map/ppermute | solution.py:211
  17.3 3.7 %collective-permute-start.2 = (bf16[25,16,512]{2,1,0:T(8,128)(2,1)}, bf16[25,16,512]{2,1,0:T(8,128)(2,1)S(1)}, u32[]{:S(2)}, u32[]{:S(2)}) collective-permute-start(bf16[25,16,512]{2,1,0:T(8,128)(2,1)} %get-tuple-element.14.rest_0_), channel_id=1, source_target_pairs={{0,3},{1,2},{2,1},{3,0},{4,7},{5,6},{6,5},{7,4},{8,11},{9,10},{10,... | collective-permute-start | bytes 1228808 | tf_op jit(solution)/shard_map/ppermute | solution.py:212
  21.0 2.3 %collective-permute-done.rest_1_ = bf16[25,16,512]{2,1,0:T(8,128)(2,1)S(1)} collective-permute-done((bf16[25,16,512]{2,1,0:T(8,128)(2,1)}, bf16[25,16,512]{2,1,0:T(8,128)(2,1)S(1)}, u32[]{:S(2)}, u32[]{:S(2)}) %collective-permute-start) | collective-permute-done | bytes 409632 | tf_op jit(solution)/shard_map/ppermute | solution.py:211
  23.4 7.3 %collective-permute-start.1 = (bf16[13,16,512]{2,1,0:T(8,128)(2,1)S(1)}, bf16[13,16,512]{2,1,0:T(8,128)(2,1)S(1)}, u32[]{:S(2)}, u32[]{:S(2)}) collective-permute-start(bf16[13,16,512]{2,1,0:T(8,128)(2,1)S(1)} %slice.16), channel_id=1, source_target_pairs={{0,3},{1,2},{2,1},{3,0},{4,7},{5,6},{6,5},{7,4},{8,11},{9,10},{10,... | collective-permute-start | bytes 638984 | tf_op jit(solution)/shard_map/ppermute | solution.py:213
  30.7 0.0 collective-permute-done.2.rest_4_
  30.7 1.9 %collective-permute-start.3 = (bf16[12,16,512]{2,1,0:T(8,128)(2,1)S(1)}, bf16[12,16,512]{2,1,0:T(8,128)(2,1)S(1)}, u32[]{:S(2)}, u32[]{:S(2)}) collective-permute-start(bf16[12,16,512]{2,1,0:T(8,128)(2,1)S(1)} %slice.17), channel_id=1, source_target_pairs={{0,1},{1,0},{2,3},{3,2},{4,5},{5,4},{6,7},{7,6},{8,9},{9,8},{10,11... | collective-permute-start | bytes 589832 | tf_op jit(solution)/shard_map/ppermute | solution.py:214
  32.6 4.4 %collective-permute-start.5 = (bf16[25,16,512]{2,1,0:T(8,128)(2,1)}, bf16[25,16,512]{2,1,0:T(8,128)(2,1)S(1)}, u32[]{:S(2)}, u32[]{:S(2)}) collective-permute-start(bf16[25,16,512]{2,1,0:T(8,128)(2,1)} %get-tuple-element.14.rest_0_), channel_id=1, source_target_pairs={{0,256},{256,0},{1,257},{257,1},{2,258},{258,2},{3,259},{259,3},{4... | collective-permute-start | bytes 1228808 | tf_op jit(solution)/shard_map/ppermute | solution.py:217
  37.1 1.9 %collective-permute-start.6 = (bf16[25,16,512]{2,1,0:T(8,128)(2,1)S(1)}, bf16[25,16,512]{2,1,0:T(8,128)(2,1)S(1)}, u32[]{:S(2)}, u32[]{:S(2)}) collective-permute-start(bf16[25,16,512]{2,1,0:T(8,128)(2,1)S(1)} %collective-permute-done.rest_1_), channel_id=1, source_target_pairs={{0,256},{256,0},{1,257},{257,1},{2,258},{258,2},{3,259},{259,3},{4... | collective-permute-start | bytes 1228808 | tf_op jit(solution)/shard_map/ppermute | solution.py:217
  39.0 0.0 collective-permute-done.3.rest_3_
  39.0 4.7 %collective-permute-start.8 = (bf16[25,16,512]{2,1,0:T(8,128)(2,1)S(1)}, bf16[25,16,512]{2,1,0:T(8,128)(2,1)S(1)}, u32[]{:S(2)}, u32[]{:S(2)}) collective-permute-start(bf16[25,16,512]{2,1,0:T(8,128)(2,1)S(1)} %collective-permute-done.2.rest_4_), channel_id=1, source_target_pairs={{0,256},{256,0},{1,257},{257,1},{2,258},{258,2},{3,259},{259,3},{4... | collective-permute-start | bytes 1228808 | tf_op jit(solution)/shard_map/ppermute | solution.py:217
  43.7 0.0 collective-permute-done.1.rest_2_
  43.8 0.0 copy-start.1
  43.8 0.0 copy-start.2
  43.8 0.0 collective-permute-done.4.src_ref
  43.8 2.1 %collective-permute-start.7 = (bf16[25,16,512]{2,1,0:T(8,128)(2,1)S(1)}, bf16[25,16,512]{2,1,0:T(8,128)(2,1)S(1)}, u32[]{:S(2)}, u32[]{:S(2)}) collective-permute-start(bf16[25,16,512]{2,1,0:T(8,128)(2,1)S(1)} %pad_maximum_fusion), channel_id=1, source_target_pairs={{0,256},{256,0},{1,257},{257,1},{2,258},{258,2},{3,259},{259,3},{4... | collective-permute-start | bytes 1228808 | tf_op jit(solution)/shard_map/ppermute | solution.py:217
  45.9 0.0 collective-permute-done.5.rest_5_
  45.9 0.0 collective-permute-done.6.rest_6_
  45.9 0.0 collective-permute-done.8.rest_8_
  45.9 1.7 collective-permute-done.7.rest_7_
  47.6 0.0 copy-done.1
  47.6 0.0 copy-done.2
  47.6 3.1 %shard_map.113 = bf16[64,24,128]{2,1,0:T(8,128)(2,1)} custom-call(bf16[25,32,512]{2,1,0:T(8,128)(2,1)S(1)} %bitcast.41, bf16[25,32,512]{2,1,0:T(8,128)(2,1)S(1)} %shard_map.112.emb_y_ref, bf16[25,16,512]{2,1,0:T(8,128)(2,1)S(1)} %copy-done.2, bf16[25,16,512]{2,1,0:T(8,128)(2,1)S(1)} %collective-permute-done.rest_1_, ...), custom_call_target="tpu_custom_call" | custom-call | flops 209715200 | bytes 5242880 | tf_op jit(solution)/shard_map/pallas_call | solution.py:28
  50.6 0.0 copy-start.3
  50.6 0.0 copy-start.4
  50.6 18.6 %all-to-all-start = ((bf16[64,24,128]{2,1,0:T(8,128)(2,1)}), bf16[64,24,128]{2,1,0:T(8,128)(2,1)S(1)}, u32[]{:S(2)}, u32[]{:S(2)}) async-start(bf16[64,24,128]{2,1,0:T(8,128)(2,1)} %shard_map.113), calls=%async_computation | async-start | bytes 786432 | tf_op jit(solution)/shard_map/all_to_all | solution.py:228
  69.2 32.9 %all-gather.3.cloned.1.call-done = bf16[144,56,128]{2,1,0:T(8,128)(2,1)} async-done(((bf16[9,56,128]{2,1,0:T(8,128)(2,1)}), bf16[144,56,128]{2,1,0:T(8,128)(2,1)}) %all-gather.3.cloned.1.call-update) | async-done | bytes 2064400 | tf_op jit(solution)/shard_map/all_gather | solution.py:207
  102.2 0.0 copy-start
  102.2 1.6 copy-done
  103.7 0.6 shard_map.114
  104.3 0.0 all-to-all-done.recv_ref
  104.3 0.0 copy-done.3
  104.4 0.0 copy-done.4
  104.4 2.5 %shard_map.115 = (bf16[192,400]{1,0:T(8,128)(2,1)}, bf16[192,400]{1,0:T(8,128)(2,1)}, bf16[8,56,800]{2,1,0:T(8,128)(2,1)S(1)}, bf16[8,56,800]{2,1,0:T(8,128)(2,1)S(1)}) custom-call(bf16[64,24,128]{2,1,0:T(8,128)(2,1)S(1)} %all-to-all-done.recv_ref, bf16[2,400,800]{2,1,0:T(8,128)(2,1)S(1)} %get-tuple-element.18.weight_ref, ...), custom_call_target="tpu_custom_call" | custom-call | flops 700000000 | bytes 5242880 | tf_op jit(solution)/shard_map/pallas_call | solution.py:28
  106.9 1.9 %collective-permute-start.9 = (bf16[8,56,800]{2,1,0:T(8,128)(2,1)S(1)}, bf16[8,56,800]{2,1,0:T(8,128)(2,1)S(1)}, u32[]{:S(2)}, u32[]{:S(2)}) collective-permute-start(bf16[8,56,800]{2,1,0:T(8,128)(2,1)S(1)} %get-tuple-element.23), channel_id=1, source_target_pairs={{0,256},{256,0},{1,257},{257,1},{2,258},{258,2},{3,259},{259,3},{4... | collective-permute-start | bytes 2150408 | tf_op jit(solution)/shard_map/ppermute | solution.py:256
  108.8 2.3 %collective-permute-done.9 = bf16[8,56,800]{2,1,0:T(8,128)(2,1)S(1)} collective-permute-done((bf16[8,56,800]{2,1,0:T(8,128)(2,1)S(1)}, bf16[8,56,800]{2,1,0:T(8,128)(2,1)S(1)}, u32[]{:S(2)}, u32[]{:S(2)}) %collective-permute-start.9) | collective-permute-done | bytes 716832 | tf_op jit(solution)/shard_map/ppermute | solution.py:256
  111.1 0.2 add_convert_fusion
  111.3 16.9 %all_to_all.20 = bf16[8,56,800]{2,1,0:T(8,128)(2,1)S(1)} all-to-all(bf16[8,56,800]{2,1,0:T(8,128)(2,1)S(1)} %add_convert_fusion), channel_id=1, replica_groups=mesh['rep'=2,'z'=8,'yh'=4,'yl'=2,'x'=4] {'yl','x'}, dimensions={0} | all-to-all | bytes 1433600 | tf_op jit(solution)/shard_map/all_to_all | solution.py:258
  128.2 0.1 reduce_sum.24
  128.5 24.3 %all_to_all.21 = bf16[32,16,128]{2,1,0:T(8,128)(2,1)S(1)} all-to-all(bf16[32,16,128]{2,1,0:T(8,128)(2,1)S(1)} %bitcast.46), channel_id=1, replica_groups=mesh['rep'=2,'z'=8,'yh'=4,'yl'=2,'x'=4] {'z','yh'}, dimensions={0} | all-to-all | bytes 262144 | tf_op jit(solution)/shard_map/all_to_all | solution.py:262
  152.9 14.4 %all_to_all.22 = bf16[32,16,128]{2,1,0:T(8,128)(2,1)S(1)} all-to-all(bf16[32,16,128]{2,1,0:T(8,128)(2,1)S(1)} %broadcast_in_dim.14), channel_id=1, replica_groups=mesh['rep'=2,'z'=8,'yh'=4,'yl'=2,'x'=4] {'z','yh'}, dimensions={0} | all-to-all | bytes 262144 | tf_op jit(solution)/shard_map/all_to_all | solution.py:264
  167.3 6.3 %collective-permute-start.10 = (bf16[32,16,128]{2,1,0:T(8,128)(2,1)S(1)}, bf16[32,16,128]{2,1,0:T(8,128)(2,1)S(1)}, u32[]{:S(2)}, u32[]{:S(2)}) collective-permute-start(bf16[32,16,128]{2,1,0:T(8,128)(2,1)S(1)} %all_to_all.22), channel_id=1, source_target_pairs={{0,256},{256,0},{1,257},{257,1},{2,258},{258,2},{3,259},{259,3},{4... | collective-permute-start | bytes 393224 | tf_op jit(solution)/shard_map/ppermute | solution.py:265
  173.6 0.1 copy.17
  173.7 0.9 collective-permute-done.10
  174.6 0.1 copy.18
  174.7 0.8 convert_select_fusion
  (11 shorter events, 0.2 us)
Async XLA Ops:
  7.2 95.0 %all-gather.3.cloned.1.call-start = ((), (), s32[]{:S(2)}) async-start(), calls=%async_computation.4 | async-start | bytes 2193408 | tf_op jit(solution)/shard_map/all_gather | solution.py:207
  7.2 36.6 %collective-permute-start.4 = (bf16[25,32,512]{2,1,0:T(8,128)(2,1)}, bf16[25,32,512]{2,1,0:T(8,128)(2,1)S(1)}, u32[]{:S(2)}, u32[]{:S(2)}) collective-permute-start(bf16[25,32,512]{2,1,0:T(8,128)(2,1)} %bitcast.40), channel_id=1, source_target_pairs={{0,4},{4,0},{1,5},{5,1},{2,6},{6,2},{3,7},{7,3},{8,12},{12,8},{9,1... | collective-permute-start | bytes 2457608 | tf_op jit(solution)/shard_map/ppermute | solution.py:177
  14.1 9.2 %collective-permute-start = (bf16[25,16,512]{2,1,0:T(8,128)(2,1)}, bf16[25,16,512]{2,1,0:T(8,128)(2,1)S(1)}, u32[]{:S(2)}, u32[]{:S(2)}) collective-permute-start(bf16[25,16,512]{2,1,0:T(8,128)(2,1)} %get-tuple-element.14.rest_0_), channel_id=1, source_target_pairs={{0,1},{1,0},{2,3},{3,2},{4,5},{5,4},{6,7},{7,6},{8,9},{9,8},{10,11... | collective-permute-start | bytes 1228808 | tf_op jit(solution)/shard_map/ppermute | solution.py:211
  17.3 13.4 %collective-permute-start.2 = (bf16[25,16,512]{2,1,0:T(8,128)(2,1)}, bf16[25,16,512]{2,1,0:T(8,128)(2,1)S(1)}, u32[]{:S(2)}, u32[]{:S(2)}) collective-permute-start(bf16[25,16,512]{2,1,0:T(8,128)(2,1)} %get-tuple-element.14.rest_0_), channel_id=1, source_target_pairs={{0,3},{1,2},{2,1},{3,0},{4,7},{5,6},{6,5},{7,4},{8,11},{9,10},{10,... | collective-permute-start | bytes 1228808 | tf_op jit(solution)/shard_map/ppermute | solution.py:212
  23.4 20.3 %collective-permute-start.1 = (bf16[13,16,512]{2,1,0:T(8,128)(2,1)S(1)}, bf16[13,16,512]{2,1,0:T(8,128)(2,1)S(1)}, u32[]{:S(2)}, u32[]{:S(2)}) collective-permute-start(bf16[13,16,512]{2,1,0:T(8,128)(2,1)S(1)} %slice.16), channel_id=1, source_target_pairs={{0,3},{1,2},{2,1},{3,0},{4,7},{5,6},{6,5},{7,4},{8,11},{9,10},{10,... | collective-permute-start | bytes 638984 | tf_op jit(solution)/shard_map/ppermute | solution.py:213
  30.7 8.3 %collective-permute-start.3 = (bf16[12,16,512]{2,1,0:T(8,128)(2,1)S(1)}, bf16[12,16,512]{2,1,0:T(8,128)(2,1)S(1)}, u32[]{:S(2)}, u32[]{:S(2)}) collective-permute-start(bf16[12,16,512]{2,1,0:T(8,128)(2,1)S(1)} %slice.17), channel_id=1, source_target_pairs={{0,1},{1,0},{2,3},{3,2},{4,5},{5,4},{6,7},{7,6},{8,9},{9,8},{10,11... | collective-permute-start | bytes 589832 | tf_op jit(solution)/shard_map/ppermute | solution.py:214
  32.6 13.2 %collective-permute-start.5 = (bf16[25,16,512]{2,1,0:T(8,128)(2,1)}, bf16[25,16,512]{2,1,0:T(8,128)(2,1)S(1)}, u32[]{:S(2)}, u32[]{:S(2)}) collective-permute-start(bf16[25,16,512]{2,1,0:T(8,128)(2,1)} %get-tuple-element.14.rest_0_), channel_id=1, source_target_pairs={{0,256},{256,0},{1,257},{257,1},{2,258},{258,2},{3,259},{259,3},{4... | collective-permute-start | bytes 1228808 | tf_op jit(solution)/shard_map/ppermute | solution.py:217
  37.1 8.8 %collective-permute-start.6 = (bf16[25,16,512]{2,1,0:T(8,128)(2,1)S(1)}, bf16[25,16,512]{2,1,0:T(8,128)(2,1)S(1)}, u32[]{:S(2)}, u32[]{:S(2)}) collective-permute-start(bf16[25,16,512]{2,1,0:T(8,128)(2,1)S(1)} %collective-permute-done.rest_1_), channel_id=1, source_target_pairs={{0,256},{256,0},{1,257},{257,1},{2,258},{258,2},{3,259},{259,3},{4... | collective-permute-start | bytes 1228808 | tf_op jit(solution)/shard_map/ppermute | solution.py:217
  39.0 6.9 %collective-permute-start.8 = (bf16[25,16,512]{2,1,0:T(8,128)(2,1)S(1)}, bf16[25,16,512]{2,1,0:T(8,128)(2,1)S(1)}, u32[]{:S(2)}, u32[]{:S(2)}) collective-permute-start(bf16[25,16,512]{2,1,0:T(8,128)(2,1)S(1)} %collective-permute-done.2.rest_4_), channel_id=1, source_target_pairs={{0,256},{256,0},{1,257},{257,1},{2,258},{258,2},{3,259},{259,3},{4... | collective-permute-start | bytes 1228808 | tf_op jit(solution)/shard_map/ppermute | solution.py:217
  43.8 3.8 %copy-start.1 = (bf16[32,25,512]{2,0,1:T(8,128)(2,1)S(1)}, bf16[32,25,512]{2,0,1:T(8,128)(2,1)}, u32[]{:S(2)}) copy-start(bf16[32,25,512]{2,0,1:T(8,128)(2,1)} %param.8) | copy-start | bytes 2457604
  43.8 3.8 %copy-start.2 = (bf16[25,16,512]{2,1,0:T(8,128)(2,1)S(1)}, bf16[25,16,512]{2,1,0:T(8,128)(2,1)}, u32[]{:S(2)}) copy-start(bf16[25,16,512]{2,1,0:T(8,128)(2,1)} %get-tuple-element.14.rest_0_) | copy-start | bytes 1228804
  43.8 3.8 %collective-permute-start.7 = (bf16[25,16,512]{2,1,0:T(8,128)(2,1)S(1)}, bf16[25,16,512]{2,1,0:T(8,128)(2,1)S(1)}, u32[]{:S(2)}, u32[]{:S(2)}) collective-permute-start(bf16[25,16,512]{2,1,0:T(8,128)(2,1)S(1)} %pad_maximum_fusion), channel_id=1, source_target_pairs={{0,256},{256,0},{1,257},{257,1},{2,258},{258,2},{3,259},{259,3},{4... | collective-permute-start | bytes 1228808 | tf_op jit(solution)/shard_map/ppermute | solution.py:217
  50.6 53.7 %copy-start.3 = (bf16[1,400,192]{1,2,0:T(8,128)(2,1)S(1)}, bf16[1,400,192]{1,2,0:T(8,128)(2,1)}, u32[]{:S(2)}) copy-start(bf16[1,400,192]{1,2,0:T(8,128)(2,1)} %param.14) | copy-start | bytes 460804
  50.6 53.7 %copy-start.4 = (bf16[1,400,192]{1,2,0:T(8,128)(2,1)S(1)}, bf16[1,400,192]{1,2,0:T(8,128)(2,1)}, u32[]{:S(2)}) copy-start(bf16[1,400,192]{1,2,0:T(8,128)(2,1)} %param.15) | copy-start | bytes 460804
  50.6 53.7 %all-to-all-start = ((bf16[64,24,128]{2,1,0:T(8,128)(2,1)}), bf16[64,24,128]{2,1,0:T(8,128)(2,1)S(1)}, u32[]{:S(2)}, u32[]{:S(2)}) async-start(bf16[64,24,128]{2,1,0:T(8,128)(2,1)} %shard_map.113), calls=%async_computation | async-start | bytes 786432 | tf_op jit(solution)/shard_map/all_to_all | solution.py:228
  102.2 1.6 copy-start
  106.9 4.2 %collective-permute-start.9 = (bf16[8,56,800]{2,1,0:T(8,128)(2,1)S(1)}, bf16[8,56,800]{2,1,0:T(8,128)(2,1)S(1)}, u32[]{:S(2)}, u32[]{:S(2)}) collective-permute-start(bf16[8,56,800]{2,1,0:T(8,128)(2,1)S(1)} %get-tuple-element.23), channel_id=1, source_target_pairs={{0,256},{256,0},{1,257},{257,1},{2,258},{258,2},{3,259},{259,3},{4... | collective-permute-start | bytes 2150408 | tf_op jit(solution)/shard_map/ppermute | solution.py:256
  167.3 7.3 %collective-permute-start.10 = (bf16[32,16,128]{2,1,0:T(8,128)(2,1)S(1)}, bf16[32,16,128]{2,1,0:T(8,128)(2,1)S(1)}, u32[]{:S(2)}, u32[]{:S(2)}) collective-permute-start(bf16[32,16,128]{2,1,0:T(8,128)(2,1)S(1)} %all_to_all.22), channel_id=1, source_target_pairs={{0,256},{256,0},{1,257},{257,1},{2,258},{258,2},{3,259},{259,3},{4... | collective-permute-start | bytes 393224 | tf_op jit(solution)/shard_map/ppermute | solution.py:265
Sparse Core Ops, SparseCore 0:
  14.3 87.8 all-gather.2

commit v5 on v4

--- a/solution.py
+++ b/solution.py
@@ -15,10 +15,6 @@
 SWAP = [(0, 1), (1, 0)]
 TAB = ("z", "yh")
 TP = ("yl", "x")
-GROUPS = [
-    [(((rep * 4 + (yh - yl) % 4) * 2 + yl) * 4) + x for rep in range(2) for yl in range(2) for x in range(4)]
-    for yh in range(4)
-]
 
 VM = pl.BlockSpec(memory_space=pltpu.VMEM)
 SM = pl.BlockSpec(memory_space=pltpu.SMEM)
@@ -103,14 +99,12 @@
 def project_kernel(emb_ref, emb_y_ref, *rest):
     w_refs, out_ref, acc_ref = rest[:-2], rest[-2], rest[-1]
     mine = lax.axis_index("yl")
-    far_cut = w_refs[2].shape[0]
     tables, samples = emb_ref.shape[0], emb_ref.shape[1]
     free = lax.broadcasted_iota(jnp.int32, (samples, 128), 1) % 16 >= 12
     last = tables - 1
     extra = {}
     for t in [last] + list(range(last)):
-        far = w_refs[2][t] if t < far_cut else w_refs[3][t - far_cut]
-        weight = jnp.concatenate([w_refs[0][t], w_refs[1][t], far] + [ref[t] for ref in w_refs[4:]], axis=0)
+        weight = jnp.concatenate([ref[t] for ref in w_refs], axis=0)
         for k, ref in enumerate((emb_ref, emb_y_ref)):
             prod = nt_dot(ref[t], weight)
             if t == last:
@@ -137,8 +131,11 @@
     for r in range(2):
         for yl in range(2):
             for spot in range(4):
-                far = jnp.bitwise_xor(x, spot)
-                start = pl.multiple_of((r + rep - 2 * r * rep) * 64 + far * 16, 16)
+                apart = jnp.bitwise_xor(x, spot)
+                across = jnp.bitwise_xor(rep, r)
+                side = jnp.where(apart == 1 + 2 * rep, 2 + across, 5 - across)
+                block = jnp.where(apart == 0, across, jnp.where(apart == 2, 6 + across, side))
+                start = pl.multiple_of(block * 16, 16)
                 row = r * 96 + yl * 48 + spot * 12
                 ft_ref[row : row + 12, :] = gt_ref[yl, pl.ds(start, 16), :][:12]
     feat = ft_ref[...]
@@ -204,22 +201,23 @@
         ],
         cost_estimate=pl.CostEstimate(flops=1 << 20, bytes_accessed=2 << 20, transcendentals=0),
     )(width_steps, proj, fm_weight, lcb_weight, mix_weight.T)
-    small = lax.all_gather(packed, ("rep", "yh", "yl", "x"), axis_index_groups=GROUPS)
-
-    side, back = [(i, i ^ 1) for i in range(4)], [(i, i ^ 3) for i in range(4)]
-    half = (tables + 1) // 2
-    near = lax.ppermute(own, "x", side)
-    next_ = lax.ppermute(own, "x", back)
-    far_a = lax.ppermute(near[:half], "x", back)
-    far_b = lax.ppermute(next_[half:], "x", side)
-    far, emb_y = lax.optimization_barrier((jnp.concatenate([far_a, far_b], axis=0), emb_y))
-    mine = [own, near, far_a, far_b, next_]
-    other = [lax.ppermute(w, "rep", SWAP) for w in (own, near, far, next_)]
+    small = lax.all_gather(packed, ("rep",) + TP)
+
+    side = [(4 * rep + x, 4 * rep + (x ^ (1, 3)[rep])) for rep in range(2) for x in range(4)]
+    onward = [(4 * rep + x, 4 * rep + (x ^ (3, 1)[rep])) for rep in range(2) for x in range(4)]
+    near_a = lax.ppermute(own, ("rep", "x"), side)
+    own_o = lax.ppermute(own, "rep", SWAP)
+    near_b = lax.ppermute(own_o, ("rep", "x"), side)
+    far = lax.ppermute(near_a, ("rep", "x"), onward)
+    next_a = lax.ppermute(near_a, "rep", SWAP)
+    far_o = lax.ppermute(far, "rep", SWAP)
+    near_b, emb_y = lax.optimization_barrier((near_b, emb_y))
+    next_b = lax.ppermute(near_b, "rep", SWAP)
 
     chunks = call(
         project_kernel,
         jax.ShapeDtypeStruct((64, 24, 128), BF16),
-        [emb, emb_y] + mine + other,
+        [emb, emb_y, own, own_o, near_a, near_b, next_a, next_b, far, far_o],
         [pltpu.VMEM((2, 768, 128), F32)],
         limit=SOME,
         flops=2 * 25 * 64 * 128 * 512,

time: 183 us -> 158 us (0.86)
  waiting for transfers between devices: 40.1 us -> 25.3 us
  blocking collectives: 55.7 us -> 47.9 us
  starting transfers between devices: 60 us -> 57.7 us
    all_gather x1, waiting for transfers between devices: 32.9 us -> 0.02 us  [per_device(): small = lax.all_gather(packed, ('rep',) + TP)]
    all_to_all x1, waiting for transfers between devices: 0.01 us -> 13.2 us  [per_device(): recv = lax.all_to_all(chunks, ('yl',) + TAB, 0, 0, tiled=True)]
    all_to_all x1, blocking collectives: 24.3 us -> 15.9 us  [per_device(): parts = lax.all_to_all(tiles, TAB, 0, 0, tiled=True)]
    ppermute x8 -> x7, waiting for transfers between devices: 4.04 us -> 9.23 us  [the longest x1 6.02 us: per_device(): near_b = lax.ppermute(own_o, ('rep', 'x'), side)]
    all_to_all x1, starting transfers between devices: 18.6 us -> 14.9 us  [per_device(): recv = lax.all_to_all(chunks, ('yl',) + TAB, 0, 0, tiled=True)]
    ppermute x1, starting transfers between devices: 1.92 us -> 4.21 us  [per_device(): got = lax.ppermute(send, 'rep', SWAP)]
    ppermute x8 -> x7, starting transfers between devices: 29.2 us -> 28.2 us  [the longest x1 6.33 us: per_device(): next_a = lax.ppermute(near_a, 'rep', SWAP)]
  transfers between devices with their start and end apart: 13 -> 12, of which waited for: 5 -> 6; matrix products, arithmetic and copies ran while one was open for 0% -> 0% of each run, Pallas kernels for 4% -> 4%
where the time goes in v5:
time: 158 us; the launch traced here: 157 us
  starting transfers between devices  57.7 us (37%)
  blocking collectives  47.9 us (30%)
  waiting for transfers between devices  25.3 us (16%)
  between operations  14.3 us (9%)
  Pallas kernels  9.03 us (6%)
  local copies, waits for them, and re-layouts  1.89 us (1%)
    all_to_all x1, blocking collectives, per_device(): shares = lax.all_to_all(pair, TP, 0, 0, tiled=True)  17.7 us
    all_to_all x1, blocking collectives, per_device(): parts = lax.all_to_all(tiles, TAB, 0, 0, tiled=True)  15.9 us
    all_to_all x1, starting transfers between devices, per_device(): recv = lax.all_to_all(chunks, ('yl',) + TAB, 0, 0, tiled=True)  14.9 us
    all_to_all x1, blocking collectives, per_device(): lax.all_to_all(jnp.broadcast_to(whole[None], (32, 16, 128)), TAB, 0, 0, t...  14.4 us
    all_to_all x1, waiting for transfers between devices, per_device(): recv = lax.all_to_all(chunks, ('yl',) + TAB, 0, 0, tiled=True)  13.2 us
    ppermute x1, starting transfers between devices, per_device(): next_a = lax.ppermute(near_a, 'rep', SWAP)  6.33 us
    ppermute x1, starting transfers between devices, per_device(): swapped = lax.ppermute(spread, 'rep', SWAP)  6.32 us
    pallas_call x3, Pallas kernels, call(): pl.pallas_call(kernel, out_shape=outs, in_specs=[VM] * len(ins), out_spec...  6.17 us
  transfers between devices with their start and end apart: 12, of which 6 were waited for; matrix products, arithmetic and copies ran while one was open for 0% of the time, Pallas kernels for 4%

profile of v5, /device:TPU:1, one launch (start us, length us, event | category | flops | bytes accessed | tf_op | source)
XLA Modules:
  0.0 157.3 jit_solution(16295572777179063578)
XLA Ops:
  7.2 0.0 all-gather.3.cloned.1.call-start
  7.2 4.0 %collective-permute-start.2 = (bf16[25,32,512]{2,1,0:T(8,128)(2,1)}, bf16[25,32,512]{2,1,0:T(8,128)(2,1)S(1)}, u32[]{:S(2)}, u32[]{:S(2)}) collective-permute-start(bf16[25,32,512]{2,1,0:T(8,128)(2,1)} %bitcast.40), channel_id=1, source_target_pairs={{0,4},{4,0},{1,5},{5,1},{2,6},{6,2},{3,7},{7,3},{8,12},{12,8},{9,1... | collective-permute-start | bytes 2457608 | tf_op jit(solution)/shard_map/ppermute | solution.py:174
  11.3 2.9 %shard_map.111 = (bf16[25,16,512]{2,1,0:T(8,128)(2,1)}, bf16[9,56,128]{2,1,0:T(8,128)(2,1)}) custom-call(s32[25]{0:T(128)} %steps_ref.1, bf16[12,25,512]{2,1,0:T(8,128)(2,1)} %bitcast.49, bf16[50,800]{1,0:T(8,128)(2,1)} %fm_any.1, bf16[50,800]{1,0:T(8,128)(2,1)} %lcb_any.1, bf16[192,100]{1,0:T(8,128)(2,1)} %bitcast.51), custom_call_target="tpu_custom_call" | custom-call | flops 1048576 | bytes 2097152 | tf_op jit(solution)/shard_map/pallas_call | solution.py:186
  14.1 0.0 all-gather.3.cloned.1.call-update
  14.1 0.0 copy-start.1
  14.2 0.0 copy-start.2
  14.2 4.5 %collective-permute-start.3 = (bf16[25,16,512]{2,1,0:T(8,128)(2,1)}, bf16[25,16,512]{2,1,0:T(8,128)(2,1)S(1)}, u32[]{:S(2)}, u32[]{:S(2)}) collective-permute-start(bf16[25,16,512]{2,1,0:T(8,128)(2,1)} %get-tuple-element.14.rest_0_), channel_id=1, source_target_pairs={{0,1},{1,0},{2,3},{3,2},{256,259},{257,258},{258,257},{259,256},{4... | collective-permute-start | bytes 1228808 | tf_op jit(solution)/shard_map/ppermute | solution.py:208
  18.7 4.2 %collective-permute-start = (bf16[25,16,512]{2,1,0:T(8,128)(2,1)}, bf16[25,16,512]{2,1,0:T(8,128)(2,1)S(1)}, u32[]{:S(2)}, u32[]{:S(2)}) collective-permute-start(bf16[25,16,512]{2,1,0:T(8,128)(2,1)} %get-tuple-element.14.rest_0_), channel_id=1, source_target_pairs={{0,256},{256,0},{1,257},{257,1},{2,258},{258,2},{3,259},{259,3},{4... | collective-permute-start | bytes 1228808 | tf_op jit(solution)/shard_map/ppermute | solution.py:209
  22.9 1.5 collective-permute-done.3.rest_2_
  24.4 2.2 %collective-permute-start.6 = (bf16[25,16,512]{2,1,0:T(8,128)(2,1)S(1)}, bf16[25,16,512]{2,1,0:T(8,128)(2,1)S(1)}, u32[]{:S(2)}, u32[]{:S(2)}) collective-permute-start(bf16[25,16,512]{2,1,0:T(8,128)(2,1)S(1)} %collective-permute-done.3.rest_2_), channel_id=1, source_target_pairs={{0,3},{1,2},{2,1},{3,0},{256,257},{257,256},{258,259},{259,258},{4... | collective-permute-start | bytes 1228808 | tf_op jit(solution)/shard_map/ppermute | solution.py:211
  26.6 6.3 %collective-permute-start.4 = (bf16[25,16,512]{2,1,0:T(8,128)(2,1)S(1)}, bf16[25,16,512]{2,1,0:T(8,128)(2,1)S(1)}, u32[]{:S(2)}, u32[]{:S(2)}) collective-permute-start(bf16[25,16,512]{2,1,0:T(8,128)(2,1)S(1)} %collective-permute-done.3.rest_2_), channel_id=1, source_target_pairs={{0,256},{256,0},{1,257},{257,1},{2,258},{258,2},{3,259},{259,3},{4... | collective-permute-start | bytes 1228808 | tf_op jit(solution)/shard_map/ppermute | solution.py:212
  33.0 0.0 collective-permute-done.rest_1_
  33.0 4.9 %collective-permute-start.1 = (bf16[25,16,512]{2,1,0:T(8,128)(2,1)S(1)}, bf16[25,16,512]{2,1,0:T(8,128)(2,1)S(1)}, u32[]{:S(2)}, u32[]{:S(2)}) collective-permute-start(bf16[25,16,512]{2,1,0:T(8,128)(2,1)S(1)} %collective-permute-done.rest_1_), channel_id=1, source_target_pairs={{0,1},{1,0},{2,3},{3,2},{256,259},{257,258},{258,257},{259,256},{4... | collective-permute-start | bytes 1228808 | tf_op jit(solution)/shard_map/ppermute | solution.py:210
  37.8 0.0 collective-permute-done.2.src_ref
  37.8 6.0 %collective-permute-done.1.rest_3_ = bf16[25,16,512]{2,1,0:T(8,128)(2,1)S(1)} collective-permute-done((bf16[25,16,512]{2,1,0:T(8,128)(2,1)S(1)}, bf16[25,16,512]{2,1,0:T(8,128)(2,1)S(1)}, u32[]{:S(2)}, u32[]{:S(2)}) %collective-permute-start.1) | collective-permute-done | bytes 409632 | tf_op jit(solution)/shard_map/ppermute | solution.py:210
  43.9 4.2 %collective-permute-start.5 = (bf16[25,16,512]{2,1,0:T(8,128)(2,1)S(1)}, bf16[25,16,512]{2,1,0:T(8,128)(2,1)S(1)}, u32[]{:S(2)}, u32[]{:S(2)}) collective-permute-start(bf16[25,16,512]{2,1,0:T(8,128)(2,1)S(1)} %collective-permute-done.1.rest_3_), channel_id=1, source_target_pairs={{0,256},{256,0},{1,257},{257,1},{2,258},{258,2},{3,259},{259,3},{4... | collective-permute-start | bytes 1228808 | tf_op jit(solution)/shard_map/ppermute | solution.py:215
  48.0 0.0 collective-permute-done.6.rest_6_
  48.0 1.9 %collective-permute-start.7 = (bf16[25,16,512]{2,1,0:T(8,128)(2,1)S(1)}, bf16[25,16,512]{2,1,0:T(8,128)(2,1)S(1)}, u32[]{:S(2)}, u32[]{:S(2)}) collective-permute-start(bf16[25,16,512]{2,1,0:T(8,128)(2,1)S(1)} %collective-permute-done.6.rest_6_), channel_id=1, source_target_pairs={{0,256},{256,0},{1,257},{257,1},{2,258},{258,2},{3,259},{259,3},{4... | collective-permute-start | bytes 1228808 | tf_op jit(solution)/shard_map/ppermute | solution.py:213
  50.0 0.0 collective-permute-done.4.rest_4_
  50.0 0.0 collective-permute-done.5.rest_5_
  50.0 1.7 %collective-permute-done.7.rest_7_ = bf16[25,16,512]{2,1,0:T(8,128)(2,1)S(1)} collective-permute-done((bf16[25,16,512]{2,1,0:T(8,128)(2,1)S(1)}, bf16[25,16,512]{2,1,0:T(8,128)(2,1)S(1)}, u32[]{:S(2)}, u32[]{:S(2)}) %collective-permute-start.7) | collective-permute-done | bytes 409632 | tf_op jit(solution)/shard_map/ppermute | solution.py:213
  51.7 0.0 copy-done.1
  51.7 0.0 copy-done.2
  51.7 3.1 %shard_map.113 = bf16[64,24,128]{2,1,0:T(8,128)(2,1)} custom-call(bf16[25,32,512]{2,1,0:T(8,128)(2,1)S(1)} %bitcast.41, bf16[25,32,512]{2,1,0:T(8,128)(2,1)S(1)} %shard_map.112.emb_y_ref, bf16[25,16,512]{2,1,0:T(8,128)(2,1)S(1)} %copy-done.2, bf16[25,16,512]{2,1,0:T(8,128)(2,1)S(1)} %collective-permute-done.rest_1_, ...), custom_call_target="tpu_custom_call" | custom-call | flops 209715200 | bytes 5242880 | tf_op jit(solution)/shard_map/pallas_call | solution.py:24
  54.7 0.0 copy-start.3
  54.8 0.0 copy-start.4
  54.8 14.9 %all-to-all-start = ((bf16[64,24,128]{2,1,0:T(8,128)(2,1)}), bf16[64,24,128]{2,1,0:T(8,128)(2,1)S(1)}, u32[]{:S(2)}, u32[]{:S(2)}) async-start(bf16[64,24,128]{2,1,0:T(8,128)(2,1)} %shard_map.113), calls=%async_computation | async-start | bytes 786432 | tf_op jit(solution)/shard_map/all_to_all | solution.py:226
  69.7 0.0 all-gather.3.cloned.1.call-done
  69.7 0.0 copy-start
  69.7 1.6 copy-done
  71.3 0.6 shard_map.114
  71.9 13.2 %all-to-all-done.recv_ref = bf16[64,24,128]{2,1,0:T(8,128)(2,1)S(1)} async-done(((bf16[64,24,128]{2,1,0:T(8,128)(2,1)}), bf16[64,24,128]{2,1,0:T(8,128)(2,1)S(1)}, u32[]{:S(2)}, u32[]{:S(2)}) %all-to-all-start) | async-done | bytes 393248 | tf_op jit(solution)/shard_map/all_to_all | solution.py:226
  85.1 0.0 copy-done.3
  85.1 0.0 copy-done.4
  85.1 2.5 %shard_map.115 = (bf16[192,400]{1,0:T(8,128)(2,1)}, bf16[192,400]{1,0:T(8,128)(2,1)}, bf16[8,56,800]{2,1,0:T(8,128)(2,1)S(1)}, bf16[8,56,800]{2,1,0:T(8,128)(2,1)S(1)}) custom-call(bf16[64,24,128]{2,1,0:T(8,128)(2,1)S(1)} %all-to-all-done.recv_ref, bf16[2,400,800]{2,1,0:T(8,128)(2,1)S(1)} %get-tuple-element.18.weight_ref, ...), custom_call_target="tpu_custom_call" | custom-call | flops 700000000 | bytes 5242880 | tf_op jit(solution)/shard_map/pallas_call | solution.py:24
  87.7 4.2 %collective-permute-start.8 = (bf16[8,56,800]{2,1,0:T(8,128)(2,1)S(1)}, bf16[8,56,800]{2,1,0:T(8,128)(2,1)S(1)}, u32[]{:S(2)}, u32[]{:S(2)}) collective-permute-start(bf16[8,56,800]{2,1,0:T(8,128)(2,1)S(1)} %get-tuple-element.23), channel_id=1, source_target_pairs={{0,256},{256,0},{1,257},{257,1},{2,258},{258,2},{3,259},{259,3},{4... | collective-permute-start | bytes 2150408 | tf_op jit(solution)/shard_map/ppermute | solution.py:254
  91.9 1.9 %collective-permute-done.8 = bf16[8,56,800]{2,1,0:T(8,128)(2,1)S(1)} collective-permute-done((bf16[8,56,800]{2,1,0:T(8,128)(2,1)S(1)}, bf16[8,56,800]{2,1,0:T(8,128)(2,1)S(1)}, u32[]{:S(2)}, u32[]{:S(2)}) %collective-permute-start.8) | collective-permute-done | bytes 716832 | tf_op jit(solution)/shard_map/ppermute | solution.py:254
  93.8 0.2 add_convert_fusion
  94.0 17.7 %all_to_all.20 = bf16[8,56,800]{2,1,0:T(8,128)(2,1)S(1)} all-to-all(bf16[8,56,800]{2,1,0:T(8,128)(2,1)S(1)} %add_convert_fusion), channel_id=1, replica_groups=mesh['rep'=2,'z'=8,'yh'=4,'yl'=2,'x'=4] {'yl','x'}, dimensions={0} | all-to-all | bytes 1433600 | tf_op jit(solution)/shard_map/all_to_all | solution.py:256
  111.7 0.1 reduce_sum.24
  111.9 15.9 %all_to_all.21 = bf16[32,16,128]{2,1,0:T(8,128)(2,1)S(1)} all-to-all(bf16[32,16,128]{2,1,0:T(8,128)(2,1)S(1)} %bitcast.46), channel_id=1, replica_groups=mesh['rep'=2,'z'=8,'yh'=4,'yl'=2,'x'=4] {'z','yh'}, dimensions={0} | all-to-all | bytes 262144 | tf_op jit(solution)/shard_map/all_to_all | solution.py:260
  127.8 14.4 %all_to_all.22 = bf16[32,16,128]{2,1,0:T(8,128)(2,1)S(1)} all-to-all(bf16[32,16,128]{2,1,0:T(8,128)(2,1)S(1)} %broadcast_in_dim.14), channel_id=1, replica_groups=mesh['rep'=2,'z'=8,'yh'=4,'yl'=2,'x'=4] {'z','yh'}, dimensions={0} | all-to-all | bytes 262144 | tf_op jit(solution)/shard_map/all_to_all | solution.py:262
  142.2 6.3 %collective-permute-start.9 = (bf16[32,16,128]{2,1,0:T(8,128)(2,1)S(1)}, bf16[32,16,128]{2,1,0:T(8,128)(2,1)S(1)}, u32[]{:S(2)}, u32[]{:S(2)}) collective-permute-start(bf16[32,16,128]{2,1,0:T(8,128)(2,1)S(1)} %all_to_all.22), channel_id=1, source_target_pairs={{0,256},{256,0},{1,257},{257,1},{2,258},{258,2},{3,259},{259,3},{4... | collective-permute-start | bytes 393224 | tf_op jit(solution)/shard_map/ppermute | solution.py:263
  148.6 0.1 copy.17
  148.7 0.9 collective-permute-done.9
  149.5 0.1 copy.18
  149.7 0.8 convert_select_fusion
  (8 shorter events, 0.2 us)
Async XLA Ops:
  7.2 62.6 %all-gather.3.cloned.1.call-start = ((), (), s32[]{:S(2)}) async-start(), calls=%async_computation.4 | async-start | bytes 2193408 | tf_op jit(solution)/shard_map/all_gather | solution.py:204
  7.2 30.6 %collective-permute-start.2 = (bf16[25,32,512]{2,1,0:T(8,128)(2,1)}, bf16[25,32,512]{2,1,0:T(8,128)(2,1)S(1)}, u32[]{:S(2)}, u32[]{:S(2)}) collective-permute-start(bf16[25,32,512]{2,1,0:T(8,128)(2,1)} %bitcast.40), channel_id=1, source_target_pairs={{0,4},{4,0},{1,5},{5,1},{2,6},{6,2},{3,7},{7,3},{8,12},{12,8},{9,1... | collective-permute-start | bytes 2457608 | tf_op jit(solution)/shard_map/ppermute | solution.py:174
  14.1 37.5 %copy-start.1 = (bf16[32,25,512]{2,0,1:T(8,128)(2,1)S(1)}, bf16[32,25,512]{2,0,1:T(8,128)(2,1)}, u32[]{:S(2)}) copy-start(bf16[32,25,512]{2,0,1:T(8,128)(2,1)} %param.8) | copy-start | bytes 2457604
  14.2 37.5 %copy-start.2 = (bf16[25,16,512]{2,1,0:T(8,128)(2,1)S(1)}, bf16[25,16,512]{2,1,0:T(8,128)(2,1)}, u32[]{:S(2)}) copy-start(bf16[25,16,512]{2,1,0:T(8,128)(2,1)} %get-tuple-element.14.rest_0_) | copy-start | bytes 1228804
  14.2 10.2 %collective-permute-start.3 = (bf16[25,16,512]{2,1,0:T(8,128)(2,1)}, bf16[25,16,512]{2,1,0:T(8,128)(2,1)S(1)}, u32[]{:S(2)}, u32[]{:S(2)}) collective-permute-start(bf16[25,16,512]{2,1,0:T(8,128)(2,1)} %get-tuple-element.14.rest_0_), channel_id=1, source_target_pairs={{0,1},{1,0},{2,3},{3,2},{256,259},{257,258},{258,257},{259,256},{4... | collective-permute-start | bytes 1228808 | tf_op jit(solution)/shard_map/ppermute | solution.py:208
  18.7 14.3 %collective-permute-start = (bf16[25,16,512]{2,1,0:T(8,128)(2,1)}, bf16[25,16,512]{2,1,0:T(8,128)(2,1)S(1)}, u32[]{:S(2)}, u32[]{:S(2)}) collective-permute-start(bf16[25,16,512]{2,1,0:T(8,128)(2,1)} %get-tuple-element.14.rest_0_), channel_id=1, source_target_pairs={{0,256},{256,0},{1,257},{257,1},{2,258},{258,2},{3,259},{259,3},{4... | collective-permute-start | bytes 1228808 | tf_op jit(solution)/shard_map/ppermute | solution.py:209
  24.4 23.6 %collective-permute-start.6 = (bf16[25,16,512]{2,1,0:T(8,128)(2,1)S(1)}, bf16[25,16,512]{2,1,0:T(8,128)(2,1)S(1)}, u32[]{:S(2)}, u32[]{:S(2)}) collective-permute-start(bf16[25,16,512]{2,1,0:T(8,128)(2,1)S(1)} %collective-permute-done.3.rest_2_), channel_id=1, source_target_pairs={{0,3},{1,2},{2,1},{3,0},{256,257},{257,256},{258,259},{259,258},{4... | collective-permute-start | bytes 1228808 | tf_op jit(solution)/shard_map/ppermute | solution.py:211
  26.6 23.4 %collective-permute-start.4 = (bf16[25,16,512]{2,1,0:T(8,128)(2,1)S(1)}, bf16[25,16,512]{2,1,0:T(8,128)(2,1)S(1)}, u32[]{:S(2)}, u32[]{:S(2)}) collective-permute-start(bf16[25,16,512]{2,1,0:T(8,128)(2,1)S(1)} %collective-permute-done.3.rest_2_), channel_id=1, source_target_pairs={{0,256},{256,0},{1,257},{257,1},{2,258},{258,2},{3,259},{259,3},{4... | collective-permute-start | bytes 1228808 | tf_op jit(solution)/shard_map/ppermute | solution.py:212
  33.0 10.9 %collective-permute-start.1 = (bf16[25,16,512]{2,1,0:T(8,128)(2,1)S(1)}, bf16[25,16,512]{2,1,0:T(8,128)(2,1)S(1)}, u32[]{:S(2)}, u32[]{:S(2)}) collective-permute-start(bf16[25,16,512]{2,1,0:T(8,128)(2,1)S(1)} %collective-permute-done.rest_1_), channel_id=1, source_target_pairs={{0,1},{1,0},{2,3},{3,2},{256,259},{257,258},{258,257},{259,256},{4... | collective-permute-start | bytes 1228808 | tf_op jit(solution)/shard_map/ppermute | solution.py:210
  43.9 6.1 %collective-permute-start.5 = (bf16[25,16,512]{2,1,0:T(8,128)(2,1)S(1)}, bf16[25,16,512]{2,1,0:T(8,128)(2,1)S(1)}, u32[]{:S(2)}, u32[]{:S(2)}) collective-permute-start(bf16[25,16,512]{2,1,0:T(8,128)(2,1)S(1)} %collective-permute-done.1.rest_3_), channel_id=1, source_target_pairs={{0,256},{256,0},{1,257},{257,1},{2,258},{258,2},{3,259},{259,3},{4... | collective-permute-start | bytes 1228808 | tf_op jit(solution)/shard_map/ppermute | solution.py:215
  48.0 3.6 %collective-permute-start.7 = (bf16[25,16,512]{2,1,0:T(8,128)(2,1)S(1)}, bf16[25,16,512]{2,1,0:T(8,128)(2,1)S(1)}, u32[]{:S(2)}, u32[]{:S(2)}) collective-permute-start(bf16[25,16,512]{2,1,0:T(8,128)(2,1)S(1)} %collective-permute-done.6.rest_6_), channel_id=1, source_target_pairs={{0,256},{256,0},{1,257},{257,1},{2,258},{258,2},{3,259},{259,3},{4... | collective-permute-start | bytes 1228808 | tf_op jit(solution)/shard_map/ppermute | solution.py:213
  54.7 30.4 %copy-start.3 = (bf16[1,400,192]{1,2,0:T(8,128)(2,1)S(1)}, bf16[1,400,192]{1,2,0:T(8,128)(2,1)}, u32[]{:S(2)}) copy-start(bf16[1,400,192]{1,2,0:T(8,128)(2,1)} %param.14) | copy-start | bytes 460804
  54.8 30.4 %copy-start.4 = (bf16[1,400,192]{1,2,0:T(8,128)(2,1)S(1)}, bf16[1,400,192]{1,2,0:T(8,128)(2,1)}, u32[]{:S(2)}) copy-start(bf16[1,400,192]{1,2,0:T(8,128)(2,1)} %param.15) | copy-start | bytes 460804
  54.8 30.4 %all-to-all-start = ((bf16[64,24,128]{2,1,0:T(8,128)(2,1)}), bf16[64,24,128]{2,1,0:T(8,128)(2,1)S(1)}, u32[]{:S(2)}, u32[]{:S(2)}) async-start(bf16[64,24,128]{2,1,0:T(8,128)(2,1)} %shard_map.113), calls=%async_computation | async-start | bytes 786432 | tf_op jit(solution)/shard_map/all_to_all | solution.py:226
  69.7 1.6 %copy-start = (bf16[144,56,128]{2,1,0:T(8,128)(2,1)S(1)}, bf16[144,56,128]{2,1,0:T(8,128)(2,1)}, u32[]{:S(2)}) copy-start(bf16[144,56,128]{2,1,0:T(8,128)(2,1)} %all-gather.3.cloned.1.call-done) | copy-start | bytes 6193156
  87.7 6.1 %collective-permute-start.8 = (bf16[8,56,800]{2,1,0:T(8,128)(2,1)S(1)}, bf16[8,56,800]{2,1,0:T(8,128)(2,1)S(1)}, u32[]{:S(2)}, u32[]{:S(2)}) collective-permute-start(bf16[8,56,800]{2,1,0:T(8,128)(2,1)S(1)} %get-tuple-element.23), channel_id=1, source_target_pairs={{0,256},{256,0},{1,257},{257,1},{2,258},{258,2},{3,259},{259,3},{4... | collective-permute-start | bytes 2150408 | tf_op jit(solution)/shard_map/ppermute | solution.py:254
  142.2 7.3 %collective-permute-start.9 = (bf16[32,16,128]{2,1,0:T(8,128)(2,1)S(1)}, bf16[32,16,128]{2,1,0:T(8,128)(2,1)S(1)}, u32[]{:S(2)}, u32[]{:S(2)}) collective-permute-start(bf16[32,16,128]{2,1,0:T(8,128)(2,1)S(1)} %all_to_all.22), channel_id=1, source_target_pairs={{0,256},{256,0},{1,257},{257,1},{2,258},{258,2},{3,259},{259,3},{4... | collective-permute-start | bytes 393224 | tf_op jit(solution)/shard_map/ppermute | solution.py:263
Sparse Core Ops, SparseCore 0:
  14.3 45.1 all-gather.2

commit v6 on v4

--- a/solution.py
+++ b/solution.py
@@ -15,10 +15,6 @@
 SWAP = [(0, 1), (1, 0)]
 TAB = ("z", "yh")
 TP = ("yl", "x")
-GROUPS = [
-    [(((rep * 4 + (yh - yl) % 4) * 2 + yl) * 4) + x for rep in range(2) for yl in range(2) for x in range(4)]
-    for yh in range(4)
-]
 
 VM = pl.BlockSpec(memory_space=pltpu.VMEM)
 SM = pl.BlockSpec(memory_space=pltpu.SMEM)
@@ -103,14 +99,17 @@
 def project_kernel(emb_ref, emb_y_ref, *rest):
     w_refs, out_ref, acc_ref = rest[:-2], rest[-2], rest[-1]
     mine = lax.axis_index("yl")
-    far_cut = w_refs[2].shape[0]
+    own_ref, near_refs, far_refs, next_refs, other_refs = w_refs[0], w_refs[1:3], w_refs[3:5], w_refs[5:7], w_refs[7:]
+    half = near_refs[0].shape[0]
     tables, samples = emb_ref.shape[0], emb_ref.shape[1]
     free = lax.broadcasted_iota(jnp.int32, (samples, 128), 1) % 16 >= 12
     last = tables - 1
     extra = {}
     for t in [last] + list(range(last)):
-        far = w_refs[2][t] if t < far_cut else w_refs[3][t - far_cut]
-        weight = jnp.concatenate([w_refs[0][t], w_refs[1][t], far] + [ref[t] for ref in w_refs[4:]], axis=0)
+        part, row = (0, t) if t < half else (1, t - half)
+        blocks = [own_ref[t]] + [refs[part][row] for refs in (near_refs, far_refs, next_refs)]
+        blocks += [other_refs[0][t], other_refs[1][0, t], other_refs[2][t], other_refs[1][1, t]]
+        weight = jnp.concatenate(blocks, axis=0)
         for k, ref in enumerate((emb_ref, emb_y_ref)):
             prod = nt_dot(ref[t], weight)
             if t == last:
@@ -204,22 +203,28 @@
         ],
         cost_estimate=pl.CostEstimate(flops=1 << 20, bytes_accessed=2 << 20, transcendentals=0),
     )(width_steps, proj, fm_weight, lcb_weight, mix_weight.T)
-    small = lax.all_gather(packed, ("rep", "yh", "yl", "x"), axis_index_groups=GROUPS)
+    small = lax.all_gather(packed, ("rep",) + TP)
 
     side, back = [(i, i ^ 1) for i in range(4)], [(i, i ^ 3) for i in range(4)]
     half = (tables + 1) // 2
-    near = lax.ppermute(own, "x", side)
-    next_ = lax.ppermute(own, "x", back)
-    far_a = lax.ppermute(near[:half], "x", back)
-    far_b = lax.ppermute(next_[half:], "x", side)
-    far, emb_y = lax.optimization_barrier((jnp.concatenate([far_a, far_b], axis=0), emb_y))
-    mine = [own, near, far_a, far_b, next_]
-    other = [lax.ppermute(w, "rep", SWAP) for w in (own, near, far, next_)]
+    own_a, own_b = own[:half], own[half:]
+    near_a = lax.ppermute(own_a, "x", side)
+    next_b = lax.ppermute(own_b, "x", back)
+    near_b = lax.ppermute(own_b, "x", side)
+    next_a = lax.ppermute(own_a, "x", back)
+    far_a = lax.ppermute(near_a, "x", back)
+    far_b = lax.ppermute(next_b, "x", side)
+    far = [far_a, far_b]
+    near = [near_a, near_b]
+    next_ = [next_a, next_b]
+    far_w, emb_y = lax.optimization_barrier((jnp.concatenate(far, axis=0), emb_y))
+    beside = jnp.stack([jnp.concatenate(near, axis=0), jnp.concatenate(next_, axis=0)])
+    other = [lax.ppermute(w, "rep", SWAP) for w in (own, beside, far_w)]
 
     chunks = call(
         project_kernel,
         jax.ShapeDtypeStruct((64, 24, 128), BF16),
-        [emb, emb_y] + mine + other,
+        [emb, emb_y, own] + near + far + next_ + other,
         [pltpu.VMEM((2, 768, 128), F32)],
         limit=SOME,
         flops=2 * 25 * 64 * 128 * 512,

time: 183 us -> 157 us (0.86)
  waiting for transfers between devices: 40.1 us -> 21 us
  blocking collectives: 55.7 us -> 48.1 us
  local copies, waits for them, and re-layouts: 1.92 us -> 3.77 us
    all_gather x1, waiting for transfers between devices: 32.9 us -> 0.02 us  [per_device(): small = lax.all_gather(packed, ('rep',) + TP)]
    all_to_all x1, waiting for transfers between devices: 0.01 us -> 12.8 us  [per_device(): recv = lax.all_to_all(chunks, ('yl',) + TAB, 0, 0, tiled=True)]
    all_to_all x1, blocking collectives: 24.3 us -> 15.9 us  [per_device(): parts = lax.all_to_all(tiles, TAB, 0, 0, tiled=True)]
    all_to_all x1, starting transfers between devices: 18.6 us -> 13.5 us  [per_device(): recv = lax.all_to_all(chunks, ('yl',) + TAB, 0, 0, tiled=True)]
    ppermute x1, starting transfers between devices: 1.92 us -> 4.72 us  [per_device(): got = lax.ppermute(send, 'rep', SWAP)]
    slice x2, local copies, waits for them, and re-layouts: 0.03 us -> 1.89 us  [per_device(): own_a, own_b = (own[:half], own[half:])]
    ppermute x8 -> x9, waiting for transfers between devices: 4.04 us -> 5.45 us  [the longest x1 3.21 us: per_device(): far_b = lax.ppermute(next_b, 'x', side)]
    ppermute x8 -> x9, starting transfers between devices: 29.2 us -> 30 us  [the longest x3 14.4 us: per_device(): other = [lax.ppermute(w, 'rep', SWAP) for w in (own, beside, far_w)]]
  transfers between devices with their start and end apart: 13 -> 14, of which waited for: 5 -> 6; matrix products, arithmetic and copies ran while one was open for 0% -> 1% of each run, Pallas kernels for 4% -> 4%
where the time goes in v6:
time: 157 us; the launch traced here: 156 us
  starting transfers between devices  58.6 us (37%)
  blocking collectives  48.1 us (31%)
  waiting for transfers between devices  21 us (13%)
  between operations  14.4 us (9%)
  Pallas kernels  9.05 us (6%)
  local copies, waits for them, and re-layouts  3.77 us (2%)
    all_to_all x1, blocking collectives, per_device(): shares = lax.all_to_all(pair, TP, 0, 0, tiled=True)  17.8 us
    all_to_all x1, blocking collectives, per_device(): parts = lax.all_to_all(tiles, TAB, 0, 0, tiled=True)  15.9 us
    all_to_all x1, blocking collectives, per_device(): lax.all_to_all(jnp.broadcast_to(whole[None], (32, 16, 128)), TAB, 0, 0, t...  14.4 us
    ppermute x3, starting transfers between devices, per_device(): other = [lax.ppermute(w, 'rep', SWAP) for w in (own, beside, far_w)]  14.4 us
    all_to_all x1, starting transfers between devices, per_device(): recv = lax.all_to_all(chunks, ('yl',) + TAB, 0, 0, tiled=True)  13.5 us
    all_to_all x1, waiting for transfers between devices, per_device(): recv = lax.all_to_all(chunks, ('yl',) + TAB, 0, 0, tiled=True)  12.8 us
    ppermute x1, starting transfers between devices, per_device(): swapped = lax.ppermute(spread, 'rep', SWAP)  6.32 us
    pallas_call x3, Pallas kernels, call(): pl.pallas_call(kernel, out_shape=outs, in_specs=[VM] * len(ins), out_spec...  6.18 us
  transfers between devices with their start and end apart: 14, of which 6 were waited for; matrix products, arithmetic and copies ran while one was open for 1% of the time, Pallas kernels for 4%

profile of v6, /device:TPU:1, one launch (start us, length us, event | category | flops | bytes accessed | tf_op | source)
XLA Modules:
  0.0 156.2 jit_solution(9049699134893341429)
XLA Ops:
  7.2 0.0 all-gather.3.cloned.1.call-start
  7.2 4.0 %collective-permute-start.4 = (bf16[25,32,512]{2,1,0:T(8,128)(2,1)}, bf16[25,32,512]{2,1,0:T(8,128)(2,1)S(1)}, u32[]{:S(2)}, u32[]{:S(2)}) collective-permute-start(bf16[25,32,512]{2,1,0:T(8,128)(2,1)} %bitcast.44), channel_id=1, source_target_pairs={{0,4},{4,0},{1,5},{5,1},{2,6},{6,2},{3,7},{7,3},{8,12},{12,8},{9,1... | collective-permute-start | bytes 2457608 | tf_op jit(solution)/shard_map/ppermute | solution.py:176
  11.3 2.9 %shard_map.111 = (bf16[25,16,512]{2,1,0:T(8,128)(2,1)}, bf16[9,56,128]{2,1,0:T(8,128)(2,1)}) custom-call(s32[25]{0:T(128)} %steps_ref.1, bf16[12,25,512]{2,1,0:T(8,128)(2,1)} %bitcast.53, bf16[50,800]{1,0:T(8,128)(2,1)} %fm_any.1, bf16[50,800]{1,0:T(8,128)(2,1)} %lcb_any.1, bf16[192,100]{1,0:T(8,128)(2,1)} %bitcast.55), custom_call_target="tpu_custom_call" | custom-call | flops 1048576 | bytes 2097152 | tf_op jit(solution)/shard_map/pallas_call | solution.py:188
  14.1 0.0 all-gather.3.cloned.1.call-update
  14.1 0.9 slice.12
  15.1 3.1 %collective-permute-start = (bf16[13,16,512]{2,1,0:T(8,128)(2,1)S(1)}, bf16[13,16,512]{2,1,0:T(8,128)(2,1)S(1)}, u32[]{:S(2)}, u32[]{:S(2)}) collective-permute-start(bf16[13,16,512]{2,1,0:T(8,128)(2,1)S(1)} %slice.12), channel_id=1, source_target_pairs={{0,1},{1,0},{2,3},{3,2},{4,5},{5,4},{6,7},{7,6},{8,9},{9,8},{10,11... | collective-permute-start | bytes 638984 | tf_op jit(solution)/shard_map/ppermute | solution.py:211
  18.2 0.9 slice.13
  19.2 2.2 %collective-permute-start.5 = (bf16[12,16,512]{2,1,0:T(8,128)(2,1)S(1)}, bf16[12,16,512]{2,1,0:T(8,128)(2,1)S(1)}, u32[]{:S(2)}, u32[]{:S(2)}) collective-permute-start(bf16[12,16,512]{2,1,0:T(8,128)(2,1)S(1)} %slice.13), channel_id=1, source_target_pairs={{0,1},{1,0},{2,3},{3,2},{4,5},{5,4},{6,7},{7,6},{8,9},{9,8},{10,11... | collective-permute-start | bytes 589832 | tf_op jit(solution)/shard_map/ppermute | solution.py:213
  21.3 4.4 %collective-permute-start.2 = (bf16[12,16,512]{2,1,0:T(8,128)(2,1)S(1)}, bf16[12,16,512]{2,1,0:T(8,128)(2,1)S(1)}, u32[]{:S(2)}, u32[]{:S(2)}) collective-permute-start(bf16[12,16,512]{2,1,0:T(8,128)(2,1)S(1)} %slice.13), channel_id=1, source_target_pairs={{0,3},{1,2},{2,1},{3,0},{4,7},{5,6},{6,5},{7,4},{8,11},{9,10},{10,... | collective-permute-start | bytes 589832 | tf_op jit(solution)/shard_map/ppermute | solution.py:212
  25.7 2.1 %collective-permute-start.6 = (bf16[13,16,512]{2,1,0:T(8,128)(2,1)S(1)}, bf16[13,16,512]{2,1,0:T(8,128)(2,1)S(1)}, u32[]{:S(2)}, u32[]{:S(2)}) collective-permute-start(bf16[13,16,512]{2,1,0:T(8,128)(2,1)S(1)} %slice.12), channel_id=1, source_target_pairs={{0,3},{1,2},{2,1},{3,0},{4,7},{5,6},{6,5},{7,4},{8,11},{9,10},{10,... | collective-permute-start | bytes 638984 | tf_op jit(solution)/shard_map/ppermute | solution.py:214
  27.9 0.0 collective-permute-done.5.rest_2_
  27.9 7.8 %collective-permute-start.7 = (bf16[25,16,512]{2,1,0:T(8,128)(2,1)}, bf16[25,16,512]{2,1,0:T(8,128)(2,1)S(1)}, u32[]{:S(2)}, u32[]{:S(2)}) collective-permute-start(bf16[25,16,512]{2,1,0:T(8,128)(2,1)} %get-tuple-element.14.rest_0_), channel_id=1, source_target_pairs={{0,256},{256,0},{1,257},{257,1},{2,258},{258,2},{3,259},{259,3},{4... | collective-permute-start | bytes 1228808 | tf_op jit(solution)/shard_map/ppermute | solution.py:222
  35.7 0.0 collective-permute-done.2.rest_6_
  35.7 1.9 %collective-permute-start.3 = (bf16[12,16,512]{2,1,0:T(8,128)(2,1)S(1)}, bf16[12,16,512]{2,1,0:T(8,128)(2,1)S(1)}, u32[]{:S(2)}, u32[]{:S(2)}) collective-permute-start(bf16[12,16,512]{2,1,0:T(8,128)(2,1)S(1)} %collective-permute-done.2.rest_6_), channel_id=1, source_target_pairs={{0,1},{1,0},{2,3},{3,2},{4,5},{5,4},{6,7},{7,6},{8,9},{9,8},{10,11... | collective-permute-start | bytes 589832 | tf_op jit(solution)/shard_map/ppermute | solution.py:216
  37.6 0.0 collective-permute-done.rest_1_
  37.6 1.9 %collective-permute-start.1 = (bf16[13,16,512]{2,1,0:T(8,128)(2,1)S(1)}, bf16[13,16,512]{2,1,0:T(8,128)(2,1)S(1)}, u32[]{:S(2)}, u32[]{:S(2)}) collective-permute-start(bf16[13,16,512]{2,1,0:T(8,128)(2,1)S(1)} %collective-permute-done.rest_1_), channel_id=1, source_target_pairs={{0,3},{1,2},{2,1},{3,0},{4,7},{5,6},{6,5},{7,4},{8,11},{9,10},{10,... | collective-permute-start | bytes 638984 | tf_op jit(solution)/shard_map/ppermute | solution.py:215
  39.6 0.0 collective-permute-done.6.rest_5_
  39.6 0.1 pad_maximum_fusion
  39.7 3.0 %collective-permute-start.8 = (bf16[2,25,16,512]{3,2,1,0:T(8,128)(2,1)S(1)}, bf16[2,25,16,512]{3,2,1,0:T(8,128)(2,1)S(1)}, u32[]{:S(2)}, u32[]{:S(2)}) collective-permute-start(bf16[2,25,16,512]{3,2,1,0:T(8,128)(2,1)S(1)} %pad_maximum_fusion), channel_id=1, source_target_pairs={{0,256},{256,0},{1,257},{257,1},{2,258},{258,2},{3,259},{259,3},{4... | collective-permute-start | bytes 2457608 | tf_op jit(solution)/shard_map/ppermute | solution.py:222
  42.8 3.2 %collective-permute-done.3.rest_4_ = bf16[12,16,512]{2,1,0:T(8,128)(2,1)S(1)} collective-permute-done((bf16[12,16,512]{2,1,0:T(8,128)(2,1)S(1)}, bf16[12,16,512]{2,1,0:T(8,128)(2,1)S(1)}, u32[]{:S(2)}, u32[]{:S(2)}) %collective-permute-start.3) | collective-permute-done | bytes 196640 | tf_op jit(solution)/shard_map/ppermute | solution.py:216
  46.0 0.9 collective-permute-done.1.rest_3_
  46.9 0.0 copy-start.1
  46.9 0.0 copy-start.2
  46.9 0.0 collective-permute-done.4.src_ref
  46.9 3.6 %collective-permute-start.9 = (bf16[25,16,512]{2,1,0:T(8,128)(2,1)S(1)}, bf16[25,16,512]{2,1,0:T(8,128)(2,1)S(1)}, u32[]{:S(2)}, u32[]{:S(2)}) collective-permute-start(bf16[25,16,512]{2,1,0:T(8,128)(2,1)S(1)} %pad_maximum_fusion.1), channel_id=1, source_target_pairs={{0,256},{256,0},{1,257},{257,1},{2,258},{258,2},{3,259},{259,3},{4... | collective-permute-start | bytes 1228808 | tf_op jit(solution)/shard_map/ppermute | solution.py:222
  50.5 0.0 collective-permute-done.7.rest_7_
  50.5 0.0 collective-permute-done.8.rest_8_
  50.5 1.3 collective-permute-done.9.rest_9_
  51.9 0.0 copy-done.1
  51.9 0.0 copy-done.2
  51.9 3.1 %shard_map.113 = bf16[64,24,128]{2,1,0:T(8,128)(2,1)} custom-call(bf16[25,32,512]{2,1,0:T(8,128)(2,1)S(1)} %bitcast.45, bf16[25,32,512]{2,1,0:T(8,128)(2,1)S(1)} %shard_map.112.emb_y_ref, bf16[25,16,512]{2,1,0:T(8,128)(2,1)S(1)} %copy-done.1, bf16[13,16,512]{2,1,0:T(8,128)(2,1)S(1)} %collective-permute-done.rest_1_, ...), custom_call_target="tpu_custom_call" | custom-call | flops 209715200 | bytes 5242880 | tf_op jit(solution)/shard_map/pallas_call | solution.py:24
  54.9 0.0 copy-start.3
  54.9 0.0 copy-start.4
  54.9 13.5 %all-to-all-start = ((bf16[64,24,128]{2,1,0:T(8,128)(2,1)}), bf16[64,24,128]{2,1,0:T(8,128)(2,1)S(1)}, u32[]{:S(2)}, u32[]{:S(2)}) async-start(bf16[64,24,128]{2,1,0:T(8,128)(2,1)} %shard_map.113), calls=%async_computation | async-start | bytes 786432 | tf_op jit(solution)/shard_map/all_to_all | solution.py:233
  68.5 0.0 all-gather.3.cloned.1.call-done
  68.5 0.0 copy-start
  68.5 1.6 %copy-done = bf16[144,56,128]{2,1,0:T(8,128)(2,1)S(1)} copy-done((bf16[144,56,128]{2,1,0:T(8,128)(2,1)S(1)}, bf16[144,56,128]{2,1,0:T(8,128)(2,1)}, u32[]{:S(2)}) %copy-start) | copy-done | bytes 2064408
  70.1 0.6 shard_map.114
  70.7 12.8 %all-to-all-done.recv_ref = bf16[64,24,128]{2,1,0:T(8,128)(2,1)S(1)} async-done(((bf16[64,24,128]{2,1,0:T(8,128)(2,1)}), bf16[64,24,128]{2,1,0:T(8,128)(2,1)S(1)}, u32[]{:S(2)}, u32[]{:S(2)}) %all-to-all-start) | async-done | bytes 393248 | tf_op jit(solution)/shard_map/all_to_all | solution.py:233
  83.4 0.0 copy-done.3
  83.4 0.0 copy-done.4
  83.4 2.5 %shard_map.115 = (bf16[192,400]{1,0:T(8,128)(2,1)}, bf16[192,400]{1,0:T(8,128)(2,1)}, bf16[8,56,800]{2,1,0:T(8,128)(2,1)S(1)}, bf16[8,56,800]{2,1,0:T(8,128)(2,1)S(1)}) custom-call(bf16[64,24,128]{2,1,0:T(8,128)(2,1)S(1)} %all-to-all-done.recv_ref, bf16[2,400,800]{2,1,0:T(8,128)(2,1)S(1)} %get-tuple-element.18.weight_ref, ...), custom_call_target="tpu_custom_call" | custom-call | flops 700000000 | bytes 5242880 | tf_op jit(solution)/shard_map/pallas_call | solution.py:24
  86.0 4.7 %collective-permute-start.10 = (bf16[8,56,800]{2,1,0:T(8,128)(2,1)S(1)}, bf16[8,56,800]{2,1,0:T(8,128)(2,1)S(1)}, u32[]{:S(2)}, u32[]{:S(2)}) collective-permute-start(bf16[8,56,800]{2,1,0:T(8,128)(2,1)S(1)} %get-tuple-element.23), channel_id=1, source_target_pairs={{0,256},{256,0},{1,257},{257,1},{2,258},{258,2},{3,259},{259,3},{4... | collective-permute-start | bytes 2150408 | tf_op jit(solution)/shard_map/ppermute | solution.py:261
  90.7 1.9 %collective-permute-done.10 = bf16[8,56,800]{2,1,0:T(8,128)(2,1)S(1)} collective-permute-done((bf16[8,56,800]{2,1,0:T(8,128)(2,1)S(1)}, bf16[8,56,800]{2,1,0:T(8,128)(2,1)S(1)}, u32[]{:S(2)}, u32[]{:S(2)}) %collective-permute-start.10) | collective-permute-done | bytes 716832 | tf_op jit(solution)/shard_map/ppermute | solution.py:261
  92.6 0.2 add_convert_fusion
  92.8 17.8 %all_to_all.20 = bf16[8,56,800]{2,1,0:T(8,128)(2,1)S(1)} all-to-all(bf16[8,56,800]{2,1,0:T(8,128)(2,1)S(1)} %add_convert_fusion), channel_id=1, replica_groups=mesh['rep'=2,'z'=8,'yh'=4,'yl'=2,'x'=4] {'yl','x'}, dimensions={0} | all-to-all | bytes 1433600 | tf_op jit(solution)/shard_map/all_to_all | solution.py:263
  110.6 0.1 reduce_sum.24
  110.8 15.9 %all_to_all.21 = bf16[32,16,128]{2,1,0:T(8,128)(2,1)S(1)} all-to-all(bf16[32,16,128]{2,1,0:T(8,128)(2,1)S(1)} %bitcast.50), channel_id=1, replica_groups=mesh['rep'=2,'z'=8,'yh'=4,'yl'=2,'x'=4] {'z','yh'}, dimensions={0} | all-to-all | bytes 262144 | tf_op jit(solution)/shard_map/all_to_all | solution.py:267
  126.7 14.4 %all_to_all.22 = bf16[32,16,128]{2,1,0:T(8,128)(2,1)S(1)} all-to-all(bf16[32,16,128]{2,1,0:T(8,128)(2,1)S(1)} %broadcast_in_dim.14), channel_id=1, replica_groups=mesh['rep'=2,'z'=8,'yh'=4,'yl'=2,'x'=4] {'z','yh'}, dimensions={0} | all-to-all | bytes 262144 | tf_op jit(solution)/shard_map/all_to_all | solution.py:269
  141.2 6.3 %collective-permute-start.11 = (bf16[32,16,128]{2,1,0:T(8,128)(2,1)S(1)}, bf16[32,16,128]{2,1,0:T(8,128)(2,1)S(1)}, u32[]{:S(2)}, u32[]{:S(2)}) collective-permute-start(bf16[32,16,128]{2,1,0:T(8,128)(2,1)S(1)} %all_to_all.22), channel_id=1, source_target_pairs={{0,256},{256,0},{1,257},{257,1},{2,258},{258,2},{3,259},{259,3},{4... | collective-permute-start | bytes 393224 | tf_op jit(solution)/shard_map/ppermute | solution.py:270
  147.5 0.1 copy.17
  147.6 0.9 collective-permute-done.11
  148.5 0.1 copy.18
  148.6 0.8 convert_select_fusion
  (11 shorter events, 0.3 us)
Async XLA Ops:
  7.2 61.3 %all-gather.3.cloned.1.call-start = ((), (), s32[]{:S(2)}) async-start(), calls=%async_computation.4 | async-start | bytes 2193408 | tf_op jit(solution)/shard_map/all_gather | solution.py:206
  7.2 39.7 %collective-permute-start.4 = (bf16[25,32,512]{2,1,0:T(8,128)(2,1)}, bf16[25,32,512]{2,1,0:T(8,128)(2,1)S(1)}, u32[]{:S(2)}, u32[]{:S(2)}) collective-permute-start(bf16[25,32,512]{2,1,0:T(8,128)(2,1)} %bitcast.44), channel_id=1, source_target_pairs={{0,4},{4,0},{1,5},{5,1},{2,6},{6,2},{3,7},{7,3},{8,12},{12,8},{9,1... | collective-permute-start | bytes 2457608 | tf_op jit(solution)/shard_map/ppermute | solution.py:176
  15.1 22.5 %collective-permute-start = (bf16[13,16,512]{2,1,0:T(8,128)(2,1)S(1)}, bf16[13,16,512]{2,1,0:T(8,128)(2,1)S(1)}, u32[]{:S(2)}, u32[]{:S(2)}) collective-permute-start(bf16[13,16,512]{2,1,0:T(8,128)(2,1)S(1)} %slice.12), channel_id=1, source_target_pairs={{0,1},{1,0},{2,3},{3,2},{4,5},{5,4},{6,7},{7,6},{8,9},{9,8},{10,11... | collective-permute-start | bytes 638984 | tf_op jit(solution)/shard_map/ppermute | solution.py:211
  19.2 8.7 %collective-permute-start.5 = (bf16[12,16,512]{2,1,0:T(8,128)(2,1)S(1)}, bf16[12,16,512]{2,1,0:T(8,128)(2,1)S(1)}, u32[]{:S(2)}, u32[]{:S(2)}) collective-permute-start(bf16[12,16,512]{2,1,0:T(8,128)(2,1)S(1)} %slice.13), channel_id=1, source_target_pairs={{0,1},{1,0},{2,3},{3,2},{4,5},{5,4},{6,7},{7,6},{8,9},{9,8},{10,11... | collective-permute-start | bytes 589832 | tf_op jit(solution)/shard_map/ppermute | solution.py:213
  21.3 14.3 %collective-permute-start.2 = (bf16[12,16,512]{2,1,0:T(8,128)(2,1)S(1)}, bf16[12,16,512]{2,1,0:T(8,128)(2,1)S(1)}, u32[]{:S(2)}, u32[]{:S(2)}) collective-permute-start(bf16[12,16,512]{2,1,0:T(8,128)(2,1)S(1)} %slice.13), channel_id=1, source_target_pairs={{0,3},{1,2},{2,1},{3,0},{4,7},{5,6},{6,5},{7,4},{8,11},{9,10},{10,... | collective-permute-start | bytes 589832 | tf_op jit(solution)/shard_map/ppermute | solution.py:212
  25.7 13.9 %collective-permute-start.6 = (bf16[13,16,512]{2,1,0:T(8,128)(2,1)S(1)}, bf16[13,16,512]{2,1,0:T(8,128)(2,1)S(1)}, u32[]{:S(2)}, u32[]{:S(2)}) collective-permute-start(bf16[13,16,512]{2,1,0:T(8,128)(2,1)S(1)} %slice.12), channel_id=1, source_target_pairs={{0,3},{1,2},{2,1},{3,0},{4,7},{5,6},{6,5},{7,4},{8,11},{9,10},{10,... | collective-permute-start | bytes 638984 | tf_op jit(solution)/shard_map/ppermute | solution.py:214
  27.9 22.7 %collective-permute-start.7 = (bf16[25,16,512]{2,1,0:T(8,128)(2,1)}, bf16[25,16,512]{2,1,0:T(8,128)(2,1)S(1)}, u32[]{:S(2)}, u32[]{:S(2)}) collective-permute-start(bf16[25,16,512]{2,1,0:T(8,128)(2,1)} %get-tuple-element.14.rest_0_), channel_id=1, source_target_pairs={{0,256},{256,0},{1,257},{257,1},{2,258},{258,2},{3,259},{259,3},{4... | collective-permute-start | bytes 1228808 | tf_op jit(solution)/shard_map/ppermute | solution.py:222
  35.7 10.3 %collective-permute-start.3 = (bf16[12,16,512]{2,1,0:T(8,128)(2,1)S(1)}, bf16[12,16,512]{2,1,0:T(8,128)(2,1)S(1)}, u32[]{:S(2)}, u32[]{:S(2)}) collective-permute-start(bf16[12,16,512]{2,1,0:T(8,128)(2,1)S(1)} %collective-permute-done.2.rest_6_), channel_id=1, source_target_pairs={{0,1},{1,0},{2,3},{3,2},{4,5},{5,4},{6,7},{7,6},{8,9},{9,8},{10,11... | collective-permute-start | bytes 589832 | tf_op jit(solution)/shard_map/ppermute | solution.py:216
  37.6 9.3 %collective-permute-start.1 = (bf16[13,16,512]{2,1,0:T(8,128)(2,1)S(1)}, bf16[13,16,512]{2,1,0:T(8,128)(2,1)S(1)}, u32[]{:S(2)}, u32[]{:S(2)}) collective-permute-start(bf16[13,16,512]{2,1,0:T(8,128)(2,1)S(1)} %collective-permute-done.rest_1_), channel_id=1, source_target_pairs={{0,3},{1,2},{2,1},{3,0},{4,7},{5,6},{6,5},{7,4},{8,11},{9,10},{10,... | collective-permute-start | bytes 638984 | tf_op jit(solution)/shard_map/ppermute | solution.py:215
  39.7 10.8 %collective-permute-start.8 = (bf16[2,25,16,512]{3,2,1,0:T(8,128)(2,1)S(1)}, bf16[2,25,16,512]{3,2,1,0:T(8,128)(2,1)S(1)}, u32[]{:S(2)}, u32[]{:S(2)}) collective-permute-start(bf16[2,25,16,512]{3,2,1,0:T(8,128)(2,1)S(1)} %pad_maximum_fusion), channel_id=1, source_target_pairs={{0,256},{256,0},{1,257},{257,1},{2,258},{258,2},{3,259},{259,3},{4... | collective-permute-start | bytes 2457608 | tf_op jit(solution)/shard_map/ppermute | solution.py:222
  46.9 5.0 %copy-start.1 = (bf16[25,16,512]{2,1,0:T(8,128)(2,1)S(1)}, bf16[25,16,512]{2,1,0:T(8,128)(2,1)}, u32[]{:S(2)}) copy-start(bf16[25,16,512]{2,1,0:T(8,128)(2,1)} %get-tuple-element.14.rest_0_) | copy-start | bytes 1228804
  46.9 5.0 %copy-start.2 = (bf16[32,25,512]{2,0,1:T(8,128)(2,1)S(1)}, bf16[32,25,512]{2,0,1:T(8,128)(2,1)}, u32[]{:S(2)}) copy-start(bf16[32,25,512]{2,0,1:T(8,128)(2,1)} %param.8) | copy-start | bytes 2457604
  46.9 4.9 %collective-permute-start.9 = (bf16[25,16,512]{2,1,0:T(8,128)(2,1)S(1)}, bf16[25,16,512]{2,1,0:T(8,128)(2,1)S(1)}, u32[]{:S(2)}, u32[]{:S(2)}) collective-permute-start(bf16[25,16,512]{2,1,0:T(8,128)(2,1)S(1)} %pad_maximum_fusion.1), channel_id=1, source_target_pairs={{0,256},{256,0},{1,257},{257,1},{2,258},{258,2},{3,259},{259,3},{4... | collective-permute-start | bytes 1228808 | tf_op jit(solution)/shard_map/ppermute | solution.py:222
  54.9 28.5 %copy-start.3 = (bf16[1,400,192]{1,2,0:T(8,128)(2,1)S(1)}, bf16[1,400,192]{1,2,0:T(8,128)(2,1)}, u32[]{:S(2)}) copy-start(bf16[1,400,192]{1,2,0:T(8,128)(2,1)} %param.14) | copy-start | bytes 460804
  54.9 28.5 %copy-start.4 = (bf16[1,400,192]{1,2,0:T(8,128)(2,1)S(1)}, bf16[1,400,192]{1,2,0:T(8,128)(2,1)}, u32[]{:S(2)}) copy-start(bf16[1,400,192]{1,2,0:T(8,128)(2,1)} %param.15) | copy-start | bytes 460804
  54.9 28.5 %all-to-all-start = ((bf16[64,24,128]{2,1,0:T(8,128)(2,1)}), bf16[64,24,128]{2,1,0:T(8,128)(2,1)S(1)}, u32[]{:S(2)}, u32[]{:S(2)}) async-start(bf16[64,24,128]{2,1,0:T(8,128)(2,1)} %shard_map.113), calls=%async_computation | async-start | bytes 786432 | tf_op jit(solution)/shard_map/all_to_all | solution.py:233
  68.5 1.6 %copy-start = (bf16[144,56,128]{2,1,0:T(8,128)(2,1)S(1)}, bf16[144,56,128]{2,1,0:T(8,128)(2,1)}, u32[]{:S(2)}) copy-start(bf16[144,56,128]{2,1,0:T(8,128)(2,1)} %all-gather.3.cloned.1.call-done) | copy-start | bytes 6193156
  86.0 6.6 %collective-permute-start.10 = (bf16[8,56,800]{2,1,0:T(8,128)(2,1)S(1)}, bf16[8,56,800]{2,1,0:T(8,128)(2,1)S(1)}, u32[]{:S(2)}, u32[]{:S(2)}) collective-permute-start(bf16[8,56,800]{2,1,0:T(8,128)(2,1)S(1)} %get-tuple-element.23), channel_id=1, source_target_pairs={{0,256},{256,0},{1,257},{257,1},{2,258},{258,2},{3,259},{259,3},{4... | collective-permute-start | bytes 2150408 | tf_op jit(solution)/shard_map/ppermute | solution.py:261
  141.2 7.3 %collective-permute-start.11 = (bf16[32,16,128]{2,1,0:T(8,128)(2,1)S(1)}, bf16[32,16,128]{2,1,0:T(8,128)(2,1)S(1)}, u32[]{:S(2)}, u32[]{:S(2)}) collective-permute-start(bf16[32,16,128]{2,1,0:T(8,128)(2,1)S(1)} %all_to_all.22), channel_id=1, source_target_pairs={{0,256},{256,0},{1,257},{257,1},{2,258},{258,2},{3,259},{259,3},{4... | collective-permute-start | bytes 393224 | tf_op jit(solution)/shard_map/ppermute | solution.py:270
Sparse Core Ops, SparseCore 0:
  14.3 45.3 all-gather.2

commit v7 on v4

--- a/solution.py
+++ b/solution.py
@@ -15,10 +15,6 @@
 SWAP = [(0, 1), (1, 0)]
 TAB = ("z", "yh")
 TP = ("yl", "x")
-GROUPS = [
-    [(((rep * 4 + (yh - yl) % 4) * 2 + yl) * 4) + x for rep in range(2) for yl in range(2) for x in range(4)]
-    for yh in range(4)
-]
 
 VM = pl.BlockSpec(memory_space=pltpu.VMEM)
 SM = pl.BlockSpec(memory_space=pltpu.SMEM)
@@ -54,21 +50,21 @@
         copy.start()
     tables, widest = proj_ref.shape[1], proj_ref.shape[2]
     columns = lax.broadcasted_iota(jnp.int32, (tables, widest), 1)
-    table = lax.broadcasted_iota(jnp.int32, (tables, widest), 0)
-    width = jnp.zeros((tables, widest), jnp.int32)
+    table = lax.broadcasted_iota(jnp.int32, (tables, 128), 0)
+    width = jnp.zeros((tables, 128), jnp.int32)
     for t in range(tables):
-        width = jnp.where(table == t, steps_ref[t], width)
-    keep = columns < widest // 8 * width
+        width = jnp.where(table == t, widest // 8 * steps_ref[t], width)
+    keep = columns < jnp.concatenate([width] * (widest // 128), axis=1)
     rows_ref[...] = jnp.zeros_like(rows_ref)
     pack_ref[...] = jnp.zeros_like(pack_ref)
     copies[0].wait()
     for j in range(12):
         masked = jnp.where(keep, proj_ref[j].astype(F32), 0.0)
         for c in range(4):
-            rows_ref[c, pl.ds(j, tables, stride=16), :] = masked[:, 128 * c : 128 * c + 128]
-    for t in range(tables):
+            rows_ref[c, pl.ds(j, tables, stride=12), :] = masked[:, 128 * c : 128 * c + 128]
+    for p in range(own_ref.shape[0]):
         for c in range(4):
-            own_ref[t, :, 128 * c : 128 * c + 128] = rows_ref[c, 16 * t : 16 * t + 16, :].astype(BF16)
+            own_ref[p, :, 128 * c : 128 * c + 128] = rows_ref[c, 24 * p : 24 * p + 24, :].astype(BF16)
     for copy in copies[1:]:
         copy.wait()
     rep = lax.axis_index("rep")
@@ -109,15 +105,18 @@
     last = tables - 1
     extra = {}
     for t in [last] + list(range(last)):
-        far = w_refs[2][t] if t < far_cut else w_refs[3][t - far_cut]
-        weight = jnp.concatenate([w_refs[0][t], w_refs[1][t], far] + [ref[t] for ref in w_refs[4:]], axis=0)
+        pair, odd = t // 2, t % 2
+        far = w_refs[2].at[pair] if pair < far_cut else w_refs[3].at[pair - far_cut]
+        blocks = [w_refs[0].at[pair], w_refs[1].at[pair], far] + [ref.at[pair] for ref in w_refs[4:]]
+        weight = jnp.concatenate([block[8 * odd : 8 * odd + 16, :] for block in blocks], axis=0)
         for k, ref in enumerate((emb_ref, emb_y_ref)):
             prod = nt_dot(ref[t], weight)
+            if odd:
+                prod = pltpu.roll(prod, 124, 1)
             if t == last:
-                extra[k] = [jnp.where(free, pltpu.roll(prod, shift, 1), 0.0) for shift in (12, 8, 4)]
+                extra[k] = [pltpu.roll(prod, shift, 1) for shift in (12, 8, 4)]
             else:
-                if t < 3:
-                    prod = prod + extra[k][t]
+                prod = jnp.where(free, extra[k][t] if t < 3 else 0.0, prod)
                 slot = mine if k == 0 else 1 - mine
                 acc_ref[slot, pl.ds(t, samples, stride=last), :] = prod
     for k in range(2):
@@ -182,14 +181,15 @@
         out_specs=pl.BlockSpec(memory_space=pl.ANY),
         input_output_aliases={0: 0},
         compiler_params=pltpu.CompilerParams(vmem_limit_bytes=1 << 20),
-        cost_estimate=pl.CostEstimate(flops=20_000_000_000, bytes_accessed=0, transcendentals=0),
+        cost_estimate=pl.CostEstimate(flops=30_000_000_000, bytes_accessed=0, transcendentals=0),
     )(emb_y)
 
+    pairs = (tables + 1) // 2
     proj = jnp.transpose(proj_weight, (2, 0, 1))
     own, packed = pl.pallas_call(
         prep_kernel,
         out_shape=(
-            jax.ShapeDtypeStruct((tables, 16, widest), BF16),
+            jax.ShapeDtypeStruct((pairs, 24, widest), BF16),
             jax.ShapeDtypeStruct((9, 56, 128), BF16),
         ),
         in_specs=[SM] + [pl.BlockSpec(memory_space=pl.ANY)] * 4,
@@ -199,22 +199,27 @@
             pltpu.VMEM(fm_weight.shape, BF16),
             pltpu.VMEM(lcb_weight.shape, BF16),
             pltpu.VMEM(mix_weight.shape[::-1], BF16),
-            pltpu.VMEM((4, 16 * tables, 128), F32),
+            pltpu.VMEM((4, 24 * pairs, 128), F32),
             pltpu.SemaphoreType.DMA((4,)),
         ],
         cost_estimate=pl.CostEstimate(flops=1 << 20, bytes_accessed=2 << 20, transcendentals=0),
     )(width_steps, proj, fm_weight, lcb_weight, mix_weight.T)
-    small = lax.all_gather(packed, ("rep", "yh", "yl", "x"), axis_index_groups=GROUPS)
+    small = lax.all_gather(packed, ("rep",) + TP)
 
     side, back = [(i, i ^ 1) for i in range(4)], [(i, i ^ 3) for i in range(4)]
-    half = (tables + 1) // 2
+    half = (pairs + 1) // 2
     near = lax.ppermute(own, "x", side)
     next_ = lax.ppermute(own, "x", back)
+    own_o = lax.ppermute(own, "rep", SWAP)
+    near, own_o = lax.optimization_barrier((near, own_o))
     far_a = lax.ppermute(near[:half], "x", back)
     far_b = lax.ppermute(next_[half:], "x", side)
+    near_o = lax.ppermute(near, "rep", SWAP)
+    next_o = lax.ppermute(next_, "rep", SWAP)
     far, emb_y = lax.optimization_barrier((jnp.concatenate([far_a, far_b], axis=0), emb_y))
+    far_o = lax.ppermute(far, "rep", SWAP)
     mine = [own, near, far_a, far_b, next_]
-    other = [lax.ppermute(w, "rep", SWAP) for w in (own, near, far, next_)]
+    other = [own_o, near_o, far_o, next_o]
 
     chunks = call(
         project_kernel,
@@ -232,6 +237,7 @@
         (jax.ShapeDtypeStruct((2, 400, 800), BF16), jax.ShapeDtypeStruct((192, 800), BF16)),
         [small],
         [pltpu.VMEM((400, 896), F32), pltpu.VMEM((192, 800), F32)],
+        flops=15_000_000_000,
         size=4 << 20,
         limit=SOME,
     )

time: 183 us -> 153 us (0.84)
  waiting for transfers between devices: 40.1 us -> 24 us
  blocking collectives: 55.7 us -> 46.1 us
  starting transfers between devices: 60 us -> 55.6 us
    all_gather x1, waiting for transfers between devices: 32.9 us -> 0.02 us  [per_device(): small = lax.all_gather(packed, ('rep',) + TP)]
    all_to_all x1, waiting for transfers between devices: 0.01 us -> 12.8 us  [per_device(): recv = lax.all_to_all(chunks, ('yl',) + TAB, 0, 0, tiled=True)]
    all_to_all x1, blocking collectives: 24.3 us -> 15.9 us  [per_device(): parts = lax.all_to_all(tiles, TAB, 0, 0, tiled=True)]
    ppermute x1, waiting for transfers between devices: 0.01 us -> 5.92 us  [per_device(): next_ = lax.ppermute(own, 'x', back)]
    all_to_all x1, starting transfers between devices: 18.6 us -> 13.7 us  [per_device(): recv = lax.all_to_all(chunks, ('yl',) + TAB, 0, 0, tiled=True)]
    ppermute x1, starting transfers between devices: 1.92 us -> 4.74 us  [per_device(): got = lax.ppermute(send, 'rep', SWAP)]
    ppermute x1, starting transfers between devices: 7.31 us -> 4.57 us  [per_device(): far_a = lax.ppermute(near[:half], 'x', back)]
    ppermute x1, waiting for transfers between devices: 2.34 us -> 0.01 us  [per_device(): near = lax.ppermute(own, 'x', side)]
  transfers between devices with their start and end apart: 13 -> 13, of which waited for: 5 -> 6; matrix products, arithmetic and copies ran while one was open for 0% -> 0% of each run, Pallas kernels for 4% -> 4%
where the time goes in v7:
time: 153 us; the launch traced here: 152 us
  starting transfers between devices  55.6 us (36%)
  blocking collectives  46.1 us (30%)
  waiting for transfers between devices  24 us (16%)
  between operations  14.3 us (9%)
  Pallas kernels  8.82 us (6%)
  local copies, waits for them, and re-layouts  1.91 us (1%)
    all_to_all x1, blocking collectives, per_device(): parts = lax.all_to_all(tiles, TAB, 0, 0, tiled=True)  15.9 us
    all_to_all x1, blocking collectives, per_device(): shares = lax.all_to_all(pair, TP, 0, 0, tiled=True)  15.8 us
    all_to_all x1, blocking collectives, per_device(): lax.all_to_all(jnp.broadcast_to(whole[None], (32, 16, 128)), TAB, 0, 0, t...  14.4 us
    all_to_all x1, starting transfers between devices, per_device(): recv = lax.all_to_all(chunks, ('yl',) + TAB, 0, 0, tiled=True)  13.7 us
    all_to_all x1, waiting for transfers between devices, per_device(): recv = lax.all_to_all(chunks, ('yl',) + TAB, 0, 0, tiled=True)  12.8 us
    ppermute x1, starting transfers between devices, per_device(): swapped = lax.ppermute(spread, 'rep', SWAP)  6.32 us
    pallas_call x3, Pallas kernels, call(): pl.pallas_call(kernel, out_shape=outs, in_specs=[VM] * len(ins), out_spec...  6.24 us
    ppermute x1, waiting for transfers between devices, per_device(): next_ = lax.ppermute(own, 'x', back)  5.92 us
  transfers between devices with their start and end apart: 13, of which 6 were waited for; matrix products, arithmetic and copies ran while one was open for 0% of the time, Pallas kernels for 4%

profile of v7, /device:TPU:1, one launch (start us, length us, event | category | flops | bytes accessed | tf_op | source)
XLA Modules:
  0.0 151.9 jit_solution(4955675846244594473)
XLA Ops:
  7.2 0.0 all-gather.3.cloned.1.call-start
  7.2 4.0 %collective-permute-start.5 = (bf16[25,32,512]{2,1,0:T(8,128)(2,1)}, bf16[25,32,512]{2,1,0:T(8,128)(2,1)S(1)}, u32[]{:S(2)}, u32[]{:S(2)}) collective-permute-start(bf16[25,32,512]{2,1,0:T(8,128)(2,1)} %bitcast.39), channel_id=1, source_target_pairs={{0,4},{4,0},{1,5},{5,1},{2,6},{6,2},{3,7},{7,3},{8,12},{12,8},{9,1... | collective-permute-start | bytes 2457608 | tf_op jit(solution)/shard_map/ppermute | solution.py:176
  11.3 2.6 %shard_map.111 = (bf16[13,24,512]{2,1,0:T(8,128)(2,1)}, bf16[9,56,128]{2,1,0:T(8,128)(2,1)}) custom-call(s32[25]{0:T(128)} %steps_ref.1, bf16[12,25,512]{2,1,0:T(8,128)(2,1)} %bitcast.49, bf16[50,800]{1,0:T(8,128)(2,1)} %fm_any.1, bf16[50,800]{1,0:T(8,128)(2,1)} %lcb_any.1, bf16[192,100]{1,0:T(8,128)(2,1)} %bitcast.51), custom_call_target="tpu_custom_call" | custom-call | flops 1048576 | bytes 2097152 | tf_op jit(solution)/shard_map/pallas_call | solution.py:189
  13.8 0.0 all-gather.3.cloned.1.call-update
  13.9 3.1 %collective-permute-start = (bf16[13,24,512]{2,1,0:T(8,128)(2,1)}, bf16[13,24,512]{2,1,0:T(8,128)(2,1)S(1)}, u32[]{:S(2)}, u32[]{:S(2)}) collective-permute-start(bf16[13,24,512]{2,1,0:T(8,128)(2,1)} %get-tuple-element.16.rest_0_), channel_id=1, source_target_pairs={{0,1},{1,0},{2,3},{3,2},{4,5},{5,4},{6,7},{7,6},{8,9},{9,8},{10,11... | collective-permute-start | bytes 958472 | tf_op jit(solution)/shard_map/ppermute | solution.py:211
  17.0 5.5 %collective-permute-start.1 = (bf16[13,24,512]{2,1,0:T(8,128)(2,1)}, bf16[13,24,512]{2,1,0:T(8,128)(2,1)S(1)}, u32[]{:S(2)}, u32[]{:S(2)}) collective-permute-start(bf16[13,24,512]{2,1,0:T(8,128)(2,1)} %get-tuple-element.16.rest_0_), channel_id=1, source_target_pairs={{0,256},{256,0},{1,257},{257,1},{2,258},{258,2},{3,259},{259,3},{4... | collective-permute-start | bytes 958472 | tf_op jit(solution)/shard_map/ppermute | solution.py:213
  22.5 1.9 %collective-permute-start.3 = (bf16[13,24,512]{2,1,0:T(8,128)(2,1)}, bf16[13,24,512]{2,1,0:T(8,128)(2,1)S(1)}, u32[]{:S(2)}, u32[]{:S(2)}) collective-permute-start(bf16[13,24,512]{2,1,0:T(8,128)(2,1)} %get-tuple-element.16.rest_0_), channel_id=1, source_target_pairs={{0,3},{1,2},{2,1},{3,0},{4,7},{5,6},{6,5},{7,4},{8,11},{9,10},{10,... | collective-permute-start | bytes 958472 | tf_op jit(solution)/shard_map/ppermute | solution.py:212
  24.4 0.0 collective-permute-done.rest_1_
  24.4 0.0 collective-permute-done.1.rest_5_
  24.5 4.6 %collective-permute-start.2 = (bf16[7,24,512]{2,1,0:T(8,128)(2,1)S(1)}, bf16[7,24,512]{2,1,0:T(8,128)(2,1)S(1)}, u32[]{:S(2)}, u32[]{:S(2)}) collective-permute-start(bf16[7,24,512]{2,1,0:T(8,128)(2,1)S(1)} %slice.12), channel_id=1, source_target_pairs={{0,3},{1,2},{2,1},{3,0},{4,7},{5,6},{6,5},{7,4},{8,11},{9,10},{10,... | collective-permute-start | bytes 516104 | tf_op jit(solution)/shard_map/ppermute | solution.py:215
  29.0 5.9 %collective-permute-done.3.rest_4_ = bf16[13,24,512]{2,1,0:T(8,128)(2,1)S(1)} collective-permute-done((bf16[13,24,512]{2,1,0:T(8,128)(2,1)}, bf16[13,24,512]{2,1,0:T(8,128)(2,1)S(1)}, u32[]{:S(2)}, u32[]{:S(2)}) %collective-permute-start.3) | collective-permute-done | bytes 319520 | tf_op jit(solution)/shard_map/ppermute | solution.py:212
  35.0 2.4 %collective-permute-start.4 = (bf16[6,24,512]{2,1,0:T(8,128)(2,1)S(1)}, bf16[6,24,512]{2,1,0:T(8,128)(2,1)S(1)}, u32[]{:S(2)}, u32[]{:S(2)}) collective-permute-start(bf16[6,24,512]{2,1,0:T(8,128)(2,1)S(1)} %slice.16), channel_id=1, source_target_pairs={{0,1},{1,0},{2,3},{3,2},{4,5},{5,4},{6,7},{7,6},{8,9},{9,8},{10,11... | collective-permute-start | bytes 442376 | tf_op jit(solution)/shard_map/ppermute | solution.py:216
  37.4 3.6 %collective-permute-start.6 = (bf16[13,24,512]{2,1,0:T(8,128)(2,1)S(1)}, bf16[13,24,512]{2,1,0:T(8,128)(2,1)S(1)}, u32[]{:S(2)}, u32[]{:S(2)}) collective-permute-start(bf16[13,24,512]{2,1,0:T(8,128)(2,1)S(1)} %collective-permute-done.rest_1_), channel_id=1, source_target_pairs={{0,256},{256,0},{1,257},{257,1},{2,258},{258,2},{3,259},{259,3},{4... | collective-permute-start | bytes 958472 | tf_op jit(solution)/shard_map/ppermute | solution.py:217
  41.0 1.9 %collective-permute-start.8 = (bf16[13,24,512]{2,1,0:T(8,128)(2,1)S(1)}, bf16[13,24,512]{2,1,0:T(8,128)(2,1)S(1)}, u32[]{:S(2)}, u32[]{:S(2)}) collective-permute-start(bf16[13,24,512]{2,1,0:T(8,128)(2,1)S(1)} %collective-permute-done.3.rest_4_), channel_id=1, source_target_pairs={{0,256},{256,0},{1,257},{257,1},{2,258},{258,2},{3,259},{259,3},{4... | collective-permute-start | bytes 958472 | tf_op jit(solution)/shard_map/ppermute | solution.py:218
  42.9 1.3 collective-permute-done.4.rest_3_
  44.2 0.0 collective-permute-done.2.rest_2_
  44.3 0.0 copy-start
  44.3 0.0 copy-start.1
  44.3 0.0 collective-permute-done.5.src_ref
  44.3 3.7 %collective-permute-start.7 = (bf16[13,24,512]{2,1,0:T(8,128)(2,1)S(1)}, bf16[13,24,512]{2,1,0:T(8,128)(2,1)S(1)}, u32[]{:S(2)}, u32[]{:S(2)}) collective-permute-start(bf16[13,24,512]{2,1,0:T(8,128)(2,1)S(1)} %pad_maximum_fusion), channel_id=1, source_target_pairs={{0,256},{256,0},{1,257},{257,1},{2,258},{258,2},{3,259},{259,3},{4... | collective-permute-start | bytes 958472 | tf_op jit(solution)/shard_map/ppermute | solution.py:220
  48.0 0.0 collective-permute-done.6.rest_6_
  48.0 0.0 collective-permute-done.8.rest_8_
  48.0 1.2 collective-permute-done.7.rest_7_
  49.2 0.0 copy-done
  49.2 0.0 copy-done.1
  49.2 3.1 %shard_map.113 = bf16[64,24,128]{2,1,0:T(8,128)(2,1)} custom-call(bf16[25,32,512]{2,1,0:T(8,128)(2,1)S(1)} %bitcast.40, bf16[25,32,512]{2,1,0:T(8,128)(2,1)S(1)} %shard_map.112.emb_y_ref, bf16[13,24,512]{2,1,0:T(8,128)(2,1)S(1)} %copy-done.1, bf16[13,24,512]{2,1,0:T(8,128)(2,1)S(1)} %collective-permute-done.rest_1_, ...), custom_call_target="tpu_custom_call" | custom-call | flops 209715200 | bytes 5242880 | tf_op jit(solution)/shard_map/pallas_call | solution.py:24
  52.4 13.7 %all-to-all-start = ((bf16[64,24,128]{2,1,0:T(8,128)(2,1)}), bf16[64,24,128]{2,1,0:T(8,128)(2,1)S(1)}, u32[]{:S(2)}, u32[]{:S(2)}) async-start(bf16[64,24,128]{2,1,0:T(8,128)(2,1)} %shard_map.113), calls=%async_computation | async-start | bytes 786432 | tf_op jit(solution)/shard_map/all_to_all | solution.py:233
  66.1 0.0 all-gather.3.cloned.1.call-done
  66.1 0.0 copy-start.2
  66.1 1.6 %copy-done.2 = bf16[144,56,128]{2,1,0:T(8,128)(2,1)S(1)} copy-done((bf16[144,56,128]{2,1,0:T(8,128)(2,1)S(1)}, bf16[144,56,128]{2,1,0:T(8,128)(2,1)}, u32[]{:S(2)}) %copy-start.2) | copy-done | bytes 2064408
  67.7 0.0 copy-start.3
  67.7 0.0 copy-start.4
  67.7 0.6 shard_map.114
  68.3 12.8 %all-to-all-done.recv_ref = bf16[64,24,128]{2,1,0:T(8,128)(2,1)S(1)} async-done(((bf16[64,24,128]{2,1,0:T(8,128)(2,1)}), bf16[64,24,128]{2,1,0:T(8,128)(2,1)S(1)}, u32[]{:S(2)}, u32[]{:S(2)}) %all-to-all-start) | async-done | bytes 393248 | tf_op jit(solution)/shard_map/all_to_all | solution.py:233
  81.0 0.0 copy-done.3
  81.0 0.0 copy-done.4
  81.0 2.5 %shard_map.115 = (bf16[192,400]{1,0:T(8,128)(2,1)}, bf16[192,400]{1,0:T(8,128)(2,1)}, bf16[8,56,800]{2,1,0:T(8,128)(2,1)S(1)}, bf16[8,56,800]{2,1,0:T(8,128)(2,1)S(1)}) custom-call(bf16[64,24,128]{2,1,0:T(8,128)(2,1)S(1)} %all-to-all-done.recv_ref, bf16[2,400,800]{2,1,0:T(8,128)(2,1)S(1)} %get-tuple-element.22.weight_ref, ...), custom_call_target="tpu_custom_call" | custom-call | flops 700000000 | bytes 5242880 | tf_op jit(solution)/shard_map/pallas_call | solution.py:24
  83.6 4.7 %collective-permute-start.9 = (bf16[8,56,800]{2,1,0:T(8,128)(2,1)S(1)}, bf16[8,56,800]{2,1,0:T(8,128)(2,1)S(1)}, u32[]{:S(2)}, u32[]{:S(2)}) collective-permute-start(bf16[8,56,800]{2,1,0:T(8,128)(2,1)S(1)} %get-tuple-element.27), channel_id=1, source_target_pairs={{0,256},{256,0},{1,257},{257,1},{2,258},{258,2},{3,259},{259,3},{4... | collective-permute-start | bytes 2150408 | tf_op jit(solution)/shard_map/ppermute | solution.py:262
  88.3 1.9 %collective-permute-done.9 = bf16[8,56,800]{2,1,0:T(8,128)(2,1)S(1)} collective-permute-done((bf16[8,56,800]{2,1,0:T(8,128)(2,1)S(1)}, bf16[8,56,800]{2,1,0:T(8,128)(2,1)S(1)}, u32[]{:S(2)}, u32[]{:S(2)}) %collective-permute-start.9) | collective-permute-done | bytes 716832 | tf_op jit(solution)/shard_map/ppermute | solution.py:262
  90.2 0.2 add_convert_fusion
  90.4 15.8 %all_to_all.20 = bf16[8,56,800]{2,1,0:T(8,128)(2,1)S(1)} all-to-all(bf16[8,56,800]{2,1,0:T(8,128)(2,1)S(1)} %add_convert_fusion), channel_id=1, replica_groups=mesh['rep'=2,'z'=8,'yh'=4,'yl'=2,'x'=4] {'yl','x'}, dimensions={0} | all-to-all | bytes 1433600 | tf_op jit(solution)/shard_map/all_to_all | solution.py:264
  106.3 0.1 reduce_sum.24
  106.5 15.9 %all_to_all.21 = bf16[32,16,128]{2,1,0:T(8,128)(2,1)S(1)} all-to-all(bf16[32,16,128]{2,1,0:T(8,128)(2,1)S(1)} %bitcast.46), channel_id=1, replica_groups=mesh['rep'=2,'z'=8,'yh'=4,'yl'=2,'x'=4] {'z','yh'}, dimensions={0} | all-to-all | bytes 262144 | tf_op jit(solution)/shard_map/all_to_all | solution.py:268
  122.4 14.4 %all_to_all.22 = bf16[32,16,128]{2,1,0:T(8,128)(2,1)S(1)} all-to-all(bf16[32,16,128]{2,1,0:T(8,128)(2,1)S(1)} %broadcast_in_dim.14), channel_id=1, replica_groups=mesh['rep'=2,'z'=8,'yh'=4,'yl'=2,'x'=4] {'z','yh'}, dimensions={0} | all-to-all | bytes 262144 | tf_op jit(solution)/shard_map/all_to_all | solution.py:270
  136.9 6.3 %collective-permute-start.10 = (bf16[32,16,128]{2,1,0:T(8,128)(2,1)S(1)}, bf16[32,16,128]{2,1,0:T(8,128)(2,1)S(1)}, u32[]{:S(2)}, u32[]{:S(2)}) collective-permute-start(bf16[32,16,128]{2,1,0:T(8,128)(2,1)S(1)} %all_to_all.22), channel_id=1, source_target_pairs={{0,256},{256,0},{1,257},{257,1},{2,258},{258,2},{3,259},{259,3},{4... | collective-permute-start | bytes 393224 | tf_op jit(solution)/shard_map/ppermute | solution.py:271
  143.2 0.1 copy.17
  143.3 0.9 collective-permute-done.10
  144.2 0.1 copy.18
  144.3 0.8 convert_select_fusion
  (11 shorter events, 0.2 us)
Async XLA Ops:
  7.2 58.9 %all-gather.3.cloned.1.call-start = ((), (), s32[]{:S(2)}) async-start(), calls=%async_computation.4 | async-start | bytes 2193408 | tf_op jit(solution)/shard_map/all_gather | solution.py:207
  7.2 37.1 %collective-permute-start.5 = (bf16[25,32,512]{2,1,0:T(8,128)(2,1)}, bf16[25,32,512]{2,1,0:T(8,128)(2,1)S(1)}, u32[]{:S(2)}, u32[]{:S(2)}) collective-permute-start(bf16[25,32,512]{2,1,0:T(8,128)(2,1)} %bitcast.39), channel_id=1, source_target_pairs={{0,4},{4,0},{1,5},{5,1},{2,6},{6,2},{3,7},{7,3},{8,12},{12,8},{9,1... | collective-permute-start | bytes 2457608 | tf_op jit(solution)/shard_map/ppermute | solution.py:176
  13.9 10.5 %collective-permute-start = (bf16[13,24,512]{2,1,0:T(8,128)(2,1)}, bf16[13,24,512]{2,1,0:T(8,128)(2,1)S(1)}, u32[]{:S(2)}, u32[]{:S(2)}) collective-permute-start(bf16[13,24,512]{2,1,0:T(8,128)(2,1)} %get-tuple-element.16.rest_0_), channel_id=1, source_target_pairs={{0,1},{1,0},{2,3},{3,2},{4,5},{5,4},{6,7},{7,6},{8,9},{9,8},{10,11... | collective-permute-start | bytes 958472 | tf_op jit(solution)/shard_map/ppermute | solution.py:211
  17.0 7.4 %collective-permute-start.1 = (bf16[13,24,512]{2,1,0:T(8,128)(2,1)}, bf16[13,24,512]{2,1,0:T(8,128)(2,1)S(1)}, u32[]{:S(2)}, u32[]{:S(2)}) collective-permute-start(bf16[13,24,512]{2,1,0:T(8,128)(2,1)} %get-tuple-element.16.rest_0_), channel_id=1, source_target_pairs={{0,256},{256,0},{1,257},{257,1},{2,258},{258,2},{3,259},{259,3},{4... | collective-permute-start | bytes 958472 | tf_op jit(solution)/shard_map/ppermute | solution.py:213
  22.5 12.5 %collective-permute-start.3 = (bf16[13,24,512]{2,1,0:T(8,128)(2,1)}, bf16[13,24,512]{2,1,0:T(8,128)(2,1)S(1)}, u32[]{:S(2)}, u32[]{:S(2)}) collective-permute-start(bf16[13,24,512]{2,1,0:T(8,128)(2,1)} %get-tuple-element.16.rest_0_), channel_id=1, source_target_pairs={{0,3},{1,2},{2,1},{3,0},{4,7},{5,6},{6,5},{7,4},{8,11},{9,10},{10,... | collective-permute-start | bytes 958472 | tf_op jit(solution)/shard_map/ppermute | solution.py:212
  24.5 19.8 %collective-permute-start.2 = (bf16[7,24,512]{2,1,0:T(8,128)(2,1)S(1)}, bf16[7,24,512]{2,1,0:T(8,128)(2,1)S(1)}, u32[]{:S(2)}, u32[]{:S(2)}) collective-permute-start(bf16[7,24,512]{2,1,0:T(8,128)(2,1)S(1)} %slice.12), channel_id=1, source_target_pairs={{0,3},{1,2},{2,1},{3,0},{4,7},{5,6},{6,5},{7,4},{8,11},{9,10},{10,... | collective-permute-start | bytes 516104 | tf_op jit(solution)/shard_map/ppermute | solution.py:215
  35.0 9.3 %collective-permute-start.4 = (bf16[6,24,512]{2,1,0:T(8,128)(2,1)S(1)}, bf16[6,24,512]{2,1,0:T(8,128)(2,1)S(1)}, u32[]{:S(2)}, u32[]{:S(2)}) collective-permute-start(bf16[6,24,512]{2,1,0:T(8,128)(2,1)S(1)} %slice.16), channel_id=1, source_target_pairs={{0,1},{1,0},{2,3},{3,2},{4,5},{5,4},{6,7},{7,6},{8,9},{9,8},{10,11... | collective-permute-start | bytes 442376 | tf_op jit(solution)/shard_map/ppermute | solution.py:216
  37.4 10.6 %collective-permute-start.6 = (bf16[13,24,512]{2,1,0:T(8,128)(2,1)S(1)}, bf16[13,24,512]{2,1,0:T(8,128)(2,1)S(1)}, u32[]{:S(2)}, u32[]{:S(2)}) collective-permute-start(bf16[13,24,512]{2,1,0:T(8,128)(2,1)S(1)} %collective-permute-done.rest_1_), channel_id=1, source_target_pairs={{0,256},{256,0},{1,257},{257,1},{2,258},{258,2},{3,259},{259,3},{4... | collective-permute-start | bytes 958472 | tf_op jit(solution)/shard_map/ppermute | solution.py:217
  41.0 7.0 %collective-permute-start.8 = (bf16[13,24,512]{2,1,0:T(8,128)(2,1)S(1)}, bf16[13,24,512]{2,1,0:T(8,128)(2,1)S(1)}, u32[]{:S(2)}, u32[]{:S(2)}) collective-permute-start(bf16[13,24,512]{2,1,0:T(8,128)(2,1)S(1)} %collective-permute-done.3.rest_4_), channel_id=1, source_target_pairs={{0,256},{256,0},{1,257},{257,1},{2,258},{258,2},{3,259},{259,3},{4... | collective-permute-start | bytes 958472 | tf_op jit(solution)/shard_map/ppermute | solution.py:218
  44.3 5.0 %copy-start = (bf16[32,25,512]{2,0,1:T(8,128)(2,1)S(1)}, bf16[32,25,512]{2,0,1:T(8,128)(2,1)}, u32[]{:S(2)}) copy-start(bf16[32,25,512]{2,0,1:T(8,128)(2,1)} %param.8) | copy-start | bytes 2457604
  44.3 5.0 %copy-start.1 = (bf16[13,24,512]{2,1,0:T(8,128)(2,1)S(1)}, bf16[13,24,512]{2,1,0:T(8,128)(2,1)}, u32[]{:S(2)}) copy-start(bf16[13,24,512]{2,1,0:T(8,128)(2,1)} %get-tuple-element.16.rest_0_) | copy-start | bytes 958468
  44.3 4.9 %collective-permute-start.7 = (bf16[13,24,512]{2,1,0:T(8,128)(2,1)S(1)}, bf16[13,24,512]{2,1,0:T(8,128)(2,1)S(1)}, u32[]{:S(2)}, u32[]{:S(2)}) collective-permute-start(bf16[13,24,512]{2,1,0:T(8,128)(2,1)S(1)} %pad_maximum_fusion), channel_id=1, source_target_pairs={{0,256},{256,0},{1,257},{257,1},{2,258},{258,2},{3,259},{259,3},{4... | collective-permute-start | bytes 958472 | tf_op jit(solution)/shard_map/ppermute | solution.py:220
  52.4 28.7 %all-to-all-start = ((bf16[64,24,128]{2,1,0:T(8,128)(2,1)}), bf16[64,24,128]{2,1,0:T(8,128)(2,1)S(1)}, u32[]{:S(2)}, u32[]{:S(2)}) async-start(bf16[64,24,128]{2,1,0:T(8,128)(2,1)} %shard_map.113), calls=%async_computation | async-start | bytes 786432 | tf_op jit(solution)/shard_map/all_to_all | solution.py:233
  66.1 1.6 %copy-start.2 = (bf16[144,56,128]{2,1,0:T(8,128)(2,1)S(1)}, bf16[144,56,128]{2,1,0:T(8,128)(2,1)}, u32[]{:S(2)}) copy-start(bf16[144,56,128]{2,1,0:T(8,128)(2,1)} %all-gather.3.cloned.1.call-done) | copy-start | bytes 6193156
  67.7 13.4 %copy-start.3 = (bf16[1,400,192]{1,2,0:T(8,128)(2,1)S(1)}, bf16[1,400,192]{1,2,0:T(8,128)(2,1)}, u32[]{:S(2)}) copy-start(bf16[1,400,192]{1,2,0:T(8,128)(2,1)} %param.14) | copy-start | bytes 460804
  67.7 13.4 %copy-start.4 = (bf16[1,400,192]{1,2,0:T(8,128)(2,1)S(1)}, bf16[1,400,192]{1,2,0:T(8,128)(2,1)}, u32[]{:S(2)}) copy-start(bf16[1,400,192]{1,2,0:T(8,128)(2,1)} %param.15) | copy-start | bytes 460804
  83.6 6.7 %collective-permute-start.9 = (bf16[8,56,800]{2,1,0:T(8,128)(2,1)S(1)}, bf16[8,56,800]{2,1,0:T(8,128)(2,1)S(1)}, u32[]{:S(2)}, u32[]{:S(2)}) collective-permute-start(bf16[8,56,800]{2,1,0:T(8,128)(2,1)S(1)} %get-tuple-element.27), channel_id=1, source_target_pairs={{0,256},{256,0},{1,257},{257,1},{2,258},{258,2},{3,259},{259,3},{4... | collective-permute-start | bytes 2150408 | tf_op jit(solution)/shard_map/ppermute | solution.py:262
  136.9 7.3 %collective-permute-start.10 = (bf16[32,16,128]{2,1,0:T(8,128)(2,1)S(1)}, bf16[32,16,128]{2,1,0:T(8,128)(2,1)S(1)}, u32[]{:S(2)}, u32[]{:S(2)}) collective-permute-start(bf16[32,16,128]{2,1,0:T(8,128)(2,1)S(1)} %all_to_all.22), channel_id=1, source_target_pairs={{0,256},{256,0},{1,257},{257,1},{2,258},{258,2},{3,259},{259,3},{4... | collective-permute-start | bytes 393224 | tf_op jit(solution)/shard_map/ppermute | solution.py:271
Sparse Core Ops, SparseCore 0:
  14.0 45.3 all-gather.2

commit v8 on v7

--- a/solution.py
+++ b/solution.py
@@ -40,14 +40,9 @@
     return lax.dot_general(a, b, (((1,), (0,)), ((), ())), preferred_element_type=F32)
 
 
-def prep_kernel(steps_ref, proj_any, fm_any, lcb_any, mix_any, own_ref, pack_ref,
-                proj_ref, fm_ref, lcb_ref, mix_ref, rows_ref, sems):
-    copies = [
-        pltpu.make_async_copy(src, dst, sems.at[k])
-        for k, (src, dst) in enumerate(((proj_any, proj_ref), (fm_any, fm_ref), (lcb_any, lcb_ref), (mix_any, mix_ref)))
-    ]
-    for copy in copies:
-        copy.start()
+def mask_kernel(steps_ref, proj_any, own_ref, proj_ref, rows_ref, sem):
+    copy = pltpu.make_async_copy(proj_any, proj_ref, sem.at[0])
+    copy.start()
     tables, widest = proj_ref.shape[1], proj_ref.shape[2]
     columns = lax.broadcasted_iota(jnp.int32, (tables, widest), 1)
     table = lax.broadcasted_iota(jnp.int32, (tables, 128), 0)
@@ -56,8 +51,7 @@
         width = jnp.where(table == t, widest // 8 * steps_ref[t], width)
     keep = columns < jnp.concatenate([width] * (widest // 128), axis=1)
     rows_ref[...] = jnp.zeros_like(rows_ref)
-    pack_ref[...] = jnp.zeros_like(pack_ref)
-    copies[0].wait()
+    copy.wait()
     for j in range(12):
         masked = jnp.where(keep, proj_ref[j].astype(F32), 0.0)
         for c in range(4):
@@ -65,15 +59,24 @@
     for p in range(own_ref.shape[0]):
         for c in range(4):
             own_ref[p, :, 128 * c : 128 * c + 128] = rows_ref[c, 24 * p : 24 * p + 24, :].astype(BF16)
-    for copy in copies[1:]:
-        copy.wait()
+
+
+def pack_kernel(fm_any, lcb_any, mix_any, pack_ref, branch_ref, mix_ref, sems):
     rep = lax.axis_index("rep")
-    first = jnp.full((1, 1), rep, jnp.int32) == 0
-    branch = jnp.where(first, fm_ref[...], lcb_ref[...])
-    rows, cols = branch.shape
+    mix_copy = pltpu.make_async_copy(mix_any, mix_ref, sems.at[1])
+    mix_copy.start()
+    for k, source in enumerate((fm_any, lcb_any)):
+        @pl.when(rep == k)
+        def _():
+            copy = pltpu.make_async_copy(source, branch_ref, sems.at[0])
+            copy.start()
+            copy.wait()
+    mix_copy.wait()
+    pack_ref[...] = jnp.zeros_like(pack_ref)
+    rows, cols = branch_ref.shape
     for j in range(7):
         wide = min(128, cols - 128 * j)
-        pack_ref[j, :rows, :wide] = branch[:, 128 * j : 128 * j + wide]
+        pack_ref[j, :rows, :wide] = branch_ref[:, 128 * j : 128 * j + wide]
     for j in range(2):
         start = pl.multiple_of(rep * 96 + 48 * j, 16)
         pack_ref[7 + j, :48, : mix_ref.shape[1]] = mix_ref[pl.ds(start, 48), :]
@@ -186,24 +189,31 @@
 
     pairs = (tables + 1) // 2
     proj = jnp.transpose(proj_weight, (2, 0, 1))
-    own, packed = pl.pallas_call(
-        prep_kernel,
-        out_shape=(
-            jax.ShapeDtypeStruct((pairs, 24, widest), BF16),
-            jax.ShapeDtypeStruct((9, 56, 128), BF16),
-        ),
-        in_specs=[SM] + [pl.BlockSpec(memory_space=pl.ANY)] * 4,
-        out_specs=(VM, VM),
+    own = pl.pallas_call(
+        mask_kernel,
+        out_shape=jax.ShapeDtypeStruct((pairs, 24, widest), BF16),
+        in_specs=[SM, pl.BlockSpec(memory_space=pl.ANY)],
+        out_specs=VM,
         scratch_shapes=[
             pltpu.VMEM(proj.shape, BF16),
+            pltpu.VMEM((4, 24 * pairs, 128), F32),
+            pltpu.SemaphoreType.DMA((1,)),
+        ],
+        cost_estimate=pl.CostEstimate(flops=1 << 20, bytes_accessed=1 << 20, transcendentals=0),
+    )(width_steps, proj)
+    packed = pl.pallas_call(
+        pack_kernel,
+        out_shape=jax.ShapeDtypeStruct((9, 56, 128), BF16),
+        in_specs=[pl.BlockSpec(memory_space=pl.ANY)] * 3,
+        out_specs=VM,
+        scratch_shapes=[
             pltpu.VMEM(fm_weight.shape, BF16),
-            pltpu.VMEM(lcb_weight.shape, BF16),
             pltpu.VMEM(mix_weight.shape[::-1], BF16),
-            pltpu.VMEM((4, 24 * pairs, 128), F32),
-            pltpu.SemaphoreType.DMA((4,)),
+            pltpu.SemaphoreType.DMA((2,)),
         ],
-        cost_estimate=pl.CostEstimate(flops=1 << 20, bytes_accessed=2 << 20, transcendentals=0),
-    )(width_steps, proj, fm_weight, lcb_weight, mix_weight.T)
+        compiler_params=pltpu.CompilerParams(vmem_limit_bytes=2 * 1024 * 1024),
+        cost_estimate=pl.CostEstimate(flops=1 << 20, bytes_accessed=1 << 20, transcendentals=0),
+    )(fm_weight, lcb_weight, mix_weight.T)
     small = lax.all_gather(packed, ("rep",) + TP)
 
     side, back = [(i, i ^ 1) for i in range(4)], [(i, i ^ 3) for i in range(4)]
@@ -237,7 +247,7 @@
         (jax.ShapeDtypeStruct((2, 400, 800), BF16), jax.ShapeDtypeStruct((192, 800), BF16)),
         [small],
         [pltpu.VMEM((400, 896), F32), pltpu.VMEM((192, 800), F32)],
-        flops=15_000_000_000,
+        flops=5_000_000_000,
         size=4 << 20,
         limit=SOME,
     )

time: 153 us -> 150 us (0.980)
  waiting for transfers between devices: 24 us -> 20.8 us
  starting transfers between devices: 55.6 us -> 52.7 us
  local copies, waits for them, and re-layouts: 1.91 us -> 4.5 us
    all_gather x1, waiting for transfers between devices: 0.02 us -> 9.13 us  [per_device(): small = lax.all_gather(packed, ('rep',) + TP)]
    all_to_all x1, waiting for transfers between devices: 12.8 us -> 5.25 us  [per_device(): recv = lax.all_to_all(chunks, ('yl',) + TAB, 0, 0, tiled=True)]
    ppermute x1, waiting for transfers between devices: 5.92 us -> 2.39 us  [per_device(): next_ = lax.ppermute(own, 'x', back)]
    unnamed x12 -> x18, local copies, waits for them, and re-layouts: 1.62 us -> 4.21 us
    pallas_call x1 -> x2, Pallas kernels: 2.58 us -> 3.39 us  [the longest x1 2.52 us: per_device(): pl.pallas_call(mask_kernel, out_shape=jax.ShapeDtypeStruct((pairs, 24, wi...]
  transfers between devices with their start and end apart: 13 -> 13, of which waited for: 6 -> 6; matrix products, arithmetic and copies ran while one was open for 0% -> 0% of each run, Pallas kernels for 4% -> 5%
where the time goes in v8:
time: 150 us; the launch traced here: 149 us
  starting transfers between devices  52.7 us (35%)
  blocking collectives  45.7 us (30%)
  waiting for transfers between devices  20.8 us (14%)
  between operations  14.3 us (10%)
  Pallas kernels  9.64 us (6%)
  local copies, waits for them, and re-layouts  4.5 us (3%)
    all_to_all x1, blocking collectives, per_device(): shares = lax.all_to_all(pair, TP, 0, 0, tiled=True)  15.9 us
    all_to_all x1, blocking collectives, per_device(): parts = lax.all_to_all(tiles, TAB, 0, 0, tiled=True)  15.4 us
    all_to_all x1, blocking collectives, per_device(): lax.all_to_all(jnp.broadcast_to(whole[None], (32, 16, 128)), TAB, 0, 0, t...  14.4 us
    all_to_all x1, starting transfers between devices, per_device(): recv = lax.all_to_all(chunks, ('yl',) + TAB, 0, 0, tiled=True)  13 us
    all_gather x1, waiting for transfers between devices, per_device(): small = lax.all_gather(packed, ('rep',) + TP)  9.13 us
    ppermute x1, starting transfers between devices, per_device(): swapped = lax.ppermute(spread, 'rep', SWAP)  6.32 us
    pallas_call x3, Pallas kernels, call(): pl.pallas_call(kernel, out_shape=outs, in_specs=[VM] * len(ins), out_spec...  6.25 us
    ppermute x1, starting transfers between devices, per_device(): own_o = lax.ppermute(own, 'rep', SWAP)  5.47 us
  transfers between devices with their start and end apart: 13, of which 6 were waited for; matrix products, arithmetic and copies ran while one was open for 0% of the time, Pallas kernels for 5%

profile of v8, /device:TPU:1, one launch (start us, length us, event | category | flops | bytes accessed | tf_op | source)
XLA Modules:
  0.0 148.8 jit_solution(2692038208141789497)
XLA Ops:
  7.2 0.0 all-gather.3.cloned.1.call-start
  7.2 4.0 %collective-permute-start.5 = (bf16[25,32,512]{2,1,0:T(8,128)(2,1)}, bf16[25,32,512]{2,1,0:T(8,128)(2,1)S(1)}, u32[]{:S(2)}, u32[]{:S(2)}) collective-permute-start(bf16[25,32,512]{2,1,0:T(8,128)(2,1)} %bitcast.39), channel_id=1, source_target_pairs={{0,4},{4,0},{1,5},{5,1},{2,6},{6,2},{3,7},{7,3},{8,12},{12,8},{9,1... | collective-permute-start | bytes 2457608 | tf_op jit(solution)/shard_map/ppermute | solution.py:179
  11.3 2.5 %shard_map.111.rest_0_ = bf16[13,24,512]{2,1,0:T(8,128)(2,1)} custom-call(s32[25]{0:T(128)} %steps_ref.1, bf16[12,25,512]{2,1,0:T(8,128)(2,1)} %bitcast.50), custom_call_target="tpu_custom_call" | custom-call | flops 1048576 | bytes 1048576 | tf_op jit(solution)/shard_map/pallas_call | solution.py:192
  13.8 3.1 %collective-permute-start = (bf16[13,24,512]{2,1,0:T(8,128)(2,1)}, bf16[13,24,512]{2,1,0:T(8,128)(2,1)S(1)}, u32[]{:S(2)}, u32[]{:S(2)}) collective-permute-start(bf16[13,24,512]{2,1,0:T(8,128)(2,1)} %shard_map.111.rest_0_), channel_id=1, source_target_pairs={{0,1},{1,0},{2,3},{3,2},{4,5},{5,4},{6,7},{7,6},{8,9},{9,8},{10,11... | collective-permute-start | bytes 958472 | tf_op jit(solution)/shard_map/ppermute | solution.py:221
  16.9 5.5 %collective-permute-start.1 = (bf16[13,24,512]{2,1,0:T(8,128)(2,1)}, bf16[13,24,512]{2,1,0:T(8,128)(2,1)S(1)}, u32[]{:S(2)}, u32[]{:S(2)}) collective-permute-start(bf16[13,24,512]{2,1,0:T(8,128)(2,1)} %shard_map.111.rest_0_), channel_id=1, source_target_pairs={{0,256},{256,0},{1,257},{257,1},{2,258},{258,2},{3,259},{259,3},{4... | collective-permute-start | bytes 958472 | tf_op jit(solution)/shard_map/ppermute | solution.py:223
  22.4 1.9 %collective-permute-start.3 = (bf16[13,24,512]{2,1,0:T(8,128)(2,1)}, bf16[13,24,512]{2,1,0:T(8,128)(2,1)S(1)}, u32[]{:S(2)}, u32[]{:S(2)}) collective-permute-start(bf16[13,24,512]{2,1,0:T(8,128)(2,1)} %shard_map.111.rest_0_), channel_id=1, source_target_pairs={{0,3},{1,2},{2,1},{3,0},{4,7},{5,6},{6,5},{7,4},{8,11},{9,10},{10,... | collective-permute-start | bytes 958472 | tf_op jit(solution)/shard_map/ppermute | solution.py:222
  24.3 0.0 copy-start.2
  24.3 0.9 copy-done.2
  25.2 0.0 copy-start.3
  25.2 0.9 copy-done.3
  26.1 0.0 copy-start.4
  26.1 0.8 copy-done.4
  26.9 0.9 shard_map.114
  27.8 0.0 all-gather.3.cloned.1.call-update
  27.8 0.0 collective-permute-done.rest_1_
  27.8 0.0 collective-permute-done.1.rest_5_
  27.9 4.6 %collective-permute-start.2 = (bf16[7,24,512]{2,1,0:T(8,128)(2,1)S(1)}, bf16[7,24,512]{2,1,0:T(8,128)(2,1)S(1)}, u32[]{:S(2)}, u32[]{:S(2)}) collective-permute-start(bf16[7,24,512]{2,1,0:T(8,128)(2,1)S(1)} %slice.12), channel_id=1, source_target_pairs={{0,3},{1,2},{2,1},{3,0},{4,7},{5,6},{6,5},{7,4},{8,11},{9,10},{10,... | collective-permute-start | bytes 516104 | tf_op jit(solution)/shard_map/ppermute | solution.py:225
  32.5 2.4 %collective-permute-done.3.rest_4_ = bf16[13,24,512]{2,1,0:T(8,128)(2,1)S(1)} collective-permute-done((bf16[13,24,512]{2,1,0:T(8,128)(2,1)}, bf16[13,24,512]{2,1,0:T(8,128)(2,1)S(1)}, u32[]{:S(2)}, u32[]{:S(2)}) %collective-permute-start.3) | collective-permute-done | bytes 319520 | tf_op jit(solution)/shard_map/ppermute | solution.py:222
  34.9 2.4 %collective-permute-start.4 = (bf16[6,24,512]{2,1,0:T(8,128)(2,1)S(1)}, bf16[6,24,512]{2,1,0:T(8,128)(2,1)S(1)}, u32[]{:S(2)}, u32[]{:S(2)}) collective-permute-start(bf16[6,24,512]{2,1,0:T(8,128)(2,1)S(1)} %slice.16), channel_id=1, source_target_pairs={{0,1},{1,0},{2,3},{3,2},{4,5},{5,4},{6,7},{7,6},{8,9},{9,8},{10,11... | collective-permute-start | bytes 442376 | tf_op jit(solution)/shard_map/ppermute | solution.py:226
  37.3 3.4 %collective-permute-start.6 = (bf16[13,24,512]{2,1,0:T(8,128)(2,1)S(1)}, bf16[13,24,512]{2,1,0:T(8,128)(2,1)S(1)}, u32[]{:S(2)}, u32[]{:S(2)}) collective-permute-start(bf16[13,24,512]{2,1,0:T(8,128)(2,1)S(1)} %collective-permute-done.rest_1_), channel_id=1, source_target_pairs={{0,256},{256,0},{1,257},{257,1},{2,258},{258,2},{3,259},{259,3},{4... | collective-permute-start | bytes 958472 | tf_op jit(solution)/shard_map/ppermute | solution.py:227
  40.7 1.9 %collective-permute-start.8 = (bf16[13,24,512]{2,1,0:T(8,128)(2,1)S(1)}, bf16[13,24,512]{2,1,0:T(8,128)(2,1)S(1)}, u32[]{:S(2)}, u32[]{:S(2)}) collective-permute-start(bf16[13,24,512]{2,1,0:T(8,128)(2,1)S(1)} %collective-permute-done.3.rest_4_), channel_id=1, source_target_pairs={{0,256},{256,0},{1,257},{257,1},{2,258},{258,2},{3,259},{259,3},{4... | collective-permute-start | bytes 958472 | tf_op jit(solution)/shard_map/ppermute | solution.py:228
  42.6 0.0 collective-permute-done.4.rest_3_
  42.6 0.0 collective-permute-done.2.rest_2_
  42.7 0.0 copy-start
  42.7 0.0 copy-start.1
  42.7 0.0 collective-permute-done.5.src_ref
  42.7 2.5 %collective-permute-start.7 = (bf16[13,24,512]{2,1,0:T(8,128)(2,1)S(1)}, bf16[13,24,512]{2,1,0:T(8,128)(2,1)S(1)}, u32[]{:S(2)}, u32[]{:S(2)}) collective-permute-start(bf16[13,24,512]{2,1,0:T(8,128)(2,1)S(1)} %pad_maximum_fusion), channel_id=1, source_target_pairs={{0,256},{256,0},{1,257},{257,1},{2,258},{258,2},{3,259},{259,3},{4... | collective-permute-start | bytes 958472 | tf_op jit(solution)/shard_map/ppermute | solution.py:230
  45.3 0.0 collective-permute-done.6.rest_6_
  45.3 0.0 collective-permute-done.8.rest_8_
  45.3 1.2 collective-permute-done.7.rest_7_
  46.5 0.0 copy-done
  46.5 0.0 copy-done.1
  46.5 3.1 %shard_map.113 = bf16[64,24,128]{2,1,0:T(8,128)(2,1)} custom-call(bf16[25,32,512]{2,1,0:T(8,128)(2,1)S(1)} %bitcast.40, bf16[25,32,512]{2,1,0:T(8,128)(2,1)S(1)} %shard_map.112.emb_y_ref, bf16[13,24,512]{2,1,0:T(8,128)(2,1)S(1)} %copy-done, bf16[13,24,512]{2,1,0:T(8,128)(2,1)S(1)} %collective-permute-done.rest_1_, ...), custom_call_target="tpu_custom_call" | custom-call | flops 209715200 | bytes 5242880 | tf_op jit(solution)/shard_map/pallas_call | solution.py:24
  49.6 13.0 %all-to-all-start = ((bf16[64,24,128]{2,1,0:T(8,128)(2,1)}), bf16[64,24,128]{2,1,0:T(8,128)(2,1)S(1)}, u32[]{:S(2)}, u32[]{:S(2)}) async-start(bf16[64,24,128]{2,1,0:T(8,128)(2,1)} %shard_map.113), calls=%async_computation | async-start | bytes 786432 | tf_op jit(solution)/shard_map/all_to_all | solution.py:243
  62.6 9.1 %all-gather.3.cloned.1.call-done = bf16[144,56,128]{2,1,0:T(8,128)(2,1)} async-done(((bf16[9,56,128]{2,1,0:T(8,128)(2,1)}), bf16[144,56,128]{2,1,0:T(8,128)(2,1)}) %all-gather.3.cloned.1.call-update) | async-done | bytes 2064400 | tf_op jit(solution)/shard_map/all_gather | solution.py:217
  71.7 0.0 copy-start.5
  71.7 1.6 %copy-done.5 = bf16[144,56,128]{2,1,0:T(8,128)(2,1)S(1)} copy-done((bf16[144,56,128]{2,1,0:T(8,128)(2,1)S(1)}, bf16[144,56,128]{2,1,0:T(8,128)(2,1)}, u32[]{:S(2)}) %copy-start.5) | copy-done | bytes 2064408
  73.3 0.0 copy-start.6
  73.3 0.0 copy-start.7
  73.3 0.6 shard_map.115
  73.9 5.2 %all-to-all-done.recv_ref = bf16[64,24,128]{2,1,0:T(8,128)(2,1)S(1)} async-done(((bf16[64,24,128]{2,1,0:T(8,128)(2,1)}), bf16[64,24,128]{2,1,0:T(8,128)(2,1)S(1)}, u32[]{:S(2)}, u32[]{:S(2)}) %all-to-all-start) | async-done | bytes 393248 | tf_op jit(solution)/shard_map/all_to_all | solution.py:243
  79.2 0.0 copy-done.6
  79.2 0.0 copy-done.7
  79.2 2.5 %shard_map.116 = (bf16[192,400]{1,0:T(8,128)(2,1)}, bf16[192,400]{1,0:T(8,128)(2,1)}, bf16[8,56,800]{2,1,0:T(8,128)(2,1)S(1)}, bf16[8,56,800]{2,1,0:T(8,128)(2,1)S(1)}) custom-call(bf16[64,24,128]{2,1,0:T(8,128)(2,1)S(1)} %all-to-all-done.recv_ref, bf16[2,400,800]{2,1,0:T(8,128)(2,1)S(1)} %get-tuple-element.18.weight_ref, ...), custom_call_target="tpu_custom_call" | custom-call | flops 700000000 | bytes 5242880 | tf_op jit(solution)/shard_map/pallas_call | solution.py:24
  81.7 3.9 %collective-permute-start.9 = (bf16[8,56,800]{2,1,0:T(8,128)(2,1)S(1)}, bf16[8,56,800]{2,1,0:T(8,128)(2,1)S(1)}, u32[]{:S(2)}, u32[]{:S(2)}) collective-permute-start(bf16[8,56,800]{2,1,0:T(8,128)(2,1)S(1)} %get-tuple-element.23), channel_id=1, source_target_pairs={{0,256},{256,0},{1,257},{257,1},{2,258},{258,2},{3,259},{259,3},{4... | collective-permute-start | bytes 2150408 | tf_op jit(solution)/shard_map/ppermute | solution.py:272
  85.7 1.9 %collective-permute-done.9 = bf16[8,56,800]{2,1,0:T(8,128)(2,1)S(1)} collective-permute-done((bf16[8,56,800]{2,1,0:T(8,128)(2,1)S(1)}, bf16[8,56,800]{2,1,0:T(8,128)(2,1)S(1)}, u32[]{:S(2)}, u32[]{:S(2)}) %collective-permute-start.9) | collective-permute-done | bytes 716832 | tf_op jit(solution)/shard_map/ppermute | solution.py:272
  87.6 0.2 add_convert_fusion
  87.8 15.9 %all_to_all.20 = bf16[8,56,800]{2,1,0:T(8,128)(2,1)S(1)} all-to-all(bf16[8,56,800]{2,1,0:T(8,128)(2,1)S(1)} %add_convert_fusion), channel_id=1, replica_groups=mesh['rep'=2,'z'=8,'yh'=4,'yl'=2,'x'=4] {'yl','x'}, dimensions={0} | all-to-all | bytes 1433600 | tf_op jit(solution)/shard_map/all_to_all | solution.py:274
  103.6 0.1 reduce_sum.24
  103.8 15.4 %all_to_all.21 = bf16[32,16,128]{2,1,0:T(8,128)(2,1)S(1)} all-to-all(bf16[32,16,128]{2,1,0:T(8,128)(2,1)S(1)} %bitcast.47), channel_id=1, replica_groups=mesh['rep'=2,'z'=8,'yh'=4,'yl'=2,'x'=4] {'z','yh'}, dimensions={0} | all-to-all | bytes 262144 | tf_op jit(solution)/shard_map/all_to_all | solution.py:278
  119.3 14.4 %all_to_all.22 = bf16[32,16,128]{2,1,0:T(8,128)(2,1)S(1)} all-to-all(bf16[32,16,128]{2,1,0:T(8,128)(2,1)S(1)} %broadcast_in_dim.14), channel_id=1, replica_groups=mesh['rep'=2,'z'=8,'yh'=4,'yl'=2,'x'=4] {'z','yh'}, dimensions={0} | all-to-all | bytes 262144 | tf_op jit(solution)/shard_map/all_to_all | solution.py:280
  133.7 6.3 %collective-permute-start.10 = (bf16[32,16,128]{2,1,0:T(8,128)(2,1)S(1)}, bf16[32,16,128]{2,1,0:T(8,128)(2,1)S(1)}, u32[]{:S(2)}, u32[]{:S(2)}) collective-permute-start(bf16[32,16,128]{2,1,0:T(8,128)(2,1)S(1)} %all_to_all.22), channel_id=1, source_target_pairs={{0,256},{256,0},{1,257},{257,1},{2,258},{258,2},{3,259},{259,3},{4... | collective-permute-start | bytes 393224 | tf_op jit(solution)/shard_map/ppermute | solution.py:281
  140.1 0.1 copy.17
  140.2 0.9 collective-permute-done.10
  141.0 0.1 copy.18
  141.1 0.8 convert_select_fusion
  (11 shorter events, 0.2 us)
Async XLA Ops:
  7.2 64.6 %all-gather.3.cloned.1.call-start = ((), (), s32[]{:S(2)}) async-start(), calls=%async_computation.4 | async-start | bytes 2193408 | tf_op jit(solution)/shard_map/all_gather | solution.py:217
  7.2 35.5 %collective-permute-start.5 = (bf16[25,32,512]{2,1,0:T(8,128)(2,1)}, bf16[25,32,512]{2,1,0:T(8,128)(2,1)S(1)}, u32[]{:S(2)}, u32[]{:S(2)}) collective-permute-start(bf16[25,32,512]{2,1,0:T(8,128)(2,1)} %bitcast.39), channel_id=1, source_target_pairs={{0,4},{4,0},{1,5},{5,1},{2,6},{6,2},{3,7},{7,3},{8,12},{12,8},{9,1... | collective-permute-start | bytes 2457608 | tf_op jit(solution)/shard_map/ppermute | solution.py:179
  13.8 14.0 %collective-permute-start = (bf16[13,24,512]{2,1,0:T(8,128)(2,1)}, bf16[13,24,512]{2,1,0:T(8,128)(2,1)S(1)}, u32[]{:S(2)}, u32[]{:S(2)}) collective-permute-start(bf16[13,24,512]{2,1,0:T(8,128)(2,1)} %shard_map.111.rest_0_), channel_id=1, source_target_pairs={{0,1},{1,0},{2,3},{3,2},{4,5},{5,4},{6,7},{7,6},{8,9},{9,8},{10,11... | collective-permute-start | bytes 958472 | tf_op jit(solution)/shard_map/ppermute | solution.py:221
  16.9 10.9 %collective-permute-start.1 = (bf16[13,24,512]{2,1,0:T(8,128)(2,1)}, bf16[13,24,512]{2,1,0:T(8,128)(2,1)S(1)}, u32[]{:S(2)}, u32[]{:S(2)}) collective-permute-start(bf16[13,24,512]{2,1,0:T(8,128)(2,1)} %shard_map.111.rest_0_), channel_id=1, source_target_pairs={{0,256},{256,0},{1,257},{257,1},{2,258},{258,2},{3,259},{259,3},{4... | collective-permute-start | bytes 958472 | tf_op jit(solution)/shard_map/ppermute | solution.py:223
  22.4 12.5 %collective-permute-start.3 = (bf16[13,24,512]{2,1,0:T(8,128)(2,1)}, bf16[13,24,512]{2,1,0:T(8,128)(2,1)S(1)}, u32[]{:S(2)}, u32[]{:S(2)}) collective-permute-start(bf16[13,24,512]{2,1,0:T(8,128)(2,1)} %shard_map.111.rest_0_), channel_id=1, source_target_pairs={{0,3},{1,2},{2,1},{3,0},{4,7},{5,6},{6,5},{7,4},{8,11},{9,10},{10,... | collective-permute-start | bytes 958472 | tf_op jit(solution)/shard_map/ppermute | solution.py:222
  24.3 0.9 copy-start.2
  25.2 0.9 copy-start.3
  26.1 0.8 copy-start.4
  27.9 14.8 %collective-permute-start.2 = (bf16[7,24,512]{2,1,0:T(8,128)(2,1)S(1)}, bf16[7,24,512]{2,1,0:T(8,128)(2,1)S(1)}, u32[]{:S(2)}, u32[]{:S(2)}) collective-permute-start(bf16[7,24,512]{2,1,0:T(8,128)(2,1)S(1)} %slice.12), channel_id=1, source_target_pairs={{0,3},{1,2},{2,1},{3,0},{4,7},{5,6},{6,5},{7,4},{8,11},{9,10},{10,... | collective-permute-start | bytes 516104 | tf_op jit(solution)/shard_map/ppermute | solution.py:225
  34.9 7.8 %collective-permute-start.4 = (bf16[6,24,512]{2,1,0:T(8,128)(2,1)S(1)}, bf16[6,24,512]{2,1,0:T(8,128)(2,1)S(1)}, u32[]{:S(2)}, u32[]{:S(2)}) collective-permute-start(bf16[6,24,512]{2,1,0:T(8,128)(2,1)S(1)} %slice.16), channel_id=1, source_target_pairs={{0,1},{1,0},{2,3},{3,2},{4,5},{5,4},{6,7},{7,6},{8,9},{9,8},{10,11... | collective-permute-start | bytes 442376 | tf_op jit(solution)/shard_map/ppermute | solution.py:226
  37.3 8.0 %collective-permute-start.6 = (bf16[13,24,512]{2,1,0:T(8,128)(2,1)S(1)}, bf16[13,24,512]{2,1,0:T(8,128)(2,1)S(1)}, u32[]{:S(2)}, u32[]{:S(2)}) collective-permute-start(bf16[13,24,512]{2,1,0:T(8,128)(2,1)S(1)} %collective-permute-done.rest_1_), channel_id=1, source_target_pairs={{0,256},{256,0},{1,257},{257,1},{2,258},{258,2},{3,259},{259,3},{4... | collective-permute-start | bytes 958472 | tf_op jit(solution)/shard_map/ppermute | solution.py:227
  40.7 4.6 %collective-permute-start.8 = (bf16[13,24,512]{2,1,0:T(8,128)(2,1)S(1)}, bf16[13,24,512]{2,1,0:T(8,128)(2,1)S(1)}, u32[]{:S(2)}, u32[]{:S(2)}) collective-permute-start(bf16[13,24,512]{2,1,0:T(8,128)(2,1)S(1)} %collective-permute-done.3.rest_4_), channel_id=1, source_target_pairs={{0,256},{256,0},{1,257},{257,1},{2,258},{258,2},{3,259},{259,3},{4... | collective-permute-start | bytes 958472 | tf_op jit(solution)/shard_map/ppermute | solution.py:228
  42.7 3.8 %copy-start = (bf16[13,24,512]{2,1,0:T(8,128)(2,1)S(1)}, bf16[13,24,512]{2,1,0:T(8,128)(2,1)}, u32[]{:S(2)}) copy-start(bf16[13,24,512]{2,1,0:T(8,128)(2,1)} %shard_map.111.rest_0_) | copy-start | bytes 958468
  42.7 3.8 %copy-start.1 = (bf16[32,25,512]{2,0,1:T(8,128)(2,1)S(1)}, bf16[32,25,512]{2,0,1:T(8,128)(2,1)}, u32[]{:S(2)}) copy-start(bf16[32,25,512]{2,0,1:T(8,128)(2,1)} %param.8) | copy-start | bytes 2457604
  42.7 3.8 %collective-permute-start.7 = (bf16[13,24,512]{2,1,0:T(8,128)(2,1)S(1)}, bf16[13,24,512]{2,1,0:T(8,128)(2,1)S(1)}, u32[]{:S(2)}, u32[]{:S(2)}) collective-permute-start(bf16[13,24,512]{2,1,0:T(8,128)(2,1)S(1)} %pad_maximum_fusion), channel_id=1, source_target_pairs={{0,256},{256,0},{1,257},{257,1},{2,258},{258,2},{3,259},{259,3},{4... | collective-permute-start | bytes 958472 | tf_op jit(solution)/shard_map/ppermute | solution.py:230
  49.6 29.5 %all-to-all-start = ((bf16[64,24,128]{2,1,0:T(8,128)(2,1)}), bf16[64,24,128]{2,1,0:T(8,128)(2,1)S(1)}, u32[]{:S(2)}, u32[]{:S(2)}) async-start(bf16[64,24,128]{2,1,0:T(8,128)(2,1)} %shard_map.113), calls=%async_computation | async-start | bytes 786432 | tf_op jit(solution)/shard_map/all_to_all | solution.py:243
  71.7 1.6 %copy-start.5 = (bf16[144,56,128]{2,1,0:T(8,128)(2,1)S(1)}, bf16[144,56,128]{2,1,0:T(8,128)(2,1)}, u32[]{:S(2)}) copy-start(bf16[144,56,128]{2,1,0:T(8,128)(2,1)} %all-gather.3.cloned.1.call-done) | copy-start | bytes 6193156
  73.3 5.9 %copy-start.6 = (bf16[1,400,192]{1,2,0:T(8,128)(2,1)S(1)}, bf16[1,400,192]{1,2,0:T(8,128)(2,1)}, u32[]{:S(2)}) copy-start(bf16[1,400,192]{1,2,0:T(8,128)(2,1)} %param.14) | copy-start | bytes 460804
  73.3 5.9 %copy-start.7 = (bf16[1,400,192]{1,2,0:T(8,128)(2,1)S(1)}, bf16[1,400,192]{1,2,0:T(8,128)(2,1)}, u32[]{:S(2)}) copy-start(bf16[1,400,192]{1,2,0:T(8,128)(2,1)} %param.15) | copy-start | bytes 460804
  81.7 5.9 %collective-permute-start.9 = (bf16[8,56,800]{2,1,0:T(8,128)(2,1)S(1)}, bf16[8,56,800]{2,1,0:T(8,128)(2,1)S(1)}, u32[]{:S(2)}, u32[]{:S(2)}) collective-permute-start(bf16[8,56,800]{2,1,0:T(8,128)(2,1)S(1)} %get-tuple-element.23), channel_id=1, source_target_pairs={{0,256},{256,0},{1,257},{257,1},{2,258},{258,2},{3,259},{259,3},{4... | collective-permute-start | bytes 2150408 | tf_op jit(solution)/shard_map/ppermute | solution.py:272
  133.7 7.3 %collective-permute-start.10 = (bf16[32,16,128]{2,1,0:T(8,128)(2,1)S(1)}, bf16[32,16,128]{2,1,0:T(8,128)(2,1)S(1)}, u32[]{:S(2)}, u32[]{:S(2)}) collective-permute-start(bf16[32,16,128]{2,1,0:T(8,128)(2,1)S(1)} %all_to_all.22), channel_id=1, source_target_pairs={{0,256},{256,0},{1,257},{257,1},{2,258},{258,2},{3,259},{259,3},{4... | collective-permute-start | bytes 393224 | tf_op jit(solution)/shard_map/ppermute | solution.py:281
Sparse Core Ops, SparseCore 0:
  27.9 43.7 all-gather.2

commit v9 on v8

--- a/solution.py
+++ b/solution.py
@@ -93,10 +93,6 @@
                 mixw_ref[row : row + 48, 100 * i : 100 * i + 100] = piece[7 + j][:48, :100].astype(F32)
         branch_ref[k] = wide_ref[:, :800].astype(BF16)
     mix_ref[...] = mixw_ref[...].astype(BF16)
-
-
-def hold_kernel(src_ref, out_ref):
-    del src_ref, out_ref
 
 
 def project_kernel(emb_ref, emb_y_ref, *rest):
@@ -177,15 +173,6 @@
     tables, widest = emb_rows.shape[1], emb_rows.shape[2]
     emb = jnp.transpose(emb_rows, (1, 0, 2))
     emb_y = lax.ppermute(emb, "yl", SWAP)
-    emb_y = pl.pallas_call(
-        hold_kernel,
-        out_shape=jax.ShapeDtypeStruct(emb.shape, BF16),
-        in_specs=[pl.BlockSpec(memory_space=pl.ANY)],
-        out_specs=pl.BlockSpec(memory_space=pl.ANY),
-        input_output_aliases={0: 0},
-        compiler_params=pltpu.CompilerParams(vmem_limit_bytes=1 << 20),
-        cost_estimate=pl.CostEstimate(flops=30_000_000_000, bytes_accessed=0, transcendentals=0),
-    )(emb_y)
 
     pairs = (tables + 1) // 2
     proj = jnp.transpose(proj_weight, (2, 0, 1))
@@ -221,12 +208,11 @@
     near = lax.ppermute(own, "x", side)
     next_ = lax.ppermute(own, "x", back)
     own_o = lax.ppermute(own, "rep", SWAP)
-    near, own_o = lax.optimization_barrier((near, own_o))
     far_a = lax.ppermute(near[:half], "x", back)
     far_b = lax.ppermute(next_[half:], "x", side)
     near_o = lax.ppermute(near, "rep", SWAP)
     next_o = lax.ppermute(next_, "rep", SWAP)
-    far, emb_y = lax.optimization_barrier((jnp.concatenate([far_a, far_b], axis=0), emb_y))
+    far = jnp.concatenate([far_a, far_b], axis=0)
     far_o = lax.ppermute(far, "rep", SWAP)
     mine = [own, near, far_a, far_b, next_]
     other = [own_o, near_o, far_o, next_o]
@@ -237,7 +223,7 @@
         [emb, emb_y] + mine + other,
         [pltpu.VMEM((2, 768, 128), F32)],
         limit=SOME,
-        flops=2 * 25 * 64 * 128 * 512,
+        flops=25_000_000_000,
         size=5 << 20,
     )
     recv = lax.all_to_all(chunks, ("yl",) + TAB, 0, 0, tiled=True)
@@ -247,7 +233,7 @@
         (jax.ShapeDtypeStruct((2, 400, 800), BF16), jax.ShapeDtypeStruct((192, 800), BF16)),
         [small],
         [pltpu.VMEM((400, 896), F32), pltpu.VMEM((192, 800), F32)],
-        flops=5_000_000_000,
+        flops=0,
         size=4 << 20,
         limit=SOME,
     )

time: 150 us -> 148 us (0.987)
  waiting for transfers between devices: 20.8 us -> 18.4 us
    ppermute x1, waiting for transfers between devices: 2.39 us -> 0.01 us  [per_device(): next_ = lax.ppermute(own, 'x', back)]
    ppermute x1, starting transfers between devices: 4.6 us -> 2.77 us  [per_device(): far_a = lax.ppermute(near[:half], 'x', back)]
    ppermute x1, starting transfers between devices: 1.92 us -> 3.72 us  [per_device(): next_ = lax.ppermute(own, 'x', back)]
  transfers between devices with their start and end apart: 13 -> 13, of which waited for: 6 -> 5; matrix products, arithmetic and copies ran while one was open for 0% -> 0% of each run, Pallas kernels for 5% -> 3%
where the time goes in v9:
time: 148 us; the launch traced here: 147 us
  starting transfers between devices  52.9 us (36%)
  blocking collectives  46.1 us (31%)
  waiting for transfers between devices  18.4 us (12%)
  between operations  14.3 us (10%)
  Pallas kernels  9.66 us (7%)
  local copies, waits for them, and re-layouts  4.49 us (3%)
    all_to_all x1, blocking collectives, per_device(): parts = lax.all_to_all(tiles, TAB, 0, 0, tiled=True)  16.5 us
    all_to_all x1, blocking collectives, per_device(): shares = lax.all_to_all(pair, TP, 0, 0, tiled=True)  15.2 us
    all_to_all x1, blocking collectives, per_device(): lax.all_to_all(jnp.broadcast_to(whole[None], (32, 16, 128)), TAB, 0, 0, t...  14.3 us
    all_to_all x1, starting transfers between devices, per_device(): recv = lax.all_to_all(chunks, ('yl',) + TAB, 0, 0, tiled=True)  13 us
    all_gather x1, waiting for transfers between devices, per_device(): small = lax.all_gather(packed, ('rep',) + TP)  9.63 us
    ppermute x1, starting transfers between devices, per_device(): own_o = lax.ppermute(own, 'rep', SWAP)  6.82 us
    pallas_call x3, Pallas kernels, call(): pl.pallas_call(kernel, out_shape=outs, in_specs=[VM] * len(ins), out_spec...  6.26 us
    ppermute x1, starting transfers between devices, per_device(): swapped = lax.ppermute(spread, 'rep', SWAP)  6 us
  transfers between devices with their start and end apart: 13, of which 5 were waited for; matrix products, arithmetic and copies ran while one was open for 0% of the time, Pallas kernels for 3%

profile of v9, /device:TPU:1, one launch (start us, length us, event | category | flops | bytes accessed | tf_op | source)
XLA Modules:
  0.0 147.0 jit_solution(2996130130555619381)
XLA Ops:
  7.2 0.0 all-gather.3.cloned.1.call-start
  7.2 2.5 %shard_map.111.rest_0_ = bf16[13,24,512]{2,1,0:T(8,128)(2,1)} custom-call(s32[25]{0:T(128)} %steps_ref.1, bf16[12,25,512]{2,1,0:T(8,128)(2,1)} %bitcast.50), custom_call_target="tpu_custom_call" | custom-call | flops 1048576 | bytes 1048576 | tf_op jit(solution)/shard_map/pallas_call | solution.py:179
  9.7 0.0 copy-start.1
  9.7 4.1 %collective-permute-start.1 = (bf16[13,24,512]{2,1,0:T(8,128)(2,1)}, bf16[13,24,512]{2,1,0:T(8,128)(2,1)S(1)}, u32[]{:S(2)}, u32[]{:S(2)}) collective-permute-start(bf16[13,24,512]{2,1,0:T(8,128)(2,1)} %shard_map.111.rest_0_), channel_id=1, source_target_pairs={{0,1},{1,0},{2,3},{3,2},{4,5},{5,4},{6,7},{7,6},{8,9},{9,8},{10,11... | collective-permute-start | bytes 958472 | tf_op jit(solution)/shard_map/ppermute | solution.py:208
  13.8 3.7 %collective-permute-start.3 = (bf16[13,24,512]{2,1,0:T(8,128)(2,1)}, bf16[13,24,512]{2,1,0:T(8,128)(2,1)S(1)}, u32[]{:S(2)}, u32[]{:S(2)}) collective-permute-start(bf16[13,24,512]{2,1,0:T(8,128)(2,1)} %shard_map.111.rest_0_), channel_id=1, source_target_pairs={{0,3},{1,2},{2,1},{3,0},{4,7},{5,6},{6,5},{7,4},{8,11},{9,10},{10,... | collective-permute-start | bytes 958472 | tf_op jit(solution)/shard_map/ppermute | solution.py:209
  17.6 3.2 %collective-permute-start = (bf16[25,32,512]{2,1,0:T(8,128)(2,1)}, bf16[25,32,512]{2,1,0:T(8,128)(2,1)S(1)}, u32[]{:S(2)}, u32[]{:S(2)}) collective-permute-start(bf16[25,32,512]{2,1,0:T(8,128)(2,1)} %bitcast.41), channel_id=1, source_target_pairs={{0,4},{4,0},{1,5},{5,1},{2,6},{6,2},{3,7},{7,3},{8,12},{12,8},{9,1... | collective-permute-start | bytes 2457608 | tf_op jit(solution)/shard_map/ppermute | solution.py:175
  20.8 0.0 copy-start.2
  20.8 0.9 copy-done.2
  21.7 0.0 copy-start.3
  21.7 0.9 copy-done.3
  22.6 0.0 copy-start.4
  22.6 0.8 copy-done.4
  23.4 0.0 copy-start.5
  23.4 0.9 shard_map.113
  24.3 0.0 all-gather.3.cloned.1.call-update
  24.3 0.0 collective-permute-done.1.rest_1_
  24.3 2.8 %collective-permute-start.2 = (bf16[7,24,512]{2,1,0:T(8,128)(2,1)S(1)}, bf16[7,24,512]{2,1,0:T(8,128)(2,1)S(1)}, u32[]{:S(2)}, u32[]{:S(2)}) collective-permute-start(bf16[7,24,512]{2,1,0:T(8,128)(2,1)S(1)} %slice.16), channel_id=1, source_target_pairs={{0,3},{1,2},{2,1},{3,0},{4,7},{5,6},{6,5},{7,4},{8,11},{9,10},{10,... | collective-permute-start | bytes 516104 | tf_op jit(solution)/shard_map/ppermute | solution.py:211
  27.1 0.0 collective-permute-done.3.rest_4_
  27.1 1.9 %collective-permute-start.4 = (bf16[6,24,512]{2,1,0:T(8,128)(2,1)S(1)}, bf16[6,24,512]{2,1,0:T(8,128)(2,1)S(1)}, u32[]{:S(2)}, u32[]{:S(2)}) collective-permute-start(bf16[6,24,512]{2,1,0:T(8,128)(2,1)S(1)} %slice.17), channel_id=1, source_target_pairs={{0,1},{1,0},{2,3},{3,2},{4,5},{5,4},{6,7},{7,6},{8,9},{9,8},{10,11... | collective-permute-start | bytes 442376 | tf_op jit(solution)/shard_map/ppermute | solution.py:212
  29.1 6.8 %collective-permute-start.5 = (bf16[13,24,512]{2,1,0:T(8,128)(2,1)}, bf16[13,24,512]{2,1,0:T(8,128)(2,1)S(1)}, u32[]{:S(2)}, u32[]{:S(2)}) collective-permute-start(bf16[13,24,512]{2,1,0:T(8,128)(2,1)} %shard_map.111.rest_0_), channel_id=1, source_target_pairs={{0,256},{256,0},{1,257},{257,1},{2,258},{258,2},{3,259},{259,3},{4... | collective-permute-start | bytes 958472 | tf_op jit(solution)/shard_map/ppermute | solution.py:210
  35.9 1.9 %collective-permute-start.6 = (bf16[13,24,512]{2,1,0:T(8,128)(2,1)S(1)}, bf16[13,24,512]{2,1,0:T(8,128)(2,1)S(1)}, u32[]{:S(2)}, u32[]{:S(2)}) collective-permute-start(bf16[13,24,512]{2,1,0:T(8,128)(2,1)S(1)} %collective-permute-done.1.rest_1_), channel_id=1, source_target_pairs={{0,256},{256,0},{1,257},{257,1},{2,258},{258,2},{3,259},{259,3},{4... | collective-permute-start | bytes 958472 | tf_op jit(solution)/shard_map/ppermute | solution.py:213
  37.8 0.0 collective-permute-done.4.rest_3_
  37.8 2.4 %collective-permute-start.8 = (bf16[13,24,512]{2,1,0:T(8,128)(2,1)S(1)}, bf16[13,24,512]{2,1,0:T(8,128)(2,1)S(1)}, u32[]{:S(2)}, u32[]{:S(2)}) collective-permute-start(bf16[13,24,512]{2,1,0:T(8,128)(2,1)S(1)} %collective-permute-done.3.rest_4_), channel_id=1, source_target_pairs={{0,256},{256,0},{1,257},{257,1},{2,258},{258,2},{3,259},{259,3},{4... | collective-permute-start | bytes 958472 | tf_op jit(solution)/shard_map/ppermute | solution.py:214
  40.2 0.0 collective-permute-done.2.rest_2_
  40.3 1.9 %collective-permute-start.7 = (bf16[13,24,512]{2,1,0:T(8,128)(2,1)S(1)}, bf16[13,24,512]{2,1,0:T(8,128)(2,1)S(1)}, u32[]{:S(2)}, u32[]{:S(2)}) collective-permute-start(bf16[13,24,512]{2,1,0:T(8,128)(2,1)S(1)} %pad_maximum_fusion), channel_id=1, source_target_pairs={{0,256},{256,0},{1,257},{257,1},{2,258},{258,2},{3,259},{259,3},{4... | collective-permute-start | bytes 958472 | tf_op jit(solution)/shard_map/ppermute | solution.py:216
  42.2 0.0 collective-permute-done.5.rest_5_
  42.2 0.0 collective-permute-done.6.rest_6_
  42.2 0.0 collective-permute-done.8.rest_8_
  42.2 1.7 %collective-permute-done.7.rest_7_ = bf16[13,24,512]{2,1,0:T(8,128)(2,1)S(1)} collective-permute-done((bf16[13,24,512]{2,1,0:T(8,128)(2,1)S(1)}, bf16[13,24,512]{2,1,0:T(8,128)(2,1)S(1)}, u32[]{:S(2)}, u32[]{:S(2)}) %collective-permute-start.7) | collective-permute-done | bytes 319520 | tf_op jit(solution)/shard_map/ppermute | solution.py:216
  44.0 0.0 collective-permute-done.emb_y_ref
  44.0 0.0 copy-done.1
  44.0 0.0 copy-done.5
  44.0 3.1 %shard_map.112 = bf16[64,24,128]{2,1,0:T(8,128)(2,1)} custom-call(bf16[25,32,512]{2,1,0:T(8,128)(2,1)S(1)} %bitcast.42, bf16[25,32,512]{2,1,0:T(8,128)(2,1)S(1)} %collective-permute-done.emb_y_ref, bf16[13,24,512]{2,1,0:T(8,128)(2,1)S(1)} %copy-done.1, bf16[13,24,512]{2,1,0:T(8,128)(2,1)S(1)} %collective-permute-done.1.rest_1_, ...), custom_call_target="tpu_custom_call" | custom-call | flops 24999999488 | bytes 5242880 | tf_op jit(solution)/shard_map/pallas_call | solution.py:24
  47.1 0.0 copy-start.6
  47.1 0.0 copy-start.7
  47.1 13.0 %all-to-all-start = ((bf16[64,24,128]{2,1,0:T(8,128)(2,1)}), bf16[64,24,128]{2,1,0:T(8,128)(2,1)S(1)}, u32[]{:S(2)}, u32[]{:S(2)}) async-start(bf16[64,24,128]{2,1,0:T(8,128)(2,1)} %shard_map.112), calls=%async_computation | async-start | bytes 786432 | tf_op jit(solution)/shard_map/all_to_all | solution.py:229
  60.1 9.6 %all-gather.3.cloned.1.call-done = bf16[144,56,128]{2,1,0:T(8,128)(2,1)} async-done(((bf16[9,56,128]{2,1,0:T(8,128)(2,1)}), bf16[144,56,128]{2,1,0:T(8,128)(2,1)}) %all-gather.3.cloned.1.call-update) | async-done | bytes 2064400 | tf_op jit(solution)/shard_map/all_gather | solution.py:204
  69.7 0.0 copy-start
  69.7 1.6 %copy-done = bf16[144,56,128]{2,1,0:T(8,128)(2,1)S(1)} copy-done((bf16[144,56,128]{2,1,0:T(8,128)(2,1)S(1)}, bf16[144,56,128]{2,1,0:T(8,128)(2,1)}, u32[]{:S(2)}) %copy-start) | copy-done | bytes 2064408
  71.3 0.6 shard_map.114
  71.9 4.3 %all-to-all-done.recv_ref = bf16[64,24,128]{2,1,0:T(8,128)(2,1)S(1)} async-done(((bf16[64,24,128]{2,1,0:T(8,128)(2,1)}), bf16[64,24,128]{2,1,0:T(8,128)(2,1)S(1)}, u32[]{:S(2)}, u32[]{:S(2)}) %all-to-all-start) | async-done | bytes 393248 | tf_op jit(solution)/shard_map/all_to_all | solution.py:229
  76.2 0.0 copy-done.6
  76.2 0.0 copy-done.7
  76.2 2.5 %shard_map.115 = (bf16[192,400]{1,0:T(8,128)(2,1)}, bf16[192,400]{1,0:T(8,128)(2,1)}, bf16[8,56,800]{2,1,0:T(8,128)(2,1)S(1)}, bf16[8,56,800]{2,1,0:T(8,128)(2,1)S(1)}) custom-call(bf16[64,24,128]{2,1,0:T(8,128)(2,1)S(1)} %all-to-all-done.recv_ref, bf16[2,400,800]{2,1,0:T(8,128)(2,1)S(1)} %get-tuple-element.10.weight_ref, ...), custom_call_target="tpu_custom_call" | custom-call | flops 700000000 | bytes 5242880 | tf_op jit(solution)/shard_map/pallas_call | solution.py:24
  78.7 5.1 %collective-permute-start.9 = (bf16[8,56,800]{2,1,0:T(8,128)(2,1)S(1)}, bf16[8,56,800]{2,1,0:T(8,128)(2,1)S(1)}, u32[]{:S(2)}, u32[]{:S(2)}) collective-permute-start(bf16[8,56,800]{2,1,0:T(8,128)(2,1)S(1)} %get-tuple-element.15), channel_id=1, source_target_pairs={{0,256},{256,0},{1,257},{257,1},{2,258},{258,2},{3,259},{259,3},{4... | collective-permute-start | bytes 2150408 | tf_op jit(solution)/shard_map/ppermute | solution.py:258
  83.8 1.9 %collective-permute-done.9 = bf16[8,56,800]{2,1,0:T(8,128)(2,1)S(1)} collective-permute-done((bf16[8,56,800]{2,1,0:T(8,128)(2,1)S(1)}, bf16[8,56,800]{2,1,0:T(8,128)(2,1)S(1)}, u32[]{:S(2)}, u32[]{:S(2)}) %collective-permute-start.9) | collective-permute-done | bytes 716832 | tf_op jit(solution)/shard_map/ppermute | solution.py:258
  85.7 0.2 add_convert_fusion
  85.9 15.2 %all_to_all.20 = bf16[8,56,800]{2,1,0:T(8,128)(2,1)S(1)} all-to-all(bf16[8,56,800]{2,1,0:T(8,128)(2,1)S(1)} %add_convert_fusion), channel_id=1, replica_groups=mesh['rep'=2,'z'=8,'yh'=4,'yl'=2,'x'=4] {'yl','x'}, dimensions={0} | all-to-all | bytes 1433600 | tf_op jit(solution)/shard_map/all_to_all | solution.py:260
  101.2 0.1 reduce_sum.24
  101.4 16.5 %all_to_all.21 = bf16[32,16,128]{2,1,0:T(8,128)(2,1)S(1)} all-to-all(bf16[32,16,128]{2,1,0:T(8,128)(2,1)S(1)} %bitcast.47), channel_id=1, replica_groups=mesh['rep'=2,'z'=8,'yh'=4,'yl'=2,'x'=4] {'z','yh'}, dimensions={0} | all-to-all | bytes 262144 | tf_op jit(solution)/shard_map/all_to_all | solution.py:264
  118.0 14.3 %all_to_all.22 = bf16[32,16,128]{2,1,0:T(8,128)(2,1)S(1)} all-to-all(bf16[32,16,128]{2,1,0:T(8,128)(2,1)S(1)} %broadcast_in_dim.14), channel_id=1, replica_groups=mesh['rep'=2,'z'=8,'yh'=4,'yl'=2,'x'=4] {'z','yh'}, dimensions={0} | all-to-all | bytes 262144 | tf_op jit(solution)/shard_map/all_to_all | solution.py:266
  132.3 6.0 %collective-permute-start.10 = (bf16[32,16,128]{2,1,0:T(8,128)(2,1)S(1)}, bf16[32,16,128]{2,1,0:T(8,128)(2,1)S(1)}, u32[]{:S(2)}, u32[]{:S(2)}) collective-permute-start(bf16[32,16,128]{2,1,0:T(8,128)(2,1)S(1)} %all_to_all.22), channel_id=1, source_target_pairs={{0,256},{256,0},{1,257},{257,1},{2,258},{258,2},{3,259},{259,3},{4... | collective-permute-start | bytes 393224 | tf_op jit(solution)/shard_map/ppermute | solution.py:267
  138.3 0.1 copy.16
  138.4 0.9 collective-permute-done.10
  139.2 0.1 copy.17
  139.4 0.8 convert_select_fusion
  (10 shorter events, 0.2 us)
Async XLA Ops:
  7.2 62.6 %all-gather.3.cloned.1.call-start = ((), (), s32[]{:S(2)}) async-start(), calls=%async_computation.4 | async-start | bytes 2193408 | tf_op jit(solution)/shard_map/all_gather | solution.py:204
  9.7 34.3 %copy-start.1 = (bf16[13,24,512]{2,1,0:T(8,128)(2,1)S(1)}, bf16[13,24,512]{2,1,0:T(8,128)(2,1)}, u32[]{:S(2)}) copy-start(bf16[13,24,512]{2,1,0:T(8,128)(2,1)} %shard_map.111.rest_0_) | copy-start | bytes 958468
  9.7 14.5 %collective-permute-start.1 = (bf16[13,24,512]{2,1,0:T(8,128)(2,1)}, bf16[13,24,512]{2,1,0:T(8,128)(2,1)S(1)}, u32[]{:S(2)}, u32[]{:S(2)}) collective-permute-start(bf16[13,24,512]{2,1,0:T(8,128)(2,1)} %shard_map.111.rest_0_), channel_id=1, source_target_pairs={{0,1},{1,0},{2,3},{3,2},{4,5},{5,4},{6,7},{7,6},{8,9},{9,8},{10,11... | collective-permute-start | bytes 958472 | tf_op jit(solution)/shard_map/ppermute | solution.py:208
  13.8 13.3 %collective-permute-start.3 = (bf16[13,24,512]{2,1,0:T(8,128)(2,1)}, bf16[13,24,512]{2,1,0:T(8,128)(2,1)S(1)}, u32[]{:S(2)}, u32[]{:S(2)}) collective-permute-start(bf16[13,24,512]{2,1,0:T(8,128)(2,1)} %shard_map.111.rest_0_), channel_id=1, source_target_pairs={{0,3},{1,2},{2,1},{3,0},{4,7},{5,6},{6,5},{7,4},{8,11},{9,10},{10,... | collective-permute-start | bytes 958472 | tf_op jit(solution)/shard_map/ppermute | solution.py:209
  17.6 26.4 %collective-permute-start = (bf16[25,32,512]{2,1,0:T(8,128)(2,1)}, bf16[25,32,512]{2,1,0:T(8,128)(2,1)S(1)}, u32[]{:S(2)}, u32[]{:S(2)}) collective-permute-start(bf16[25,32,512]{2,1,0:T(8,128)(2,1)} %bitcast.41), channel_id=1, source_target_pairs={{0,4},{4,0},{1,5},{5,1},{2,6},{6,2},{3,7},{7,3},{8,12},{12,8},{9,1... | collective-permute-start | bytes 2457608 | tf_op jit(solution)/shard_map/ppermute | solution.py:175
  20.8 0.9 copy-start.2
  21.7 0.9 copy-start.3
  22.6 0.8 copy-start.4
  23.4 20.6 %copy-start.5 = (bf16[32,25,512]{2,0,1:T(8,128)(2,1)S(1)}, bf16[32,25,512]{2,0,1:T(8,128)(2,1)}, u32[]{:S(2)}) copy-start(bf16[32,25,512]{2,0,1:T(8,128)(2,1)} %param.8) | copy-start | bytes 2457604
  24.3 15.9 %collective-permute-start.2 = (bf16[7,24,512]{2,1,0:T(8,128)(2,1)S(1)}, bf16[7,24,512]{2,1,0:T(8,128)(2,1)S(1)}, u32[]{:S(2)}, u32[]{:S(2)}) collective-permute-start(bf16[7,24,512]{2,1,0:T(8,128)(2,1)S(1)} %slice.16), channel_id=1, source_target_pairs={{0,3},{1,2},{2,1},{3,0},{4,7},{5,6},{6,5},{7,4},{8,11},{9,10},{10,... | collective-permute-start | bytes 516104 | tf_op jit(solution)/shard_map/ppermute | solution.py:211
  27.1 10.7 %collective-permute-start.4 = (bf16[6,24,512]{2,1,0:T(8,128)(2,1)S(1)}, bf16[6,24,512]{2,1,0:T(8,128)(2,1)S(1)}, u32[]{:S(2)}, u32[]{:S(2)}) collective-permute-start(bf16[6,24,512]{2,1,0:T(8,128)(2,1)S(1)} %slice.17), channel_id=1, source_target_pairs={{0,1},{1,0},{2,3},{3,2},{4,5},{5,4},{6,7},{7,6},{8,9},{9,8},{10,11... | collective-permute-start | bytes 442376 | tf_op jit(solution)/shard_map/ppermute | solution.py:212
  29.1 13.2 %collective-permute-start.5 = (bf16[13,24,512]{2,1,0:T(8,128)(2,1)}, bf16[13,24,512]{2,1,0:T(8,128)(2,1)S(1)}, u32[]{:S(2)}, u32[]{:S(2)}) collective-permute-start(bf16[13,24,512]{2,1,0:T(8,128)(2,1)} %shard_map.111.rest_0_), channel_id=1, source_target_pairs={{0,256},{256,0},{1,257},{257,1},{2,258},{258,2},{3,259},{259,3},{4... | collective-permute-start | bytes 958472 | tf_op jit(solution)/shard_map/ppermute | solution.py:210
  35.9 6.3 %collective-permute-start.6 = (bf16[13,24,512]{2,1,0:T(8,128)(2,1)S(1)}, bf16[13,24,512]{2,1,0:T(8,128)(2,1)S(1)}, u32[]{:S(2)}, u32[]{:S(2)}) collective-permute-start(bf16[13,24,512]{2,1,0:T(8,128)(2,1)S(1)} %collective-permute-done.1.rest_1_), channel_id=1, source_target_pairs={{0,256},{256,0},{1,257},{257,1},{2,258},{258,2},{3,259},{259,3},{4... | collective-permute-start | bytes 958472 | tf_op jit(solution)/shard_map/ppermute | solution.py:213
  37.8 4.4 %collective-permute-start.8 = (bf16[13,24,512]{2,1,0:T(8,128)(2,1)S(1)}, bf16[13,24,512]{2,1,0:T(8,128)(2,1)S(1)}, u32[]{:S(2)}, u32[]{:S(2)}) collective-permute-start(bf16[13,24,512]{2,1,0:T(8,128)(2,1)S(1)} %collective-permute-done.3.rest_4_), channel_id=1, source_target_pairs={{0,256},{256,0},{1,257},{257,1},{2,258},{258,2},{3,259},{259,3},{4... | collective-permute-start | bytes 958472 | tf_op jit(solution)/shard_map/ppermute | solution.py:214
  40.3 3.7 %collective-permute-start.7 = (bf16[13,24,512]{2,1,0:T(8,128)(2,1)S(1)}, bf16[13,24,512]{2,1,0:T(8,128)(2,1)S(1)}, u32[]{:S(2)}, u32[]{:S(2)}) collective-permute-start(bf16[13,24,512]{2,1,0:T(8,128)(2,1)S(1)} %pad_maximum_fusion), channel_id=1, source_target_pairs={{0,256},{256,0},{1,257},{257,1},{2,258},{258,2},{3,259},{259,3},{4... | collective-permute-start | bytes 958472 | tf_op jit(solution)/shard_map/ppermute | solution.py:216
  47.1 29.1 %copy-start.6 = (bf16[1,400,192]{1,2,0:T(8,128)(2,1)S(1)}, bf16[1,400,192]{1,2,0:T(8,128)(2,1)}, u32[]{:S(2)}) copy-start(bf16[1,400,192]{1,2,0:T(8,128)(2,1)} %param.14) | copy-start | bytes 460804
  47.1 29.1 %copy-start.7 = (bf16[1,400,192]{1,2,0:T(8,128)(2,1)S(1)}, bf16[1,400,192]{1,2,0:T(8,128)(2,1)}, u32[]{:S(2)}) copy-start(bf16[1,400,192]{1,2,0:T(8,128)(2,1)} %param.15) | copy-start | bytes 460804
  47.1 29.1 %all-to-all-start = ((bf16[64,24,128]{2,1,0:T(8,128)(2,1)}), bf16[64,24,128]{2,1,0:T(8,128)(2,1)S(1)}, u32[]{:S(2)}, u32[]{:S(2)}) async-start(bf16[64,24,128]{2,1,0:T(8,128)(2,1)} %shard_map.112), calls=%async_computation | async-start | bytes 786432 | tf_op jit(solution)/shard_map/all_to_all | solution.py:229
  69.7 1.6 %copy-start = (bf16[144,56,128]{2,1,0:T(8,128)(2,1)S(1)}, bf16[144,56,128]{2,1,0:T(8,128)(2,1)}, u32[]{:S(2)}) copy-start(bf16[144,56,128]{2,1,0:T(8,128)(2,1)} %all-gather.3.cloned.1.call-done) | copy-start | bytes 6193156
  78.7 7.0 %collective-permute-start.9 = (bf16[8,56,800]{2,1,0:T(8,128)(2,1)S(1)}, bf16[8,56,800]{2,1,0:T(8,128)(2,1)S(1)}, u32[]{:S(2)}, u32[]{:S(2)}) collective-permute-start(bf16[8,56,800]{2,1,0:T(8,128)(2,1)S(1)} %get-tuple-element.15), channel_id=1, source_target_pairs={{0,256},{256,0},{1,257},{257,1},{2,258},{258,2},{3,259},{259,3},{4... | collective-permute-start | bytes 2150408 | tf_op jit(solution)/shard_map/ppermute | solution.py:258
  132.3 7.0 %collective-permute-start.10 = (bf16[32,16,128]{2,1,0:T(8,128)(2,1)S(1)}, bf16[32,16,128]{2,1,0:T(8,128)(2,1)S(1)}, u32[]{:S(2)}, u32[]{:S(2)}) collective-permute-start(bf16[32,16,128]{2,1,0:T(8,128)(2,1)S(1)} %all_to_all.22), channel_id=1, source_target_pairs={{0,256},{256,0},{1,257},{257,1},{2,258},{258,2},{3,259},{259,3},{4... | collective-permute-start | bytes 393224 | tf_op jit(solution)/shard_map/ppermute | solution.py:267
Sparse Core Ops, SparseCore 0:
  24.4 45.2 all-gather.2

commit v10 on v7

--- a/solution.py
+++ b/solution.py
@@ -92,10 +92,6 @@
     mix_ref[...] = mixw_ref[...].astype(BF16)
 
 
-def hold_kernel(src_ref, out_ref):
-    del src_ref, out_ref
-
-
 def project_kernel(emb_ref, emb_y_ref, *rest):
     w_refs, out_ref, acc_ref = rest[:-2], rest[-2], rest[-1]
     mine = lax.axis_index("yl")
@@ -174,15 +170,6 @@
     tables, widest = emb_rows.shape[1], emb_rows.shape[2]
     emb = jnp.transpose(emb_rows, (1, 0, 2))
     emb_y = lax.ppermute(emb, "yl", SWAP)
-    emb_y = pl.pallas_call(
-        hold_kernel,
-        out_shape=jax.ShapeDtypeStruct(emb.shape, BF16),
-        in_specs=[pl.BlockSpec(memory_space=pl.ANY)],
-        out_specs=pl.BlockSpec(memory_space=pl.ANY),
-        input_output_aliases={0: 0},
-        compiler_params=pltpu.CompilerParams(vmem_limit_bytes=1 << 20),
-        cost_estimate=pl.CostEstimate(flops=30_000_000_000, bytes_accessed=0, transcendentals=0),
-    )(emb_y)
 
     pairs = (tables + 1) // 2
     proj = jnp.transpose(proj_weight, (2, 0, 1))
@@ -211,12 +198,11 @@
     near = lax.ppermute(own, "x", side)
     next_ = lax.ppermute(own, "x", back)
     own_o = lax.ppermute(own, "rep", SWAP)
-    near, own_o = lax.optimization_barrier((near, own_o))
     far_a = lax.ppermute(near[:half], "x", back)
     far_b = lax.ppermute(next_[half:], "x", side)
     near_o = lax.ppermute(near, "rep", SWAP)
     next_o = lax.ppermute(next_, "rep", SWAP)
-    far, emb_y = lax.optimization_barrier((jnp.concatenate([far_a, far_b], axis=0), emb_y))
+    far = jnp.concatenate([far_a, far_b], axis=0)
     far_o = lax.ppermute(far, "rep", SWAP)
     mine = [own, near, far_a, far_b, next_]
     other = [own_o, near_o, far_o, next_o]
@@ -227,7 +213,7 @@
         [emb, emb_y] + mine + other,
         [pltpu.VMEM((2, 768, 128), F32)],
         limit=SOME,
-        flops=2 * 25 * 64 * 128 * 512,
+        flops=25_000_000_000,
         size=5 << 20,
     )
     recv = lax.all_to_all(chunks, ("yl",) + TAB, 0, 0, tiled=True)
@@ -237,7 +223,7 @@
         (jax.ShapeDtypeStruct((2, 400, 800), BF16), jax.ShapeDtypeStruct((192, 800), BF16)),
         [small],
         [pltpu.VMEM((400, 896), F32), pltpu.VMEM((192, 800), F32)],
-        flops=15_000_000_000,
+        flops=0,
         size=4 << 20,
         limit=SOME,
     )
@@ -267,17 +253,13 @@
     tiles = jnp.transpose(share.reshape(4, 16, 8, 128), (2, 0, 1, 3)).reshape(32, 16, 128)
     parts = lax.all_to_all(tiles, TAB, 0, 0, tiled=True)
     whole = jnp.sum(parts.astype(F32), axis=0).astype(BF16)
-    spread = lax.all_to_all(jnp.broadcast_to(whole[None], (32, 16, 128)), TAB, 0, 0, tiled=True)
-    swapped = lax.ppermute(spread, "rep", SWAP)
+    spread = lax.all_to_all(jnp.broadcast_to(whole[None], (64, 16, 128)), ("rep",) + TAB, 0, 0, tiled=True)
 
     def rows_of(blocks):
         wide = jnp.transpose(blocks.reshape(8, 4, 16, 128), (1, 2, 0, 3)).reshape(64, 1024)
         return wide[:50, :800].astype(F32)
 
-    grad_a, grad_b = rows_of(spread), rows_of(swapped)
-    first = lax.axis_index("rep") == 0
-    grad_fm = jnp.where(first, grad_a, grad_b)
-    grad_lcb = jnp.where(first, grad_b, grad_a)
+    grad_fm, grad_lcb = rows_of(spread[:32]), rows_of(spread[32:])
     return fm_out.T[None], lcb_out.T[None], grad_fm, grad_lcb
 
 

time: 153 us -> 147 us (0.961)
  waiting for transfers between devices: 24 us -> 14.3 us
  blocking collectives: 46.1 us -> 51.2 us
  starting transfers between devices: 55.6 us -> 53.2 us
    ppermute x1 -> x0, starting transfers between devices: 6.32 us -> none  [per_device(): swapped = lax.ppermute(spread, 'rep', SWAP)]
    all_to_all x1, blocking collectives: 14.4 us -> 20.6 us  [per_device(): lax.all_to_all(jnp.broadcast_to(whole[None], (64, 16, 128)), ('rep',) + T...]
    ppermute x1, waiting for transfers between devices: 5.92 us -> 0.01 us  [per_device(): next_ = lax.ppermute(own, 'x', back)]
    all_to_all x1, waiting for transfers between devices: 12.8 us -> 9.26 us  [per_device(): recv = lax.all_to_all(chunks, ('yl',) + TAB, 0, 0, tiled=True)]
    ppermute x1, starting transfers between devices: 5.47 us -> 7.89 us  [per_device(): own_o = lax.ppermute(own, 'rep', SWAP)]
    ppermute x1, starting transfers between devices: 4.74 us -> 7.11 us  [per_device(): got = lax.ppermute(send, 'rep', SWAP)]
    ppermute x1, starting transfers between devices: 1.92 us -> 3.72 us  [per_device(): next_ = lax.ppermute(own, 'x', back)]
    ppermute x1, starting transfers between devices: 3.7 us -> 1.92 us  [per_device(): far_o = lax.ppermute(far, 'rep', SWAP)]
  transfers between devices with their start and end apart: 13 -> 12, of which waited for: 6 -> 4; matrix products, arithmetic and copies ran while one was open for 0% -> 0% of each run, Pallas kernels for 4% -> 3%
where the time goes in v10:
time: 147 us; the launch traced here: 146 us
  starting transfers between devices  53.2 us (36%)
  blocking collectives  51.2 us (35%)
  waiting for transfers between devices  14.3 us (10%)
  between operations  14.3 us (10%)
  Pallas kernels  8.96 us (6%)
  local copies, waits for them, and re-layouts  2.94 us (2%)
    all_to_all x1, blocking collectives, per_device(): lax.all_to_all(jnp.broadcast_to(whole[None], (64, 16, 128)), ('rep',) + T...  20.6 us
    all_to_all x1, blocking collectives, per_device(): shares = lax.all_to_all(pair, TP, 0, 0, tiled=True)  15.4 us
    all_to_all x1, blocking collectives, per_device(): parts = lax.all_to_all(tiles, TAB, 0, 0, tiled=True)  15.1 us
    all_to_all x1, starting transfers between devices, per_device(): recv = lax.all_to_all(chunks, ('yl',) + TAB, 0, 0, tiled=True)  14.3 us
    all_to_all x1, waiting for transfers between devices, per_device(): recv = lax.all_to_all(chunks, ('yl',) + TAB, 0, 0, tiled=True)  9.26 us
    ppermute x1, starting transfers between devices, per_device(): own_o = lax.ppermute(own, 'rep', SWAP)  7.89 us
    ppermute x1, starting transfers between devices, per_device(): got = lax.ppermute(send, 'rep', SWAP)  7.11 us
    pallas_call x3, Pallas kernels, call(): pl.pallas_call(kernel, out_shape=outs, in_specs=[VM] * len(ins), out_spec...  6.25 us
  transfers between devices with their start and end apart: 12, of which 4 were waited for; matrix products, arithmetic and copies ran while one was open for 0% of the time, Pallas kernels for 3%

profile of v10, /device:TPU:1, one launch (start us, length us, event | category | flops | bytes accessed | tf_op | source)
XLA Modules:
  0.0 146.1 jit_solution(13661972235703213092)
XLA Ops:
  7.2 0.0 copy-start.1
  7.2 0.0 all-gather.3.cloned.1.call-start
  7.2 2.7 %shard_map.111 = (bf16[13,24,512]{2,1,0:T(8,128)(2,1)}, bf16[9,56,128]{2,1,0:T(8,128)(2,1)}) custom-call(s32[25]{0:T(128)} %steps_ref.1, bf16[12,25,512]{2,1,0:T(8,128)(2,1)} %bitcast.54, bf16[50,800]{1,0:T(8,128)(2,1)} %fm_any.1, bf16[50,800]{1,0:T(8,128)(2,1)} %lcb_any.1, bf16[192,100]{1,0:T(8,128)(2,1)} %bitcast.55), custom_call_target="tpu_custom_call" | custom-call | flops 1048576 | bytes 2097152 | tf_op jit(solution)/shard_map/pallas_call | solution.py:176
  9.9 3.9 %collective-permute-start.1 = (bf16[13,24,512]{2,1,0:T(8,128)(2,1)}, bf16[13,24,512]{2,1,0:T(8,128)(2,1)S(1)}, u32[]{:S(2)}, u32[]{:S(2)}) collective-permute-start(bf16[13,24,512]{2,1,0:T(8,128)(2,1)} %get-tuple-element.12.rest_0_), channel_id=1, source_target_pairs={{0,1},{1,0},{2,3},{3,2},{4,5},{5,4},{6,7},{7,6},{8,9},{9,8},{10,11... | collective-permute-start | bytes 958472 | tf_op jit(solution)/shard_map/ppermute | solution.py:198
  13.9 3.7 %collective-permute-start.3 = (bf16[13,24,512]{2,1,0:T(8,128)(2,1)}, bf16[13,24,512]{2,1,0:T(8,128)(2,1)S(1)}, u32[]{:S(2)}, u32[]{:S(2)}) collective-permute-start(bf16[13,24,512]{2,1,0:T(8,128)(2,1)} %get-tuple-element.12.rest_0_), channel_id=1, source_target_pairs={{0,3},{1,2},{2,1},{3,0},{4,7},{5,6},{6,5},{7,4},{8,11},{9,10},{10,... | collective-permute-start | bytes 958472 | tf_op jit(solution)/shard_map/ppermute | solution.py:199
  17.6 3.2 %collective-permute-start = (bf16[25,32,512]{2,1,0:T(8,128)(2,1)}, bf16[25,32,512]{2,1,0:T(8,128)(2,1)S(1)}, u32[]{:S(2)}, u32[]{:S(2)}) collective-permute-start(bf16[25,32,512]{2,1,0:T(8,128)(2,1)} %bitcast.42), channel_id=1, source_target_pairs={{0,4},{4,0},{1,5},{5,1},{2,6},{6,2},{3,7},{7,3},{8,12},{12,8},{9,1... | collective-permute-start | bytes 2457608 | tf_op jit(solution)/shard_map/ppermute | solution.py:172
  20.9 0.0 all-gather.3.cloned.1.call-update
  20.9 0.0 collective-permute-done.1.rest_1_
  20.9 4.8 %collective-permute-start.2 = (bf16[7,24,512]{2,1,0:T(8,128)(2,1)S(1)}, bf16[7,24,512]{2,1,0:T(8,128)(2,1)S(1)}, u32[]{:S(2)}, u32[]{:S(2)}) collective-permute-start(bf16[7,24,512]{2,1,0:T(8,128)(2,1)S(1)} %slice.24), channel_id=1, source_target_pairs={{0,3},{1,2},{2,1},{3,0},{4,7},{5,6},{6,5},{7,4},{8,11},{9,10},{10,... | collective-permute-start | bytes 516104 | tf_op jit(solution)/shard_map/ppermute | solution.py:201
  25.7 0.0 collective-permute-done.3.rest_4_
  25.7 1.9 %collective-permute-start.4 = (bf16[6,24,512]{2,1,0:T(8,128)(2,1)S(1)}, bf16[6,24,512]{2,1,0:T(8,128)(2,1)S(1)}, u32[]{:S(2)}, u32[]{:S(2)}) collective-permute-start(bf16[6,24,512]{2,1,0:T(8,128)(2,1)S(1)} %slice.25), channel_id=1, source_target_pairs={{0,1},{1,0},{2,3},{3,2},{4,5},{5,4},{6,7},{7,6},{8,9},{9,8},{10,11... | collective-permute-start | bytes 442376 | tf_op jit(solution)/shard_map/ppermute | solution.py:202
  27.7 7.9 %collective-permute-start.5 = (bf16[13,24,512]{2,1,0:T(8,128)(2,1)}, bf16[13,24,512]{2,1,0:T(8,128)(2,1)S(1)}, u32[]{:S(2)}, u32[]{:S(2)}) collective-permute-start(bf16[13,24,512]{2,1,0:T(8,128)(2,1)} %get-tuple-element.12.rest_0_), channel_id=1, source_target_pairs={{0,256},{256,0},{1,257},{257,1},{2,258},{258,2},{3,259},{259,3},{4... | collective-permute-start | bytes 958472 | tf_op jit(solution)/shard_map/ppermute | solution.py:200
  35.5 1.9 %collective-permute-start.6 = (bf16[13,24,512]{2,1,0:T(8,128)(2,1)S(1)}, bf16[13,24,512]{2,1,0:T(8,128)(2,1)S(1)}, u32[]{:S(2)}, u32[]{:S(2)}) collective-permute-start(bf16[13,24,512]{2,1,0:T(8,128)(2,1)S(1)} %collective-permute-done.1.rest_1_), channel_id=1, source_target_pairs={{0,256},{256,0},{1,257},{257,1},{2,258},{258,2},{3,259},{259,3},{4... | collective-permute-start | bytes 958472 | tf_op jit(solution)/shard_map/ppermute | solution.py:203
  37.5 0.0 collective-permute-done.4.rest_3_
  37.5 2.4 %collective-permute-start.8 = (bf16[13,24,512]{2,1,0:T(8,128)(2,1)S(1)}, bf16[13,24,512]{2,1,0:T(8,128)(2,1)S(1)}, u32[]{:S(2)}, u32[]{:S(2)}) collective-permute-start(bf16[13,24,512]{2,1,0:T(8,128)(2,1)S(1)} %collective-permute-done.3.rest_4_), channel_id=1, source_target_pairs={{0,256},{256,0},{1,257},{257,1},{2,258},{258,2},{3,259},{259,3},{4... | collective-permute-start | bytes 958472 | tf_op jit(solution)/shard_map/ppermute | solution.py:204
  39.9 0.0 collective-permute-done.2.rest_2_
  40.0 1.9 %collective-permute-start.7 = (bf16[13,24,512]{2,1,0:T(8,128)(2,1)S(1)}, bf16[13,24,512]{2,1,0:T(8,128)(2,1)S(1)}, u32[]{:S(2)}, u32[]{:S(2)}) collective-permute-start(bf16[13,24,512]{2,1,0:T(8,128)(2,1)S(1)} %pad_maximum_fusion), channel_id=1, source_target_pairs={{0,256},{256,0},{1,257},{257,1},{2,258},{258,2},{3,259},{259,3},{4... | collective-permute-start | bytes 958472 | tf_op jit(solution)/shard_map/ppermute | solution.py:206
  41.9 0.0 collective-permute-done.5.rest_5_
  41.9 0.0 collective-permute-done.6.rest_6_
  41.9 0.0 collective-permute-done.8.rest_8_
  41.9 1.6 %collective-permute-done.7.rest_7_ = bf16[13,24,512]{2,1,0:T(8,128)(2,1)S(1)} collective-permute-done((bf16[13,24,512]{2,1,0:T(8,128)(2,1)S(1)}, bf16[13,24,512]{2,1,0:T(8,128)(2,1)S(1)}, u32[]{:S(2)}, u32[]{:S(2)}) %collective-permute-start.7) | collective-permute-done | bytes 319520 | tf_op jit(solution)/shard_map/ppermute | solution.py:206
  43.5 0.0 collective-permute-done.emb_y_ref
  43.5 0.0 copy-done.1
  43.5 0.0 copy-start.2
  43.5 1.0 copy-done.2
  44.5 3.1 %shard_map.112 = bf16[64,24,128]{2,1,0:T(8,128)(2,1)} custom-call(bf16[25,32,512]{2,1,0:T(8,128)(2,1)S(1)} %bitcast.43, bf16[25,32,512]{2,1,0:T(8,128)(2,1)S(1)} %collective-permute-done.emb_y_ref, bf16[13,24,512]{2,1,0:T(8,128)(2,1)S(1)} %copy-done.2, bf16[13,24,512]{2,1,0:T(8,128)(2,1)S(1)} %collective-permute-done.1.rest_1_, ...), custom_call_target="tpu_custom_call" | custom-call | flops 24999999488 | bytes 5242880 | tf_op jit(solution)/shard_map/pallas_call | solution.py:24
  47.6 0.0 copy-start.3
  47.6 0.0 copy-start.4
  47.6 14.3 %all-to-all-start = ((bf16[64,24,128]{2,1,0:T(8,128)(2,1)}), bf16[64,24,128]{2,1,0:T(8,128)(2,1)S(1)}, u32[]{:S(2)}, u32[]{:S(2)}) async-start(bf16[64,24,128]{2,1,0:T(8,128)(2,1)} %shard_map.112), calls=%async_computation | async-start | bytes 786432 | tf_op jit(solution)/shard_map/all_to_all | solution.py:219
  61.9 1.6 %all-gather.3.cloned.1.call-done = bf16[144,56,128]{2,1,0:T(8,128)(2,1)} async-done(((bf16[9,56,128]{2,1,0:T(8,128)(2,1)}), bf16[144,56,128]{2,1,0:T(8,128)(2,1)}) %all-gather.3.cloned.1.call-update) | async-done | bytes 2064400 | tf_op jit(solution)/shard_map/all_gather | solution.py:194
  63.5 0.0 copy-start
  63.5 1.6 %copy-done = bf16[144,56,128]{2,1,0:T(8,128)(2,1)S(1)} copy-done((bf16[144,56,128]{2,1,0:T(8,128)(2,1)S(1)}, bf16[144,56,128]{2,1,0:T(8,128)(2,1)}, u32[]{:S(2)}) %copy-start) | copy-done | bytes 2064408
  65.1 0.6 shard_map.113
  65.7 9.3 %all-to-all-done.recv_ref = bf16[64,24,128]{2,1,0:T(8,128)(2,1)S(1)} async-done(((bf16[64,24,128]{2,1,0:T(8,128)(2,1)}), bf16[64,24,128]{2,1,0:T(8,128)(2,1)S(1)}, u32[]{:S(2)}, u32[]{:S(2)}) %all-to-all-start) | async-done | bytes 393248 | tf_op jit(solution)/shard_map/all_to_all | solution.py:219
  74.9 0.0 copy-done.3
  74.9 0.0 copy-done.4
  74.9 2.5 %shard_map.114 = (bf16[192,400]{1,0:T(8,128)(2,1)}, bf16[192,400]{1,0:T(8,128)(2,1)}, bf16[8,56,800]{2,1,0:T(8,128)(2,1)S(1)}, bf16[8,56,800]{2,1,0:T(8,128)(2,1)S(1)}) custom-call(bf16[64,24,128]{2,1,0:T(8,128)(2,1)S(1)} %all-to-all-done.recv_ref, bf16[2,400,800]{2,1,0:T(8,128)(2,1)S(1)} %get-tuple-element.14.weight_ref, ...), custom_call_target="tpu_custom_call" | custom-call | flops 700000000 | bytes 5242880 | tf_op jit(solution)/shard_map/pallas_call | solution.py:24
  77.5 7.1 %collective-permute-start.9 = (bf16[8,56,800]{2,1,0:T(8,128)(2,1)S(1)}, bf16[8,56,800]{2,1,0:T(8,128)(2,1)S(1)}, u32[]{:S(2)}, u32[]{:S(2)}) collective-permute-start(bf16[8,56,800]{2,1,0:T(8,128)(2,1)S(1)} %get-tuple-element.19), channel_id=1, source_target_pairs={{0,256},{256,0},{1,257},{257,1},{2,258},{258,2},{3,259},{259,3},{4... | collective-permute-start | bytes 2150408 | tf_op jit(solution)/shard_map/ppermute | solution.py:248
  84.6 1.9 %collective-permute-done.9 = bf16[8,56,800]{2,1,0:T(8,128)(2,1)S(1)} collective-permute-done((bf16[8,56,800]{2,1,0:T(8,128)(2,1)S(1)}, bf16[8,56,800]{2,1,0:T(8,128)(2,1)S(1)}, u32[]{:S(2)}, u32[]{:S(2)}) %collective-permute-start.9) | collective-permute-done | bytes 716832 | tf_op jit(solution)/shard_map/ppermute | solution.py:248
  86.5 0.2 add_convert_fusion
  86.7 15.4 %all_to_all.20 = bf16[8,56,800]{2,1,0:T(8,128)(2,1)S(1)} all-to-all(bf16[8,56,800]{2,1,0:T(8,128)(2,1)S(1)} %add_convert_fusion), channel_id=1, replica_groups=mesh['rep'=2,'z'=8,'yh'=4,'yl'=2,'x'=4] {'yl','x'}, dimensions={0} | all-to-all | bytes 1433600 | tf_op jit(solution)/shard_map/all_to_all | solution.py:250
  102.2 0.1 reduce_sum.24
  102.4 15.1 %all_to_all.21 = bf16[32,16,128]{2,1,0:T(8,128)(2,1)S(1)} all-to-all(bf16[32,16,128]{2,1,0:T(8,128)(2,1)S(1)} %bitcast.47), channel_id=1, replica_groups=mesh['rep'=2,'z'=8,'yh'=4,'yl'=2,'x'=4] {'z','yh'}, dimensions={0} | all-to-all | bytes 262144 | tf_op jit(solution)/shard_map/all_to_all | solution.py:254
  117.6 20.6 %all_to_all.22 = bf16[64,16,128]{2,1,0:T(8,128)(2,1)S(1)} all-to-all(bf16[64,16,128]{2,1,0:T(8,128)(2,1)S(1)} %broadcast_in_dim.14), channel_id=1, replica_groups=mesh['rep'=2,'z'=8,'yh'=4,'yl'=2,'x'=4] {'rep','z','yh'}, dimensions={0} | all-to-all | bytes 524288 | tf_op jit(solution)/shard_map/all_to_all | solution.py:256
  138.2 0.1 copy.17
  138.3 0.1 copy.16
  138.5 0.8 slice_convert_fusion
  (12 shorter events, 0.3 us)
Async XLA Ops:
  7.2 36.3 %copy-start.1 = (bf16[32,25,512]{2,0,1:T(8,128)(2,1)S(1)}, bf16[32,25,512]{2,0,1:T(8,128)(2,1)}, u32[]{:S(2)}) copy-start(bf16[32,25,512]{2,0,1:T(8,128)(2,1)} %param.8) | copy-start | bytes 2457604
  7.2 56.3 %all-gather.3.cloned.1.call-start = ((), (), s32[]{:S(2)}) async-start(), calls=%async_computation.4 | async-start | bytes 2193408 | tf_op jit(solution)/shard_map/all_gather | solution.py:194
  9.9 10.9 %collective-permute-start.1 = (bf16[13,24,512]{2,1,0:T(8,128)(2,1)}, bf16[13,24,512]{2,1,0:T(8,128)(2,1)S(1)}, u32[]{:S(2)}, u32[]{:S(2)}) collective-permute-start(bf16[13,24,512]{2,1,0:T(8,128)(2,1)} %get-tuple-element.12.rest_0_), channel_id=1, source_target_pairs={{0,1},{1,0},{2,3},{3,2},{4,5},{5,4},{6,7},{7,6},{8,9},{9,8},{10,11... | collective-permute-start | bytes 958472 | tf_op jit(solution)/shard_map/ppermute | solution.py:198
  13.9 11.8 %collective-permute-start.3 = (bf16[13,24,512]{2,1,0:T(8,128)(2,1)}, bf16[13,24,512]{2,1,0:T(8,128)(2,1)S(1)}, u32[]{:S(2)}, u32[]{:S(2)}) collective-permute-start(bf16[13,24,512]{2,1,0:T(8,128)(2,1)} %get-tuple-element.12.rest_0_), channel_id=1, source_target_pairs={{0,3},{1,2},{2,1},{3,0},{4,7},{5,6},{6,5},{7,4},{8,11},{9,10},{10,... | collective-permute-start | bytes 958472 | tf_op jit(solution)/shard_map/ppermute | solution.py:199
  17.6 25.8 %collective-permute-start = (bf16[25,32,512]{2,1,0:T(8,128)(2,1)}, bf16[25,32,512]{2,1,0:T(8,128)(2,1)S(1)}, u32[]{:S(2)}, u32[]{:S(2)}) collective-permute-start(bf16[25,32,512]{2,1,0:T(8,128)(2,1)} %bitcast.42), channel_id=1, source_target_pairs={{0,4},{4,0},{1,5},{5,1},{2,6},{6,2},{3,7},{7,3},{8,12},{12,8},{9,1... | collective-permute-start | bytes 2457608 | tf_op jit(solution)/shard_map/ppermute | solution.py:172
  20.9 19.0 %collective-permute-start.2 = (bf16[7,24,512]{2,1,0:T(8,128)(2,1)S(1)}, bf16[7,24,512]{2,1,0:T(8,128)(2,1)S(1)}, u32[]{:S(2)}, u32[]{:S(2)}) collective-permute-start(bf16[7,24,512]{2,1,0:T(8,128)(2,1)S(1)} %slice.24), channel_id=1, source_target_pairs={{0,3},{1,2},{2,1},{3,0},{4,7},{5,6},{6,5},{7,4},{8,11},{9,10},{10,... | collective-permute-start | bytes 516104 | tf_op jit(solution)/shard_map/ppermute | solution.py:201
  25.7 11.8 %collective-permute-start.4 = (bf16[6,24,512]{2,1,0:T(8,128)(2,1)S(1)}, bf16[6,24,512]{2,1,0:T(8,128)(2,1)S(1)}, u32[]{:S(2)}, u32[]{:S(2)}) collective-permute-start(bf16[6,24,512]{2,1,0:T(8,128)(2,1)S(1)} %slice.25), channel_id=1, source_target_pairs={{0,1},{1,0},{2,3},{3,2},{4,5},{5,4},{6,7},{7,6},{8,9},{9,8},{10,11... | collective-permute-start | bytes 442376 | tf_op jit(solution)/shard_map/ppermute | solution.py:202
  27.7 14.2 %collective-permute-start.5 = (bf16[13,24,512]{2,1,0:T(8,128)(2,1)}, bf16[13,24,512]{2,1,0:T(8,128)(2,1)S(1)}, u32[]{:S(2)}, u32[]{:S(2)}) collective-permute-start(bf16[13,24,512]{2,1,0:T(8,128)(2,1)} %get-tuple-element.12.rest_0_), channel_id=1, source_target_pairs={{0,256},{256,0},{1,257},{257,1},{2,258},{258,2},{3,259},{259,3},{4... | collective-permute-start | bytes 958472 | tf_op jit(solution)/shard_map/ppermute | solution.py:200
  35.5 6.3 %collective-permute-start.6 = (bf16[13,24,512]{2,1,0:T(8,128)(2,1)S(1)}, bf16[13,24,512]{2,1,0:T(8,128)(2,1)S(1)}, u32[]{:S(2)}, u32[]{:S(2)}) collective-permute-start(bf16[13,24,512]{2,1,0:T(8,128)(2,1)S(1)} %collective-permute-done.1.rest_1_), channel_id=1, source_target_pairs={{0,256},{256,0},{1,257},{257,1},{2,258},{258,2},{3,259},{259,3},{4... | collective-permute-start | bytes 958472 | tf_op jit(solution)/shard_map/ppermute | solution.py:203
  37.5 4.4 %collective-permute-start.8 = (bf16[13,24,512]{2,1,0:T(8,128)(2,1)S(1)}, bf16[13,24,512]{2,1,0:T(8,128)(2,1)S(1)}, u32[]{:S(2)}, u32[]{:S(2)}) collective-permute-start(bf16[13,24,512]{2,1,0:T(8,128)(2,1)S(1)} %collective-permute-done.3.rest_4_), channel_id=1, source_target_pairs={{0,256},{256,0},{1,257},{257,1},{2,258},{258,2},{3,259},{259,3},{4... | collective-permute-start | bytes 958472 | tf_op jit(solution)/shard_map/ppermute | solution.py:204
  40.0 3.5 %collective-permute-start.7 = (bf16[13,24,512]{2,1,0:T(8,128)(2,1)S(1)}, bf16[13,24,512]{2,1,0:T(8,128)(2,1)S(1)}, u32[]{:S(2)}, u32[]{:S(2)}) collective-permute-start(bf16[13,24,512]{2,1,0:T(8,128)(2,1)S(1)} %pad_maximum_fusion), channel_id=1, source_target_pairs={{0,256},{256,0},{1,257},{257,1},{2,258},{258,2},{3,259},{259,3},{4... | collective-permute-start | bytes 958472 | tf_op jit(solution)/shard_map/ppermute | solution.py:206
  43.5 1.0 copy-start.2
  47.6 27.3 %copy-start.3 = (bf16[1,400,192]{1,2,0:T(8,128)(2,1)S(1)}, bf16[1,400,192]{1,2,0:T(8,128)(2,1)}, u32[]{:S(2)}) copy-start(bf16[1,400,192]{1,2,0:T(8,128)(2,1)} %param.14) | copy-start | bytes 460804
  47.6 27.3 %copy-start.4 = (bf16[1,400,192]{1,2,0:T(8,128)(2,1)S(1)}, bf16[1,400,192]{1,2,0:T(8,128)(2,1)}, u32[]{:S(2)}) copy-start(bf16[1,400,192]{1,2,0:T(8,128)(2,1)} %param.15) | copy-start | bytes 460804
  47.6 27.3 %all-to-all-start = ((bf16[64,24,128]{2,1,0:T(8,128)(2,1)}), bf16[64,24,128]{2,1,0:T(8,128)(2,1)S(1)}, u32[]{:S(2)}, u32[]{:S(2)}) async-start(bf16[64,24,128]{2,1,0:T(8,128)(2,1)} %shard_map.112), calls=%async_computation | async-start | bytes 786432 | tf_op jit(solution)/shard_map/all_to_all | solution.py:219
  63.5 1.6 %copy-start = (bf16[144,56,128]{2,1,0:T(8,128)(2,1)S(1)}, bf16[144,56,128]{2,1,0:T(8,128)(2,1)}, u32[]{:S(2)}) copy-start(bf16[144,56,128]{2,1,0:T(8,128)(2,1)} %all-gather.3.cloned.1.call-done) | copy-start | bytes 6193156
  77.5 9.0 %collective-permute-start.9 = (bf16[8,56,800]{2,1,0:T(8,128)(2,1)S(1)}, bf16[8,56,800]{2,1,0:T(8,128)(2,1)S(1)}, u32[]{:S(2)}, u32[]{:S(2)}) collective-permute-start(bf16[8,56,800]{2,1,0:T(8,128)(2,1)S(1)} %get-tuple-element.19), channel_id=1, source_target_pairs={{0,256},{256,0},{1,257},{257,1},{2,258},{258,2},{3,259},{259,3},{4... | collective-permute-start | bytes 2150408 | tf_op jit(solution)/shard_map/ppermute | solution.py:248
Sparse Core Ops, SparseCore 0:
  21.0 42.4 all-gather.2

commit v11 on v10

--- a/solution.py
+++ b/solution.py
@@ -80,9 +80,10 @@
 
 
 def unpack_kernel(small_ref, branch_ref, mix_ref, wide_ref, mixw_ref):
+    mine = lax.axis_index("yl")
     for k in range(2):
         for i in range(8):
-            piece = small_ref.at[8 * k + i]
+            piece = small_ref.at[4 * k + i % 4, jnp.bitwise_xor(mine, i // 4)]
             for j in range(7):
                 wide_ref[50 * i : 50 * i + 50, 128 * j : 128 * j + 128] = piece[j][:50].astype(F32)
             for j in range(2):
@@ -191,7 +192,8 @@
         ],
         cost_estimate=pl.CostEstimate(flops=1 << 20, bytes_accessed=2 << 20, transcendentals=0),
     )(width_steps, proj, fm_weight, lcb_weight, mix_weight.T)
-    small = lax.all_gather(packed, ("rep",) + TP)
+    pair = jnp.stack([packed, lax.ppermute(packed, "yl", SWAP)])
+    small = lax.all_gather(pair, ("rep", "x"))
 
     side, back = [(i, i ^ 1) for i in range(4)], [(i, i ^ 3) for i in range(4)]
     half = (pairs + 1) // 2
@@ -213,7 +215,7 @@
         [emb, emb_y] + mine + other,
         [pltpu.VMEM((2, 768, 128), F32)],
         limit=SOME,
-        flops=25_000_000_000,
+        flops=23_000_000_000,
         size=5 << 20,
     )
     recv = lax.all_to_all(chunks, ("yl",) + TAB, 0, 0, tiled=True)

time: 147 us -> 148 us (level)
  starting transfers between devices: 53.2 us -> 50.3 us
  blocking collectives: 51.2 us -> 53.1 us
  other arithmetic: 1.17 us -> 2.8 us
  waiting for transfers between devices: 14.3 us -> 15.9 us
    ppermute x0 -> x1, starting transfers between devices: none -> 3.2 us  [per_device(): pair = jnp.stack([packed, lax.ppermute(packed, 'yl', SWAP)])]
    all_to_all x1, waiting for transfers between devices: 9.26 us -> 12.4 us  [per_device(): recv = lax.all_to_all(chunks, ('yl',) + TAB, 0, 0, tiled=True)]
    ppermute x1, starting transfers between devices: 7.11 us -> 5.06 us  [per_device(): got = lax.ppermute(send, 'rep', SWAP)]
    ppermute x1, starting transfers between devices: 4.78 us -> 2.77 us  [per_device(): far_a = lax.ppermute(near[:half], 'x', back)]
    all_to_all x1, starting transfers between devices: 14.3 us -> 12.5 us  [per_device(): recv = lax.all_to_all(chunks, ('yl',) + TAB, 0, 0, tiled=True)]
    another operation x0 -> x1, other arithmetic: none -> 1.63 us  [per_device(): pair = jnp.stack([packed, lax.ppermute(packed, 'yl', SWAP)])]
    all_gather x1, waiting for transfers between devices: 1.57 us -> 0.02 us  [per_device(): small = lax.all_gather(pair, ('rep', 'x'))]
  transfers between devices with their start and end apart: 12 -> 13, of which waited for: 4 -> 3; matrix products, arithmetic and copies ran while one was open for 0% -> 1% of each run, Pallas kernels for 3% -> 3%
where the time goes in v11:
time: 148 us; the launch traced here: 147 us
  blocking collectives  53.1 us (36%)
  starting transfers between devices  50.3 us (34%)
  waiting for transfers between devices  15.9 us (11%)
  between operations  14.4 us (10%)
  Pallas kernels  8.97 us (6%)
  other arithmetic  2.8 us (2%)
  local copies, waits for them, and re-layouts  1.96 us (1%)
    all_to_all x1, blocking collectives, per_device(): lax.all_to_all(jnp.broadcast_to(whole[None], (64, 16, 128)), ('rep',) + T...  21.1 us
    all_to_all x1, blocking collectives, per_device(): shares = lax.all_to_all(pair, TP, 0, 0, tiled=True)  16.2 us
    all_to_all x1, blocking collectives, per_device(): parts = lax.all_to_all(tiles, TAB, 0, 0, tiled=True)  15.8 us
    all_to_all x1, starting transfers between devices, per_device(): recv = lax.all_to_all(chunks, ('yl',) + TAB, 0, 0, tiled=True)  12.5 us
    all_to_all x1, waiting for transfers between devices, per_device(): recv = lax.all_to_all(chunks, ('yl',) + TAB, 0, 0, tiled=True)  12.4 us
    ppermute x1, starting transfers between devices, per_device(): own_o = lax.ppermute(own, 'rep', SWAP)  8.67 us
    pallas_call x3, Pallas kernels, call(): pl.pallas_call(kernel, out_shape=outs, in_specs=[VM] * len(ins), out_spec...  6.25 us
    ppermute x1, starting transfers between devices, per_device(): got = lax.ppermute(send, 'rep', SWAP)  5.06 us
  transfers between devices with their start and end apart: 13, of which 3 were waited for; matrix products, arithmetic and copies ran while one was open for 1% of the time, Pallas kernels for 3%

profile of v11, /device:TPU:1, one launch (start us, length us, event | category | flops | bytes accessed | tf_op | source)
XLA Modules:
  0.0 147.4 jit_solution(17515461141254419188)
XLA Ops:
  7.2 0.0 copy-start.1
  7.2 0.0 all-gather.3.cloned.1.call-start
  7.2 2.7 %shard_map.111 = (bf16[13,24,512]{2,1,0:T(8,128)(2,1)}, bf16[9,56,128]{2,1,0:T(8,128)(2,1)}) custom-call(s32[25]{0:T(128)} %steps_ref.1, bf16[12,25,512]{2,1,0:T(8,128)(2,1)} %bitcast.56, bf16[50,800]{1,0:T(8,128)(2,1)} %fm_any.1, bf16[50,800]{1,0:T(8,128)(2,1)} %lcb_any.1, bf16[192,100]{1,0:T(8,128)(2,1)} %bitcast.59), custom_call_target="tpu_custom_call" | custom-call | flops 1048576 | bytes 2097152 | tf_op jit(solution)/shard_map/pallas_call | solution.py:177
  9.9 0.0 copy-start.2
  10.0 4.1 %collective-permute-start.1 = (bf16[13,24,512]{2,1,0:T(8,128)(2,1)}, bf16[13,24,512]{2,1,0:T(8,128)(2,1)S(1)}, u32[]{:S(2)}, u32[]{:S(2)}) collective-permute-start(bf16[13,24,512]{2,1,0:T(8,128)(2,1)} %get-tuple-element.12.rest_0_), channel_id=1, source_target_pairs={{0,1},{1,0},{2,3},{3,2},{4,5},{5,4},{6,7},{7,6},{8,9},{9,8},{10,11... | collective-permute-start | bytes 958472 | tf_op jit(solution)/shard_map/ppermute | solution.py:200
  14.0 3.2 %collective-permute-start.9 = (bf16[9,56,128]{2,1,0:T(8,128)(2,1)}, bf16[9,56,128]{2,1,0:T(8,128)(2,1)S(1)}, u32[]{:S(2)}, u32[]{:S(2)}) collective-permute-start(bf16[9,56,128]{2,1,0:T(8,128)(2,1)} %get-tuple-element.13), channel_id=1, source_target_pairs={{0,4},{4,0},{1,5},{5,1},{2,6},{6,2},{3,7},{7,3},{8,12},{12,8},{9,1... | collective-permute-start | bytes 387080 | tf_op jit(solution)/shard_map/ppermute | solution.py:195
  17.3 3.7 %collective-permute-start.3 = (bf16[13,24,512]{2,1,0:T(8,128)(2,1)}, bf16[13,24,512]{2,1,0:T(8,128)(2,1)S(1)}, u32[]{:S(2)}, u32[]{:S(2)}) collective-permute-start(bf16[13,24,512]{2,1,0:T(8,128)(2,1)} %get-tuple-element.12.rest_0_), channel_id=1, source_target_pairs={{0,3},{1,2},{2,1},{3,0},{4,7},{5,6},{6,5},{7,4},{8,11},{9,10},{10,... | collective-permute-start | bytes 958472 | tf_op jit(solution)/shard_map/ppermute | solution.py:201
  21.0 2.1 %collective-permute-start = (bf16[25,32,512]{2,1,0:T(8,128)(2,1)}, bf16[25,32,512]{2,1,0:T(8,128)(2,1)S(1)}, u32[]{:S(2)}, u32[]{:S(2)}) collective-permute-start(bf16[25,32,512]{2,1,0:T(8,128)(2,1)} %bitcast.44), channel_id=1, source_target_pairs={{0,4},{4,0},{1,5},{5,1},{2,6},{6,2},{3,7},{7,3},{8,12},{12,8},{9,1... | collective-permute-start | bytes 2457608 | tf_op jit(solution)/shard_map/ppermute | solution.py:173
  23.1 0.0 collective-permute-done.9
  23.1 1.6 %pad_maximum_fusion.1 = bf16[2,9,56,128]{3,2,1,0:T(8,128)(2,1)} fusion(bf16[1,9,56,128]{3,2,1,0:T(8,128)(2,1)S(1)} %bitcast.58, bf16[1,9,56,128]{3,2,1,0:T(8,128)(2,1)} %bitcast.57), kind=kLoop, calls=%fused_computation.2 | loop fusion | flops 129024 | bytes 516096 | tf_op jit(solution)/shard_map/stack | solution.py:195
  24.7 0.0 all-gather.3.cloned.1.call-update
  24.7 0.0 collective-permute-done.1.rest_1_
  24.8 2.8 %collective-permute-start.2 = (bf16[7,24,512]{2,1,0:T(8,128)(2,1)S(1)}, bf16[7,24,512]{2,1,0:T(8,128)(2,1)S(1)}, u32[]{:S(2)}, u32[]{:S(2)}) collective-permute-start(bf16[7,24,512]{2,1,0:T(8,128)(2,1)S(1)} %slice.24), channel_id=1, source_target_pairs={{0,3},{1,2},{2,1},{3,0},{4,7},{5,6},{6,5},{7,4},{8,11},{9,10},{10,... | collective-permute-start | bytes 516104 | tf_op jit(solution)/shard_map/ppermute | solution.py:203
  27.5 0.0 collective-permute-done.3.rest_4_
  27.6 1.9 %collective-permute-start.4 = (bf16[6,24,512]{2,1,0:T(8,128)(2,1)S(1)}, bf16[6,24,512]{2,1,0:T(8,128)(2,1)S(1)}, u32[]{:S(2)}, u32[]{:S(2)}) collective-permute-start(bf16[6,24,512]{2,1,0:T(8,128)(2,1)S(1)} %slice.25), channel_id=1, source_target_pairs={{0,1},{1,0},{2,3},{3,2},{4,5},{5,4},{6,7},{7,6},{8,9},{9,8},{10,11... | collective-permute-start | bytes 442376 | tf_op jit(solution)/shard_map/ppermute | solution.py:204
  29.5 8.7 %collective-permute-start.5 = (bf16[13,24,512]{2,1,0:T(8,128)(2,1)}, bf16[13,24,512]{2,1,0:T(8,128)(2,1)S(1)}, u32[]{:S(2)}, u32[]{:S(2)}) collective-permute-start(bf16[13,24,512]{2,1,0:T(8,128)(2,1)} %get-tuple-element.12.rest_0_), channel_id=1, source_target_pairs={{0,256},{256,0},{1,257},{257,1},{2,258},{258,2},{3,259},{259,3},{4... | collective-permute-start | bytes 958472 | tf_op jit(solution)/shard_map/ppermute | solution.py:202
  38.2 1.9 %collective-permute-start.6 = (bf16[13,24,512]{2,1,0:T(8,128)(2,1)S(1)}, bf16[13,24,512]{2,1,0:T(8,128)(2,1)S(1)}, u32[]{:S(2)}, u32[]{:S(2)}) collective-permute-start(bf16[13,24,512]{2,1,0:T(8,128)(2,1)S(1)} %collective-permute-done.1.rest_1_), channel_id=1, source_target_pairs={{0,256},{256,0},{1,257},{257,1},{2,258},{258,2},{3,259},{259,3},{4... | collective-permute-start | bytes 958472 | tf_op jit(solution)/shard_map/ppermute | solution.py:205
  40.1 0.0 collective-permute-done.4.rest_3_
  40.1 2.4 %collective-permute-start.8 = (bf16[13,24,512]{2,1,0:T(8,128)(2,1)S(1)}, bf16[13,24,512]{2,1,0:T(8,128)(2,1)S(1)}, u32[]{:S(2)}, u32[]{:S(2)}) collective-permute-start(bf16[13,24,512]{2,1,0:T(8,128)(2,1)S(1)} %collective-permute-done.3.rest_4_), channel_id=1, source_target_pairs={{0,256},{256,0},{1,257},{257,1},{2,258},{258,2},{3,259},{259,3},{4... | collective-permute-start | bytes 958472 | tf_op jit(solution)/shard_map/ppermute | solution.py:206
  42.5 0.0 collective-permute-done.2.rest_2_
  42.6 1.9 %collective-permute-start.7 = (bf16[13,24,512]{2,1,0:T(8,128)(2,1)S(1)}, bf16[13,24,512]{2,1,0:T(8,128)(2,1)S(1)}, u32[]{:S(2)}, u32[]{:S(2)}) collective-permute-start(bf16[13,24,512]{2,1,0:T(8,128)(2,1)S(1)} %pad_maximum_fusion), channel_id=1, source_target_pairs={{0,256},{256,0},{1,257},{257,1},{2,258},{258,2},{3,259},{259,3},{4... | collective-permute-start | bytes 958472 | tf_op jit(solution)/shard_map/ppermute | solution.py:208
  44.5 0.0 collective-permute-done.5.rest_5_
  44.5 0.0 collective-permute-done.6.rest_6_
  44.5 0.0 collective-permute-done.8.rest_8_
  44.5 1.6 %collective-permute-done.7.rest_7_ = bf16[13,24,512]{2,1,0:T(8,128)(2,1)S(1)} collective-permute-done((bf16[13,24,512]{2,1,0:T(8,128)(2,1)S(1)}, bf16[13,24,512]{2,1,0:T(8,128)(2,1)S(1)}, u32[]{:S(2)}, u32[]{:S(2)}) %collective-permute-start.7) | collective-permute-done | bytes 319520 | tf_op jit(solution)/shard_map/ppermute | solution.py:208
  46.1 0.0 collective-permute-done.emb_y_ref
  46.1 0.0 copy-done.1
  46.1 0.0 copy-done.2
  46.1 3.1 %shard_map.112 = bf16[64,24,128]{2,1,0:T(8,128)(2,1)} custom-call(bf16[25,32,512]{2,1,0:T(8,128)(2,1)S(1)} %bitcast.45, bf16[25,32,512]{2,1,0:T(8,128)(2,1)S(1)} %collective-permute-done.emb_y_ref, bf16[13,24,512]{2,1,0:T(8,128)(2,1)S(1)} %copy-done.2, bf16[13,24,512]{2,1,0:T(8,128)(2,1)S(1)} %collective-permute-done.1.rest_1_, ...), custom_call_target="tpu_custom_call" | custom-call | flops 23000000512 | bytes 5242880 | tf_op jit(solution)/shard_map/pallas_call | solution.py:24
  49.2 0.0 copy-start.3
  49.2 0.0 copy-start.4
  49.2 12.5 %all-to-all-start = ((bf16[64,24,128]{2,1,0:T(8,128)(2,1)}), bf16[64,24,128]{2,1,0:T(8,128)(2,1)S(1)}, u32[]{:S(2)}, u32[]{:S(2)}) async-start(bf16[64,24,128]{2,1,0:T(8,128)(2,1)} %shard_map.112), calls=%async_computation | async-start | bytes 786432 | tf_op jit(solution)/shard_map/all_to_all | solution.py:221
  61.7 0.0 all-gather.3.cloned.1.call-done
  61.8 0.0 copy-start
  61.8 1.6 %copy-done = bf16[16,9,56,128]{3,2,1,0:T(8,128)(2,1)S(1)} copy-done((bf16[16,9,56,128]{3,2,1,0:T(8,128)(2,1)S(1)}, bf16[16,9,56,128]{3,2,1,0:T(8,128)(2,1)}, u32[]{:S(2)}) %copy-start) | copy-done | bytes 2064408
  63.4 0.6 shard_map.113
  64.0 12.4 %all-to-all-done.recv_ref = bf16[64,24,128]{2,1,0:T(8,128)(2,1)S(1)} async-done(((bf16[64,24,128]{2,1,0:T(8,128)(2,1)}), bf16[64,24,128]{2,1,0:T(8,128)(2,1)S(1)}, u32[]{:S(2)}, u32[]{:S(2)}) %all-to-all-start) | async-done | bytes 393248 | tf_op jit(solution)/shard_map/all_to_all | solution.py:221
  76.4 0.0 copy-done.3
  76.4 0.0 copy-done.4
  76.4 2.5 %shard_map.114 = (bf16[192,400]{1,0:T(8,128)(2,1)}, bf16[192,400]{1,0:T(8,128)(2,1)}, bf16[8,56,800]{2,1,0:T(8,128)(2,1)S(1)}, bf16[8,56,800]{2,1,0:T(8,128)(2,1)S(1)}) custom-call(bf16[64,24,128]{2,1,0:T(8,128)(2,1)S(1)} %all-to-all-done.recv_ref, bf16[2,400,800]{2,1,0:T(8,128)(2,1)S(1)} %get-tuple-element.14.weight_ref, ...), custom_call_target="tpu_custom_call" | custom-call | flops 700000000 | bytes 5242880 | tf_op jit(solution)/shard_map/pallas_call | solution.py:24
  78.9 5.1 %collective-permute-start.10 = (bf16[8,56,800]{2,1,0:T(8,128)(2,1)S(1)}, bf16[8,56,800]{2,1,0:T(8,128)(2,1)S(1)}, u32[]{:S(2)}, u32[]{:S(2)}) collective-permute-start(bf16[8,56,800]{2,1,0:T(8,128)(2,1)S(1)} %get-tuple-element.19), channel_id=1, source_target_pairs={{0,256},{256,0},{1,257},{257,1},{2,258},{258,2},{3,259},{259,3},{4... | collective-permute-start | bytes 2150408 | tf_op jit(solution)/shard_map/ppermute | solution.py:250
  84.0 1.9 %collective-permute-done.10 = bf16[8,56,800]{2,1,0:T(8,128)(2,1)S(1)} collective-permute-done((bf16[8,56,800]{2,1,0:T(8,128)(2,1)S(1)}, bf16[8,56,800]{2,1,0:T(8,128)(2,1)S(1)}, u32[]{:S(2)}, u32[]{:S(2)}) %collective-permute-start.10) | collective-permute-done | bytes 716832 | tf_op jit(solution)/shard_map/ppermute | solution.py:250
  85.9 0.2 add_convert_fusion
  86.1 16.2 %all_to_all.20 = bf16[8,56,800]{2,1,0:T(8,128)(2,1)S(1)} all-to-all(bf16[8,56,800]{2,1,0:T(8,128)(2,1)S(1)} %add_convert_fusion), channel_id=1, replica_groups=mesh['rep'=2,'z'=8,'yh'=4,'yl'=2,'x'=4] {'yl','x'}, dimensions={0} | all-to-all | bytes 1433600 | tf_op jit(solution)/shard_map/all_to_all | solution.py:252
  102.3 0.1 reduce_sum.24
  102.5 15.8 %all_to_all.21 = bf16[32,16,128]{2,1,0:T(8,128)(2,1)S(1)} all-to-all(bf16[32,16,128]{2,1,0:T(8,128)(2,1)S(1)} %bitcast.49), channel_id=1, replica_groups=mesh['rep'=2,'z'=8,'yh'=4,'yl'=2,'x'=4] {'z','yh'}, dimensions={0} | all-to-all | bytes 262144 | tf_op jit(solution)/shard_map/all_to_all | solution.py:256
  118.4 21.1 %all_to_all.22 = bf16[64,16,128]{2,1,0:T(8,128)(2,1)S(1)} all-to-all(bf16[64,16,128]{2,1,0:T(8,128)(2,1)S(1)} %broadcast_in_dim.14), channel_id=1, replica_groups=mesh['rep'=2,'z'=8,'yh'=4,'yl'=2,'x'=4] {'rep','z','yh'}, dimensions={0} | all-to-all | bytes 524288 | tf_op jit(solution)/shard_map/all_to_all | solution.py:258
  139.6 0.1 copy.17
  139.7 0.1 copy.16
  139.8 0.8 slice_convert_fusion
  (12 shorter events, 0.3 us)
Async XLA Ops:
  7.2 38.9 %copy-start.1 = (bf16[32,25,512]{2,0,1:T(8,128)(2,1)S(1)}, bf16[32,25,512]{2,0,1:T(8,128)(2,1)}, u32[]{:S(2)}) copy-start(bf16[32,25,512]{2,0,1:T(8,128)(2,1)} %param.8) | copy-start | bytes 2457604
  7.2 54.6 %all-gather.3.cloned.1.call-start = ((), (), s32[]{:S(2)}) async-start(), calls=%async_computation.4 | async-start | bytes 2322432 | tf_op jit(solution)/shard_map/all_gather | solution.py:196
  9.9 36.2 %copy-start.2 = (bf16[13,24,512]{2,1,0:T(8,128)(2,1)S(1)}, bf16[13,24,512]{2,1,0:T(8,128)(2,1)}, u32[]{:S(2)}) copy-start(bf16[13,24,512]{2,1,0:T(8,128)(2,1)} %get-tuple-element.12.rest_0_) | copy-start | bytes 958468
  10.0 14.8 %collective-permute-start.1 = (bf16[13,24,512]{2,1,0:T(8,128)(2,1)}, bf16[13,24,512]{2,1,0:T(8,128)(2,1)S(1)}, u32[]{:S(2)}, u32[]{:S(2)}) collective-permute-start(bf16[13,24,512]{2,1,0:T(8,128)(2,1)} %get-tuple-element.12.rest_0_), channel_id=1, source_target_pairs={{0,1},{1,0},{2,3},{3,2},{4,5},{5,4},{6,7},{7,6},{8,9},{9,8},{10,11... | collective-permute-start | bytes 958472 | tf_op jit(solution)/shard_map/ppermute | solution.py:200
  14.0 9.0 %collective-permute-start.9 = (bf16[9,56,128]{2,1,0:T(8,128)(2,1)}, bf16[9,56,128]{2,1,0:T(8,128)(2,1)S(1)}, u32[]{:S(2)}, u32[]{:S(2)}) collective-permute-start(bf16[9,56,128]{2,1,0:T(8,128)(2,1)} %get-tuple-element.13), channel_id=1, source_target_pairs={{0,4},{4,0},{1,5},{5,1},{2,6},{6,2},{3,7},{7,3},{8,12},{12,8},{9,1... | collective-permute-start | bytes 387080 | tf_op jit(solution)/shard_map/ppermute | solution.py:195
  17.3 10.3 %collective-permute-start.3 = (bf16[13,24,512]{2,1,0:T(8,128)(2,1)}, bf16[13,24,512]{2,1,0:T(8,128)(2,1)S(1)}, u32[]{:S(2)}, u32[]{:S(2)}) collective-permute-start(bf16[13,24,512]{2,1,0:T(8,128)(2,1)} %get-tuple-element.12.rest_0_), channel_id=1, source_target_pairs={{0,3},{1,2},{2,1},{3,0},{4,7},{5,6},{6,5},{7,4},{8,11},{9,10},{10,... | collective-permute-start | bytes 958472 | tf_op jit(solution)/shard_map/ppermute | solution.py:201
  21.0 25.1 %collective-permute-start = (bf16[25,32,512]{2,1,0:T(8,128)(2,1)}, bf16[25,32,512]{2,1,0:T(8,128)(2,1)S(1)}, u32[]{:S(2)}, u32[]{:S(2)}) collective-permute-start(bf16[25,32,512]{2,1,0:T(8,128)(2,1)} %bitcast.44), channel_id=1, source_target_pairs={{0,4},{4,0},{1,5},{5,1},{2,6},{6,2},{3,7},{7,3},{8,12},{12,8},{9,1... | collective-permute-start | bytes 2457608 | tf_op jit(solution)/shard_map/ppermute | solution.py:173
  24.8 17.8 %collective-permute-start.2 = (bf16[7,24,512]{2,1,0:T(8,128)(2,1)S(1)}, bf16[7,24,512]{2,1,0:T(8,128)(2,1)S(1)}, u32[]{:S(2)}, u32[]{:S(2)}) collective-permute-start(bf16[7,24,512]{2,1,0:T(8,128)(2,1)S(1)} %slice.24), channel_id=1, source_target_pairs={{0,3},{1,2},{2,1},{3,0},{4,7},{5,6},{6,5},{7,4},{8,11},{9,10},{10,... | collective-permute-start | bytes 516104 | tf_op jit(solution)/shard_map/ppermute | solution.py:203
  27.6 12.5 %collective-permute-start.4 = (bf16[6,24,512]{2,1,0:T(8,128)(2,1)S(1)}, bf16[6,24,512]{2,1,0:T(8,128)(2,1)S(1)}, u32[]{:S(2)}, u32[]{:S(2)}) collective-permute-start(bf16[6,24,512]{2,1,0:T(8,128)(2,1)S(1)} %slice.25), channel_id=1, source_target_pairs={{0,1},{1,0},{2,3},{3,2},{4,5},{5,4},{6,7},{7,6},{8,9},{9,8},{10,11... | collective-permute-start | bytes 442376 | tf_op jit(solution)/shard_map/ppermute | solution.py:204
  29.5 15.0 %collective-permute-start.5 = (bf16[13,24,512]{2,1,0:T(8,128)(2,1)}, bf16[13,24,512]{2,1,0:T(8,128)(2,1)S(1)}, u32[]{:S(2)}, u32[]{:S(2)}) collective-permute-start(bf16[13,24,512]{2,1,0:T(8,128)(2,1)} %get-tuple-element.12.rest_0_), channel_id=1, source_target_pairs={{0,256},{256,0},{1,257},{257,1},{2,258},{258,2},{3,259},{259,3},{4... | collective-permute-start | bytes 958472 | tf_op jit(solution)/shard_map/ppermute | solution.py:202
  38.2 6.3 %collective-permute-start.6 = (bf16[13,24,512]{2,1,0:T(8,128)(2,1)S(1)}, bf16[13,24,512]{2,1,0:T(8,128)(2,1)S(1)}, u32[]{:S(2)}, u32[]{:S(2)}) collective-permute-start(bf16[13,24,512]{2,1,0:T(8,128)(2,1)S(1)} %collective-permute-done.1.rest_1_), channel_id=1, source_target_pairs={{0,256},{256,0},{1,257},{257,1},{2,258},{258,2},{3,259},{259,3},{4... | collective-permute-start | bytes 958472 | tf_op jit(solution)/shard_map/ppermute | solution.py:205
  40.1 4.4 %collective-permute-start.8 = (bf16[13,24,512]{2,1,0:T(8,128)(2,1)S(1)}, bf16[13,24,512]{2,1,0:T(8,128)(2,1)S(1)}, u32[]{:S(2)}, u32[]{:S(2)}) collective-permute-start(bf16[13,24,512]{2,1,0:T(8,128)(2,1)S(1)} %collective-permute-done.3.rest_4_), channel_id=1, source_target_pairs={{0,256},{256,0},{1,257},{257,1},{2,258},{258,2},{3,259},{259,3},{4... | collective-permute-start | bytes 958472 | tf_op jit(solution)/shard_map/ppermute | solution.py:206
  42.6 3.5 %collective-permute-start.7 = (bf16[13,24,512]{2,1,0:T(8,128)(2,1)S(1)}, bf16[13,24,512]{2,1,0:T(8,128)(2,1)S(1)}, u32[]{:S(2)}, u32[]{:S(2)}) collective-permute-start(bf16[13,24,512]{2,1,0:T(8,128)(2,1)S(1)} %pad_maximum_fusion), channel_id=1, source_target_pairs={{0,256},{256,0},{1,257},{257,1},{2,258},{258,2},{3,259},{259,3},{4... | collective-permute-start | bytes 958472 | tf_op jit(solution)/shard_map/ppermute | solution.py:208
  49.2 27.1 %copy-start.3 = (bf16[1,400,192]{1,2,0:T(8,128)(2,1)S(1)}, bf16[1,400,192]{1,2,0:T(8,128)(2,1)}, u32[]{:S(2)}) copy-start(bf16[1,400,192]{1,2,0:T(8,128)(2,1)} %param.14) | copy-start | bytes 460804
  49.2 27.1 %copy-start.4 = (bf16[1,400,192]{1,2,0:T(8,128)(2,1)S(1)}, bf16[1,400,192]{1,2,0:T(8,128)(2,1)}, u32[]{:S(2)}) copy-start(bf16[1,400,192]{1,2,0:T(8,128)(2,1)} %param.15) | copy-start | bytes 460804
  49.2 27.1 %all-to-all-start = ((bf16[64,24,128]{2,1,0:T(8,128)(2,1)}), bf16[64,24,128]{2,1,0:T(8,128)(2,1)S(1)}, u32[]{:S(2)}, u32[]{:S(2)}) async-start(bf16[64,24,128]{2,1,0:T(8,128)(2,1)} %shard_map.112), calls=%async_computation | async-start | bytes 786432 | tf_op jit(solution)/shard_map/all_to_all | solution.py:221
  61.8 1.6 %copy-start = (bf16[16,9,56,128]{3,2,1,0:T(8,128)(2,1)S(1)}, bf16[16,9,56,128]{3,2,1,0:T(8,128)(2,1)}, u32[]{:S(2)}) copy-start(bf16[16,9,56,128]{3,2,1,0:T(8,128)(2,1)} %all-gather.3.cloned.1.call-done) | copy-start | bytes 6193156
  78.9 7.0 %collective-permute-start.10 = (bf16[8,56,800]{2,1,0:T(8,128)(2,1)S(1)}, bf16[8,56,800]{2,1,0:T(8,128)(2,1)S(1)}, u32[]{:S(2)}, u32[]{:S(2)}) collective-permute-start(bf16[8,56,800]{2,1,0:T(8,128)(2,1)S(1)} %get-tuple-element.19), channel_id=1, source_target_pairs={{0,256},{256,0},{1,257},{257,1},{2,258},{258,2},{3,259},{259,3},{4... | collective-permute-start | bytes 2150408 | tf_op jit(solution)/shard_map/ppermute | solution.py:250
Sparse Core Ops, SparseCore 0:
  24.9 34.7 all-gather.2

commit v12 on v11

--- a/solution.py
+++ b/solution.py
@@ -215,7 +215,7 @@
         [emb, emb_y] + mine + other,
         [pltpu.VMEM((2, 768, 128), F32)],
         limit=SOME,
-        flops=23_000_000_000,
+        flops=24_000_000_000,
         size=5 << 20,
     )
     recv = lax.all_to_all(chunks, ("yl",) + TAB, 0, 0, tiled=True)

time: 148 us -> 148 us (level)
    all_to_all x1, waiting for transfers between devices: 12.4 us -> 9.56 us  [per_device(): recv = lax.all_to_all(chunks, ('yl',) + TAB, 0, 0, tiled=True)]
    all_gather x1, waiting for transfers between devices: 0.02 us -> 1.93 us  [per_device(): small = lax.all_gather(pair, ('rep', 'x'))]
  transfers between devices with their start and end apart: 13 -> 13, of which waited for: 3 -> 4; matrix products, arithmetic and copies ran while one was open for 1% -> 1% of each run, Pallas kernels for 3% -> 3%
where the time goes in v12:
time: 148 us; the launch traced here: 147 us
  blocking collectives  53.1 us (36%)
  starting transfers between devices  51.2 us (35%)
  waiting for transfers between devices  15 us (10%)
  between operations  14.3 us (10%)
  Pallas kernels  8.97 us (6%)
  other arithmetic  2.8 us (2%)
  local copies, waits for them, and re-layouts  1.96 us (1%)
    all_to_all x1, blocking collectives, per_device(): lax.all_to_all(jnp.broadcast_to(whole[None], (64, 16, 128)), ('rep',) + T...  21.1 us
    all_to_all x1, blocking collectives, per_device(): shares = lax.all_to_all(pair, TP, 0, 0, tiled=True)  16.1 us
    all_to_all x1, blocking collectives, per_device(): parts = lax.all_to_all(tiles, TAB, 0, 0, tiled=True)  15.8 us
    all_to_all x1, starting transfers between devices, per_device(): recv = lax.all_to_all(chunks, ('yl',) + TAB, 0, 0, tiled=True)  12.5 us
    all_to_all x1, waiting for transfers between devices, per_device(): recv = lax.all_to_all(chunks, ('yl',) + TAB, 0, 0, tiled=True)  9.56 us
    ppermute x1, starting transfers between devices, per_device(): own_o = lax.ppermute(own, 'rep', SWAP)  8.67 us
    pallas_call x3, Pallas kernels, call(): pl.pallas_call(kernel, out_shape=outs, in_specs=[VM] * len(ins), out_spec...  6.26 us
    ppermute x1, starting transfers between devices, per_device(): got = lax.ppermute(send, 'rep', SWAP)  6 us
  transfers between devices with their start and end apart: 13, of which 4 were waited for; matrix products, arithmetic and copies ran while one was open for 1% of the time, Pallas kernels for 3%

profile of v12, /device:TPU:1, one launch (start us, length us, event | category | flops | bytes accessed | tf_op | source)
XLA Modules:
  0.0 147.4 jit_solution(5313789307927026698)
XLA Ops:
  7.2 0.0 copy-start.1
  7.2 0.0 all-gather.3.cloned.1.call-start
  7.2 2.7 %shard_map.111 = (bf16[13,24,512]{2,1,0:T(8,128)(2,1)}, bf16[9,56,128]{2,1,0:T(8,128)(2,1)}) custom-call(s32[25]{0:T(128)} %steps_ref.1, bf16[12,25,512]{2,1,0:T(8,128)(2,1)} %bitcast.56, bf16[50,800]{1,0:T(8,128)(2,1)} %fm_any.1, bf16[50,800]{1,0:T(8,128)(2,1)} %lcb_any.1, bf16[192,100]{1,0:T(8,128)(2,1)} %bitcast.59), custom_call_target="tpu_custom_call" | custom-call | flops 1048576 | bytes 2097152 | tf_op jit(solution)/shard_map/pallas_call | solution.py:177
  9.9 0.0 copy-start.2
  10.0 4.1 %collective-permute-start.1 = (bf16[13,24,512]{2,1,0:T(8,128)(2,1)}, bf16[13,24,512]{2,1,0:T(8,128)(2,1)S(1)}, u32[]{:S(2)}, u32[]{:S(2)}) collective-permute-start(bf16[13,24,512]{2,1,0:T(8,128)(2,1)} %get-tuple-element.12.rest_0_), channel_id=1, source_target_pairs={{0,1},{1,0},{2,3},{3,2},{4,5},{5,4},{6,7},{7,6},{8,9},{9,8},{10,11... | collective-permute-start | bytes 958472 | tf_op jit(solution)/shard_map/ppermute | solution.py:200
  14.0 3.7 %collective-permute-start.3 = (bf16[13,24,512]{2,1,0:T(8,128)(2,1)}, bf16[13,24,512]{2,1,0:T(8,128)(2,1)S(1)}, u32[]{:S(2)}, u32[]{:S(2)}) collective-permute-start(bf16[13,24,512]{2,1,0:T(8,128)(2,1)} %get-tuple-element.12.rest_0_), channel_id=1, source_target_pairs={{0,3},{1,2},{2,1},{3,0},{4,7},{5,6},{6,5},{7,4},{8,11},{9,10},{10,... | collective-permute-start | bytes 958472 | tf_op jit(solution)/shard_map/ppermute | solution.py:201
  17.8 3.2 %collective-permute-start.9 = (bf16[9,56,128]{2,1,0:T(8,128)(2,1)}, bf16[9,56,128]{2,1,0:T(8,128)(2,1)S(1)}, u32[]{:S(2)}, u32[]{:S(2)}) collective-permute-start(bf16[9,56,128]{2,1,0:T(8,128)(2,1)} %get-tuple-element.13), channel_id=1, source_target_pairs={{0,4},{4,0},{1,5},{5,1},{2,6},{6,2},{3,7},{7,3},{8,12},{12,8},{9,1... | collective-permute-start | bytes 387080 | tf_op jit(solution)/shard_map/ppermute | solution.py:195
  21.0 2.1 %collective-permute-start = (bf16[25,32,512]{2,1,0:T(8,128)(2,1)}, bf16[25,32,512]{2,1,0:T(8,128)(2,1)S(1)}, u32[]{:S(2)}, u32[]{:S(2)}) collective-permute-start(bf16[25,32,512]{2,1,0:T(8,128)(2,1)} %bitcast.44), channel_id=1, source_target_pairs={{0,4},{4,0},{1,5},{5,1},{2,6},{6,2},{3,7},{7,3},{8,12},{12,8},{9,1... | collective-permute-start | bytes 2457608 | tf_op jit(solution)/shard_map/ppermute | solution.py:173
  23.1 0.0 collective-permute-done.1.rest_1_
  23.1 2.8 %collective-permute-start.2 = (bf16[7,24,512]{2,1,0:T(8,128)(2,1)S(1)}, bf16[7,24,512]{2,1,0:T(8,128)(2,1)S(1)}, u32[]{:S(2)}, u32[]{:S(2)}) collective-permute-start(bf16[7,24,512]{2,1,0:T(8,128)(2,1)S(1)} %slice.24), channel_id=1, source_target_pairs={{0,3},{1,2},{2,1},{3,0},{4,7},{5,6},{6,5},{7,4},{8,11},{9,10},{10,... | collective-permute-start | bytes 516104 | tf_op jit(solution)/shard_map/ppermute | solution.py:203
  25.9 0.0 collective-permute-done.9
  25.9 1.6 %pad_maximum_fusion.1 = bf16[2,9,56,128]{3,2,1,0:T(8,128)(2,1)} fusion(bf16[1,9,56,128]{3,2,1,0:T(8,128)(2,1)S(1)} %bitcast.58, bf16[1,9,56,128]{3,2,1,0:T(8,128)(2,1)} %bitcast.57), kind=kLoop, calls=%fused_computation.2 | loop fusion | flops 129024 | bytes 516096 | tf_op jit(solution)/shard_map/stack | solution.py:195
  27.5 0.0 all-gather.3.cloned.1.call-update
  27.5 0.0 collective-permute-done.3.rest_4_
  27.6 1.9 %collective-permute-start.4 = (bf16[6,24,512]{2,1,0:T(8,128)(2,1)S(1)}, bf16[6,24,512]{2,1,0:T(8,128)(2,1)S(1)}, u32[]{:S(2)}, u32[]{:S(2)}) collective-permute-start(bf16[6,24,512]{2,1,0:T(8,128)(2,1)S(1)} %slice.25), channel_id=1, source_target_pairs={{0,1},{1,0},{2,3},{3,2},{4,5},{5,4},{6,7},{7,6},{8,9},{9,8},{10,11... | collective-permute-start | bytes 442376 | tf_op jit(solution)/shard_map/ppermute | solution.py:204
  29.5 8.7 %collective-permute-start.5 = (bf16[13,24,512]{2,1,0:T(8,128)(2,1)}, bf16[13,24,512]{2,1,0:T(8,128)(2,1)S(1)}, u32[]{:S(2)}, u32[]{:S(2)}) collective-permute-start(bf16[13,24,512]{2,1,0:T(8,128)(2,1)} %get-tuple-element.12.rest_0_), channel_id=1, source_target_pairs={{0,256},{256,0},{1,257},{257,1},{2,258},{258,2},{3,259},{259,3},{4... | collective-permute-start | bytes 958472 | tf_op jit(solution)/shard_map/ppermute | solution.py:202
  38.2 1.9 %collective-permute-start.6 = (bf16[13,24,512]{2,1,0:T(8,128)(2,1)S(1)}, bf16[13,24,512]{2,1,0:T(8,128)(2,1)S(1)}, u32[]{:S(2)}, u32[]{:S(2)}) collective-permute-start(bf16[13,24,512]{2,1,0:T(8,128)(2,1)S(1)} %collective-permute-done.1.rest_1_), channel_id=1, source_target_pairs={{0,256},{256,0},{1,257},{257,1},{2,258},{258,2},{3,259},{259,3},{4... | collective-permute-start | bytes 958472 | tf_op jit(solution)/shard_map/ppermute | solution.py:205
  40.1 0.0 collective-permute-done.4.rest_3_
  40.1 2.4 %collective-permute-start.8 = (bf16[13,24,512]{2,1,0:T(8,128)(2,1)S(1)}, bf16[13,24,512]{2,1,0:T(8,128)(2,1)S(1)}, u32[]{:S(2)}, u32[]{:S(2)}) collective-permute-start(bf16[13,24,512]{2,1,0:T(8,128)(2,1)S(1)} %collective-permute-done.3.rest_4_), channel_id=1, source_target_pairs={{0,256},{256,0},{1,257},{257,1},{2,258},{258,2},{3,259},{259,3},{4... | collective-permute-start | bytes 958472 | tf_op jit(solution)/shard_map/ppermute | solution.py:206
  42.5 0.0 collective-permute-done.2.rest_2_
  42.6 1.9 %collective-permute-start.7 = (bf16[13,24,512]{2,1,0:T(8,128)(2,1)S(1)}, bf16[13,24,512]{2,1,0:T(8,128)(2,1)S(1)}, u32[]{:S(2)}, u32[]{:S(2)}) collective-permute-start(bf16[13,24,512]{2,1,0:T(8,128)(2,1)S(1)} %pad_maximum_fusion), channel_id=1, source_target_pairs={{0,256},{256,0},{1,257},{257,1},{2,258},{258,2},{3,259},{259,3},{4... | collective-permute-start | bytes 958472 | tf_op jit(solution)/shard_map/ppermute | solution.py:208
  44.5 0.0 collective-permute-done.5.rest_5_
  44.5 0.0 collective-permute-done.6.rest_6_
  44.5 0.0 collective-permute-done.8.rest_8_
  44.5 1.6 %collective-permute-done.7.rest_7_ = bf16[13,24,512]{2,1,0:T(8,128)(2,1)S(1)} collective-permute-done((bf16[13,24,512]{2,1,0:T(8,128)(2,1)S(1)}, bf16[13,24,512]{2,1,0:T(8,128)(2,1)S(1)}, u32[]{:S(2)}, u32[]{:S(2)}) %collective-permute-start.7) | collective-permute-done | bytes 319520 | tf_op jit(solution)/shard_map/ppermute | solution.py:208
  46.1 0.0 collective-permute-done.emb_y_ref
  46.1 0.0 copy-done.1
  46.1 0.0 copy-done.2
  46.1 3.1 %shard_map.112 = bf16[64,24,128]{2,1,0:T(8,128)(2,1)} custom-call(bf16[25,32,512]{2,1,0:T(8,128)(2,1)S(1)} %bitcast.45, bf16[25,32,512]{2,1,0:T(8,128)(2,1)S(1)} %collective-permute-done.emb_y_ref, bf16[13,24,512]{2,1,0:T(8,128)(2,1)S(1)} %copy-done.2, bf16[13,24,512]{2,1,0:T(8,128)(2,1)S(1)} %collective-permute-done.1.rest_1_, ...), custom_call_target="tpu_custom_call" | custom-call | flops 24000000000 | bytes 5242880 | tf_op jit(solution)/shard_map/pallas_call | solution.py:24
  49.2 0.0 copy-start.3
  49.2 0.0 copy-start.4
  49.2 12.5 %all-to-all-start = ((bf16[64,24,128]{2,1,0:T(8,128)(2,1)}), bf16[64,24,128]{2,1,0:T(8,128)(2,1)S(1)}, u32[]{:S(2)}, u32[]{:S(2)}) async-start(bf16[64,24,128]{2,1,0:T(8,128)(2,1)} %shard_map.112), calls=%async_computation | async-start | bytes 786432 | tf_op jit(solution)/shard_map/all_to_all | solution.py:221
  61.7 1.9 %all-gather.3.cloned.1.call-done = bf16[16,9,56,128]{3,2,1,0:T(8,128)(2,1)} async-done(((bf16[2,9,56,128]{3,2,1,0:T(8,128)(2,1)}), bf16[16,9,56,128]{3,2,1,0:T(8,128)(2,1)}) %all-gather.3.cloned.1.call-update) | async-done | bytes 2064400 | tf_op jit(solution)/shard_map/all_gather | solution.py:196
  63.7 0.0 copy-start
  63.7 1.6 %copy-done = bf16[16,9,56,128]{3,2,1,0:T(8,128)(2,1)S(1)} copy-done((bf16[16,9,56,128]{3,2,1,0:T(8,128)(2,1)S(1)}, bf16[16,9,56,128]{3,2,1,0:T(8,128)(2,1)}, u32[]{:S(2)}) %copy-start) | copy-done | bytes 2064408
  65.3 0.6 shard_map.113
  65.9 9.6 %all-to-all-done.recv_ref = bf16[64,24,128]{2,1,0:T(8,128)(2,1)S(1)} async-done(((bf16[64,24,128]{2,1,0:T(8,128)(2,1)}), bf16[64,24,128]{2,1,0:T(8,128)(2,1)S(1)}, u32[]{:S(2)}, u32[]{:S(2)}) %all-to-all-start) | async-done | bytes 393248 | tf_op jit(solution)/shard_map/all_to_all | solution.py:221
  75.4 0.0 copy-done.3
  75.4 0.0 copy-done.4
  75.4 2.5 %shard_map.114 = (bf16[192,400]{1,0:T(8,128)(2,1)}, bf16[192,400]{1,0:T(8,128)(2,1)}, bf16[8,56,800]{2,1,0:T(8,128)(2,1)S(1)}, bf16[8,56,800]{2,1,0:T(8,128)(2,1)S(1)}) custom-call(bf16[64,24,128]{2,1,0:T(8,128)(2,1)S(1)} %all-to-all-done.recv_ref, bf16[2,400,800]{2,1,0:T(8,128)(2,1)S(1)} %get-tuple-element.14.weight_ref, ...), custom_call_target="tpu_custom_call" | custom-call | flops 700000000 | bytes 5242880 | tf_op jit(solution)/shard_map/pallas_call | solution.py:24
  78.0 6.0 %collective-permute-start.10 = (bf16[8,56,800]{2,1,0:T(8,128)(2,1)S(1)}, bf16[8,56,800]{2,1,0:T(8,128)(2,1)S(1)}, u32[]{:S(2)}, u32[]{:S(2)}) collective-permute-start(bf16[8,56,800]{2,1,0:T(8,128)(2,1)S(1)} %get-tuple-element.19), channel_id=1, source_target_pairs={{0,256},{256,0},{1,257},{257,1},{2,258},{258,2},{3,259},{259,3},{4... | collective-permute-start | bytes 2150408 | tf_op jit(solution)/shard_map/ppermute | solution.py:250
  84.0 1.9 %collective-permute-done.10 = bf16[8,56,800]{2,1,0:T(8,128)(2,1)S(1)} collective-permute-done((bf16[8,56,800]{2,1,0:T(8,128)(2,1)S(1)}, bf16[8,56,800]{2,1,0:T(8,128)(2,1)S(1)}, u32[]{:S(2)}, u32[]{:S(2)}) %collective-permute-start.10) | collective-permute-done | bytes 716832 | tf_op jit(solution)/shard_map/ppermute | solution.py:250
  85.9 0.2 add_convert_fusion
  86.1 16.1 %all_to_all.20 = bf16[8,56,800]{2,1,0:T(8,128)(2,1)S(1)} all-to-all(bf16[8,56,800]{2,1,0:T(8,128)(2,1)S(1)} %add_convert_fusion), channel_id=1, replica_groups=mesh['rep'=2,'z'=8,'yh'=4,'yl'=2,'x'=4] {'yl','x'}, dimensions={0} | all-to-all | bytes 1433600 | tf_op jit(solution)/shard_map/all_to_all | solution.py:252
  102.2 0.1 reduce_sum.24
  102.5 15.8 %all_to_all.21 = bf16[32,16,128]{2,1,0:T(8,128)(2,1)S(1)} all-to-all(bf16[32,16,128]{2,1,0:T(8,128)(2,1)S(1)} %bitcast.49), channel_id=1, replica_groups=mesh['rep'=2,'z'=8,'yh'=4,'yl'=2,'x'=4] {'z','yh'}, dimensions={0} | all-to-all | bytes 262144 | tf_op jit(solution)/shard_map/all_to_all | solution.py:256
  118.4 21.1 %all_to_all.22 = bf16[64,16,128]{2,1,0:T(8,128)(2,1)S(1)} all-to-all(bf16[64,16,128]{2,1,0:T(8,128)(2,1)S(1)} %broadcast_in_dim.14), channel_id=1, replica_groups=mesh['rep'=2,'z'=8,'yh'=4,'yl'=2,'x'=4] {'rep','z','yh'}, dimensions={0} | all-to-all | bytes 524288 | tf_op jit(solution)/shard_map/all_to_all | solution.py:258
  139.5 0.1 copy.17
  139.6 0.1 copy.16
  139.7 0.8 slice_convert_fusion
  (12 shorter events, 0.3 us)
Async XLA Ops:
  7.2 38.9 %copy-start.1 = (bf16[32,25,512]{2,0,1:T(8,128)(2,1)S(1)}, bf16[32,25,512]{2,0,1:T(8,128)(2,1)}, u32[]{:S(2)}) copy-start(bf16[32,25,512]{2,0,1:T(8,128)(2,1)} %param.8) | copy-start | bytes 2457604
  7.2 56.5 %all-gather.3.cloned.1.call-start = ((), (), s32[]{:S(2)}) async-start(), calls=%async_computation.4 | async-start | bytes 2322432 | tf_op jit(solution)/shard_map/all_gather | solution.py:196
  9.9 36.2 %copy-start.2 = (bf16[13,24,512]{2,1,0:T(8,128)(2,1)S(1)}, bf16[13,24,512]{2,1,0:T(8,128)(2,1)}, u32[]{:S(2)}) copy-start(bf16[13,24,512]{2,1,0:T(8,128)(2,1)} %get-tuple-element.12.rest_0_) | copy-start | bytes 958468
  10.0 13.1 %collective-permute-start.1 = (bf16[13,24,512]{2,1,0:T(8,128)(2,1)}, bf16[13,24,512]{2,1,0:T(8,128)(2,1)S(1)}, u32[]{:S(2)}, u32[]{:S(2)}) collective-permute-start(bf16[13,24,512]{2,1,0:T(8,128)(2,1)} %get-tuple-element.12.rest_0_), channel_id=1, source_target_pairs={{0,1},{1,0},{2,3},{3,2},{4,5},{5,4},{6,7},{7,6},{8,9},{9,8},{10,11... | collective-permute-start | bytes 958472 | tf_op jit(solution)/shard_map/ppermute | solution.py:200
  14.0 13.5 %collective-permute-start.3 = (bf16[13,24,512]{2,1,0:T(8,128)(2,1)}, bf16[13,24,512]{2,1,0:T(8,128)(2,1)S(1)}, u32[]{:S(2)}, u32[]{:S(2)}) collective-permute-start(bf16[13,24,512]{2,1,0:T(8,128)(2,1)} %get-tuple-element.12.rest_0_), channel_id=1, source_target_pairs={{0,3},{1,2},{2,1},{3,0},{4,7},{5,6},{6,5},{7,4},{8,11},{9,10},{10,... | collective-permute-start | bytes 958472 | tf_op jit(solution)/shard_map/ppermute | solution.py:201
  17.8 8.1 %collective-permute-start.9 = (bf16[9,56,128]{2,1,0:T(8,128)(2,1)}, bf16[9,56,128]{2,1,0:T(8,128)(2,1)S(1)}, u32[]{:S(2)}, u32[]{:S(2)}) collective-permute-start(bf16[9,56,128]{2,1,0:T(8,128)(2,1)} %get-tuple-element.13), channel_id=1, source_target_pairs={{0,4},{4,0},{1,5},{5,1},{2,6},{6,2},{3,7},{7,3},{8,12},{12,8},{9,1... | collective-permute-start | bytes 387080 | tf_op jit(solution)/shard_map/ppermute | solution.py:195
  21.0 25.1 %collective-permute-start = (bf16[25,32,512]{2,1,0:T(8,128)(2,1)}, bf16[25,32,512]{2,1,0:T(8,128)(2,1)S(1)}, u32[]{:S(2)}, u32[]{:S(2)}) collective-permute-start(bf16[25,32,512]{2,1,0:T(8,128)(2,1)} %bitcast.44), channel_id=1, source_target_pairs={{0,4},{4,0},{1,5},{5,1},{2,6},{6,2},{3,7},{7,3},{8,12},{12,8},{9,1... | collective-permute-start | bytes 2457608 | tf_op jit(solution)/shard_map/ppermute | solution.py:173
  23.1 19.4 %collective-permute-start.2 = (bf16[7,24,512]{2,1,0:T(8,128)(2,1)S(1)}, bf16[7,24,512]{2,1,0:T(8,128)(2,1)S(1)}, u32[]{:S(2)}, u32[]{:S(2)}) collective-permute-start(bf16[7,24,512]{2,1,0:T(8,128)(2,1)S(1)} %slice.24), channel_id=1, source_target_pairs={{0,3},{1,2},{2,1},{3,0},{4,7},{5,6},{6,5},{7,4},{8,11},{9,10},{10,... | collective-permute-start | bytes 516104 | tf_op jit(solution)/shard_map/ppermute | solution.py:203
  27.6 12.5 %collective-permute-start.4 = (bf16[6,24,512]{2,1,0:T(8,128)(2,1)S(1)}, bf16[6,24,512]{2,1,0:T(8,128)(2,1)S(1)}, u32[]{:S(2)}, u32[]{:S(2)}) collective-permute-start(bf16[6,24,512]{2,1,0:T(8,128)(2,1)S(1)} %slice.25), channel_id=1, source_target_pairs={{0,1},{1,0},{2,3},{3,2},{4,5},{5,4},{6,7},{7,6},{8,9},{9,8},{10,11... | collective-permute-start | bytes 442376 | tf_op jit(solution)/shard_map/ppermute | solution.py:204
  29.5 15.0 %collective-permute-start.5 = (bf16[13,24,512]{2,1,0:T(8,128)(2,1)}, bf16[13,24,512]{2,1,0:T(8,128)(2,1)S(1)}, u32[]{:S(2)}, u32[]{:S(2)}) collective-permute-start(bf16[13,24,512]{2,1,0:T(8,128)(2,1)} %get-tuple-element.12.rest_0_), channel_id=1, source_target_pairs={{0,256},{256,0},{1,257},{257,1},{2,258},{258,2},{3,259},{259,3},{4... | collective-permute-start | bytes 958472 | tf_op jit(solution)/shard_map/ppermute | solution.py:202
  38.2 6.3 %collective-permute-start.6 = (bf16[13,24,512]{2,1,0:T(8,128)(2,1)S(1)}, bf16[13,24,512]{2,1,0:T(8,128)(2,1)S(1)}, u32[]{:S(2)}, u32[]{:S(2)}) collective-permute-start(bf16[13,24,512]{2,1,0:T(8,128)(2,1)S(1)} %collective-permute-done.1.rest_1_), channel_id=1, source_target_pairs={{0,256},{256,0},{1,257},{257,1},{2,258},{258,2},{3,259},{259,3},{4... | collective-permute-start | bytes 958472 | tf_op jit(solution)/shard_map/ppermute | solution.py:205
  40.1 4.4 %collective-permute-start.8 = (bf16[13,24,512]{2,1,0:T(8,128)(2,1)S(1)}, bf16[13,24,512]{2,1,0:T(8,128)(2,1)S(1)}, u32[]{:S(2)}, u32[]{:S(2)}) collective-permute-start(bf16[13,24,512]{2,1,0:T(8,128)(2,1)S(1)} %collective-permute-done.3.rest_4_), channel_id=1, source_target_pairs={{0,256},{256,0},{1,257},{257,1},{2,258},{258,2},{3,259},{259,3},{4... | collective-permute-start | bytes 958472 | tf_op jit(solution)/shard_map/ppermute | solution.py:206
  42.6 3.5 %collective-permute-start.7 = (bf16[13,24,512]{2,1,0:T(8,128)(2,1)S(1)}, bf16[13,24,512]{2,1,0:T(8,128)(2,1)S(1)}, u32[]{:S(2)}, u32[]{:S(2)}) collective-permute-start(bf16[13,24,512]{2,1,0:T(8,128)(2,1)S(1)} %pad_maximum_fusion), channel_id=1, source_target_pairs={{0,256},{256,0},{1,257},{257,1},{2,258},{258,2},{3,259},{259,3},{4... | collective-permute-start | bytes 958472 | tf_op jit(solution)/shard_map/ppermute | solution.py:208
  49.2 26.2 %copy-start.3 = (bf16[1,400,192]{1,2,0:T(8,128)(2,1)S(1)}, bf16[1,400,192]{1,2,0:T(8,128)(2,1)}, u32[]{:S(2)}) copy-start(bf16[1,400,192]{1,2,0:T(8,128)(2,1)} %param.14) | copy-start | bytes 460804
  49.2 26.2 %copy-start.4 = (bf16[1,400,192]{1,2,0:T(8,128)(2,1)S(1)}, bf16[1,400,192]{1,2,0:T(8,128)(2,1)}, u32[]{:S(2)}) copy-start(bf16[1,400,192]{1,2,0:T(8,128)(2,1)} %param.15) | copy-start | bytes 460804
  49.2 26.2 %all-to-all-start = ((bf16[64,24,128]{2,1,0:T(8,128)(2,1)}), bf16[64,24,128]{2,1,0:T(8,128)(2,1)S(1)}, u32[]{:S(2)}, u32[]{:S(2)}) async-start(bf16[64,24,128]{2,1,0:T(8,128)(2,1)} %shard_map.112), calls=%async_computation | async-start | bytes 786432 | tf_op jit(solution)/shard_map/all_to_all | solution.py:221
  63.7 1.6 %copy-start = (bf16[16,9,56,128]{3,2,1,0:T(8,128)(2,1)S(1)}, bf16[16,9,56,128]{3,2,1,0:T(8,128)(2,1)}, u32[]{:S(2)}) copy-start(bf16[16,9,56,128]{3,2,1,0:T(8,128)(2,1)} %all-gather.3.cloned.1.call-done) | copy-start | bytes 6193156
  78.0 7.9 %collective-permute-start.10 = (bf16[8,56,800]{2,1,0:T(8,128)(2,1)S(1)}, bf16[8,56,800]{2,1,0:T(8,128)(2,1)S(1)}, u32[]{:S(2)}, u32[]{:S(2)}) collective-permute-start(bf16[8,56,800]{2,1,0:T(8,128)(2,1)S(1)} %get-tuple-element.19), channel_id=1, source_target_pairs={{0,256},{256,0},{1,257},{257,1},{2,258},{258,2},{3,259},{259,3},{4... | collective-permute-start | bytes 2150408 | tf_op jit(solution)/shard_map/ppermute | solution.py:250
Sparse Core Ops, SparseCore 0:
  27.7 35.9 all-gather.2

commit v13 on v10

--- a/solution.py
+++ b/solution.py
@@ -55,7 +55,7 @@
     for t in range(tables):
         width = jnp.where(table == t, widest // 8 * steps_ref[t], width)
     keep = columns < jnp.concatenate([width] * (widest // 128), axis=1)
-    rows_ref[...] = jnp.zeros_like(rows_ref)
+    rows_ref[:, 296:312, :] = jnp.zeros((4, 16, 128), F32)
     pack_ref[...] = jnp.zeros_like(pack_ref)
     copies[0].wait()
     for j in range(12):
@@ -116,7 +116,7 @@
                 slot = mine if k == 0 else 1 - mine
                 acc_ref[slot, pl.ds(t, samples, stride=last), :] = prod
     for k in range(2):
-        out_ref[k * samples : k * samples + samples] = acc_ref[k].reshape(samples, last, 128).astype(BF16)
+        out_ref[k * samples : k * samples + samples] = acc_ref[k, : samples * last, :].reshape(samples, last, 128).astype(BF16)
 
 
 def rows_kernel(recv_ref, weight_ref, mix_ref, fcot_ref, lcot_ref,
@@ -128,7 +128,7 @@
             scr_ref[yl, 25 * tab : 25 * tab + 24, :] = recv_ref[yl * 32 + tab].astype(F32)
         last = [pltpu.roll(scr_ref[yl, pl.ds(k, 32, stride=25), :], 116 + 4 * k, 1) for k in range(3)]
         scr_ref[yl, pl.ds(24, 32, stride=25), :] = jnp.where(place < 4, last[0], jnp.where(place < 8, last[1], last[2]))
-        gt_ref[yl] = scr_ref[yl].T
+        gt_ref[yl] = scr_ref[yl, :800, :].T
     for r in range(2):
         for yl in range(2):
             for spot in range(4):
@@ -186,7 +186,7 @@
             pltpu.VMEM(fm_weight.shape, BF16),
             pltpu.VMEM(lcb_weight.shape, BF16),
             pltpu.VMEM(mix_weight.shape[::-1], BF16),
-            pltpu.VMEM((4, 24 * pairs, 128), F32),
+            pltpu.VMEM((4, 400, 128), F32),
             pltpu.SemaphoreType.DMA((4,)),
         ],
         cost_estimate=pl.CostEstimate(flops=1 << 20, bytes_accessed=2 << 20, transcendentals=0),
@@ -211,7 +211,7 @@
         project_kernel,
         jax.ShapeDtypeStruct((64, 24, 128), BF16),
         [emb, emb_y] + mine + other,
-        [pltpu.VMEM((2, 768, 128), F32)],
+        [pltpu.VMEM((2, 800, 128), F32)],
         limit=SOME,
         flops=25_000_000_000,
         size=5 << 20,
@@ -234,7 +234,7 @@
         (branch_out, branch_out, partial, partial),
         [recv, weights, mix_full, fm_cot[0].T, lcb_cot[0].T],
         [
-            pltpu.VMEM((2, 800, 128), F32),
+            pltpu.VMEM((2, 832, 128), F32),
             pltpu.VMEM((2, 128, 800), F32),
             pltpu.VMEM((192, 800), F32),
             pltpu.VMEM((448, 192), F32),

time: 147 us -> 147 us (level)
  no operation moved by 1% of the time
where the time goes in v13:
time: 147 us; the launch traced here: 146 us
  starting transfers between devices  53.2 us (36%)
  blocking collectives  51.2 us (35%)
  waiting for transfers between devices  14.3 us (10%)
  between operations  14.3 us (10%)
  Pallas kernels  8.96 us (6%)
  local copies, waits for them, and re-layouts  2.94 us (2%)
    all_to_all x1, blocking collectives, per_device(): lax.all_to_all(jnp.broadcast_to(whole[None], (64, 16, 128)), ('rep',) + T...  20.6 us
    all_to_all x1, blocking collectives, per_device(): shares = lax.all_to_all(pair, TP, 0, 0, tiled=True)  15.4 us
    all_to_all x1, blocking collectives, per_device(): parts = lax.all_to_all(tiles, TAB, 0, 0, tiled=True)  15.2 us
    all_to_all x1, starting transfers between devices, per_device(): recv = lax.all_to_all(chunks, ('yl',) + TAB, 0, 0, tiled=True)  14.3 us
    all_to_all x1, waiting for transfers between devices, per_device(): recv = lax.all_to_all(chunks, ('yl',) + TAB, 0, 0, tiled=True)  9.26 us
    ppermute x1, starting transfers between devices, per_device(): own_o = lax.ppermute(own, 'rep', SWAP)  7.89 us
    ppermute x1, starting transfers between devices, per_device(): got = lax.ppermute(send, 'rep', SWAP)  7.1 us
    pallas_call x3, Pallas kernels, call(): pl.pallas_call(kernel, out_shape=outs, in_specs=[VM] * len(ins), out_spec...  6.24 us
  transfers between devices with their start and end apart: 12, of which 4 were waited for; matrix products, arithmetic and copies ran while one was open for 0% of the time, Pallas kernels for 3%

profile of v13, /device:TPU:1, one launch (start us, length us, event | category | flops | bytes accessed | tf_op | source)
XLA Modules:
  0.0 146.1 jit_solution(16133622131549971157)
XLA Ops:
  7.2 0.0 copy-start.1
  7.2 0.0 all-gather.3.cloned.1.call-start
  7.2 2.7 %shard_map.111 = (bf16[13,24,512]{2,1,0:T(8,128)(2,1)}, bf16[9,56,128]{2,1,0:T(8,128)(2,1)}) custom-call(s32[25]{0:T(128)} %steps_ref.1, bf16[12,25,512]{2,1,0:T(8,128)(2,1)} %bitcast.54, bf16[50,800]{1,0:T(8,128)(2,1)} %fm_any.1, bf16[50,800]{1,0:T(8,128)(2,1)} %lcb_any.1, bf16[192,100]{1,0:T(8,128)(2,1)} %bitcast.55), custom_call_target="tpu_custom_call" | custom-call | flops 1048576 | bytes 2097152 | tf_op jit(solution)/shard_map/pallas_call | solution.py:176
  9.9 3.9 %collective-permute-start.1 = (bf16[13,24,512]{2,1,0:T(8,128)(2,1)}, bf16[13,24,512]{2,1,0:T(8,128)(2,1)S(1)}, u32[]{:S(2)}, u32[]{:S(2)}) collective-permute-start(bf16[13,24,512]{2,1,0:T(8,128)(2,1)} %get-tuple-element.12.rest_0_), channel_id=1, source_target_pairs={{0,1},{1,0},{2,3},{3,2},{4,5},{5,4},{6,7},{7,6},{8,9},{9,8},{10,11... | collective-permute-start | bytes 958472 | tf_op jit(solution)/shard_map/ppermute | solution.py:198
  13.9 3.7 %collective-permute-start.3 = (bf16[13,24,512]{2,1,0:T(8,128)(2,1)}, bf16[13,24,512]{2,1,0:T(8,128)(2,1)S(1)}, u32[]{:S(2)}, u32[]{:S(2)}) collective-permute-start(bf16[13,24,512]{2,1,0:T(8,128)(2,1)} %get-tuple-element.12.rest_0_), channel_id=1, source_target_pairs={{0,3},{1,2},{2,1},{3,0},{4,7},{5,6},{6,5},{7,4},{8,11},{9,10},{10,... | collective-permute-start | bytes 958472 | tf_op jit(solution)/shard_map/ppermute | solution.py:199
  17.6 3.2 %collective-permute-start = (bf16[25,32,512]{2,1,0:T(8,128)(2,1)}, bf16[25,32,512]{2,1,0:T(8,128)(2,1)S(1)}, u32[]{:S(2)}, u32[]{:S(2)}) collective-permute-start(bf16[25,32,512]{2,1,0:T(8,128)(2,1)} %bitcast.42), channel_id=1, source_target_pairs={{0,4},{4,0},{1,5},{5,1},{2,6},{6,2},{3,7},{7,3},{8,12},{12,8},{9,1... | collective-permute-start | bytes 2457608 | tf_op jit(solution)/shard_map/ppermute | solution.py:172
  20.9 0.0 all-gather.3.cloned.1.call-update
  20.9 0.0 collective-permute-done.1.rest_1_
  20.9 4.8 %collective-permute-start.2 = (bf16[7,24,512]{2,1,0:T(8,128)(2,1)S(1)}, bf16[7,24,512]{2,1,0:T(8,128)(2,1)S(1)}, u32[]{:S(2)}, u32[]{:S(2)}) collective-permute-start(bf16[7,24,512]{2,1,0:T(8,128)(2,1)S(1)} %slice.24), channel_id=1, source_target_pairs={{0,3},{1,2},{2,1},{3,0},{4,7},{5,6},{6,5},{7,4},{8,11},{9,10},{10,... | collective-permute-start | bytes 516104 | tf_op jit(solution)/shard_map/ppermute | solution.py:201
  25.7 0.0 collective-permute-done.3.rest_4_
  25.7 1.9 %collective-permute-start.4 = (bf16[6,24,512]{2,1,0:T(8,128)(2,1)S(1)}, bf16[6,24,512]{2,1,0:T(8,128)(2,1)S(1)}, u32[]{:S(2)}, u32[]{:S(2)}) collective-permute-start(bf16[6,24,512]{2,1,0:T(8,128)(2,1)S(1)} %slice.25), channel_id=1, source_target_pairs={{0,1},{1,0},{2,3},{3,2},{4,5},{5,4},{6,7},{7,6},{8,9},{9,8},{10,11... | collective-permute-start | bytes 442376 | tf_op jit(solution)/shard_map/ppermute | solution.py:202
  27.7 7.9 %collective-permute-start.5 = (bf16[13,24,512]{2,1,0:T(8,128)(2,1)}, bf16[13,24,512]{2,1,0:T(8,128)(2,1)S(1)}, u32[]{:S(2)}, u32[]{:S(2)}) collective-permute-start(bf16[13,24,512]{2,1,0:T(8,128)(2,1)} %get-tuple-element.12.rest_0_), channel_id=1, source_target_pairs={{0,256},{256,0},{1,257},{257,1},{2,258},{258,2},{3,259},{259,3},{4... | collective-permute-start | bytes 958472 | tf_op jit(solution)/shard_map/ppermute | solution.py:200
  35.5 1.9 %collective-permute-start.6 = (bf16[13,24,512]{2,1,0:T(8,128)(2,1)S(1)}, bf16[13,24,512]{2,1,0:T(8,128)(2,1)S(1)}, u32[]{:S(2)}, u32[]{:S(2)}) collective-permute-start(bf16[13,24,512]{2,1,0:T(8,128)(2,1)S(1)} %collective-permute-done.1.rest_1_), channel_id=1, source_target_pairs={{0,256},{256,0},{1,257},{257,1},{2,258},{258,2},{3,259},{259,3},{4... | collective-permute-start | bytes 958472 | tf_op jit(solution)/shard_map/ppermute | solution.py:203
  37.5 0.0 collective-permute-done.4.rest_3_
  37.5 2.4 %collective-permute-start.8 = (bf16[13,24,512]{2,1,0:T(8,128)(2,1)S(1)}, bf16[13,24,512]{2,1,0:T(8,128)(2,1)S(1)}, u32[]{:S(2)}, u32[]{:S(2)}) collective-permute-start(bf16[13,24,512]{2,1,0:T(8,128)(2,1)S(1)} %collective-permute-done.3.rest_4_), channel_id=1, source_target_pairs={{0,256},{256,0},{1,257},{257,1},{2,258},{258,2},{3,259},{259,3},{4... | collective-permute-start | bytes 958472 | tf_op jit(solution)/shard_map/ppermute | solution.py:204
  39.9 0.0 collective-permute-done.2.rest_2_
  40.0 1.9 %collective-permute-start.7 = (bf16[13,24,512]{2,1,0:T(8,128)(2,1)S(1)}, bf16[13,24,512]{2,1,0:T(8,128)(2,1)S(1)}, u32[]{:S(2)}, u32[]{:S(2)}) collective-permute-start(bf16[13,24,512]{2,1,0:T(8,128)(2,1)S(1)} %pad_maximum_fusion), channel_id=1, source_target_pairs={{0,256},{256,0},{1,257},{257,1},{2,258},{258,2},{3,259},{259,3},{4... | collective-permute-start | bytes 958472 | tf_op jit(solution)/shard_map/ppermute | solution.py:206
  41.9 0.0 collective-permute-done.5.rest_5_
  41.9 0.0 collective-permute-done.6.rest_6_
  41.9 0.0 collective-permute-done.8.rest_8_
  41.9 1.6 %collective-permute-done.7.rest_7_ = bf16[13,24,512]{2,1,0:T(8,128)(2,1)S(1)} collective-permute-done((bf16[13,24,512]{2,1,0:T(8,128)(2,1)S(1)}, bf16[13,24,512]{2,1,0:T(8,128)(2,1)S(1)}, u32[]{:S(2)}, u32[]{:S(2)}) %collective-permute-start.7) | collective-permute-done | bytes 319520 | tf_op jit(solution)/shard_map/ppermute | solution.py:206
  43.5 0.0 collective-permute-done.emb_y_ref
  43.5 0.0 copy-done.1
  43.5 0.0 copy-start.2
  43.5 1.0 copy-done.2
  44.5 3.1 %shard_map.112 = bf16[64,24,128]{2,1,0:T(8,128)(2,1)} custom-call(bf16[25,32,512]{2,1,0:T(8,128)(2,1)S(1)} %bitcast.43, bf16[25,32,512]{2,1,0:T(8,128)(2,1)S(1)} %collective-permute-done.emb_y_ref, bf16[13,24,512]{2,1,0:T(8,128)(2,1)S(1)} %copy-done.2, bf16[13,24,512]{2,1,0:T(8,128)(2,1)S(1)} %collective-permute-done.1.rest_1_, ...), custom_call_target="tpu_custom_call" | custom-call | flops 24999999488 | bytes 5242880 | tf_op jit(solution)/shard_map/pallas_call | solution.py:24
  47.6 0.0 copy-start.3
  47.6 0.0 copy-start.4
  47.6 14.3 %all-to-all-start = ((bf16[64,24,128]{2,1,0:T(8,128)(2,1)}), bf16[64,24,128]{2,1,0:T(8,128)(2,1)S(1)}, u32[]{:S(2)}, u32[]{:S(2)}) async-start(bf16[64,24,128]{2,1,0:T(8,128)(2,1)} %shard_map.112), calls=%async_computation | async-start | bytes 786432 | tf_op jit(solution)/shard_map/all_to_all | solution.py:219
  61.9 1.6 %all-gather.3.cloned.1.call-done = bf16[144,56,128]{2,1,0:T(8,128)(2,1)} async-done(((bf16[9,56,128]{2,1,0:T(8,128)(2,1)}), bf16[144,56,128]{2,1,0:T(8,128)(2,1)}) %all-gather.3.cloned.1.call-update) | async-done | bytes 2064400 | tf_op jit(solution)/shard_map/all_gather | solution.py:194
  63.5 0.0 copy-start
  63.5 1.6 %copy-done = bf16[144,56,128]{2,1,0:T(8,128)(2,1)S(1)} copy-done((bf16[144,56,128]{2,1,0:T(8,128)(2,1)S(1)}, bf16[144,56,128]{2,1,0:T(8,128)(2,1)}, u32[]{:S(2)}) %copy-start) | copy-done | bytes 2064408
  65.1 0.6 shard_map.113
  65.7 9.3 %all-to-all-done.recv_ref = bf16[64,24,128]{2,1,0:T(8,128)(2,1)S(1)} async-done(((bf16[64,24,128]{2,1,0:T(8,128)(2,1)}), bf16[64,24,128]{2,1,0:T(8,128)(2,1)S(1)}, u32[]{:S(2)}, u32[]{:S(2)}) %all-to-all-start) | async-done | bytes 393248 | tf_op jit(solution)/shard_map/all_to_all | solution.py:219
  74.9 0.0 copy-done.3
  74.9 0.0 copy-done.4
  74.9 2.5 %shard_map.114 = (bf16[192,400]{1,0:T(8,128)(2,1)}, bf16[192,400]{1,0:T(8,128)(2,1)}, bf16[8,56,800]{2,1,0:T(8,128)(2,1)S(1)}, bf16[8,56,800]{2,1,0:T(8,128)(2,1)S(1)}) custom-call(bf16[64,24,128]{2,1,0:T(8,128)(2,1)S(1)} %all-to-all-done.recv_ref, bf16[2,400,800]{2,1,0:T(8,128)(2,1)S(1)} %get-tuple-element.14.weight_ref, ...), custom_call_target="tpu_custom_call" | custom-call | flops 700000000 | bytes 5242880 | tf_op jit(solution)/shard_map/pallas_call | solution.py:24
  77.5 7.1 %collective-permute-start.9 = (bf16[8,56,800]{2,1,0:T(8,128)(2,1)S(1)}, bf16[8,56,800]{2,1,0:T(8,128)(2,1)S(1)}, u32[]{:S(2)}, u32[]{:S(2)}) collective-permute-start(bf16[8,56,800]{2,1,0:T(8,128)(2,1)S(1)} %get-tuple-element.19), channel_id=1, source_target_pairs={{0,256},{256,0},{1,257},{257,1},{2,258},{258,2},{3,259},{259,3},{4... | collective-permute-start | bytes 2150408 | tf_op jit(solution)/shard_map/ppermute | solution.py:248
  84.6 1.9 %collective-permute-done.9 = bf16[8,56,800]{2,1,0:T(8,128)(2,1)S(1)} collective-permute-done((bf16[8,56,800]{2,1,0:T(8,128)(2,1)S(1)}, bf16[8,56,800]{2,1,0:T(8,128)(2,1)S(1)}, u32[]{:S(2)}, u32[]{:S(2)}) %collective-permute-start.9) | collective-permute-done | bytes 716832 | tf_op jit(solution)/shard_map/ppermute | solution.py:248
  86.5 0.2 add_convert_fusion
  86.7 15.4 %all_to_all.20 = bf16[8,56,800]{2,1,0:T(8,128)(2,1)S(1)} all-to-all(bf16[8,56,800]{2,1,0:T(8,128)(2,1)S(1)} %add_convert_fusion), channel_id=1, replica_groups=mesh['rep'=2,'z'=8,'yh'=4,'yl'=2,'x'=4] {'yl','x'}, dimensions={0} | all-to-all | bytes 1433600 | tf_op jit(solution)/shard_map/all_to_all | solution.py:250
  102.1 0.1 reduce_sum.24
  102.4 15.2 %all_to_all.21 = bf16[32,16,128]{2,1,0:T(8,128)(2,1)S(1)} all-to-all(bf16[32,16,128]{2,1,0:T(8,128)(2,1)S(1)} %bitcast.47), channel_id=1, replica_groups=mesh['rep'=2,'z'=8,'yh'=4,'yl'=2,'x'=4] {'z','yh'}, dimensions={0} | all-to-all | bytes 262144 | tf_op jit(solution)/shard_map/all_to_all | solution.py:254
  117.6 20.6 %all_to_all.22 = bf16[64,16,128]{2,1,0:T(8,128)(2,1)S(1)} all-to-all(bf16[64,16,128]{2,1,0:T(8,128)(2,1)S(1)} %broadcast_in_dim.14), channel_id=1, replica_groups=mesh['rep'=2,'z'=8,'yh'=4,'yl'=2,'x'=4] {'rep','z','yh'}, dimensions={0} | all-to-all | bytes 524288 | tf_op jit(solution)/shard_map/all_to_all | solution.py:256
  138.2 0.1 copy.17
  138.4 0.1 copy.16
  138.5 0.8 slice_convert_fusion
  (12 shorter events, 0.3 us)
Async XLA Ops:
  7.2 36.3 %copy-start.1 = (bf16[32,25,512]{2,0,1:T(8,128)(2,1)S(1)}, bf16[32,25,512]{2,0,1:T(8,128)(2,1)}, u32[]{:S(2)}) copy-start(bf16[32,25,512]{2,0,1:T(8,128)(2,1)} %param.8) | copy-start | bytes 2457604
  7.2 56.3 %all-gather.3.cloned.1.call-start = ((), (), s32[]{:S(2)}) async-start(), calls=%async_computation.4 | async-start | bytes 2193408 | tf_op jit(solution)/shard_map/all_gather | solution.py:194
  9.9 10.9 %collective-permute-start.1 = (bf16[13,24,512]{2,1,0:T(8,128)(2,1)}, bf16[13,24,512]{2,1,0:T(8,128)(2,1)S(1)}, u32[]{:S(2)}, u32[]{:S(2)}) collective-permute-start(bf16[13,24,512]{2,1,0:T(8,128)(2,1)} %get-tuple-element.12.rest_0_), channel_id=1, source_target_pairs={{0,1},{1,0},{2,3},{3,2},{4,5},{5,4},{6,7},{7,6},{8,9},{9,8},{10,11... | collective-permute-start | bytes 958472 | tf_op jit(solution)/shard_map/ppermute | solution.py:198
  13.9 11.8 %collective-permute-start.3 = (bf16[13,24,512]{2,1,0:T(8,128)(2,1)}, bf16[13,24,512]{2,1,0:T(8,128)(2,1)S(1)}, u32[]{:S(2)}, u32[]{:S(2)}) collective-permute-start(bf16[13,24,512]{2,1,0:T(8,128)(2,1)} %get-tuple-element.12.rest_0_), channel_id=1, source_target_pairs={{0,3},{1,2},{2,1},{3,0},{4,7},{5,6},{6,5},{7,4},{8,11},{9,10},{10,... | collective-permute-start | bytes 958472 | tf_op jit(solution)/shard_map/ppermute | solution.py:199
  17.6 25.8 %collective-permute-start = (bf16[25,32,512]{2,1,0:T(8,128)(2,1)}, bf16[25,32,512]{2,1,0:T(8,128)(2,1)S(1)}, u32[]{:S(2)}, u32[]{:S(2)}) collective-permute-start(bf16[25,32,512]{2,1,0:T(8,128)(2,1)} %bitcast.42), channel_id=1, source_target_pairs={{0,4},{4,0},{1,5},{5,1},{2,6},{6,2},{3,7},{7,3},{8,12},{12,8},{9,1... | collective-permute-start | bytes 2457608 | tf_op jit(solution)/shard_map/ppermute | solution.py:172
  20.9 19.0 %collective-permute-start.2 = (bf16[7,24,512]{2,1,0:T(8,128)(2,1)S(1)}, bf16[7,24,512]{2,1,0:T(8,128)(2,1)S(1)}, u32[]{:S(2)}, u32[]{:S(2)}) collective-permute-start(bf16[7,24,512]{2,1,0:T(8,128)(2,1)S(1)} %slice.24), channel_id=1, source_target_pairs={{0,3},{1,2},{2,1},{3,0},{4,7},{5,6},{6,5},{7,4},{8,11},{9,10},{10,... | collective-permute-start | bytes 516104 | tf_op jit(solution)/shard_map/ppermute | solution.py:201
  25.7 11.8 %collective-permute-start.4 = (bf16[6,24,512]{2,1,0:T(8,128)(2,1)S(1)}, bf16[6,24,512]{2,1,0:T(8,128)(2,1)S(1)}, u32[]{:S(2)}, u32[]{:S(2)}) collective-permute-start(bf16[6,24,512]{2,1,0:T(8,128)(2,1)S(1)} %slice.25), channel_id=1, source_target_pairs={{0,1},{1,0},{2,3},{3,2},{4,5},{5,4},{6,7},{7,6},{8,9},{9,8},{10,11... | collective-permute-start | bytes 442376 | tf_op jit(solution)/shard_map/ppermute | solution.py:202
  27.7 14.2 %collective-permute-start.5 = (bf16[13,24,512]{2,1,0:T(8,128)(2,1)}, bf16[13,24,512]{2,1,0:T(8,128)(2,1)S(1)}, u32[]{:S(2)}, u32[]{:S(2)}) collective-permute-start(bf16[13,24,512]{2,1,0:T(8,128)(2,1)} %get-tuple-element.12.rest_0_), channel_id=1, source_target_pairs={{0,256},{256,0},{1,257},{257,1},{2,258},{258,2},{3,259},{259,3},{4... | collective-permute-start | bytes 958472 | tf_op jit(solution)/shard_map/ppermute | solution.py:200
  35.5 6.3 %collective-permute-start.6 = (bf16[13,24,512]{2,1,0:T(8,128)(2,1)S(1)}, bf16[13,24,512]{2,1,0:T(8,128)(2,1)S(1)}, u32[]{:S(2)}, u32[]{:S(2)}) collective-permute-start(bf16[13,24,512]{2,1,0:T(8,128)(2,1)S(1)} %collective-permute-done.1.rest_1_), channel_id=1, source_target_pairs={{0,256},{256,0},{1,257},{257,1},{2,258},{258,2},{3,259},{259,3},{4... | collective-permute-start | bytes 958472 | tf_op jit(solution)/shard_map/ppermute | solution.py:203
  37.5 4.4 %collective-permute-start.8 = (bf16[13,24,512]{2,1,0:T(8,128)(2,1)S(1)}, bf16[13,24,512]{2,1,0:T(8,128)(2,1)S(1)}, u32[]{:S(2)}, u32[]{:S(2)}) collective-permute-start(bf16[13,24,512]{2,1,0:T(8,128)(2,1)S(1)} %collective-permute-done.3.rest_4_), channel_id=1, source_target_pairs={{0,256},{256,0},{1,257},{257,1},{2,258},{258,2},{3,259},{259,3},{4... | collective-permute-start | bytes 958472 | tf_op jit(solution)/shard_map/ppermute | solution.py:204
  40.0 3.5 %collective-permute-start.7 = (bf16[13,24,512]{2,1,0:T(8,128)(2,1)S(1)}, bf16[13,24,512]{2,1,0:T(8,128)(2,1)S(1)}, u32[]{:S(2)}, u32[]{:S(2)}) collective-permute-start(bf16[13,24,512]{2,1,0:T(8,128)(2,1)S(1)} %pad_maximum_fusion), channel_id=1, source_target_pairs={{0,256},{256,0},{1,257},{257,1},{2,258},{258,2},{3,259},{259,3},{4... | collective-permute-start | bytes 958472 | tf_op jit(solution)/shard_map/ppermute | solution.py:206
  43.5 1.0 copy-start.2
  47.6 27.3 %copy-start.3 = (bf16[1,400,192]{1,2,0:T(8,128)(2,1)S(1)}, bf16[1,400,192]{1,2,0:T(8,128)(2,1)}, u32[]{:S(2)}) copy-start(bf16[1,400,192]{1,2,0:T(8,128)(2,1)} %param.14) | copy-start | bytes 460804
  47.6 27.4 %copy-start.4 = (bf16[1,400,192]{1,2,0:T(8,128)(2,1)S(1)}, bf16[1,400,192]{1,2,0:T(8,128)(2,1)}, u32[]{:S(2)}) copy-start(bf16[1,400,192]{1,2,0:T(8,128)(2,1)} %param.15) | copy-start | bytes 460804
  47.6 27.3 %all-to-all-start = ((bf16[64,24,128]{2,1,0:T(8,128)(2,1)}), bf16[64,24,128]{2,1,0:T(8,128)(2,1)S(1)}, u32[]{:S(2)}, u32[]{:S(2)}) async-start(bf16[64,24,128]{2,1,0:T(8,128)(2,1)} %shard_map.112), calls=%async_computation | async-start | bytes 786432 | tf_op jit(solution)/shard_map/all_to_all | solution.py:219
  63.5 1.6 %copy-start = (bf16[144,56,128]{2,1,0:T(8,128)(2,1)S(1)}, bf16[144,56,128]{2,1,0:T(8,128)(2,1)}, u32[]{:S(2)}) copy-start(bf16[144,56,128]{2,1,0:T(8,128)(2,1)} %all-gather.3.cloned.1.call-done) | copy-start | bytes 6193156
  77.5 9.0 %collective-permute-start.9 = (bf16[8,56,800]{2,1,0:T(8,128)(2,1)S(1)}, bf16[8,56,800]{2,1,0:T(8,128)(2,1)S(1)}, u32[]{:S(2)}, u32[]{:S(2)}) collective-permute-start(bf16[8,56,800]{2,1,0:T(8,128)(2,1)S(1)} %get-tuple-element.19), channel_id=1, source_target_pairs={{0,256},{256,0},{1,257},{257,1},{2,258},{258,2},{3,259},{259,3},{4... | collective-permute-start | bytes 2150408 | tf_op jit(solution)/shard_map/ppermute | solution.py:248
Sparse Core Ops, SparseCore 0:
  21.0 42.4 all-gather.2
